TPU v7x, 32 devices: a whole 2x2x4 slice. The times are simulated.
32 devices in a mesh: groups: 2 (over y), gx: 4 (over z), gy: 2 (over x), gz: 2 (over core).
Axes of the slice: x: 2, y: 2, z: 4, core: 2. Of those that a mesh axis runs over, the one named last changes fastest.
Arguments:
- log_perm: float32 [32, 32, 1024], P(('groups', 'gx'), 'gy', 'gz'), parts along dimension 0, may hold values from -4 to 4
- source: float32 [32, 32, 1024], P(('groups', 'gx'), 'gy', 'gz'), parts along dimension 0, may hold values from -24 to 24
- low_bound: float32 [1], replicated, may hold values from 0.05 to 0.4
- high_bound: float32 [1], replicated, may hold values from 1.8 to 2.4
Outputs:
- fine_pressure: float32 [32, 32, 1024], P(('groups', 'gx'), 'gy', 'gz'), parts along dimension 0
- difference: float32 [32, 32, 1024], P(('groups', 'gx'), 'gy', 'gz'), parts along dimension 0
There are 2 independent parts, one for each index of `groups`. A program takes and returns all parts, laid end to end along the dimension named above; an argument that names none is the same for every part. Nothing has to cross between parts.
All inputs are finite; a program needn't handle non-finite values.
Results may differ from a plain program's by a relative error of at most 0.00002.
Values sent between devices are 32-bit elements; how exact they have to be, the bound alone decides.
No kernel may reach another device: no remote copies, remote signals or barrier semaphores. Data moves between devices by JAX's collectives and lax.ppermute only.
A program may use at most 64 MiB of HBM per device.

v0:
```python
import jax
import jax.numpy as jnp
from jax import lax
from jax.sharding import PartitionSpec as P

DEGREE = 3


storage_rate = 0.1


def extended_2(array, sides, width):
    for axis, dim in sides:
        peers, length = (lax.axis_size(axis), array.shape[dim])
        up = [(i, (i + 1) % peers) for i in range(peers - 1)]
        down = [(j, i) for i, j in up]
        last = lax.slice_in_dim(array, length - width, length, axis=dim)
        leading = lax.slice_in_dim(array, 0, width, axis=dim)
        before = lax.ppermute(last, axis, up)
        after = lax.ppermute(leading, axis, down)
        array = jnp.concatenate([before, array, after], axis=dim)
    return array


def harmonic(first_perm, second_perm, face_scale):
    total = first_perm + second_perm
    inside = total > 0.0
    safe_total = jnp.where(inside, total, 1.0)
    return jnp.where(inside, face_scale * 2.0 * first_perm * second_perm / safe_total, 0.0)


def coefficients(padded, face_scale, storage):
    centre = padded[1:-1, 1:-1, 1:-1]
    east_face = harmonic(centre, padded[2:, 1:-1, 1:-1], face_scale)
    west_face = harmonic(centre, padded[:-2, 1:-1, 1:-1], face_scale)
    north_face = harmonic(centre, padded[1:-1, 2:, 1:-1], face_scale)
    south_face = harmonic(centre, padded[1:-1, :-2, 1:-1], face_scale)
    upper_face = harmonic(centre, padded[1:-1, 1:-1, 2:], face_scale)
    lower_face = harmonic(centre, padded[1:-1, 1:-1, :-2], face_scale)
    diagonal = storage + east_face + west_face + north_face + south_face + upper_face + lower_face
    return (east_face, west_face, north_face, south_face, upper_face, lower_face, diagonal)


def operate(padded, face_terms):
    east_face, west_face, north_face, south_face, upper_face, lower_face, diagonal = face_terms
    centre = padded[1:-1, 1:-1, 1:-1]
    beside = east_face * padded[2:, 1:-1, 1:-1] + west_face * padded[:-2, 1:-1, 1:-1]
    beside = beside + north_face * padded[1:-1, 2:, 1:-1] + south_face * padded[1:-1, :-2, 1:-1]
    beside = beside + upper_face * padded[1:-1, 1:-1, 2:] + lower_face * padded[1:-1, 1:-1, :-2]
    return diagonal * centre - beside


def chebyshev_terms(lower_edge, upper_edge):
    centre_value = (upper_edge + lower_edge) * 0.5
    half_width = (upper_edge - lower_edge) * 0.5
    return (centre_value, half_width, centre_value / half_width)


def chebyshev_levels(
    exchange, padded_perms, sources, face_scales, storages, lower_edge, upper_edge
):
    term_sets = [
        coefficients(padded, scale, storage)
        for padded, scale, storage in zip(padded_perms, face_scales, storages)
    ]
    centre_value, half_width, ratio_sigma = chebyshev_terms(lower_edge, upper_edge)
    rho_now = 1.0 / ratio_sigma
    directions = [
        source_part / (centre_value * face_terms[6])
        for source_part, face_terms in zip(sources, term_sets)
    ]
    solutions = list(directions)
    residuals = list(sources)
    for iteration in range(DEGREE):
        padded_dirs = exchange(tuple(directions))
        rho_next = 1.0 / (2.0 * ratio_sigma - rho_now)
        face_terms = term_sets[0]
        residuals[0] = residuals[0] - operate(padded_dirs[0], face_terms)
        directions[0] = (
            rho_next * rho_now * directions[0]
            + 2.0 * rho_next / half_width * residuals[0] / face_terms[6]
        )
        solutions[0] = solutions[0] + directions[0]
        rho_now = rho_next
    return tuple(solutions)


def crop_one(field):
    return field[1:-1, 1:-1, 1:-1]


def refine(field):
    size_x, size_y, size_z = field.shape
    widened = jnp.broadcast_to(field[:, None, :, None, :, None], (size_x, 2, size_y, 2, size_z, 2))
    return widened.reshape(2 * size_x, 2 * size_y, 2 * size_z)


def coarse_single(fields):
    return (extended_2(fields[0], (("gx", 0), ("gy", 1), ("gz", 2)), 1),)


def deep_extend(layers):
    stacked = jnp.stack(layers)
    return extended_2(stacked, (("gx", 1), ("gy", 2), ("gz", 3)), DEGREE + 1)


def fine_deep(extended, lower_edge, upper_edge):
    face_terms = coefficients(extended[0], 1.0, storage_rate)
    centre_value, half_width, ratio_sigma = chebyshev_terms(lower_edge, upper_edge)
    rho_now = 1.0 / ratio_sigma
    residual = crop_one(extended[1])
    direction = residual / (centre_value * face_terms[6])
    solution = direction
    for iteration in range(DEGREE):
        face_terms = tuple((crop_one(member) for member in face_terms))
        residual = crop_one(residual) - operate(direction, face_terms)
        rho_next = 1.0 / (2.0 * ratio_sigma - rho_now)
        direction = (
            rho_next * rho_now * crop_one(direction)
            + 2.0 * rho_next / half_width * residual / face_terms[6]
        )
        solution = crop_one(solution) + direction
        rho_now = rho_next
    return solution


def shards(log_perm, source, low_bound, high_bound):
    lower_edge = low_bound[0]
    upper_edge = high_bound[0]
    cells_x, cells_y, cells_z = log_perm.shape
    perm_field = jnp.exp(log_perm)
    blocks = (cells_x // 2, 2, cells_y // 2, 2, cells_z // 2, 2)
    coarse_perm = jnp.exp(log_perm.reshape(blocks).mean(axis=(1, 3, 5)))
    coarse_source = source.reshape(blocks).sum(axis=(1, 3, 5))
    coarse_storage = 8.0 * storage_rate
    fine = fine_deep(deep_extend((perm_field, source)), lower_edge, upper_edge)
    coarse = chebyshev_levels(
        coarse_single,
        coarse_single((coarse_perm,)),
        (coarse_source,),
        (2.0,),
        (coarse_storage,),
        lower_edge,
        upper_edge,
    )[0]
    spread = refine(coarse)
    return (fine, fine - spread)


def solution(mesh):
    return jax.shard_map(
        shards,
        mesh=mesh,
        in_specs=(P(("groups", "gx"), "gy", "gz"), P(("groups", "gx"), "gy", "gz"), P(), P()),
        out_specs=(P(("groups", "gx"), "gy", "gz"), P(("groups", "gx"), "gy", "gz")),
        check_vma=False,
    )
```

profile of v0, /device:TPU:0, one launch (start us, length us, event | category | flops | bytes accessed | tf_op | source)
XLA Modules:
  0.0 140.4 jit_solution(17191093065461808956)
XLA Ops:
  0.6 10.5 %reshape.21 = f32[2,2,8,2,256,2]{5,4,3,2,1,0:T(8,128)} reshape(f32[4,16,512]{2,1,0:T(8,128)} %param.4) | data formatting | bytes 262144 | tf_op jit(solution)/shard_map/reshape | solution.py:133
  11.2 4.1 %reduce_sum.19 = f32[2,8,256]{2,1,0:T(8,128)S(1)} reduce(f32[2,2,8,2,256,2]{5,4,3,2,1,0:T(8,128)} %reshape.21, f32[]{:T(128)} %constant.9.clone.1), dimensions={1,3,5}, to_apply=%region_1.0 | reduce | flops 28672 | bytes 147460 | tf_op jit(solution)/shard_map/reduce_sum | solution.py:133
  15.3 1.3 collective-permute-start.6
  16.6 5.6 %collective-permute-start.7 = (f32[1,8,256]{2,1,0:T(8,128)S(1)}, f32[1,8,256]{2,1,0:T(8,128)S(1)}, u32[]{:S(2)}, u32[]{:S(2)}) collective-permute-start(f32[1,8,256]{2,1,0:T(8,128)S(1)} %get-tuple-element.52), channel_id=1, source_target_pairs={{0,4},{4,8},{8,12},{1,5},{5,9},{9,13},{2,6},{6,10},{10,14},{3,7},{... | collective-permute-start | bytes 24584 | tf_op jit(solution)/shard_map/ppermute | solution.py:19
  22.1 1.3 collective-permute-done.7
  24.8 4.5 %collective-permute-start.9 = (f32[4,1,256]{2,1,0:T(1,128)S(1)}, f32[4,1,256]{2,1,0:T(1,128)S(1)}, u32[]{:S(2)}, u32[]{:S(2)}) collective-permute-start(f32[4,1,256]{2,1,0:T(1,128)S(1)} %get-tuple-element.44), channel_id=1, source_target_pairs={{0,2},{1,3},{4,6},{5,7},{8,10},{9,11},{12,14},{13,15},{16,18},{17,... | collective-permute-start | bytes 12296 | tf_op jit(solution)/shard_map/ppermute | solution.py:19
  29.3 9.8 %reshape.20 = f32[2,2,8,2,256,2]{5,4,3,2,1,0:T(8,128)} reshape(f32[4,16,512]{2,1,0:T(8,128)S(1)} %copy-done) | data formatting | bytes 262144 | tf_op jit(solution)/shard_map/reshape | solution.py:134
  39.1 4.1 %reduce_sum.18 = f32[2,8,256]{2,1,0:T(8,128)S(1)} reduce(f32[2,2,8,2,256,2]{5,4,3,2,1,0:T(8,128)} %reshape.20, f32[]{:T(128)} %constant.9.clone.1), dimensions={1,3,5}, to_apply=%region_0.0 | reduce | flops 28672 | bytes 147460 | tf_op jit(solution)/shard_map/reduce_sum | solution.py:134
  45.9 3.0 %collective-permute-start.11 = (f32[4,10,1]{2,1,0:T(8,128)S(1)}, f32[4,10,1]{2,1,0:T(8,128)S(1)}, u32[]{:S(2)}, u32[]{:S(2)}) collective-permute-start(f32[4,10,1]{2,1,0:T(8,128)S(1)} %get-tuple-element.36), channel_id=1, source_target_pairs={{0,1},{2,3},{4,5},{6,7},{8,9},{10,11},{12,13},{14,15},{16,17},{18,... | collective-permute-start | bytes 488 | tf_op jit(solution)/shard_map/ppermute | solution.py:19
  49.9 1.3 collective-permute-start.12
  51.2 4.8 %collective-permute-start.13 = (f32[1,8,256]{2,1,0:T(8,128)S(1)}, f32[1,8,256]{2,1,0:T(8,128)S(1)}, u32[]{:S(2)}, u32[]{:S(2)}) collective-permute-start(f32[1,8,256]{2,1,0:T(8,128)S(1)} %get-tuple-element.50), channel_id=1, source_target_pairs={{0,4},{4,8},{8,12},{1,5},{5,9},{9,13},{2,6},{6,10},{10,14},{3,7},{... | collective-permute-start | bytes 24584 | tf_op jit(solution)/shard_map/ppermute | solution.py:19
  56.0 1.3 collective-permute-done.13
  58.7 4.5 %collective-permute-start.15 = (f32[4,1,256]{2,1,0:T(1,128)S(1)}, f32[4,1,256]{2,1,0:T(1,128)S(1)}, u32[]{:S(2)}, u32[]{:S(2)}) collective-permute-start(f32[4,1,256]{2,1,0:T(1,128)S(1)} %get-tuple-element.42), channel_id=1, source_target_pairs={{0,2},{1,3},{4,6},{5,7},{8,10},{9,11},{12,14},{13,15},{16,18},{17,... | collective-permute-start | bytes 12296 | tf_op jit(solution)/shard_map/ppermute | solution.py:19
  65.9 1.3 collective-permute-start.16
  67.3 1.7 %collective-permute-done.16 = f32[4,10,1]{2,1,0:T(8,128)S(1)} collective-permute-done((f32[4,10,1]{2,1,0:T(8,128)S(1)}, f32[4,10,1]{2,1,0:T(8,128)S(1)}, u32[]{:S(2)}, u32[]{:S(2)}) %collective-permute-start.16) | collective-permute-done | bytes 192 | tf_op jit(solution)/shard_map/ppermute | solution.py:20
  69.1 1.3 collective-permute-start.18
  70.4 4.8 %collective-permute-start.19 = (f32[1,8,256]{2,1,0:T(8,128)S(1)}, f32[1,8,256]{2,1,0:T(8,128)S(1)}, u32[]{:S(2)}, u32[]{:S(2)}) collective-permute-start(f32[1,8,256]{2,1,0:T(8,128)S(1)} %get-tuple-element.48), channel_id=1, source_target_pairs={{0,4},{4,8},{8,12},{1,5},{5,9},{9,13},{2,6},{6,10},{10,14},{3,7},{... | collective-permute-start | bytes 24584 | tf_op jit(solution)/shard_map/ppermute | solution.py:19
  75.3 1.3 collective-permute-done.19
  77.9 4.5 %collective-permute-start.21 = (f32[4,1,256]{2,1,0:T(1,128)S(1)}, f32[4,1,256]{2,1,0:T(1,128)S(1)}, u32[]{:S(2)}, u32[]{:S(2)}) collective-permute-start(f32[4,1,256]{2,1,0:T(1,128)S(1)} %get-tuple-element.40), channel_id=1, source_target_pairs={{0,2},{1,3},{4,6},{5,7},{8,10},{9,11},{12,14},{13,15},{16,18},{17,... | collective-permute-start | bytes 12296 | tf_op jit(solution)/shard_map/ppermute | solution.py:19
  83.8 4.8 %collective-permute-start = (f32[2,4,16,512]{3,2,1,0:T(8,128)S(1)}, f32[2,4,16,512]{3,2,1,0:T(8,128)S(1)}, u32[]{:S(2)}, u32[]{:S(2)}) collective-permute-start(f32[2,4,16,512]{3,2,1,0:T(8,128)S(1)} %pad_maximum_fusion.7), channel_id=1, source_target_pairs={{0,4},{4,8},{8,12},{1,5},{5,9},{9,13},{2,6},{6,10},{10,14},{3,7},{... | collective-permute-start | bytes 786440 | tf_op jit(solution)/shard_map/ppermute | solution.py:19
  91.4 1.7 %collective-permute-done.22 = f32[4,10,1]{2,1,0:T(8,128)S(1)} collective-permute-done((f32[4,10,1]{2,1,0:T(8,128)S(1)}, f32[4,10,1]{2,1,0:T(8,128)S(1)}, u32[]{:S(2)}, u32[]{:S(2)}) %collective-permute-start.22) | collective-permute-done | bytes 192 | tf_op jit(solution)/shard_map/ppermute | solution.py:20
  94.6 4.5 %collective-permute-start.25 = (f32[1,8,256]{2,1,0:T(8,128)S(1)}, f32[1,8,256]{2,1,0:T(8,128)S(1)}, u32[]{:S(2)}, u32[]{:S(2)}) collective-permute-start(f32[1,8,256]{2,1,0:T(8,128)S(1)} %get-tuple-element.46), channel_id=1, source_target_pairs={{0,4},{4,8},{8,12},{1,5},{5,9},{9,13},{2,6},{6,10},{10,14},{3,7},{... | collective-permute-start | bytes 24584 | tf_op jit(solution)/shard_map/ppermute | solution.py:19
  99.2 1.3 collective-permute-done.25
  101.8 4.5 %collective-permute-start.27 = (f32[4,1,256]{2,1,0:T(1,128)S(1)}, f32[4,1,256]{2,1,0:T(1,128)S(1)}, u32[]{:S(2)}, u32[]{:S(2)}) collective-permute-start(f32[4,1,256]{2,1,0:T(1,128)S(1)} %get-tuple-element.38), channel_id=1, source_target_pairs={{0,2},{1,3},{4,6},{5,7},{8,10},{9,11},{12,14},{13,15},{16,18},{17,... | collective-permute-start | bytes 12296 | tf_op jit(solution)/shard_map/ppermute | solution.py:19
  109.1 4.6 %collective-permute-start.2 = (f32[2,12,4,512]{3,2,1,0:T(4,128)S(1)}, f32[2,12,4,512]{3,2,1,0:T(4,128)S(1)}, u32[]{:S(2)}, u32[]{:S(2)}) collective-permute-start(f32[2,12,4,512]{3,2,1,0:T(4,128)S(1)} %get-tuple-element.27), channel_id=1, source_target_pairs={{0,2},{1,3},{4,6},{5,7},{8,10},{9,11},{12,14},{13,15},{16,18},{17,... | collective-permute-start | bytes 589832 | tf_op jit(solution)/shard_map/ppermute | solution.py:19
  118.3 3.2 %collective-permute-start.4 = (f32[2,12,24,4]{3,2,1,0:T(8,128)S(1)}, f32[2,12,24,4]{3,2,1,0:T(8,128)S(1)}, u32[]{:S(2)}, u32[]{:S(2)}) collective-permute-start(f32[2,12,24,4]{3,2,1,0:T(8,128)S(1)} %get-tuple-element.25), channel_id=1, source_target_pairs={{0,1},{2,3},{4,5},{6,7},{8,9},{10,11},{12,13},{14,15},{16,17},{18,... | collective-permute-start | bytes 27656 | tf_op jit(solution)/shard_map/ppermute | solution.py:19
  121.7 3.8 %broadcast_in_dim.38 = f32[2,2,8,2,256,2]{5,4,3,2,1,0:T(8,128)} broadcast(f32[2,8,256]{2,1,0:T(8,128)S(1)} %fusion.45), dimensions={0,2,4} | broadcast | bytes 147456 | tf_op jit(solution)/shard_map/broadcast_in_dim | solution.py:94
  125.6 6.9 %reshape.22 = f32[4,16,512]{2,1,0:T(8,128)S(1)} reshape(f32[2,2,8,2,256,2]{5,4,3,2,1,0:T(8,128)} %broadcast_in_dim.38) | data formatting | bytes 262144 | tf_op jit(solution)/shard_map/reshape | solution.py:95
  133.5 1.5 %slice_divide_fusion = (f32[10,22,518]{2,1,0:T(8,128)S(1)}, f32[10,22,518]{2,1,0:T(8,128)S(1)}, f32[10,22,518]{2,1,0:T(8,128)S(1)}, f32[10,22,518]{2,1,0:T(8,128...) fusion(f32[12,24,520]{2,1,0:T(8,128)S(1)} %get-tuple-element.24, ...), kind=kLoop, calls=%fused_computation.21 | loop fusion | flops 5128200 | bytes 7293444 | tf_op jit(solution)/shard_map/div | solution.py:112
  135.2 2.2 %divide_add_fusion = (f32[8,20,516]{2,1,0:T(8,128)S(1)}, f32[8,20,516]{2,1,0:T(8,128)S(1)}) fusion(f32[10,22,518]{2,1,0:T(8,128)S(1)} %get-tuple-element.16, f32[]{:T(128)S(6)} %div.108, f32[]{:T(128)S(6)} %mul.321, f32[10,22,518]{2,1,0:T(8,128)S(1)} %get-tuple-element.15, f32[10,22,518]{2,1,0:T(8,128)S(1)} %get-tuple-element.22, ...), kind=kLoop, calls=%fused_computation.36 | loop fusion | flops 1486080 | bytes 5614088 | tf_op jit(solution)/shard_map/add | solution.py:119
  137.3 1.6 %divide_add_fusion.1 = (f32[6,18,514]{2,1,0:T(8,128)S(1)}, f32[6,18,514]{2,1,0:T(8,128)S(1)}, f32[6,18,514]{2,1,0:T(8,128)S(1)}) fusion(f32[10,22,518]{2,1,0:T(8,128)S(1)} %get-tuple-element.16, f32[]{:T(128)S(6)} %div.111, f32[]{:T(128)S(6)} %mul.334, f32[8,20,516]{2,1,0:T(8,128)S(1)} %get-tuple-element.13, f32[10,22,518]{2,1,0:T(8,128)S(1)} %get-tuple-element.22, ...), kind=kLoop, calls=%fused_computation.50 | loop fusion | flops 999216 | bytes 3996872 | tf_op jit(solution)/shard_map/add | solution.py:119
  139.0 1.4 fusion.85
  (70 shorter events, 24.0 us)
Async XLA Ops:
  11.2 18.1 %copy-start = (f32[4,16,512]{2,1,0:T(8,128)S(1)}, f32[4,16,512]{2,1,0:T(8,128)}, u32[]{:S(2)}) copy-start(f32[4,16,512]{2,1,0:T(8,128)} %param.5) | copy-start | bytes 393220
  15.3 6.9 %collective-permute-start.6 = (f32[1,8,256]{2,1,0:T(8,128)S(1)}, f32[1,8,256]{2,1,0:T(8,128)S(1)}, u32[]{:S(2)}, u32[]{:S(2)}) collective-permute-start(f32[1,8,256]{2,1,0:T(8,128)S(1)} %get-tuple-element.53), channel_id=1, source_target_pairs={{4,0},{8,4},{12,8},{5,1},{9,5},{13,9},{6,2},{10,6},{14,10},{7,3},{... | collective-permute-start | bytes 24584 | tf_op jit(solution)/shard_map/ppermute | solution.py:20
  16.6 6.9 %collective-permute-start.7 = (f32[1,8,256]{2,1,0:T(8,128)S(1)}, f32[1,8,256]{2,1,0:T(8,128)S(1)}, u32[]{:S(2)}, u32[]{:S(2)}) collective-permute-start(f32[1,8,256]{2,1,0:T(8,128)S(1)} %get-tuple-element.52), channel_id=1, source_target_pairs={{0,4},{4,8},{8,12},{1,5},{5,9},{9,13},{2,6},{6,10},{10,14},{3,7},{... | collective-permute-start | bytes 24584 | tf_op jit(solution)/shard_map/ppermute | solution.py:19
  23.5 21.0 %collective-permute-start.8 = (f32[4,1,256]{2,1,0:T(1,128)S(1)}, f32[4,1,256]{2,1,0:T(1,128)S(1)}, u32[]{:S(2)}, u32[]{:S(2)}) collective-permute-start(f32[4,1,256]{2,1,0:T(1,128)S(1)} %get-tuple-element.45), channel_id=1, source_target_pairs={{2,0},{3,1},{6,4},{7,5},{10,8},{11,9},{14,12},{15,13},{18,16},{19,... | collective-permute-start | bytes 12296 | tf_op jit(solution)/shard_map/ppermute | solution.py:20
  24.8 19.7 %collective-permute-start.9 = (f32[4,1,256]{2,1,0:T(1,128)S(1)}, f32[4,1,256]{2,1,0:T(1,128)S(1)}, u32[]{:S(2)}, u32[]{:S(2)}) collective-permute-start(f32[4,1,256]{2,1,0:T(1,128)S(1)} %get-tuple-element.44), channel_id=1, source_target_pairs={{0,2},{1,3},{4,6},{5,7},{8,10},{9,11},{12,14},{13,15},{16,18},{17,... | collective-permute-start | bytes 12296 | tf_op jit(solution)/shard_map/ppermute | solution.py:19
  39.1 36.1 %copy-start.1 = (f32[4,16,512]{2,1,0:T(8,128)S(1)}, f32[4,16,512]{2,1,0:T(8,128)}, u32[]{:S(2)}) copy-start(f32[4,16,512]{2,1,0:T(8,128)} %param.4) | copy-start | bytes 393220
  44.6 4.3 %collective-permute-start.10 = (f32[4,10,1]{2,1,0:T(8,128)S(1)}, f32[4,10,1]{2,1,0:T(8,128)S(1)}, u32[]{:S(2)}, u32[]{:S(2)}) collective-permute-start(f32[4,10,1]{2,1,0:T(8,128)S(1)} %get-tuple-element.37), channel_id=1, source_target_pairs={{1,0},{3,2},{5,4},{7,6},{9,8},{11,10},{13,12},{15,14},{17,16},{19,... | collective-permute-start | bytes 488 | tf_op jit(solution)/shard_map/ppermute | solution.py:20
  45.9 3.9 %collective-permute-start.11 = (f32[4,10,1]{2,1,0:T(8,128)S(1)}, f32[4,10,1]{2,1,0:T(8,128)S(1)}, u32[]{:S(2)}, u32[]{:S(2)}) collective-permute-start(f32[4,10,1]{2,1,0:T(8,128)S(1)} %get-tuple-element.36), channel_id=1, source_target_pairs={{0,1},{2,3},{4,5},{6,7},{8,9},{10,11},{12,13},{14,15},{16,17},{18,... | collective-permute-start | bytes 488 | tf_op jit(solution)/shard_map/ppermute | solution.py:19
  49.9 6.1 %collective-permute-start.12 = (f32[1,8,256]{2,1,0:T(8,128)S(1)}, f32[1,8,256]{2,1,0:T(8,128)S(1)}, u32[]{:S(2)}, u32[]{:S(2)}) collective-permute-start(f32[1,8,256]{2,1,0:T(8,128)S(1)} %get-tuple-element.51), channel_id=1, source_target_pairs={{4,0},{8,4},{12,8},{5,1},{9,5},{13,9},{6,2},{10,6},{14,10},{7,3},{... | collective-permute-start | bytes 24584 | tf_op jit(solution)/shard_map/ppermute | solution.py:20
  51.2 6.2 %collective-permute-start.13 = (f32[1,8,256]{2,1,0:T(8,128)S(1)}, f32[1,8,256]{2,1,0:T(8,128)S(1)}, u32[]{:S(2)}, u32[]{:S(2)}) collective-permute-start(f32[1,8,256]{2,1,0:T(8,128)S(1)} %get-tuple-element.50), channel_id=1, source_target_pairs={{0,4},{4,8},{8,12},{1,5},{5,9},{9,13},{2,6},{6,10},{10,14},{3,7},{... | collective-permute-start | bytes 24584 | tf_op jit(solution)/shard_map/ppermute | solution.py:19
  57.4 6.0 %collective-permute-start.14 = (f32[4,1,256]{2,1,0:T(1,128)S(1)}, f32[4,1,256]{2,1,0:T(1,128)S(1)}, u32[]{:S(2)}, u32[]{:S(2)}) collective-permute-start(f32[4,1,256]{2,1,0:T(1,128)S(1)} %get-tuple-element.43), channel_id=1, source_target_pairs={{2,0},{3,1},{6,4},{7,5},{10,8},{11,9},{14,12},{15,13},{18,16},{19,... | collective-permute-start | bytes 12296 | tf_op jit(solution)/shard_map/ppermute | solution.py:20
  58.7 5.9 %collective-permute-start.15 = (f32[4,1,256]{2,1,0:T(1,128)S(1)}, f32[4,1,256]{2,1,0:T(1,128)S(1)}, u32[]{:S(2)}, u32[]{:S(2)}) collective-permute-start(f32[4,1,256]{2,1,0:T(1,128)S(1)} %get-tuple-element.42), channel_id=1, source_target_pairs={{0,2},{1,3},{4,6},{5,7},{8,10},{9,11},{12,14},{13,15},{16,18},{17,... | collective-permute-start | bytes 12296 | tf_op jit(solution)/shard_map/ppermute | solution.py:19
  64.6 2.6 %collective-permute-start.17 = (f32[4,10,1]{2,1,0:T(8,128)S(1)}, f32[4,10,1]{2,1,0:T(8,128)S(1)}, u32[]{:S(2)}, u32[]{:S(2)}) collective-permute-start(f32[4,10,1]{2,1,0:T(8,128)S(1)} %get-tuple-element.35), channel_id=1, source_target_pairs={{0,1},{2,3},{4,5},{6,7},{8,9},{10,11},{12,13},{14,15},{16,17},{18,... | collective-permute-start | bytes 488 | tf_op jit(solution)/shard_map/ppermute | solution.py:19
  65.9 3.1 %collective-permute-start.16 = (f32[4,10,1]{2,1,0:T(8,128)S(1)}, f32[4,10,1]{2,1,0:T(8,128)S(1)}, u32[]{:S(2)}, u32[]{:S(2)}) collective-permute-start(f32[4,10,1]{2,1,0:T(8,128)S(1)} %get-tuple-element.34), channel_id=1, source_target_pairs={{1,0},{3,2},{5,4},{7,6},{9,8},{11,10},{13,12},{15,14},{17,16},{19,... | collective-permute-start | bytes 488 | tf_op jit(solution)/shard_map/ppermute | solution.py:20
  69.1 6.2 %collective-permute-start.18 = (f32[1,8,256]{2,1,0:T(8,128)S(1)}, f32[1,8,256]{2,1,0:T(8,128)S(1)}, u32[]{:S(2)}, u32[]{:S(2)}) collective-permute-start(f32[1,8,256]{2,1,0:T(8,128)S(1)} %get-tuple-element.49), channel_id=1, source_target_pairs={{4,0},{8,4},{12,8},{5,1},{9,5},{13,9},{6,2},{10,6},{14,10},{7,3},{... | collective-permute-start | bytes 24584 | tf_op jit(solution)/shard_map/ppermute | solution.py:20
  70.4 6.2 %collective-permute-start.19 = (f32[1,8,256]{2,1,0:T(8,128)S(1)}, f32[1,8,256]{2,1,0:T(8,128)S(1)}, u32[]{:S(2)}, u32[]{:S(2)}) collective-permute-start(f32[1,8,256]{2,1,0:T(8,128)S(1)} %get-tuple-element.48), channel_id=1, source_target_pairs={{0,4},{4,8},{8,12},{1,5},{5,9},{9,13},{2,6},{6,10},{10,14},{3,7},{... | collective-permute-start | bytes 24584 | tf_op jit(solution)/shard_map/ppermute | solution.py:19
  76.6 12.1 %collective-permute-start.20 = (f32[4,1,256]{2,1,0:T(1,128)S(1)}, f32[4,1,256]{2,1,0:T(1,128)S(1)}, u32[]{:S(2)}, u32[]{:S(2)}) collective-permute-start(f32[4,1,256]{2,1,0:T(1,128)S(1)} %get-tuple-element.41), channel_id=1, source_target_pairs={{2,0},{3,1},{6,4},{7,5},{10,8},{11,9},{14,12},{15,13},{18,16},{19,... | collective-permute-start | bytes 12296 | tf_op jit(solution)/shard_map/ppermute | solution.py:20
  77.9 10.8 %collective-permute-start.21 = (f32[4,1,256]{2,1,0:T(1,128)S(1)}, f32[4,1,256]{2,1,0:T(1,128)S(1)}, u32[]{:S(2)}, u32[]{:S(2)}) collective-permute-start(f32[4,1,256]{2,1,0:T(1,128)S(1)} %get-tuple-element.40), channel_id=1, source_target_pairs={{0,2},{1,3},{4,6},{5,7},{8,10},{9,11},{12,14},{13,15},{16,18},{17,... | collective-permute-start | bytes 12296 | tf_op jit(solution)/shard_map/ppermute | solution.py:19
  82.5 25.2 %collective-permute-start.1 = (f32[2,4,16,512]{3,2,1,0:T(8,128)S(1)}, f32[2,4,16,512]{3,2,1,0:T(8,128)S(1)}, u32[]{:S(2)}, u32[]{:S(2)}) collective-permute-start(f32[2,4,16,512]{3,2,1,0:T(8,128)S(1)} %pad_maximum_fusion.7), channel_id=1, source_target_pairs={{4,0},{8,4},{12,8},{5,1},{9,5},{13,9},{6,2},{10,6},{14,10},{7,3},{... | collective-permute-start | bytes 786440 | tf_op jit(solution)/shard_map/ppermute | solution.py:20
  83.8 23.9 %collective-permute-start = (f32[2,4,16,512]{3,2,1,0:T(8,128)S(1)}, f32[2,4,16,512]{3,2,1,0:T(8,128)S(1)}, u32[]{:S(2)}, u32[]{:S(2)}) collective-permute-start(f32[2,4,16,512]{3,2,1,0:T(8,128)S(1)} %pad_maximum_fusion.7), channel_id=1, source_target_pairs={{0,4},{4,8},{8,12},{1,5},{5,9},{9,13},{2,6},{6,10},{10,14},{3,7},{... | collective-permute-start | bytes 786440 | tf_op jit(solution)/shard_map/ppermute | solution.py:19
  88.8 2.6 %collective-permute-start.23 = (f32[4,10,1]{2,1,0:T(8,128)S(1)}, f32[4,10,1]{2,1,0:T(8,128)S(1)}, u32[]{:S(2)}, u32[]{:S(2)}) collective-permute-start(f32[4,10,1]{2,1,0:T(8,128)S(1)} %get-tuple-element.33), channel_id=1, source_target_pairs={{0,1},{2,3},{4,5},{6,7},{8,9},{10,11},{12,13},{14,15},{16,17},{18,... | collective-permute-start | bytes 488 | tf_op jit(solution)/shard_map/ppermute | solution.py:19
  90.1 3.1 %collective-permute-start.22 = (f32[4,10,1]{2,1,0:T(8,128)S(1)}, f32[4,10,1]{2,1,0:T(8,128)S(1)}, u32[]{:S(2)}, u32[]{:S(2)}) collective-permute-start(f32[4,10,1]{2,1,0:T(8,128)S(1)} %get-tuple-element.32), channel_id=1, source_target_pairs={{1,0},{3,2},{5,4},{7,6},{9,8},{11,10},{13,12},{15,14},{17,16},{19,... | collective-permute-start | bytes 488 | tf_op jit(solution)/shard_map/ppermute | solution.py:20
  93.3 5.9 %collective-permute-start.24 = (f32[1,8,256]{2,1,0:T(8,128)S(1)}, f32[1,8,256]{2,1,0:T(8,128)S(1)}, u32[]{:S(2)}, u32[]{:S(2)}) collective-permute-start(f32[1,8,256]{2,1,0:T(8,128)S(1)} %get-tuple-element.47), channel_id=1, source_target_pairs={{4,0},{8,4},{12,8},{5,1},{9,5},{13,9},{6,2},{10,6},{14,10},{7,3},{... | collective-permute-start | bytes 24584 | tf_op jit(solution)/shard_map/ppermute | solution.py:20
  94.6 5.9 %collective-permute-start.25 = (f32[1,8,256]{2,1,0:T(8,128)S(1)}, f32[1,8,256]{2,1,0:T(8,128)S(1)}, u32[]{:S(2)}, u32[]{:S(2)}) collective-permute-start(f32[1,8,256]{2,1,0:T(8,128)S(1)} %get-tuple-element.46), channel_id=1, source_target_pairs={{0,4},{4,8},{8,12},{1,5},{5,9},{9,13},{2,6},{6,10},{10,14},{3,7},{... | collective-permute-start | bytes 24584 | tf_op jit(solution)/shard_map/ppermute | solution.py:19
  100.5 5.9 %collective-permute-start.26 = (f32[4,1,256]{2,1,0:T(1,128)S(1)}, f32[4,1,256]{2,1,0:T(1,128)S(1)}, u32[]{:S(2)}, u32[]{:S(2)}) collective-permute-start(f32[4,1,256]{2,1,0:T(1,128)S(1)} %get-tuple-element.39), channel_id=1, source_target_pairs={{2,0},{3,1},{6,4},{7,5},{10,8},{11,9},{14,12},{15,13},{18,16},{19,... | collective-permute-start | bytes 12296 | tf_op jit(solution)/shard_map/ppermute | solution.py:20
  101.8 5.9 %collective-permute-start.27 = (f32[4,1,256]{2,1,0:T(1,128)S(1)}, f32[4,1,256]{2,1,0:T(1,128)S(1)}, u32[]{:S(2)}, u32[]{:S(2)}) collective-permute-start(f32[4,1,256]{2,1,0:T(1,128)S(1)} %get-tuple-element.38), channel_id=1, source_target_pairs={{0,2},{1,3},{4,6},{5,7},{8,10},{9,11},{12,14},{13,15},{16,18},{17,... | collective-permute-start | bytes 12296 | tf_op jit(solution)/shard_map/ppermute | solution.py:19
  107.8 8.5 %collective-permute-start.3 = (f32[2,12,4,512]{3,2,1,0:T(4,128)S(1)}, f32[2,12,4,512]{3,2,1,0:T(4,128)S(1)}, u32[]{:S(2)}, u32[]{:S(2)}) collective-permute-start(f32[2,12,4,512]{3,2,1,0:T(4,128)S(1)} %get-tuple-element.28), channel_id=1, source_target_pairs={{2,0},{3,1},{6,4},{7,5},{10,8},{11,9},{14,12},{15,13},{18,16},{19,... | collective-permute-start | bytes 589832 | tf_op jit(solution)/shard_map/ppermute | solution.py:20
  109.1 7.7 %collective-permute-start.2 = (f32[2,12,4,512]{3,2,1,0:T(4,128)S(1)}, f32[2,12,4,512]{3,2,1,0:T(4,128)S(1)}, u32[]{:S(2)}, u32[]{:S(2)}) collective-permute-start(f32[2,12,4,512]{3,2,1,0:T(4,128)S(1)} %get-tuple-element.27), channel_id=1, source_target_pairs={{0,2},{1,3},{4,6},{5,7},{8,10},{9,11},{12,14},{13,15},{16,18},{17,... | collective-permute-start | bytes 589832 | tf_op jit(solution)/shard_map/ppermute | solution.py:19
  113.7 7.8 %collective-permute-start.29 = (f32[4,10,1]{2,1,0:T(8,128)S(1)}, f32[4,10,1]{2,1,0:T(8,128)S(1)}, u32[]{:S(2)}, u32[]{:S(2)}) collective-permute-start(f32[4,10,1]{2,1,0:T(8,128)S(1)} %get-tuple-element.31), channel_id=1, source_target_pairs={{0,1},{2,3},{4,5},{6,7},{8,9},{10,11},{12,13},{14,15},{16,17},{18,... | collective-permute-start | bytes 488 | tf_op jit(solution)/shard_map/ppermute | solution.py:19
  115.0 6.6 %collective-permute-start.28 = (f32[4,10,1]{2,1,0:T(8,128)S(1)}, f32[4,10,1]{2,1,0:T(8,128)S(1)}, u32[]{:S(2)}, u32[]{:S(2)}) collective-permute-start(f32[4,10,1]{2,1,0:T(8,128)S(1)} %get-tuple-element.30), channel_id=1, source_target_pairs={{1,0},{3,2},{5,4},{7,6},{9,8},{11,10},{13,12},{15,14},{17,16},{19,... | collective-permute-start | bytes 488 | tf_op jit(solution)/shard_map/ppermute | solution.py:20
  117.0 15.5 %collective-permute-start.5 = (f32[2,12,24,4]{3,2,1,0:T(8,128)S(1)}, f32[2,12,24,4]{3,2,1,0:T(8,128)S(1)}, u32[]{:S(2)}, u32[]{:S(2)}) collective-permute-start(f32[2,12,24,4]{3,2,1,0:T(8,128)S(1)} %get-tuple-element.26), channel_id=1, source_target_pairs={{1,0},{3,2},{5,4},{7,6},{9,8},{11,10},{13,12},{15,14},{17,16},{19,... | collective-permute-start | bytes 27656 | tf_op jit(solution)/shard_map/ppermute | solution.py:20
  118.3 14.2 %collective-permute-start.4 = (f32[2,12,24,4]{3,2,1,0:T(8,128)S(1)}, f32[2,12,24,4]{3,2,1,0:T(8,128)S(1)}, u32[]{:S(2)}, u32[]{:S(2)}) collective-permute-start(f32[2,12,24,4]{3,2,1,0:T(8,128)S(1)} %get-tuple-element.25), channel_id=1, source_target_pairs={{0,1},{2,3},{4,5},{6,7},{8,9},{10,11},{12,13},{14,15},{16,17},{18,... | collective-permute-start | bytes 27656 | tf_op jit(solution)/shard_map/ppermute | solution.py:19
where the time goes:
time: 143 us; the launch traced here: 140 us
  starting transfers between devices  76.8 us (54%)
  local copies, waits for them, and re-layouts  31.7 us (22%)
  other arithmetic  16.5 us (12%)
  waiting for transfers between devices  12.5 us (9%)
  between operations  2.84 us (2%)
    ppermute x15, starting transfers between devices, extended_2(): before = lax.ppermute(last, axis, up)  57.4 us
    ppermute x15, starting transfers between devices, extended_2(): after = lax.ppermute(leading, axis, down)  19.3 us
    reshape x1, local copies, waits for them, and re-layouts, shards(): coarse_perm = jnp.exp(log_perm.reshape(blocks).mean(axis=(1, 3, 5)))  10.5 us
    reshape x1, local copies, waits for them, and re-layouts, shards(): coarse_source = source.reshape(blocks).sum(axis=(1, 3, 5))  9.8 us
    ppermute x15, waiting for transfers between devices, extended_2(): before = lax.ppermute(last, axis, up)  9.02 us
    reshape x1, local copies, waits for them, and re-layouts, refine(): return widened.reshape(2 * size_x, 2 * size_y, 2 * size_z)  6.94 us
    reduce_sum x1, other arithmetic, shards(): coarse_perm = jnp.exp(log_perm.reshape(blocks).mean(axis=(1, 3, 5)))  4.06 us
    reduce_sum x1, other arithmetic, shards(): coarse_source = source.reshape(blocks).sum(axis=(1, 3, 5))  4.06 us
  transfers between devices with their start and end apart: 30, of which 10 were waited for; matrix products, arithmetic and copies ran while one was open for 18% of the time, Pallas kernels for 0%

commit v1 on v0

v1 whole, which is shorter than its diff:
```python
import functools

import jax
import jax.numpy as jnp
from jax import lax
from jax.experimental import pallas as pl
from jax.experimental.pallas import tpu as pltpu
from jax.sharding import PartitionSpec as P

DEGREE = 3
REACH = DEGREE + 1
LANES = 128
storage_rate = 0.1
AXES = ("gx", "gy", "gz")
VMEM = pl.BlockSpec(memory_space=pltpu.VMEM)
SMEM = pl.BlockSpec(memory_space=pltpu.SMEM)


def up_pairs(peers):
    return [(i, i + 1) for i in range(peers - 1)]


def down_pairs(peers):
    return [(i + 1, i) for i in range(peers - 1)]


def iota(shape, dim):
    return lax.broadcasted_iota(jnp.int32, shape, dim)


def turned(value, shift, axis):
    size = value.shape[axis]
    return pltpu.roll(value, shift % size, axis)


def numerators(shape, dim, own, index, peers, face_scale):
    place = iota(shape, dim)
    right = jnp.where(index < peers - 1, 2.0 * face_scale, 0.0)
    left = jnp.where(index > 0, 2.0 * face_scale, 0.0)
    return jnp.where(
        place == own - 1, right, jnp.where(place == shape[dim] - 1, left, 2.0 * face_scale)
    )


def iterate(count, log_at, source_at, x_faces, y_top, z_top, low, high, storage, refs):
    tx_ref, ty_ref, tz_ref, w_ref, d_ref, r_ref, p_ref = refs
    theta, delta = (high + low) * 0.5, (high - low) * 0.5
    sigma = theta / delta
    rho = 1.0 / sigma
    over_theta = 1.0 / theta
    after = jnp.exp(-log_at(0))
    tx_before = None
    for k in range(count):
        here = after
        if k + 1 < count:
            after = jnp.exp(-log_at(k + 1))
            tx = x_faces[k] / (here + after)
            tx_ref[k] = tx
        if 1 <= k <= count - 2:
            ty = y_top / (here + turned(here, -1, 0))
            tz = z_top / (here + turned(here, -1, 1))
            diagonal = storage + (tx_before + tx) + (ty + turned(ty, 1, 0)) + (tz + turned(tz, 1, 1))
            w = 1.0 / diagonal
            source = source_at(k)
            d_ref[k] = source * (over_theta * w)
            if 2 <= k <= count - 3:
                ty_ref[k] = ty
                tz_ref[k] = tz
                w_ref[k] = w
                r_ref[k] = source
        tx_before = tx
    for step in range(DEGREE):
        first, last = 2 + step, count - 2 - step
        rho_next = 1.0 / (2.0 * sigma - rho)
        keep, gain = rho_next * rho, 2.0 * rho_next / delta
        rho = rho_next
        here = d_ref[first]
        fx_before = tx_ref[first - 1] * (d_ref[first - 1] - here)
        for k in range(first, last):
            after = d_ref[k + 1]
            fx = tx_ref[k] * (here - after)
            fy = ty_ref[k] * (here - turned(here, -1, 0))
            fz = tz_ref[k] * (here - turned(here, -1, 1))
            applied = storage * here + (fx - fx_before) + (fy - turned(fy, 1, 0)) + (fz - turned(fz, 1, 1))
            residual = r_ref[k] - applied
            fresh = keep * here + gain * (residual * w_ref[k])
            if REACH <= k < count - REACH:
                so_far = here if step == 0 else p_ref[k]
                p_ref[k] = so_far + fresh
            if step < DEGREE - 1:
                r_ref[k] = residual
                d_ref[k] = fresh
            here, fx_before = after, fx


def window_scratch(count, rows, lanes):
    return [pltpu.VMEM((count, rows, lanes), jnp.float32)] * 7


def pool_kernel(log_ref, source_ref, out_ref, sum_ref):
    layers, rows, lanes = log_ref.shape
    pick = (iota((lanes, lanes // 2), 0) // 2 == iota((lanes, lanes // 2), 1)).astype(jnp.float32)
    for a, ref in enumerate((log_ref, source_ref)):
        for x in range(layers // 2):
            both = []
            for tile in range(lanes // LANES):
                columns = pl.ds(tile * LANES, LANES)
                sum_ref[tile] = ref[2 * x, :, columns] + ref[2 * x + 1, :, columns]
                both.append(
                    sum_ref[tile, pl.ds(0, rows // 2, stride=2), :]
                    + sum_ref[tile, pl.ds(1, rows // 2, stride=2), :]
                )
            both = jnp.concatenate(both, axis=1)
            pooled = jnp.dot(
                both, pick, precision=lax.Precision.HIGHEST, preferred_element_type=jnp.float32
            )
            out_ref[a, x] = pooled * 0.125 if a == 0 else pooled


def pool(log_perm, source):
    layers, rows, lanes = log_perm.shape
    return pl.pallas_call(
        pool_kernel,
        out_shape=jax.ShapeDtypeStruct((2, layers // 2, rows // 2, lanes // 2), jnp.float32),
        in_specs=[VMEM, VMEM],
        out_specs=VMEM,
        scratch_shapes=[pltpu.VMEM((lanes // LANES, rows, LANES), jnp.float32)],
        compiler_params=pltpu.CompilerParams(vmem_limit_bytes=8 << 20),
        cost_estimate=pl.CostEstimate(flops=10_000_000, bytes_accessed=300_000, transcendentals=0),
        name="pool",
    )(log_perm, source)


def coarse_kernel(peers, low_ref, high_ref, all_ref, out_ref, wide_ref, *refs):
    _, _, layers, rows, lanes = all_ref.shape
    ix, iy, iz = (lax.axis_index(axis) for axis in AXES)
    nx, ny, nz = peers
    y_right, y_left = jnp.minimum(iy + 1, ny - 1), jnp.maximum(iy - 1, 0)
    z_right, z_left = jnp.minimum(iz + 1, nz - 1), jnp.maximum(iz - 1, 0)
    tile_right = iota((rows, LANES), 1) < LANES // 2
    rows_right = iota((rows, lanes + LANES), 0) < rows // 2

    def strip(a, block, layer, y):
        x = jnp.clip(ix + block, 0, nx - 1)
        base = (x * ny + y) * nz
        own = all_ref[base + iz, a, layer]
        right = all_ref[base + z_right, a, layer, :, :LANES]
        left = all_ref[base + z_left, a, layer, :, lanes - LANES :]
        return jnp.concatenate([own, jnp.where(tile_right, right, left)], axis=1)

    around = -(-REACH // layers)
    skip = around * layers - REACH
    count = layers + 2 * REACH

    def window(a, k):
        block, layer = (k + skip) // layers - around, (k + skip) % layers
        halo = jnp.where(rows_right, strip(a, block, layer, y_right), strip(a, block, layer, y_left))
        return jnp.concatenate([strip(a, block, layer, iy), halo], axis=0)

    faces = []
    for k in range(count - 1):
        block = (k + skip) // layers - around
        beyond = (k + 1 + skip) // layers - around
        if block == beyond:
            faces.append(4.0)
        else:
            open_face = (ix + beyond <= nx - 1) if beyond > 0 else (ix + block >= 0)
            faces.append(jnp.where(open_face, 4.0, 0.0))
    shape = (2 * rows, lanes + LANES)
    iterate(
        count,
        functools.partial(window, 0),
        functools.partial(window, 1),
        faces,
        numerators(shape, 0, rows, iy, ny, 2.0),
        numerators(shape, 1, lanes, iz, nz, 2.0),
        jnp.full((1, shape[1]), low_ref[0]),
        jnp.full((1, shape[1]), high_ref[0]),
        8.0 * storage_rate,
        refs,
    )
    p_ref = refs[-1]
    widen = (iota((lanes, 2 * lanes), 0) == iota((lanes, 2 * lanes), 1) // 2).astype(jnp.float32)
    for x in range(layers):
        wide = jnp.dot(
            p_ref[REACH + x, :rows, :lanes],
            widen,
            precision=lax.Precision.HIGHEST,
            preferred_element_type=jnp.float32,
        )
        for tile in range(2 * lanes // LANES):
            columns = slice(tile * LANES, (tile + 1) * LANES)
            for half in range(2):
                wide_ref[tile, pl.ds(half, rows, stride=2), :] = wide[:, columns]
            for twin in range(2):
                out_ref[2 * x + twin, :, columns] = wide_ref[tile]


def coarse_level(everyone, low_bound, high_bound, peers):
    _, _, layers, rows, lanes = everyone.shape
    window = (layers + 2 * REACH, 2 * rows, lanes + LANES)
    return pl.pallas_call(
        functools.partial(coarse_kernel, peers),
        out_shape=jax.ShapeDtypeStruct((2 * layers, 2 * rows, 2 * lanes), jnp.float32),
        in_specs=[SMEM, SMEM, VMEM],
        out_specs=VMEM,
        scratch_shapes=[pltpu.VMEM((2 * lanes // LANES, 2 * rows, LANES), jnp.float32)]
        + window_scratch(*window),
        compiler_params=pltpu.CompilerParams(vmem_limit_bytes=24 << 20),
        cost_estimate=pl.CostEstimate(flops=20_000_000, bytes_accessed=4_000_000, transcendentals=0),
        name="coarse_level",
    )(low_bound, high_bound, everyone)


def unpacked(packed, rows, both_sides):
    log_own, source_own = packed[:rows], packed[rows : 2 * rows]
    if both_sides:
        log_halo, source_halo = packed[2 * rows : 2 * rows + 8], packed[2 * rows + 8 :]
    else:
        halo = packed[2 * rows :]
        swapped = turned(halo, REACH, 0)
        first = iota(halo.shape, 0) < REACH
        log_halo, source_halo = jnp.where(first, halo, swapped), jnp.where(first, swapped, halo)
    return (
        jnp.concatenate([log_own, log_halo], axis=0),
        jnp.concatenate([source_own, source_halo], axis=0),
    )


def fine_kernel(
    peers, low_ref, high_ref, left_ref, own_ref, right_ref, tile_ref, spread_ref, fine_ref, diff_ref, *refs
):
    layers, rows, lanes = fine_ref.shape
    ix, iy, iz = (lax.axis_index(axis) for axis in AXES)
    nx, ny, nz = peers
    blocks = (left_ref, own_ref, right_ref)
    count = layers + 2 * REACH
    skip = layers - REACH

    def window(a, k):
        block, layer = (k + skip) // layers, (k + skip) % layers
        core = unpacked(blocks[block][layer], rows, ny > 2)[a]
        tile = unpacked(tile_ref[block, layer], rows, ny > 2)[a]
        return jnp.concatenate([core, tile], axis=1)

    faces = [2.0] * (count - 1)
    faces[REACH - 1] = jnp.where(ix > 0, 2.0, 0.0)
    faces[REACH + layers - 1] = jnp.where(ix < nx - 1, 2.0, 0.0)
    shape = (rows + 2 * REACH, lanes + LANES)
    iterate(
        count,
        functools.partial(window, 0),
        functools.partial(window, 1),
        faces,
        numerators(shape, 0, rows, iy, ny, 1.0),
        numerators(shape, 1, lanes, iz, nz, 1.0),
        jnp.full((1, shape[1]), low_ref[0]),
        jnp.full((1, shape[1]), high_ref[0]),
        storage_rate,
        refs,
    )
    p_ref = refs[-1]
    for x in range(layers):
        fine = p_ref[REACH + x, :rows, :lanes]
        fine_ref[x] = fine
        diff_ref[x] = fine - spread_ref[x]


def fine_level(left, own, right, tile, spread, low_bound, high_bound, peers):
    layers, rows, lanes = spread.shape
    window = (layers + 2 * REACH, rows + 2 * REACH, lanes + LANES)
    out = jax.ShapeDtypeStruct(spread.shape, jnp.float32)
    return pl.pallas_call(
        functools.partial(fine_kernel, peers),
        out_shape=(out, out),
        in_specs=[SMEM, SMEM, VMEM, VMEM, VMEM, VMEM, VMEM],
        out_specs=(VMEM, VMEM),
        scratch_shapes=window_scratch(*window),
        compiler_params=pltpu.CompilerParams(vmem_limit_bytes=24 << 20),
        cost_estimate=pl.CostEstimate(flops=20_000_000, bytes_accessed=10_000_000, transcendentals=0),
        name="fine_level",
    )(low_bound, high_bound, left, own, right, tile, spread)


def exchange_rows(log_perm, source, peers):
    rows = log_perm.shape[1]
    last = jnp.concatenate([log_perm[:, rows - REACH :], source[:, rows - REACH :]], axis=1)
    first = jnp.concatenate([log_perm[:, :REACH], source[:, :REACH]], axis=1)
    if peers == 2:
        sent = jnp.where(lax.axis_index("gy") == 0, last, first)
        return lax.ppermute(sent, "gy", [(0, 1), (1, 0)])
    left = lax.ppermute(last, "gy", up_pairs(peers))
    right = lax.ppermute(first, "gy", down_pairs(peers))
    return jnp.concatenate(
        [right[:, :REACH], left[:, :REACH], right[:, REACH:], left[:, REACH:]], axis=1
    )


def exchange_lanes(blocks, peers):
    lanes = blocks[0].shape[-1]
    last = jnp.stack([block[..., lanes - LANES :] for block in blocks])
    first = jnp.stack([block[..., :LANES] for block in blocks])
    if peers == 2:
        sent = jnp.where(lax.axis_index("gz") == 0, last, first)
        return lax.ppermute(sent, "gz", [(0, 1), (1, 0)])
    left = lax.ppermute(last, "gz", up_pairs(peers))
    right = lax.ppermute(first, "gz", down_pairs(peers))
    return jnp.where(iota(left.shape, left.ndim - 1) < LANES // 2, right, left)


def shards(peers, log_perm, source, low_bound, high_bound):
    nx, ny, nz = peers
    everyone = lax.all_gather(pool(log_perm, source), AXES)
    halo = exchange_rows(log_perm, source, ny)
    own = jnp.concatenate([log_perm, source, halo], axis=1)
    left = lax.ppermute(own, "gx", up_pairs(nx))
    right = lax.ppermute(own, "gx", down_pairs(nx))
    tile = exchange_lanes((left, own, right), nz)
    spread = coarse_level(everyone, low_bound, high_bound, peers)
    return fine_level(left, own, right, tile, spread, low_bound, high_bound, peers)


def solution(mesh):
    peers = tuple(mesh.shape[axis] for axis in AXES)
    split = P(("groups", "gx"), "gy", "gz")
    return jax.shard_map(
        functools.partial(shards, peers),
        mesh=mesh,
        in_specs=(split, split, P(), P()),
        out_specs=(split, split),
        check_vma=False,
    )
```

time: 143 us -> 49.6 us (0.35); the launches traced: 140 us -> 49.4 us
  starting transfers between devices: 76.8 us -> 9.02 us
  local copies, waits for them, and re-layouts: 31.7 us -> 1.04 us
  blocking collectives: 0 us -> 24.2 us
  other arithmetic: 16.5 us -> 0.07 us
  Pallas kernels: 0 us -> 5.05 us
  waiting for transfers between devices: 12.5 us -> 7.95 us
    ppermute x30 -> x4, starting transfers between devices: 76.8 us -> 9.02 us  [the longest x1 4.66 us: shards(): left = lax.ppermute(own, 'gx', up_pairs(nx))]
    reshape x3 -> x0, local copies, waits for them, and re-layouts: 27.3 us -> none  [the longest x1 10.5 us: shards(): coarse_perm = jnp.exp(log_perm.reshape(blocks).mean(axis=(1, 3, 5)))]
    all_gather x0 -> x1, blocking collectives: none -> 24.2 us  [shards(): everyone = lax.all_gather(pool(log_perm, source), AXES)]
    reduce_sum x2 -> x0, other arithmetic: 8.11 us -> none  [the longest x1 4.06 us: shards(): coarse_perm = jnp.exp(log_perm.reshape(blocks).mean(axis=(1, 3, 5)))]
    pallas_call x0 -> x3, Pallas kernels: none -> 5.05 us  [the longest x1 2.99 us: fine_level(): pl.pallas_call(functools.partial(fine_kernel, peers), out_shape=(out, out...]
    ppermute x30 -> x4, waiting for transfers between devices: 12.5 us -> 7.95 us  [the longest x1 3.4 us: shards(): left = lax.ppermute(own, 'gx', up_pairs(nx))]
    add x5 -> x0, other arithmetic: 4.14 us -> none  [the longest x2 3.83 us: fine_deep(): rho_next * rho_now * crop_one(direction)]
    broadcast_in_dim x1 -> x0, local copies, waits for them, and re-layouts: 3.84 us -> none  [refine(): jnp.broadcast_to(field[:, None, :, None, :, None], (size_x, 2, size_y, 2,...]
  transfers between devices with their start and end apart: 30 -> 4, of which waited for: 10 -> 3; matrix products, arithmetic and copies ran while one was open for 18% -> 0% of each run, Pallas kernels for 0% -> 4%
where the time goes in v1:
time: 49.6 us; the launch traced here: 49.4 us
  blocking collectives  24.2 us (49%)
  starting transfers between devices  9.02 us (18%)
  waiting for transfers between devices  7.95 us (16%)
  Pallas kernels  5.05 us (10%)
  between operations  2.04 us (4%)
  local copies, waits for them, and re-layouts  1.04 us (2%)
    all_gather x1, blocking collectives, shards(): everyone = lax.all_gather(pool(log_perm, source), AXES)  24.2 us
    ppermute x1, starting transfers between devices, shards(): left = lax.ppermute(own, 'gx', up_pairs(nx))  4.66 us
    ppermute x1, waiting for transfers between devices, shards(): left = lax.ppermute(own, 'gx', up_pairs(nx))  3.4 us
    ppermute x1, starting transfers between devices, exchange_rows(): return lax.ppermute(sent, 'gy', [(0, 1), (1, 0)])  3 us
    pallas_call x1, Pallas kernels, fine_level(): pl.pallas_call(functools.partial(fine_kernel, peers), out_shape=(out, out...  2.99 us
    ppermute x1, waiting for transfers between devices, shards(): right = lax.ppermute(own, 'gx', down_pairs(nx))  2.35 us
    ppermute x1, waiting for transfers between devices, exchange_rows(): return lax.ppermute(sent, 'gy', [(0, 1), (1, 0)])  2.2 us
    ppermute x1, starting transfers between devices, shards(): right = lax.ppermute(own, 'gx', down_pairs(nx))  1.28 us
  transfers between devices with their start and end apart: 4, of which 3 were waited for; matrix products, arithmetic and copies ran while one was open for 0% of the time, Pallas kernels for 4%

profile of v1, /device:TPU:0, one launch (start us, length us, event | category | flops | bytes accessed | tf_op | source)
XLA Modules:
  0.0 49.4 jit_solution(5425301949690941052)
XLA Ops:
  0.6 1.0 %fusion = (f32[4,4,512]{2,1,0:T(4,128)S(1)}, f32[4,4,512]{2,1,0:T(4,128)S(1)}, f32[4,4,512]{2,1,0:T(4,128)S(1)}, f32[4,4,512]{2,1,0:T(4,128)S(1)}) fusion(f32[4,16,512]{2,1,0:T(8,128)} %log_ref.1, f32[4,16,512]{2,1,0:T(8,128)} %source_ref.1), kind=kLoop, calls=%fused_computation.11 | loop fusion | bytes 262144 | tf_op jit(solution)/shard_map/slice | solution.py:288
  1.6 0.0 copy-start
  1.7 0.0 copy-start.1
  1.7 3.0 %collective-permute-start = (f32[4,8,512]{2,1,0:T(8,128)S(1)}, f32[4,8,512]{2,1,0:T(8,128)S(1)}, u32[]{:S(2)}, u32[]{:S(2)}) collective-permute-start(f32[4,8,512]{2,1,0:T(8,128)S(1)} %maximum_select_fusion.1), channel_id=1, source_target_pairs={{0,2},{2,0},{1,3},{3,1},{4,6},{6,4},{5,7},{7,5},{8,10},{10,8},{9,1... | collective-permute-start | bytes 196616 | tf_op jit(solution)/shard_map/ppermute | solution.py:291
  4.7 0.0 copy-done
  4.7 0.0 copy-done.1
  4.7 2.2 %collective-permute-done = f32[4,8,512]{2,1,0:T(8,128)S(1)} collective-permute-done((f32[4,8,512]{2,1,0:T(8,128)S(1)}, f32[4,8,512]{2,1,0:T(8,128)S(1)}, u32[]{:S(2)}, u32[]{:S(2)}) %collective-permute-start) | collective-permute-done | bytes 65568 | tf_op jit(solution)/shard_map/ppermute | solution.py:291
  6.9 1.3 %collective-permute-start.2 = (f32[4,40,512]{2,1,0:T(8,128)S(1)}, f32[4,40,512]{2,1,0:T(8,128)S(1)}, u32[]{:S(2)}, u32[]{:S(2)}) collective-permute-start(f32[4,40,512]{2,1,0:T(8,128)S(1)} %constant_dynamic-update-slice_fusion.own_ref), channel_id=1, source_target_pairs={{4,0},{8,4},{12,8},{5,1},{9,5},{13,9},{6,2},{10,6},{14,10},{7,3},{... | collective-permute-start | bytes 983048 | tf_op jit(solution)/shard_map/ppermute | solution.py:317
  9.5 0.9 %pool.1 = f32[2,2,8,256]{3,2,1,0:T(8,128)S(1)} custom-call(f32[4,16,512]{2,1,0:T(8,128)S(1)} %copy-done, f32[4,16,512]{2,1,0:T(8,128)S(1)} %copy-done.1), custom_call_target="tpu_custom_call" | custom-call | flops 10000000 | bytes 300000 | tf_op jit(solution)/shard_map/pool/pallas_call | solution.py:122
  10.4 4.7 %collective-permute-start.1 = (f32[4,40,512]{2,1,0:T(8,128)S(1)}, f32[4,40,512]{2,1,0:T(8,128)S(1)}, u32[]{:S(2)}, u32[]{:S(2)}) collective-permute-start(f32[4,40,512]{2,1,0:T(8,128)S(1)} %constant_dynamic-update-slice_fusion.own_ref), channel_id=1, source_target_pairs={{0,4},{4,8},{8,12},{1,5},{5,9},{9,13},{2,6},{6,10},{10,14},{3,7},{... | collective-permute-start | bytes 983048 | tf_op jit(solution)/shard_map/ppermute | solution.py:316
  15.1 2.3 %collective-permute-done.2.right_ref = f32[4,40,512]{2,1,0:T(8,128)S(1)} collective-permute-done((f32[4,40,512]{2,1,0:T(8,128)S(1)}, f32[4,40,512]{2,1,0:T(8,128)S(1)}, u32[]{:S(2)}, u32[]{:S(2)}) %collective-permute-start.2) | collective-permute-done | bytes 327712 | tf_op jit(solution)/shard_map/ppermute | solution.py:317
  17.5 3.4 %collective-permute-done.1.left_ref = f32[4,40,512]{2,1,0:T(8,128)S(1)} collective-permute-done((f32[4,40,512]{2,1,0:T(8,128)S(1)}, f32[4,40,512]{2,1,0:T(8,128)S(1)}, u32[]{:S(2)}, u32[]{:S(2)}) %collective-permute-start.1) | collective-permute-done | bytes 327712 | tf_op jit(solution)/shard_map/ppermute | solution.py:316
  20.9 0.1 collective-permute-start.3
  21.0 24.2 %all-gather = f32[32,2,8,256]{3,2,1,0:T(8,128)S(1)} all-gather(f32[2,2,8,256]{3,2,1,0:T(8,128)S(1)} %pool.1), channel_id=2, replica_groups=mesh['groups'=2,'gx'=4,'gy'=2,'gz'=2] {'gx','gy','gz'}, dimensions={0}, use_global_device_ids=true | all-gather | bytes 557056 | tf_op jit(solution)/shard_map/all_gather | solution.py:313
  45.2 1.1 %coarse_level.1.spread_ref = f32[4,16,512]{2,1,0:T(8,128)S(1)} custom-call(f32[1]{0:T(128)S(6)} %copy.8.low_ref, f32[1]{0:T(128)S(6)} %copy.9.high_ref, f32[16,2,2,8,256]{4,3,2,1,0:T(8,128)S(1)} %bitcast.13), custom_call_target="tpu_custom_call" | custom-call | flops 20000000 | bytes 4000000 | tf_op jit(solution)/shard_map/coarse_level/pallas_call | solution.py:202
  46.4 0.0 collective-permute-done.3.tile_ref
  46.4 3.0 %fine_level.1 = (f32[4,16,512]{2,1,0:T(8,128)}, f32[4,16,512]{2,1,0:T(8,128)}) custom-call(f32[1]{0:T(128)S(6)} %copy.8.low_ref, f32[1]{0:T(128)S(6)} %copy.9.high_ref, f32[4,40,512]{2,1,0:T(8,128)S(1)} %collective-permute-done.1.left_ref, f32[4,40,512]{2,1,0:T(8,128)S(1)} %constant_dynamic-update-slice_fusion.own_ref, ...), custom_call_target="tpu_custom_call" | custom-call | flops 20000000 | bytes 10000000 | tf_op jit(solution)/shard_map/fine_level/pallas_call | solution.py:273
  (8 shorter events, 0.1 us)
Async XLA Ops:
  1.6 3.1 %copy-start = (f32[4,16,512]{2,1,0:T(8,128)S(1)}, f32[4,16,512]{2,1,0:T(8,128)}, u32[]{:S(2)}) copy-start(f32[4,16,512]{2,1,0:T(8,128)} %log_ref.1) | copy-start | bytes 393220
  1.7 3.0 %copy-start.1 = (f32[4,16,512]{2,1,0:T(8,128)S(1)}, f32[4,16,512]{2,1,0:T(8,128)}, u32[]{:S(2)}) copy-start(f32[4,16,512]{2,1,0:T(8,128)} %source_ref.1) | copy-start | bytes 393220
  1.7 5.2 %collective-permute-start = (f32[4,8,512]{2,1,0:T(8,128)S(1)}, f32[4,8,512]{2,1,0:T(8,128)S(1)}, u32[]{:S(2)}, u32[]{:S(2)}) collective-permute-start(f32[4,8,512]{2,1,0:T(8,128)S(1)} %maximum_select_fusion.1), channel_id=1, source_target_pairs={{0,2},{2,0},{1,3},{3,1},{4,6},{6,4},{5,7},{7,5},{8,10},{10,8},{9,1... | collective-permute-start | bytes 196616 | tf_op jit(solution)/shard_map/ppermute | solution.py:291
  6.9 10.6 %collective-permute-start.2 = (f32[4,40,512]{2,1,0:T(8,128)S(1)}, f32[4,40,512]{2,1,0:T(8,128)S(1)}, u32[]{:S(2)}, u32[]{:S(2)}) collective-permute-start(f32[4,40,512]{2,1,0:T(8,128)S(1)} %constant_dynamic-update-slice_fusion.own_ref), channel_id=1, source_target_pairs={{4,0},{8,4},{12,8},{5,1},{9,5},{13,9},{6,2},{10,6},{14,10},{7,3},{... | collective-permute-start | bytes 983048 | tf_op jit(solution)/shard_map/ppermute | solution.py:317
  10.4 10.5 %collective-permute-start.1 = (f32[4,40,512]{2,1,0:T(8,128)S(1)}, f32[4,40,512]{2,1,0:T(8,128)S(1)}, u32[]{:S(2)}, u32[]{:S(2)}) collective-permute-start(f32[4,40,512]{2,1,0:T(8,128)S(1)} %constant_dynamic-update-slice_fusion.own_ref), channel_id=1, source_target_pairs={{0,4},{4,8},{8,12},{1,5},{5,9},{9,13},{2,6},{6,10},{10,14},{3,7},{... | collective-permute-start | bytes 983048 | tf_op jit(solution)/shard_map/ppermute | solution.py:316
  20.9 25.4 %collective-permute-start.3 = (f32[3,4,40,128]{3,2,1,0:T(8,128)S(1)}, f32[3,4,40,128]{3,2,1,0:T(8,128)S(1)}, u32[]{:S(2)}, u32[]{:S(2)}) collective-permute-start(f32[3,4,40,128]{3,2,1,0:T(8,128)S(1)} %maximum_select_fusion), channel_id=1, source_target_pairs={{0,1},{1,0},{2,3},{3,2},{4,5},{5,4},{6,7},{7,6},{8,9},{9,8},{10,11... | collective-permute-start | bytes 737288 | tf_op jit(solution)/shard_map/ppermute | solution.py:305

commit v2 on v1

v2 whole, which is shorter than its diff:
```python
import functools

import jax
import jax.numpy as jnp
from jax import lax
from jax.experimental import pallas as pl
from jax.experimental.pallas import tpu as pltpu
from jax.sharding import PartitionSpec as P

DEGREE = 3
REACH = DEGREE + 1
LANES = 128
SUBLANES = 8
storage_rate = 0.1
AXES = ("gx", "gy", "gz")
VMEM = pl.BlockSpec(memory_space=pltpu.VMEM)
SMEM = pl.BlockSpec(memory_space=pltpu.SMEM)


def iota(shape, dim):
    return lax.broadcasted_iota(jnp.int32, shape, dim)


def turned(value, shift, axis):
    size = value.shape[axis]
    return pltpu.roll(value, shift % size, axis)


def both_ways(pairs):
    return [pair for i, j in pairs for pair in ((i, j), (j, i))]


def swap(axis, peers, right, left):
    even = lax.axis_index(axis) % 2 == 0
    first = lax.ppermute(
        right if right is left else jnp.where(even, right, left),
        axis,
        both_ways([(i, i + 1) for i in range(0, peers - 1, 2)]),
    )
    if peers == 2:
        return (first,)
    second = lax.ppermute(
        left if right is left else jnp.where(even, left, right),
        axis,
        both_ways([(i, i + 1) for i in range(1, peers - 1, 2)]),
    )
    return (first, second)


def far_swap(axis, peers, right, left):
    low = lax.axis_index(axis) % 4 < 2
    pairs = [(i, i + 2) for i in range(peers - 2)]
    near = [pair for pair in pairs if pair[0] % 4 < 2]
    rest = [pair for pair in pairs if pair[0] % 4 >= 2]
    got = []
    for chosen, sent in ((near, (right, left)), (rest, (left, right))):
        if chosen:
            got.append(lax.ppermute(jnp.where(low, *sent), axis, both_ways(chosen)))
    return tuple(got)


def from_right(is_first, got):
    return got[0] if len(got) == 1 else jnp.where(is_first, got[0], got[1])


def from_left(is_first, got):
    return got[0] if len(got) == 1 else jnp.where(is_first, got[1], got[0])


def numerators(shape, dim, own, index, peers, face_scale):
    place = iota(shape, dim)
    right = jnp.where(index < peers - 1, 2.0 * face_scale, 0.0)
    left = jnp.where(index > 0, 2.0 * face_scale, 0.0)
    return jnp.where(
        place == own - 1, right, jnp.where(place == shape[dim] - 1, left, 2.0 * face_scale)
    )


def iterate(count, log_at, source_at, x_faces, y_top, z_top, low, high, storage, refs):
    tx_ref, ty_ref, tz_ref, w_ref, d_ref, r_ref, p_ref = refs
    theta, delta = (high + low) * 0.5, (high - low) * 0.5
    sigma = theta / delta
    rho = 1.0 / sigma
    over_theta = 1.0 / theta
    after = jnp.exp(-log_at(0))
    tx_before = None
    for k in range(count):
        here = after
        if k + 1 < count:
            after = jnp.exp(-log_at(k + 1))
            tx = x_faces[k] / (here + after)
            tx_ref[k] = tx
        if 1 <= k <= count - 2:
            ty = y_top / (here + turned(here, -1, 0))
            tz = z_top / (here + turned(here, -1, 1))
            diagonal = storage + (tx_before + tx) + (ty + turned(ty, 1, 0)) + (tz + turned(tz, 1, 1))
            w = 1.0 / diagonal
            source = source_at(k)
            d_ref[k] = source * (over_theta * w)
            if 2 <= k <= count - 3:
                ty_ref[k] = ty
                tz_ref[k] = tz
                w_ref[k] = w
                r_ref[k] = source
        tx_before = tx
    for step in range(DEGREE):
        first, last = 2 + step, count - 2 - step
        rho_next = 1.0 / (2.0 * sigma - rho)
        keep, gain = rho_next * rho, 2.0 * rho_next / delta
        rho = rho_next
        here = d_ref[first]
        fx_before = tx_ref[first - 1] * (d_ref[first - 1] - here)
        for k in range(first, last):
            after = d_ref[k + 1]
            fx = tx_ref[k] * (here - after)
            fy = ty_ref[k] * (here - turned(here, -1, 0))
            fz = tz_ref[k] * (here - turned(here, -1, 1))
            applied = storage * here + (fx - fx_before) + (fy - turned(fy, 1, 0)) + (fz - turned(fz, 1, 1))
            residual = r_ref[k] - applied
            fresh = keep * here + gain * (residual * w_ref[k])
            if REACH <= k < count - REACH:
                so_far = here if step == 0 else p_ref[k]
                p_ref[k] = so_far + fresh
            if step < DEGREE - 1:
                r_ref[k] = residual
                d_ref[k] = fresh
            here, fx_before = after, fx


def window_scratch(count, rows, lanes):
    return [pltpu.VMEM((count, rows, lanes), jnp.float32)] * 7


def exact_dot(value, zero_one):
    parts = []
    for _ in range(3):
        part = value.astype(jnp.bfloat16)
        parts.append(part)
        value = value - part.astype(jnp.float32)
    rows = value.shape[0]
    out = jnp.dot(jnp.concatenate(parts, axis=0), zero_one, preferred_element_type=jnp.float32)
    return (out[2 * rows :] + out[rows : 2 * rows]) + out[:rows]


def pack_kernel(log_ref, source_ref, *refs):
    *halo_refs, out_ref, sum_ref = refs
    layers, rows, lanes = log_ref.shape
    even = lax.axis_index("gy") % 2 == 0
    starts = lax.axis_index("gy") == 0
    half = lanes // 2
    first_rows = iota((SUBLANES, lanes), 0) < REACH
    wide = len(halo_refs) == 2

    def halo(a, layer):
        got = tuple(ref[a * layers + layer] for ref in halo_refs)
        return from_right(even, got), from_left(even, got)

    slot = 0
    strips = []
    for layer in range(layers):
        tiles = []
        for a in range(2):
            right, left = halo(a, layer)
            tiles.append(jnp.where(first_rows, right, left) if wide else right)
        if wide:
            for tile in tiles:
                out_ref[slot] = tile
                slot += 1
        else:
            out_ref[slot] = jnp.where(first_rows == starts, tiles[0], turned(tiles[1], REACH, 0))
            slot += 1
    pieces = []

    def gather(top, bottom):
        for tile in range(lanes // LANES):
            columns = slice(tile * LANES, (tile + 1) * LANES)
            sum_ref[tile, :SUBLANES] = top[:, columns]
            sum_ref[tile, SUBLANES:] = bottom[:, columns]
        pieces.append(
            jnp.concatenate(
                [
                    sum_ref[tile, pl.ds(0, SUBLANES, stride=2), :]
                    + sum_ref[tile, pl.ds(1, SUBLANES, stride=2), :]
                    for tile in range(lanes // LANES)
                ],
                axis=1,
            )
        )

    for x in range(layers // 2):
        for ref in (log_ref, source_ref):
            both = ref[2 * x] + ref[2 * x + 1]
            gather(both[:SUBLANES], both[SUBLANES:])
    sums = []
    for x in range(layers // 2):
        for a in range(2):
            right, left = zip(halo(a, 2 * x), halo(a, 2 * x + 1))
            sums.append((right[0] + right[1], left[0] + left[1]))
    for x in range(layers // 2):
        if wide:
            continue
        gather(sums[2 * x][0], sums[2 * x + 1][0])
    if wide:
        for a in range(2):
            for x in range(layers // 2):
                gather(*sums[2 * x + a])
    pick = (iota((lanes, half), 0) // 2 == iota((lanes, half), 1)).astype(jnp.bfloat16)
    pooled = exact_dot(jnp.concatenate(pieces, axis=0), pick)
    tile = [pooled[SUBLANES * i : SUBLANES * (i + 1)] for i in range(len(pieces))]
    for x in range(layers // 2):
        tile[2 * x] = tile[2 * x] * 0.125
    if wide:
        for x in range(layers // 2):
            tile[layers + x] = tile[layers + x] * 0.125
    else:
        scale = jnp.where(iota((SUBLANES, half), 0) < REACH, 0.125, 1.0)
        for x in range(layers // 2):
            tile[layers + x] = tile[layers + x] * scale
    for i in range(0, len(tile), 2):
        out_ref[slot] = jnp.concatenate(tile[i : i + 2], axis=1)
        slot += 1


def pack(log_perm, source, got):
    layers, rows, lanes = log_perm.shape
    slots = len(got) * layers + 2 + len(got)
    return pl.pallas_call(
        pack_kernel,
        out_shape=jax.ShapeDtypeStruct((slots, SUBLANES, lanes), jnp.float32),
        in_specs=[VMEM] * (2 + len(got)),
        out_specs=VMEM,
        scratch_shapes=[pltpu.VMEM((lanes // LANES, 2 * SUBLANES, LANES), jnp.float32)],
        compiler_params=pltpu.CompilerParams(vmem_limit_bytes=8 << 20),
        cost_estimate=pl.CostEstimate(flops=5_000_000, bytes_accessed=700_000, transcendentals=0),
        name="pack",
    )(log_perm, source, *got)


def halves(both_sides, packed, partner):
    if both_sides:
        return packed, partner
    swapped = turned(packed, REACH, 0)
    return packed, swapped


def coarse_kernel(peers, slots, n_far, low_ref, high_ref, own_ref, *refs):
    near_refs, far_refs = refs[:2], refs[2 : 2 + n_far]
    tile_ref, out_ref, wide_ref, *scratch = refs[2 + n_far :]
    ix, iy, iz = (lax.axis_index(axis) for axis in AXES)
    nx, ny, nz = peers
    both_sides = ny > 2
    lanes = own_ref.shape[2] // 2
    rows = SUBLANES
    even, low = ix % 2 == 0, ix % 4 < 2
    strips, own_rows, near_rows, far_rows = slots
    top = iota((rows, lanes + LANES), 0) < REACH

    def packed(side, slot, half):
        columns = slice(half * lanes, (half + 1) * lanes)
        if side == 0:
            core = own_ref[strips + slot, :, columns]
            start = own_rows
        else:
            pick = from_left if side < 0 else from_right
            core = pick(even, tuple(ref[strips + slot, :, columns] for ref in near_refs))
            start = pick(even, tuple(near_rows))
        row = pl.multiple_of(start + (2 * slot + half) * rows, rows)
        return jnp.concatenate([core, tile_ref[pl.ds(row, rows), :]], axis=1)

    def far(side, slot, half):
        columns = slice(half * lanes, (half + 1) * lanes)
        pick = from_left if side < 0 else from_right
        core = pick(low, tuple(ref[slot, :, columns] for ref in far_refs))
        start = pick(low, tuple(far_rows))
        return jnp.concatenate([core, tile_ref[pl.ds(pl.multiple_of(start, rows), rows), :]], axis=1)

    def window(a, k):
        block, layer = k // 2 - 2, k % 2
        if abs(block) == 2:
            nearest = layer == (1 if block < 0 else 0)
            if a == 1:
                core = far(block, 1, 0)
                return jnp.concatenate([core, jnp.zeros_like(core)], axis=0)
            core = far(block, 0, 0 if nearest else 1)
            halo = far(block, 1, 1)
            if not both_sides:
                halo = jnp.where(top, halo, turned(halo, REACH, 0))
            return jnp.concatenate([core, halo], axis=0)
        core = packed(block, layer, a)
        if both_sides:
            halo = packed(block, 2 + a, layer)
        else:
            tile = packed(block, 2, layer)
            other = turned(tile, REACH, 0)
            halo = jnp.where(top, tile, other) if a == 0 else jnp.where(top, other, tile)
        return jnp.concatenate([core, halo], axis=0)

    def open_face(inside):
        return jnp.where(inside, 4.0, 0.0)

    faces = [4.0] * 9
    faces[1], faces[3] = open_face(ix > 1), open_face(ix > 0)
    faces[5], faces[7] = open_face(ix < nx - 1), open_face(ix < nx - 2)
    shape = (2 * rows, lanes + LANES)
    iterate(
        2 + 2 * REACH,
        functools.partial(window, 0),
        functools.partial(window, 1),
        faces,
        numerators(shape, 0, rows, iy, ny, 2.0),
        numerators(shape, 1, lanes, iz, nz, 2.0),
        jnp.full((1, shape[1]), low_ref[0]),
        jnp.full((1, shape[1]), high_ref[0]),
        8.0 * storage_rate,
        scratch,
    )
    p_ref = scratch[-1]
    widen = (iota((lanes, 2 * lanes), 0) == iota((lanes, 2 * lanes), 1) // 2).astype(jnp.bfloat16)
    pressure = jnp.concatenate([p_ref[REACH + x, :rows, :lanes] for x in range(2)], axis=0)
    wide = exact_dot(pressure, widen)
    for x in range(2):
        for tile in range(2 * lanes // LANES):
            columns = slice(tile * LANES, (tile + 1) * LANES)
            for half in range(2):
                wide_ref[tile, pl.ds(half, rows, stride=2), :] = wide[x * rows : (x + 1) * rows, columns]
            for twin in range(2):
                out_ref[2 * x + twin, :, columns] = wide_ref[tile]


def coarse_level(low_bound, high_bound, own, near, far, tile, slots, peers):
    lanes = own.shape[2] // 2
    window = (2 + 2 * REACH, 2 * SUBLANES, lanes + LANES)
    return pl.pallas_call(
        functools.partial(coarse_kernel, peers, slots, len(far)),
        out_shape=jax.ShapeDtypeStruct((REACH, 2 * SUBLANES, 2 * lanes), jnp.float32),
        in_specs=[SMEM, SMEM] + [VMEM] * (4 + len(far)),
        out_specs=VMEM,
        scratch_shapes=[pltpu.VMEM((2 * lanes // LANES, 2 * SUBLANES, LANES), jnp.float32)]
        + window_scratch(*window),
        compiler_params=pltpu.CompilerParams(vmem_limit_bytes=24 << 20),
        cost_estimate=pl.CostEstimate(flops=20_000_000, bytes_accessed=4_000_000, transcendentals=0),
        name="coarse_level",
    )(low_bound, high_bound, own, *near, *far, tile)


def fine_kernel(
    peers,
    slots,
    low_ref,
    high_ref,
    log_ref,
    source_ref,
    own_ref,
    first_ref,
    second_ref,
    first_pack_ref,
    second_pack_ref,
    tile_ref,
    spread_ref,
    fine_ref,
    diff_ref,
    *refs,
):
    layers, rows, lanes = fine_ref.shape
    ix, iy, iz = (lax.axis_index(axis) for axis in AXES)
    nx, ny, nz = peers
    both_sides = ny > 2
    even = ix % 2 == 0
    count = 3 * layers
    own_rows, own_strip_rows, raw_rows, strip_rows = slots

    def lane_tile(start, size):
        return tile_ref[pl.ds(pl.multiple_of(start, SUBLANES), size), :]

    def window(a, k):
        side, layer = k // layers - 1, k % layers
        if side == 0:
            core = (log_ref, source_ref)[a][layer]
            core_tile = lane_tile(own_rows + (a * layers + layer) * rows, rows)
            strip = lambda slot: own_ref[slot]
            strip_start = own_strip_rows
        else:
            pick = from_left if side < 0 else from_right
            slot = layer if a == 0 else layers + layer - (1 if side < 0 else 0)
            core = pick(even, (first_ref[slot], second_ref[slot]))
            core_tile = lane_tile(pick(even, tuple(raw_rows)) + slot * rows, rows)
            strip = lambda slot: pick(even, (first_pack_ref[slot], second_pack_ref[slot]))
            strip_start = pick(even, tuple(strip_rows))
        if both_sides:
            slot = 2 * layer + a
        else:
            slot = layer
        halo = jnp.concatenate(
            [strip(slot), lane_tile(strip_start + slot * SUBLANES, SUBLANES)], axis=1
        )
        if a == 1 and not both_sides:
            halo = turned(halo, REACH, 0)
        return jnp.concatenate([jnp.concatenate([core, core_tile], axis=1), halo], axis=0)

    faces = [2.0] * (count - 1)
    faces[layers - 1] = jnp.where(ix > 0, 2.0, 0.0)
    faces[2 * layers - 1] = jnp.where(ix < nx - 1, 2.0, 0.0)
    shape = (rows + 2 * REACH, lanes + LANES)
    iterate(
        count,
        functools.partial(window, 0),
        functools.partial(window, 1),
        faces,
        numerators(shape, 0, rows, iy, ny, 1.0),
        numerators(shape, 1, lanes, iz, nz, 1.0),
        jnp.full((1, shape[1]), low_ref[0]),
        jnp.full((1, shape[1]), high_ref[0]),
        storage_rate,
        refs,
    )
    p_ref = refs[-1]
    for x in range(layers):
        fine = p_ref[REACH + x, :rows, :lanes]
        fine_ref[x] = fine
        diff_ref[x] = fine - spread_ref[x]


def fine_level(low_bound, high_bound, log_perm, source, own, raw, near, tile, spread, slots, peers):
    layers, rows, lanes = log_perm.shape
    window = (layers + 2 * REACH, rows + 2 * REACH, lanes + LANES)
    out = jax.ShapeDtypeStruct(log_perm.shape, jnp.float32)
    return pl.pallas_call(
        functools.partial(fine_kernel, peers, slots),
        out_shape=(out, out),
        in_specs=[SMEM, SMEM] + [VMEM] * 9,
        out_specs=(VMEM, VMEM),
        scratch_shapes=window_scratch(*window),
        compiler_params=pltpu.CompilerParams(vmem_limit_bytes=24 << 20),
        cost_estimate=pl.CostEstimate(flops=20_000_000, bytes_accessed=10_000_000, transcendentals=0),
        name="fine_level",
    )(low_bound, high_bound, log_perm, source, own, *raw, *near, tile, spread)


def shards(peers, log_perm, source, low_bound, high_bound):
    nx, ny, nz = peers
    layers, rows, lanes = log_perm.shape
    assert layers == REACH and rows == 2 * SUBLANES and nx > 2
    half = lanes // 2
    stacked = jnp.concatenate([log_perm, source], axis=0)
    got_rows = swap("gy", ny, stacked[:, rows - SUBLANES :], stacked[:, :SUBLANES])
    raw = swap("gx", nx, jnp.concatenate([log_perm, source[1:]]), jnp.concatenate([log_perm, source[:-1]]))
    own = pack(log_perm, source, got_rows)
    near = swap("gx", nx, own, own)
    strips = len(got_rows) * layers
    pooled = own[strips:]
    left_half, right_half = pooled[..., :half], pooled[..., half:]

    def far_pack(inner, outer):
        halo = (left_half, right_half)[inner][2]
        return jnp.stack(
            [
                jnp.concatenate([left_half[inner], left_half[outer]], axis=1),
                jnp.concatenate([right_half[inner], halo], axis=1),
            ]
        )

    far = far_swap("gx", nx, far_pack(1, 0), far_pack(0, 1))
    offset, edges = 0, []

    def add(array, columns):
        nonlocal offset
        start = offset
        flat = array.reshape(-1, array.shape[-1])[:, columns]
        edges.append(flat)
        offset += flat.shape[0]
        return start

    whole = slice(0, lanes)

    def add_pooled(array):
        return add(array[strips:].reshape(-1, SUBLANES, 2, half).swapaxes(1, 2), slice(0, half))

    own_rows = add(stacked, whole)
    raw_rows = [add(block, whole) for block in raw]
    own_strip_rows = add(own[:strips], whole)
    strip_rows = [add(block[:strips], whole) for block in near]
    own_pooled = add_pooled(own)
    near_pooled = [add_pooled(block) for block in near]
    far_rows = [add(block[0], slice(0, half)) for block in far]
    last = jnp.concatenate([flat[:, -LANES:] for flat in edges])
    first = jnp.concatenate([flat[:, :LANES] for flat in edges])
    if nz == 2:
        sent = jnp.where(lax.axis_index("gz") == 0, last, first)
        tile = lax.ppermute(sent, "gz", [(0, 1), (1, 0)])
    else:
        even = lax.axis_index("gz") % 2 == 0
        got = swap("gz", nz, last, first)
        tile = jnp.where(
            iota(last.shape, 1) < LANES // 2, from_right(even, got), from_left(even, got)
        )
    spread = coarse_level(
        low_bound,
        high_bound,
        own,
        near,
        far,
        tile,
        (strips, own_pooled, near_pooled, far_rows),
        peers,
    )
    return fine_level(
        low_bound,
        high_bound,
        log_perm,
        source,
        own,
        raw,
        near,
        tile,
        spread,
        (own_rows, own_strip_rows, raw_rows, strip_rows),
        peers,
    )


def solution(mesh):
    peers = tuple(mesh.shape[axis] for axis in AXES)
    split = P(("groups", "gx"), "gy", "gz")
    return jax.shard_map(
        functools.partial(shards, peers),
        mesh=mesh,
        in_specs=(split, split, P(), P()),
        out_specs=(split, split),
        check_vma=False,
    )
```

time: 49.6 us -> 25.3 us (0.51)
  blocking collectives: 24.2 us -> 0 us
  starting transfers between devices: 9.02 us -> 12.2 us
  waiting for transfers between devices: 7.95 us -> 5.47 us
  Pallas kernels: 5.05 us -> 3.96 us
    all_gather x1 -> x0, blocking collectives: 24.2 us -> none  [shards(): everyone = lax.all_gather(pool(log_perm, source), AXES)]
    ppermute x4 -> x7, starting transfers between devices: 9.02 us -> 12.2 us  [the longest x3 8.05 us: swap(): lax.ppermute(right if right is left else jnp.where(even, right, left), ax...]
    ppermute x4 -> x7, waiting for transfers between devices: 7.95 us -> 5.47 us  [the longest x1 4.11 us: far_swap(): got.append(lax.ppermute(jnp.where(low, *sent), axis, both_ways(chosen)))]
    pallas_call x3, Pallas kernels: 5.05 us -> 3.96 us  [the longest x1 2.95 us: fine_level(): pl.pallas_call(functools.partial(fine_kernel, peers, slots), out_shape=(o...]
    unnamed x6 -> x14, local copies, waits for them, and re-layouts: 0.03 us -> 1.03 us
    slice x1 -> x4, local copies, waits for them, and re-layouts: 0.96 us -> 0.03 us  [the longest x3 0.01 us: add_pooled(): array[strips:].reshape(-1, SUBLANES, 2, half).swapaxes(1, 2)]
  transfers between devices with their start and end apart: 4 -> 7, of which waited for: 3 -> 3; matrix products, arithmetic and copies ran while one was open for 0% -> 1% of each run, Pallas kernels for 4% -> 1%
where the time goes in v2:
time: 25.3 us; the launch traced here: 25.1 us
  starting transfers between devices  12.2 us (48%)
  waiting for transfers between devices  5.47 us (22%)
  Pallas kernels  3.96 us (16%)
  between operations  2.25 us (9%)
  local copies, waits for them, and re-layouts  1.1 us (4%)
    ppermute x3, starting transfers between devices, swap(): lax.ppermute(right if right is left else jnp.where(even, right, left), ax...  8.05 us
    ppermute x1, waiting for transfers between devices, far_swap(): got.append(lax.ppermute(jnp.where(low, *sent), axis, both_ways(chosen)))  4.11 us
    pallas_call x1, Pallas kernels, fine_level(): pl.pallas_call(functools.partial(fine_kernel, peers, slots), out_shape=(o...  2.95 us
    ppermute x1, starting transfers between devices, far_swap(): got.append(lax.ppermute(jnp.where(low, *sent), axis, both_ways(chosen)))  2.79 us
    ppermute x2, starting transfers between devices, swap(): lax.ppermute(left if right is left else jnp.where(even, left, right), axi...  1.32 us
    ppermute x3, waiting for transfers between devices, swap(): lax.ppermute(right if right is left else jnp.where(even, right, left), ax...  1.06 us
    unnamed x14, local copies, waits for them, and re-layouts  1.03 us
    pallas_call x1, Pallas kernels, coarse_level(): pl.pallas_call(functools.partial(coarse_kernel, peers, slots, len(far)),...  0.78 us
  transfers between devices with their start and end apart: 7, of which 3 were waited for; matrix products, arithmetic and copies ran while one was open for 1% of the time, Pallas kernels for 1%

profile of v2, /device:TPU:0, one launch (start us, length us, event | category | flops | bytes accessed | tf_op | source)
XLA Modules:
  0.0 25.1 jit_solution(1953285989256915115)
XLA Ops:
  0.6 0.0 copy-start
  0.6 1.0 %constant_dynamic-update-slice_fusion.1 = f32[8,16,512]{2,1,0:T(8,128)S(1)} fusion(f32[4,16,512]{2,1,0:T(8,128)} %log_ref.3), kind=kLoop, calls=%fused_computation.16 | loop fusion | bytes 262144
  1.6 0.0 copy-done
  1.7 0.0 copy-start.1
  1.7 3.0 %collective-permute-start = (f32[8,8,512]{2,1,0:T(8,128)S(1)}, f32[8,8,512]{2,1,0:T(8,128)S(1)}, u32[]{:S(2)}, u32[]{:S(2)}) collective-permute-start(f32[8,8,512]{2,1,0:T(8,128)S(1)} %slice_select_fusion), channel_id=1, source_target_pairs={{0,2},{2,0},{1,3},{3,1},{4,6},{6,4},{5,7},{7,5},{8,10},{10,8},{9,1... | collective-permute-start | bytes 393224 | tf_op jit(solution)/shard_map/ppermute | solution.py:35
  4.7 0.0 copy-done.1
  4.8 1.6 %collective-permute-start.1 = (f32[7,16,512]{2,1,0:T(8,128)S(1)}, f32[7,16,512]{2,1,0:T(8,128)S(1)}, u32[]{:S(2)}, u32[]{:S(2)}) collective-permute-start(f32[7,16,512]{2,1,0:T(8,128)S(1)} %get-tuple-element.3), channel_id=1, source_target_pairs={{0,4},{4,0},{8,12},{12,8},{1,5},{5,1},{9,13},{13,9},{2,6},{6,2},{1... | collective-permute-start | bytes 688136 | tf_op jit(solution)/shard_map/ppermute | solution.py:35
  6.4 0.7 %collective-permute-start.2 = (f32[7,16,512]{2,1,0:T(8,128)S(1)}, f32[7,16,512]{2,1,0:T(8,128)S(1)}, u32[]{:S(2)}, u32[]{:S(2)}) collective-permute-start(f32[7,16,512]{2,1,0:T(8,128)S(1)} %get-tuple-element.2), channel_id=1, source_target_pairs={{4,8},{8,4},{5,9},{9,5},{6,10},{10,6},{7,11},{11,7},{20,24},{24,20... | collective-permute-start | bytes 688136 | tf_op jit(solution)/shard_map/ppermute | solution.py:42
  7.1 1.1 %collective-permute-done.refs_0_ = f32[8,8,512]{2,1,0:T(8,128)S(1)} collective-permute-done((f32[8,8,512]{2,1,0:T(8,128)S(1)}, f32[8,8,512]{2,1,0:T(8,128)S(1)}, u32[]{:S(2)}, u32[]{:S(2)}) %collective-permute-start) | collective-permute-done | bytes 131104 | tf_op jit(solution)/shard_map/ppermute | solution.py:35
  8.2 0.2 pack.1.own_ref
  8.4 3.4 %collective-permute-start.3 = (f32[7,8,512]{2,1,0:T(8,128)S(1)}, f32[7,8,512]{2,1,0:T(8,128)S(1)}, u32[]{:S(2)}, u32[]{:S(2)}) collective-permute-start(f32[7,8,512]{2,1,0:T(8,128)S(1)} %pack.1.own_ref), channel_id=1, source_target_pairs={{0,4},{4,0},{8,12},{12,8},{1,5},{5,1},{9,13},{13,9},{2,6},{6,2},{1... | collective-permute-start | bytes 344072 | tf_op jit(solution)/shard_map/ppermute | solution.py:35
  11.8 0.7 %collective-permute-start.4 = (f32[7,8,512]{2,1,0:T(8,128)S(1)}, f32[7,8,512]{2,1,0:T(8,128)S(1)}, u32[]{:S(2)}, u32[]{:S(2)}) collective-permute-start(f32[7,8,512]{2,1,0:T(8,128)S(1)} %pack.1.own_ref), channel_id=1, source_target_pairs={{4,8},{8,4},{5,9},{9,5},{6,10},{10,6},{7,11},{11,7},{20,24},{24,20... | collective-permute-start | bytes 344072 | tf_op jit(solution)/shard_map/ppermute | solution.py:42
  12.5 2.8 %collective-permute-start.5 = (f32[2,8,512]{2,1,0:T(8,128)S(1)}, f32[2,8,512]{2,1,0:T(8,128)S(1)}, u32[]{:S(2)}, u32[]{:S(2)}) collective-permute-start(f32[2,8,512]{2,1,0:T(8,128)S(1)} %maximum_select_fusion), channel_id=1, source_target_pairs={{0,8},{8,0},{4,12},{12,4},{1,9},{9,1},{5,13},{13,5},{2,10},{10,2},... | collective-permute-start | bytes 98312 | tf_op jit(solution)/shard_map/ppermute | solution.py:58
  15.3 4.1 %collective-permute-done.5.refs_2_ = f32[2,8,512]{2,1,0:T(8,128)S(1)} collective-permute-done((f32[2,8,512]{2,1,0:T(8,128)S(1)}, f32[2,8,512]{2,1,0:T(8,128)S(1)}, u32[]{:S(2)}, u32[]{:S(2)}) %collective-permute-start.5) | collective-permute-done | bytes 32800 | tf_op jit(solution)/shard_map/ppermute | solution.py:58
  19.5 0.0 collective-permute-done.1.first_ref
  19.5 0.0 collective-permute-done.2.second_ref
  19.5 0.0 collective-permute-done.3.refs_0_.first_pack_ref
  19.6 0.0 collective-permute-done.4.refs_1_.second_pack_ref
  19.7 0.1 collective-permute-start.6
  21.1 0.3 %collective-permute-done.6.refs_3_.tile_ref = f32[600,128]{1,0:T(8,128)S(1)} collective-permute-done((f32[600,128]{1,0:T(8,128)S(1)}, f32[600,128]{1,0:T(8,128)S(1)}, u32[]{:S(2)}, u32[]{:S(2)}) %collective-permute-start.6) | collective-permute-done | bytes 307232 | tf_op jit(solution)/shard_map/ppermute | solution.py:489
  21.4 0.8 %coarse_level.1.spread_ref = f32[4,16,512]{2,1,0:T(8,128)S(1)} custom-call(f32[1]{0:T(128)S(6)} %copy.25.low_ref, f32[1]{0:T(128)S(6)} %copy.26.high_ref, f32[7,8,512]{2,1,0:T(8,128)S(1)} %pack.1.own_ref, f32[7,8,512]{2,1,0:T(8,128)S(1)} %collective-permute-done.3.refs_0_.first_pack_ref, f32[7,8,512]{2,1,0:T(8,128)S(1)} %collective-permute-done.4.refs_1_.second_pack_ref, ...), custom_call_target="tpu_custom_call" | custom-call | flops 20000000 | bytes 4000000 | tf_op jit(solution)/shard_map/coarse_level/pallas_call | solution.py:333
  22.2 3.0 %fine_level.1 = (f32[4,16,512]{2,1,0:T(8,128)}, f32[4,16,512]{2,1,0:T(8,128)}) custom-call(f32[1]{0:T(128)S(6)} %copy.25.low_ref, f32[1]{0:T(128)S(6)} %copy.26.high_ref, f32[4,16,512]{2,1,0:T(8,128)S(1)} %copy-done.1, f32[4,16,512]{2,1,0:T(8,128)S(1)} %copy-done, f32[7,8,512]{2,1,0:T(8,128)S(1)} %pack.1.own_ref, ...), custom_call_target="tpu_custom_call" | custom-call | flops 20000000 | bytes 10000000 | tf_op jit(solution)/shard_map/fine_level/pallas_call | solution.py:427
  (26 shorter events, 0.3 us)
Async XLA Ops:
  0.6 1.0 %copy-start = (f32[4,16,512]{2,1,0:T(8,128)S(1)}, f32[4,16,512]{2,1,0:T(8,128)}, u32[]{:S(2)}) copy-start(f32[4,16,512]{2,1,0:T(8,128)} %source_ref.3) | copy-start | bytes 393220
  1.7 3.0 %copy-start.1 = (f32[4,16,512]{2,1,0:T(8,128)S(1)}, f32[4,16,512]{2,1,0:T(8,128)}, u32[]{:S(2)}) copy-start(f32[4,16,512]{2,1,0:T(8,128)} %log_ref.3) | copy-start | bytes 393220
  1.7 6.5 %collective-permute-start = (f32[8,8,512]{2,1,0:T(8,128)S(1)}, f32[8,8,512]{2,1,0:T(8,128)S(1)}, u32[]{:S(2)}, u32[]{:S(2)}) collective-permute-start(f32[8,8,512]{2,1,0:T(8,128)S(1)} %slice_select_fusion), channel_id=1, source_target_pairs={{0,2},{2,0},{1,3},{3,1},{4,6},{6,4},{5,7},{7,5},{8,10},{10,8},{9,1... | collective-permute-start | bytes 393224 | tf_op jit(solution)/shard_map/ppermute | solution.py:35
  4.8 14.7 %collective-permute-start.1 = (f32[7,16,512]{2,1,0:T(8,128)S(1)}, f32[7,16,512]{2,1,0:T(8,128)S(1)}, u32[]{:S(2)}, u32[]{:S(2)}) collective-permute-start(f32[7,16,512]{2,1,0:T(8,128)S(1)} %get-tuple-element.3), channel_id=1, source_target_pairs={{0,4},{4,0},{8,12},{12,8},{1,5},{5,1},{9,13},{13,9},{2,6},{6,2},{1... | collective-permute-start | bytes 688136 | tf_op jit(solution)/shard_map/ppermute | solution.py:35
  6.4 13.1 %collective-permute-start.2 = (f32[7,16,512]{2,1,0:T(8,128)S(1)}, f32[7,16,512]{2,1,0:T(8,128)S(1)}, u32[]{:S(2)}, u32[]{:S(2)}) collective-permute-start(f32[7,16,512]{2,1,0:T(8,128)S(1)} %get-tuple-element.2), channel_id=1, source_target_pairs={{4,8},{8,4},{5,9},{9,5},{6,10},{10,6},{7,11},{11,7},{20,24},{24,20... | collective-permute-start | bytes 688136 | tf_op jit(solution)/shard_map/ppermute | solution.py:42
  8.4 11.1 %collective-permute-start.3 = (f32[7,8,512]{2,1,0:T(8,128)S(1)}, f32[7,8,512]{2,1,0:T(8,128)S(1)}, u32[]{:S(2)}, u32[]{:S(2)}) collective-permute-start(f32[7,8,512]{2,1,0:T(8,128)S(1)} %pack.1.own_ref), channel_id=1, source_target_pairs={{0,4},{4,0},{8,12},{12,8},{1,5},{5,1},{9,13},{13,9},{2,6},{6,2},{1... | collective-permute-start | bytes 344072 | tf_op jit(solution)/shard_map/ppermute | solution.py:35
  11.8 7.7 %collective-permute-start.4 = (f32[7,8,512]{2,1,0:T(8,128)S(1)}, f32[7,8,512]{2,1,0:T(8,128)S(1)}, u32[]{:S(2)}, u32[]{:S(2)}) collective-permute-start(f32[7,8,512]{2,1,0:T(8,128)S(1)} %pack.1.own_ref), channel_id=1, source_target_pairs={{4,8},{8,4},{5,9},{9,5},{6,10},{10,6},{7,11},{11,7},{20,24},{24,20... | collective-permute-start | bytes 344072 | tf_op jit(solution)/shard_map/ppermute | solution.py:42
  12.5 6.9 %collective-permute-start.5 = (f32[2,8,512]{2,1,0:T(8,128)S(1)}, f32[2,8,512]{2,1,0:T(8,128)S(1)}, u32[]{:S(2)}, u32[]{:S(2)}) collective-permute-start(f32[2,8,512]{2,1,0:T(8,128)S(1)} %maximum_select_fusion), channel_id=1, source_target_pairs={{0,8},{8,0},{4,12},{12,4},{1,9},{9,1},{5,13},{13,5},{2,10},{10,2},... | collective-permute-start | bytes 98312 | tf_op jit(solution)/shard_map/ppermute | solution.py:58
  19.7 1.7 %collective-permute-start.6 = (f32[600,128]{1,0:T(8,128)S(1)}, f32[600,128]{1,0:T(8,128)S(1)}, u32[]{:S(2)}, u32[]{:S(2)}) collective-permute-start(f32[600,128]{1,0:T(8,128)S(1)} %broadcast_select_fusion), channel_id=1, source_target_pairs={{0,1},{1,0},{2,3},{3,2},{4,5},{5,4},{6,7},{7,6},{8,9},{9,8},{10,11... | collective-permute-start | bytes 921608 | tf_op jit(solution)/shard_map/ppermute | solution.py:489

commit v3 on v2

--- a/solution.py
+++ b/solution.py
@@ -26,8 +26,11 @@
     return pltpu.roll(value, shift % size, axis)
 
 
-def both_ways(pairs):
-    return [pair for i, j in pairs for pair in ((i, j), (j, i))]
+def both_ways(peers, pairs):
+    partner = list(range(peers))
+    for i, j in pairs:
+        partner[i], partner[j] = j, i
+    return list(enumerate(partner))
 
 
 def swap(axis, peers, right, left):
@@ -35,14 +38,14 @@
     first = lax.ppermute(
         right if right is left else jnp.where(even, right, left),
         axis,
-        both_ways([(i, i + 1) for i in range(0, peers - 1, 2)]),
+        both_ways(peers, [(i, i + 1) for i in range(0, peers - 1, 2)]),
     )
     if peers == 2:
         return (first,)
     second = lax.ppermute(
         left if right is left else jnp.where(even, left, right),
         axis,
-        both_ways([(i, i + 1) for i in range(1, peers - 1, 2)]),
+        both_ways(peers, [(i, i + 1) for i in range(1, peers - 1, 2)]),
     )
     return (first, second)
 
@@ -55,7 +58,7 @@
     got = []
     for chosen, sent in ((near, (right, left)), (rest, (left, right))):
         if chosen:
-            got.append(lax.ppermute(jnp.where(low, *sent), axis, both_ways(chosen)))
+            got.append(lax.ppermute(jnp.where(low, *sent), axis, both_ways(peers, chosen)))
     return tuple(got)
 
 

time: 25.3 us -> 25.3 us (level)
  no operation moved by 1% of the time
where the time goes in v3:
time: 25.3 us; the launch traced here: 25.1 us
  starting transfers between devices  12.2 us (48%)
  waiting for transfers between devices  5.47 us (22%)
  Pallas kernels  3.96 us (16%)
  between operations  2.25 us (9%)
  local copies, waits for them, and re-layouts  1.1 us (4%)
    ppermute x3, starting transfers between devices, swap(): lax.ppermute(right if right is left else jnp.where(even, right, left), ax...  8.05 us
    ppermute x1, waiting for transfers between devices, far_swap(): lax.ppermute(jnp.where(low, *sent), axis, both_ways(peers, chosen))  4.11 us
    pallas_call x1, Pallas kernels, fine_level(): pl.pallas_call(functools.partial(fine_kernel, peers, slots), out_shape=(o...  2.95 us
    ppermute x1, starting transfers between devices, far_swap(): lax.ppermute(jnp.where(low, *sent), axis, both_ways(peers, chosen))  2.79 us
    ppermute x2, starting transfers between devices, swap(): lax.ppermute(left if right is left else jnp.where(even, left, right), axi...  1.32 us
    ppermute x3, waiting for transfers between devices, swap(): lax.ppermute(right if right is left else jnp.where(even, right, left), ax...  1.06 us
    unnamed x14, local copies, waits for them, and re-layouts  1.03 us
    pallas_call x1, Pallas kernels, coarse_level(): pl.pallas_call(functools.partial(coarse_kernel, peers, slots, len(far)),...  0.78 us
  transfers between devices with their start and end apart: 7, of which 3 were waited for; matrix products, arithmetic and copies ran while one was open for 1% of the time, Pallas kernels for 1%

profile of v3, /device:TPU:0, one launch (start us, length us, event | category | flops | bytes accessed | tf_op | source)
XLA Modules:
  0.0 25.1 jit_solution(3396672782872468761)
XLA Ops:
  0.6 0.0 copy-start
  0.6 1.0 %constant_dynamic-update-slice_fusion.1 = f32[8,16,512]{2,1,0:T(8,128)S(1)} fusion(f32[4,16,512]{2,1,0:T(8,128)} %log_ref.3), kind=kLoop, calls=%fused_computation.16 | loop fusion | bytes 262144
  1.6 0.0 copy-done
  1.7 0.0 copy-start.1
  1.7 3.0 %collective-permute-start = (f32[8,8,512]{2,1,0:T(8,128)S(1)}, f32[8,8,512]{2,1,0:T(8,128)S(1)}, u32[]{:S(2)}, u32[]{:S(2)}) collective-permute-start(f32[8,8,512]{2,1,0:T(8,128)S(1)} %slice_select_fusion), channel_id=1, source_target_pairs={{0,2},{2,0},{1,3},{3,1},{4,6},{6,4},{5,7},{7,5},{8,10},{10,8},{9,1... | collective-permute-start | bytes 393224 | tf_op jit(solution)/shard_map/ppermute | solution.py:38
  4.7 0.0 copy-done.1
  4.8 1.6 %collective-permute-start.1 = (f32[7,16,512]{2,1,0:T(8,128)S(1)}, f32[7,16,512]{2,1,0:T(8,128)S(1)}, u32[]{:S(2)}, u32[]{:S(2)}) collective-permute-start(f32[7,16,512]{2,1,0:T(8,128)S(1)} %get-tuple-element.3), channel_id=1, source_target_pairs={{0,4},{4,0},{8,12},{12,8},{1,5},{5,1},{9,13},{13,9},{2,6},{6,2},{1... | collective-permute-start | bytes 688136 | tf_op jit(solution)/shard_map/ppermute | solution.py:38
  6.4 0.7 %collective-permute-start.2 = (f32[7,16,512]{2,1,0:T(8,128)S(1)}, f32[7,16,512]{2,1,0:T(8,128)S(1)}, u32[]{:S(2)}, u32[]{:S(2)}) collective-permute-start(f32[7,16,512]{2,1,0:T(8,128)S(1)} %get-tuple-element.2), channel_id=1, source_target_pairs={{0,0},{4,8},{8,4},{12,12},{1,1},{5,9},{9,5},{13,13},{2,2},{6,10},{... | collective-permute-start | bytes 688136 | tf_op jit(solution)/shard_map/ppermute | solution.py:45
  7.1 1.1 %collective-permute-done.refs_0_ = f32[8,8,512]{2,1,0:T(8,128)S(1)} collective-permute-done((f32[8,8,512]{2,1,0:T(8,128)S(1)}, f32[8,8,512]{2,1,0:T(8,128)S(1)}, u32[]{:S(2)}, u32[]{:S(2)}) %collective-permute-start) | collective-permute-done | bytes 131104 | tf_op jit(solution)/shard_map/ppermute | solution.py:38
  8.2 0.2 pack.1.own_ref
  8.4 3.4 %collective-permute-start.3 = (f32[7,8,512]{2,1,0:T(8,128)S(1)}, f32[7,8,512]{2,1,0:T(8,128)S(1)}, u32[]{:S(2)}, u32[]{:S(2)}) collective-permute-start(f32[7,8,512]{2,1,0:T(8,128)S(1)} %pack.1.own_ref), channel_id=1, source_target_pairs={{0,4},{4,0},{8,12},{12,8},{1,5},{5,1},{9,13},{13,9},{2,6},{6,2},{1... | collective-permute-start | bytes 344072 | tf_op jit(solution)/shard_map/ppermute | solution.py:38
  11.8 0.7 %collective-permute-start.4 = (f32[7,8,512]{2,1,0:T(8,128)S(1)}, f32[7,8,512]{2,1,0:T(8,128)S(1)}, u32[]{:S(2)}, u32[]{:S(2)}) collective-permute-start(f32[7,8,512]{2,1,0:T(8,128)S(1)} %pack.1.own_ref), channel_id=1, source_target_pairs={{0,0},{4,8},{8,4},{12,12},{1,1},{5,9},{9,5},{13,13},{2,2},{6,10},{... | collective-permute-start | bytes 344072 | tf_op jit(solution)/shard_map/ppermute | solution.py:45
  12.5 2.8 %collective-permute-start.5 = (f32[2,8,512]{2,1,0:T(8,128)S(1)}, f32[2,8,512]{2,1,0:T(8,128)S(1)}, u32[]{:S(2)}, u32[]{:S(2)}) collective-permute-start(f32[2,8,512]{2,1,0:T(8,128)S(1)} %maximum_select_fusion), channel_id=1, source_target_pairs={{0,8},{4,12},{8,0},{12,4},{1,9},{5,13},{9,1},{13,5},{2,10},{6,14},... | collective-permute-start | bytes 98312 | tf_op jit(solution)/shard_map/ppermute | solution.py:61
  15.3 4.1 %collective-permute-done.5.refs_2_ = f32[2,8,512]{2,1,0:T(8,128)S(1)} collective-permute-done((f32[2,8,512]{2,1,0:T(8,128)S(1)}, f32[2,8,512]{2,1,0:T(8,128)S(1)}, u32[]{:S(2)}, u32[]{:S(2)}) %collective-permute-start.5) | collective-permute-done | bytes 32800 | tf_op jit(solution)/shard_map/ppermute | solution.py:61
  19.5 0.0 collective-permute-done.1.first_ref
  19.5 0.0 collective-permute-done.2.second_ref
  19.5 0.0 collective-permute-done.3.refs_0_.first_pack_ref
  19.6 0.0 collective-permute-done.4.refs_1_.second_pack_ref
  19.7 0.1 collective-permute-start.6
  21.1 0.3 %collective-permute-done.6.refs_3_.tile_ref = f32[600,128]{1,0:T(8,128)S(1)} collective-permute-done((f32[600,128]{1,0:T(8,128)S(1)}, f32[600,128]{1,0:T(8,128)S(1)}, u32[]{:S(2)}, u32[]{:S(2)}) %collective-permute-start.6) | collective-permute-done | bytes 307232 | tf_op jit(solution)/shard_map/ppermute | solution.py:492
  21.4 0.8 %coarse_level.1.spread_ref = f32[4,16,512]{2,1,0:T(8,128)S(1)} custom-call(f32[1]{0:T(128)S(6)} %copy.25.low_ref, f32[1]{0:T(128)S(6)} %copy.26.high_ref, f32[7,8,512]{2,1,0:T(8,128)S(1)} %pack.1.own_ref, f32[7,8,512]{2,1,0:T(8,128)S(1)} %collective-permute-done.3.refs_0_.first_pack_ref, f32[7,8,512]{2,1,0:T(8,128)S(1)} %collective-permute-done.4.refs_1_.second_pack_ref, ...), custom_call_target="tpu_custom_call" | custom-call | flops 20000000 | bytes 4000000 | tf_op jit(solution)/shard_map/coarse_level/pallas_call | solution.py:336
  22.2 3.0 %fine_level.1 = (f32[4,16,512]{2,1,0:T(8,128)}, f32[4,16,512]{2,1,0:T(8,128)}) custom-call(f32[1]{0:T(128)S(6)} %copy.25.low_ref, f32[1]{0:T(128)S(6)} %copy.26.high_ref, f32[4,16,512]{2,1,0:T(8,128)S(1)} %copy-done.1, f32[4,16,512]{2,1,0:T(8,128)S(1)} %copy-done, f32[7,8,512]{2,1,0:T(8,128)S(1)} %pack.1.own_ref, ...), custom_call_target="tpu_custom_call" | custom-call | flops 20000000 | bytes 10000000 | tf_op jit(solution)/shard_map/fine_level/pallas_call | solution.py:430
  (26 shorter events, 0.3 us)
Async XLA Ops:
  0.6 1.0 %copy-start = (f32[4,16,512]{2,1,0:T(8,128)S(1)}, f32[4,16,512]{2,1,0:T(8,128)}, u32[]{:S(2)}) copy-start(f32[4,16,512]{2,1,0:T(8,128)} %source_ref.3) | copy-start | bytes 393220
  1.7 3.0 %copy-start.1 = (f32[4,16,512]{2,1,0:T(8,128)S(1)}, f32[4,16,512]{2,1,0:T(8,128)}, u32[]{:S(2)}) copy-start(f32[4,16,512]{2,1,0:T(8,128)} %log_ref.3) | copy-start | bytes 393220
  1.7 6.5 %collective-permute-start = (f32[8,8,512]{2,1,0:T(8,128)S(1)}, f32[8,8,512]{2,1,0:T(8,128)S(1)}, u32[]{:S(2)}, u32[]{:S(2)}) collective-permute-start(f32[8,8,512]{2,1,0:T(8,128)S(1)} %slice_select_fusion), channel_id=1, source_target_pairs={{0,2},{2,0},{1,3},{3,1},{4,6},{6,4},{5,7},{7,5},{8,10},{10,8},{9,1... | collective-permute-start | bytes 393224 | tf_op jit(solution)/shard_map/ppermute | solution.py:38
  4.8 14.7 %collective-permute-start.1 = (f32[7,16,512]{2,1,0:T(8,128)S(1)}, f32[7,16,512]{2,1,0:T(8,128)S(1)}, u32[]{:S(2)}, u32[]{:S(2)}) collective-permute-start(f32[7,16,512]{2,1,0:T(8,128)S(1)} %get-tuple-element.3), channel_id=1, source_target_pairs={{0,4},{4,0},{8,12},{12,8},{1,5},{5,1},{9,13},{13,9},{2,6},{6,2},{1... | collective-permute-start | bytes 688136 | tf_op jit(solution)/shard_map/ppermute | solution.py:38
  6.4 13.1 %collective-permute-start.2 = (f32[7,16,512]{2,1,0:T(8,128)S(1)}, f32[7,16,512]{2,1,0:T(8,128)S(1)}, u32[]{:S(2)}, u32[]{:S(2)}) collective-permute-start(f32[7,16,512]{2,1,0:T(8,128)S(1)} %get-tuple-element.2), channel_id=1, source_target_pairs={{0,0},{4,8},{8,4},{12,12},{1,1},{5,9},{9,5},{13,13},{2,2},{6,10},{... | collective-permute-start | bytes 688136 | tf_op jit(solution)/shard_map/ppermute | solution.py:45
  8.4 11.1 %collective-permute-start.3 = (f32[7,8,512]{2,1,0:T(8,128)S(1)}, f32[7,8,512]{2,1,0:T(8,128)S(1)}, u32[]{:S(2)}, u32[]{:S(2)}) collective-permute-start(f32[7,8,512]{2,1,0:T(8,128)S(1)} %pack.1.own_ref), channel_id=1, source_target_pairs={{0,4},{4,0},{8,12},{12,8},{1,5},{5,1},{9,13},{13,9},{2,6},{6,2},{1... | collective-permute-start | bytes 344072 | tf_op jit(solution)/shard_map/ppermute | solution.py:38
  11.8 7.7 %collective-permute-start.4 = (f32[7,8,512]{2,1,0:T(8,128)S(1)}, f32[7,8,512]{2,1,0:T(8,128)S(1)}, u32[]{:S(2)}, u32[]{:S(2)}) collective-permute-start(f32[7,8,512]{2,1,0:T(8,128)S(1)} %pack.1.own_ref), channel_id=1, source_target_pairs={{0,0},{4,8},{8,4},{12,12},{1,1},{5,9},{9,5},{13,13},{2,2},{6,10},{... | collective-permute-start | bytes 344072 | tf_op jit(solution)/shard_map/ppermute | solution.py:45
  12.5 6.9 %collective-permute-start.5 = (f32[2,8,512]{2,1,0:T(8,128)S(1)}, f32[2,8,512]{2,1,0:T(8,128)S(1)}, u32[]{:S(2)}, u32[]{:S(2)}) collective-permute-start(f32[2,8,512]{2,1,0:T(8,128)S(1)} %maximum_select_fusion), channel_id=1, source_target_pairs={{0,8},{4,12},{8,0},{12,4},{1,9},{5,13},{9,1},{13,5},{2,10},{6,14},... | collective-permute-start | bytes 98312 | tf_op jit(solution)/shard_map/ppermute | solution.py:61
  19.7 1.7 %collective-permute-start.6 = (f32[600,128]{1,0:T(8,128)S(1)}, f32[600,128]{1,0:T(8,128)S(1)}, u32[]{:S(2)}, u32[]{:S(2)}) collective-permute-start(f32[600,128]{1,0:T(8,128)S(1)} %broadcast_select_fusion), channel_id=1, source_target_pairs={{0,1},{1,0},{2,3},{3,2},{4,5},{5,4},{6,7},{7,6},{8,9},{9,8},{10,11... | collective-permute-start | bytes 921608 | tf_op jit(solution)/shard_map/ppermute | solution.py:492

commit v4 on v3

--- a/solution.py
+++ b/solution.py
@@ -26,26 +26,36 @@
     return pltpu.roll(value, shift % size, axis)
 
 
-def both_ways(peers, pairs):
-    partner = list(range(peers))
+def permute(value, axis, peers, pairs):
+    cores = lax.axis_size("gz")
+    if axis == "gz" or cores % 2:
+        return lax.ppermute(value, axis, [pair for i, j in pairs for pair in ((i, j), (j, i))])
+    partner = {}
     for i, j in pairs:
         partner[i], partner[j] = j, i
-    return list(enumerate(partner))
+    moves = [
+        (i * cores + core, partner[i] * cores + core if i in partner else i * cores + (core ^ 1))
+        for i in range(peers)
+        for core in range(cores)
+    ]
+    return lax.ppermute(value, (axis, "gz"), moves)
 
 
 def swap(axis, peers, right, left):
     even = lax.axis_index(axis) % 2 == 0
-    first = lax.ppermute(
+    first = permute(
         right if right is left else jnp.where(even, right, left),
         axis,
-        both_ways(peers, [(i, i + 1) for i in range(0, peers - 1, 2)]),
+        peers,
+        [(i, i + 1) for i in range(0, peers - 1, 2)],
     )
     if peers == 2:
         return (first,)
-    second = lax.ppermute(
+    second = permute(
         left if right is left else jnp.where(even, left, right),
         axis,
-        both_ways(peers, [(i, i + 1) for i in range(1, peers - 1, 2)]),
+        peers,
+        [(i, i + 1) for i in range(1, peers - 1, 2)],
     )
     return (first, second)
 
@@ -58,7 +68,7 @@
     got = []
     for chosen, sent in ((near, (right, left)), (rest, (left, right))):
         if chosen:
-            got.append(lax.ppermute(jnp.where(low, *sent), axis, both_ways(peers, chosen)))
+            got.append(permute(jnp.where(low, *sent), axis, peers, chosen))
     return tuple(got)
 
 

time: 25.3 us -> 23.4 us (0.925)
  starting transfers between devices: 12.2 us -> 9.27 us
  waiting for transfers between devices: 5.47 us -> 6.6 us
    ppermute x6, starting transfers between devices: 12.2 us -> 9.19 us  [permute(): return lax.ppermute(value, (axis, 'gz'), moves)]
    ppermute x6, waiting for transfers between devices: 5.18 us -> 6.31 us  [permute(): return lax.ppermute(value, (axis, 'gz'), moves)]
where the time goes in v4:
time: 23.4 us; the launch traced here: 23.2 us
  starting transfers between devices  9.27 us (40%)
  waiting for transfers between devices  6.6 us (28%)
  Pallas kernels  3.96 us (17%)
  between operations  2.2 us (9%)
  local copies, waits for them, and re-layouts  1.09 us (5%)
    ppermute x6, starting transfers between devices, permute(): return lax.ppermute(value, (axis, 'gz'), moves)  9.19 us
    ppermute x6, waiting for transfers between devices, permute(): return lax.ppermute(value, (axis, 'gz'), moves)  6.31 us
    pallas_call x1, Pallas kernels, fine_level(): pl.pallas_call(functools.partial(fine_kernel, peers, slots), out_shape=(o...  2.95 us
    unnamed x14, local copies, waits for them, and re-layouts  1.03 us
    pallas_call x1, Pallas kernels, coarse_level(): pl.pallas_call(functools.partial(coarse_kernel, peers, slots, len(far)),...  0.78 us
  transfers between devices with their start and end apart: 7, of which 3 were waited for; matrix products, arithmetic and copies ran while one was open for 1% of the time, Pallas kernels for 1%

profile of v4, /device:TPU:0, one launch (start us, length us, event | category | flops | bytes accessed | tf_op | source)
XLA Modules:
  0.0 23.2 jit_solution(16543272552617673356)
XLA Ops:
  0.6 0.0 copy-start
  0.6 1.0 %constant_dynamic-update-slice_fusion.1 = f32[8,16,512]{2,1,0:T(8,128)S(1)} fusion(f32[4,16,512]{2,1,0:T(8,128)} %log_ref.3), kind=kLoop, calls=%fused_computation.16 | loop fusion | bytes 262144
  1.6 0.0 copy-done
  1.7 0.0 copy-start.1
  1.7 3.0 %collective-permute-start = (f32[8,8,512]{2,1,0:T(8,128)S(1)}, f32[8,8,512]{2,1,0:T(8,128)S(1)}, u32[]{:S(2)}, u32[]{:S(2)}) collective-permute-start(f32[8,8,512]{2,1,0:T(8,128)S(1)} %slice_select_fusion), channel_id=1, source_target_pairs={{0,2},{1,3},{2,0},{3,1},{4,6},{5,7},{6,4},{7,5},{8,10},{9,11},{10,... | collective-permute-start | bytes 393224 | tf_op jit(solution)/shard_map/ppermute | solution.py:41
  4.7 0.0 copy-done.1
  4.8 1.6 %collective-permute-start.1 = (f32[7,16,512]{2,1,0:T(8,128)S(1)}, f32[7,16,512]{2,1,0:T(8,128)S(1)}, u32[]{:S(2)}, u32[]{:S(2)}) collective-permute-start(f32[7,16,512]{2,1,0:T(8,128)S(1)} %get-tuple-element.3), channel_id=1, source_target_pairs={{0,4},{1,5},{4,0},{5,1},{8,12},{9,13},{12,8},{13,9},{2,6},{3,7},{6... | collective-permute-start | bytes 688136 | tf_op jit(solution)/shard_map/ppermute | solution.py:41
  6.4 0.0 collective-permute-start.2
  6.4 1.8 %collective-permute-done.refs_0_ = f32[8,8,512]{2,1,0:T(8,128)S(1)} collective-permute-done((f32[8,8,512]{2,1,0:T(8,128)S(1)}, f32[8,8,512]{2,1,0:T(8,128)S(1)}, u32[]{:S(2)}, u32[]{:S(2)}) %collective-permute-start) | collective-permute-done | bytes 131104 | tf_op jit(solution)/shard_map/ppermute | solution.py:41
  8.2 0.2 pack.1.own_ref
  8.4 1.9 %collective-permute-start.3 = (f32[7,8,512]{2,1,0:T(8,128)S(1)}, f32[7,8,512]{2,1,0:T(8,128)S(1)}, u32[]{:S(2)}, u32[]{:S(2)}) collective-permute-start(f32[7,8,512]{2,1,0:T(8,128)S(1)} %pack.1.own_ref), channel_id=1, source_target_pairs={{0,4},{1,5},{4,0},{5,1},{8,12},{9,13},{12,8},{13,9},{2,6},{3,7},{6... | collective-permute-start | bytes 344072 | tf_op jit(solution)/shard_map/ppermute | solution.py:41
  10.3 0.0 collective-permute-start.4
  10.4 2.7 %collective-permute-start.5 = (f32[2,8,512]{2,1,0:T(8,128)S(1)}, f32[2,8,512]{2,1,0:T(8,128)S(1)}, u32[]{:S(2)}, u32[]{:S(2)}) collective-permute-start(f32[2,8,512]{2,1,0:T(8,128)S(1)} %maximum_select_fusion), channel_id=1, source_target_pairs={{0,8},{1,9},{4,12},{5,13},{8,0},{9,1},{12,4},{13,5},{2,10},{3,11},... | collective-permute-start | bytes 98312 | tf_op jit(solution)/shard_map/ppermute | solution.py:41
  13.0 4.5 %collective-permute-done.5.refs_2_ = f32[2,8,512]{2,1,0:T(8,128)S(1)} collective-permute-done((f32[2,8,512]{2,1,0:T(8,128)S(1)}, f32[2,8,512]{2,1,0:T(8,128)S(1)}, u32[]{:S(2)}, u32[]{:S(2)}) %collective-permute-start.5) | collective-permute-done | bytes 32800 | tf_op jit(solution)/shard_map/ppermute | solution.py:41
  17.6 0.0 collective-permute-done.1.first_ref
  17.6 0.0 collective-permute-done.2.second_ref
  17.6 0.0 collective-permute-done.3.refs_0_.first_pack_ref
  17.7 0.0 collective-permute-done.4.refs_1_.second_pack_ref
  17.8 0.1 collective-permute-start.6
  19.2 0.3 %collective-permute-done.6.refs_3_.tile_ref = f32[600,128]{1,0:T(8,128)S(1)} collective-permute-done((f32[600,128]{1,0:T(8,128)S(1)}, f32[600,128]{1,0:T(8,128)S(1)}, u32[]{:S(2)}, u32[]{:S(2)}) %collective-permute-start.6) | collective-permute-done | bytes 307232 | tf_op jit(solution)/shard_map/ppermute | solution.py:502
  19.5 0.8 %coarse_level.1.spread_ref = f32[4,16,512]{2,1,0:T(8,128)S(1)} custom-call(f32[1]{0:T(128)S(6)} %copy.25.low_ref, f32[1]{0:T(128)S(6)} %copy.26.high_ref, f32[7,8,512]{2,1,0:T(8,128)S(1)} %pack.1.own_ref, f32[7,8,512]{2,1,0:T(8,128)S(1)} %collective-permute-done.3.refs_0_.first_pack_ref, f32[7,8,512]{2,1,0:T(8,128)S(1)} %collective-permute-done.4.refs_1_.second_pack_ref, ...), custom_call_target="tpu_custom_call" | custom-call | flops 20000000 | bytes 4000000 | tf_op jit(solution)/shard_map/coarse_level/pallas_call | solution.py:346
  20.3 3.0 %fine_level.1 = (f32[4,16,512]{2,1,0:T(8,128)}, f32[4,16,512]{2,1,0:T(8,128)}) custom-call(f32[1]{0:T(128)S(6)} %copy.25.low_ref, f32[1]{0:T(128)S(6)} %copy.26.high_ref, f32[4,16,512]{2,1,0:T(8,128)S(1)} %copy-done.1, f32[4,16,512]{2,1,0:T(8,128)S(1)} %copy-done, f32[7,8,512]{2,1,0:T(8,128)S(1)} %pack.1.own_ref, ...), custom_call_target="tpu_custom_call" | custom-call | flops 20000000 | bytes 10000000 | tf_op jit(solution)/shard_map/fine_level/pallas_call | solution.py:440
  (26 shorter events, 0.3 us)
Async XLA Ops:
  0.6 1.0 %copy-start = (f32[4,16,512]{2,1,0:T(8,128)S(1)}, f32[4,16,512]{2,1,0:T(8,128)}, u32[]{:S(2)}) copy-start(f32[4,16,512]{2,1,0:T(8,128)} %source_ref.3) | copy-start | bytes 393220
  1.7 3.0 %copy-start.1 = (f32[4,16,512]{2,1,0:T(8,128)S(1)}, f32[4,16,512]{2,1,0:T(8,128)}, u32[]{:S(2)}) copy-start(f32[4,16,512]{2,1,0:T(8,128)} %log_ref.3) | copy-start | bytes 393220
  1.7 6.5 %collective-permute-start = (f32[8,8,512]{2,1,0:T(8,128)S(1)}, f32[8,8,512]{2,1,0:T(8,128)S(1)}, u32[]{:S(2)}, u32[]{:S(2)}) collective-permute-start(f32[8,8,512]{2,1,0:T(8,128)S(1)} %slice_select_fusion), channel_id=1, source_target_pairs={{0,2},{1,3},{2,0},{3,1},{4,6},{5,7},{6,4},{7,5},{8,10},{9,11},{10,... | collective-permute-start | bytes 393224 | tf_op jit(solution)/shard_map/ppermute | solution.py:41
  4.8 12.8 %collective-permute-start.1 = (f32[7,16,512]{2,1,0:T(8,128)S(1)}, f32[7,16,512]{2,1,0:T(8,128)S(1)}, u32[]{:S(2)}, u32[]{:S(2)}) collective-permute-start(f32[7,16,512]{2,1,0:T(8,128)S(1)} %get-tuple-element.3), channel_id=1, source_target_pairs={{0,4},{1,5},{4,0},{5,1},{8,12},{9,13},{12,8},{13,9},{2,6},{3,7},{6... | collective-permute-start | bytes 688136 | tf_op jit(solution)/shard_map/ppermute | solution.py:41
  6.4 11.2 %collective-permute-start.2 = (f32[7,16,512]{2,1,0:T(8,128)S(1)}, f32[7,16,512]{2,1,0:T(8,128)S(1)}, u32[]{:S(2)}, u32[]{:S(2)}) collective-permute-start(f32[7,16,512]{2,1,0:T(8,128)S(1)} %get-tuple-element.2), channel_id=1, source_target_pairs={{0,1},{1,0},{4,8},{5,9},{8,4},{9,5},{12,13},{13,12},{2,3},{3,2},{6... | collective-permute-start | bytes 688136 | tf_op jit(solution)/shard_map/ppermute | solution.py:41
  8.4 9.2 %collective-permute-start.3 = (f32[7,8,512]{2,1,0:T(8,128)S(1)}, f32[7,8,512]{2,1,0:T(8,128)S(1)}, u32[]{:S(2)}, u32[]{:S(2)}) collective-permute-start(f32[7,8,512]{2,1,0:T(8,128)S(1)} %pack.1.own_ref), channel_id=1, source_target_pairs={{0,4},{1,5},{4,0},{5,1},{8,12},{9,13},{12,8},{13,9},{2,6},{3,7},{6... | collective-permute-start | bytes 344072 | tf_op jit(solution)/shard_map/ppermute | solution.py:41
  10.3 7.4 %collective-permute-start.4 = (f32[7,8,512]{2,1,0:T(8,128)S(1)}, f32[7,8,512]{2,1,0:T(8,128)S(1)}, u32[]{:S(2)}, u32[]{:S(2)}) collective-permute-start(f32[7,8,512]{2,1,0:T(8,128)S(1)} %pack.1.own_ref), channel_id=1, source_target_pairs={{0,1},{1,0},{4,8},{5,9},{8,4},{9,5},{12,13},{13,12},{2,3},{3,2},{6... | collective-permute-start | bytes 344072 | tf_op jit(solution)/shard_map/ppermute | solution.py:41
  10.4 7.2 %collective-permute-start.5 = (f32[2,8,512]{2,1,0:T(8,128)S(1)}, f32[2,8,512]{2,1,0:T(8,128)S(1)}, u32[]{:S(2)}, u32[]{:S(2)}) collective-permute-start(f32[2,8,512]{2,1,0:T(8,128)S(1)} %maximum_select_fusion), channel_id=1, source_target_pairs={{0,8},{1,9},{4,12},{5,13},{8,0},{9,1},{12,4},{13,5},{2,10},{3,11},... | collective-permute-start | bytes 98312 | tf_op jit(solution)/shard_map/ppermute | solution.py:41
  17.8 1.7 %collective-permute-start.6 = (f32[600,128]{1,0:T(8,128)S(1)}, f32[600,128]{1,0:T(8,128)S(1)}, u32[]{:S(2)}, u32[]{:S(2)}) collective-permute-start(f32[600,128]{1,0:T(8,128)S(1)} %broadcast_select_fusion), channel_id=1, source_target_pairs={{0,1},{1,0},{2,3},{3,2},{4,5},{5,4},{6,7},{7,6},{8,9},{9,8},{10,11... | collective-permute-start | bytes 921608 | tf_op jit(solution)/shard_map/ppermute | solution.py:502

commit v5 on v4

v5 whole, which is shorter than its diff:
```python
import functools

import jax
import jax.numpy as jnp
from jax import lax
from jax.experimental import pallas as pl
from jax.experimental.pallas import tpu as pltpu
from jax.sharding import PartitionSpec as P

DEGREE = 3
REACH = DEGREE + 1
LANES = 128
SUBLANES = 8
storage_rate = 0.1
AXES = ("gx", "gy", "gz")
VMEM = pl.BlockSpec(memory_space=pltpu.VMEM)
SMEM = pl.BlockSpec(memory_space=pltpu.SMEM)


def iota(shape, dim):
    return lax.broadcasted_iota(jnp.int32, shape, dim)


def turned(value, shift, axis):
    size = value.shape[axis]
    return pltpu.roll(value, shift % size, axis)


def permute(value, axis, peers, pairs):
    cores = lax.axis_size("gz")
    if axis == "gz" or cores % 2:
        return lax.ppermute(value, axis, [pair for i, j in pairs for pair in ((i, j), (j, i))])
    partner = {}
    for i, j in pairs:
        partner[i], partner[j] = j, i
    moves = [
        (i * cores + core, partner[i] * cores + core if i in partner else i * cores + (core ^ 1))
        for i in range(peers)
        for core in range(cores)
    ]
    return lax.ppermute(value, (axis, "gz"), moves)


def neighbour_pairs(peers, start):
    return [(i, i + 1) for i in range(start, peers - 1, 2)]


def first_swap(axis, peers, right, left):
    even = lax.axis_index(axis) % 2 == 0
    return permute(jnp.where(even, right, left), axis, peers, neighbour_pairs(peers, 0))


def second_swap(axis, peers, right, left):
    even = lax.axis_index(axis) % 2 == 0
    return permute(jnp.where(even, left, right), axis, peers, neighbour_pairs(peers, 1))


def swap(axis, peers, right, left):
    got = (first_swap(axis, peers, right, left),)
    return got if peers == 2 else got + (second_swap(axis, peers, right, left),)


def far_pairs(peers):
    pairs = [(i, i + 2) for i in range(peers - 2)]
    groups = [[pair for pair in pairs if pair[0] % 4 < 2], [pair for pair in pairs if pair[0] % 4 >= 2]]
    return [group for group in groups if group]


def from_right(is_first, got):
    return got[0] if len(got) == 1 else jnp.where(is_first, got[0], got[1])


def from_left(is_first, got):
    return got[0] if len(got) == 1 else jnp.where(is_first, got[1], got[0])


def numerators(shape, dim, own, index, peers, face_scale):
    place = iota(shape, dim)
    right = jnp.where(index < peers - 1, 2.0 * face_scale, 0.0)
    left = jnp.where(index > 0, 2.0 * face_scale, 0.0)
    return jnp.where(
        place == own - 1, right, jnp.where(place == shape[dim] - 1, left, 2.0 * face_scale)
    )


def iterate(count, log_at, source_at, x_faces, y_top, z_top, low, high, storage, refs):
    tx_ref, ty_ref, tz_ref, w_ref, d_ref, r_ref, p_ref = refs
    theta, delta = (high + low) * 0.5, (high - low) * 0.5
    sigma = theta / delta
    rho = 1.0 / sigma
    over_theta = 1.0 / theta
    after = jnp.exp(-log_at(0))
    tx_before = None
    for k in range(count):
        here = after
        if k + 1 < count:
            after = jnp.exp(-log_at(k + 1))
            tx = x_faces[k] / (here + after)
            tx_ref[k] = tx
        if 1 <= k <= count - 2:
            ty = y_top / (here + turned(here, -1, 0))
            tz = z_top / (here + turned(here, -1, 1))
            diagonal = storage + (tx_before + tx) + (ty + turned(ty, 1, 0)) + (tz + turned(tz, 1, 1))
            w = 1.0 / diagonal
            source = source_at(k)
            d_ref[k] = source * (over_theta * w)
            if 2 <= k <= count - 3:
                ty_ref[k] = ty
                tz_ref[k] = tz
                w_ref[k] = w
                r_ref[k] = source
        tx_before = tx
    for step in range(DEGREE):
        first, last = 2 + step, count - 2 - step
        rho_next = 1.0 / (2.0 * sigma - rho)
        keep, gain = rho_next * rho, 2.0 * rho_next / delta
        rho = rho_next
        here = d_ref[first]
        fx_before = tx_ref[first - 1] * (d_ref[first - 1] - here)
        for k in range(first, last):
            after = d_ref[k + 1]
            fx = tx_ref[k] * (here - after)
            fy = ty_ref[k] * (here - turned(here, -1, 0))
            fz = tz_ref[k] * (here - turned(here, -1, 1))
            applied = storage * here + (fx - fx_before) + (fy - turned(fy, 1, 0)) + (fz - turned(fz, 1, 1))
            residual = r_ref[k] - applied
            fresh = keep * here + gain * (residual * w_ref[k])
            if REACH <= k < count - REACH:
                so_far = here if step == 0 else p_ref[k]
                p_ref[k] = so_far + fresh
            if step < DEGREE - 1:
                r_ref[k] = residual
                d_ref[k] = fresh
            here, fx_before = after, fx


def window_scratch(count, rows, lanes):
    return [pltpu.VMEM((count, rows, lanes), jnp.float32)] * 7


def exact_dot(value, zero_one):
    parts = []
    for _ in range(3):
        part = value.astype(jnp.bfloat16)
        parts.append(part)
        value = value - part.astype(jnp.float32)
    rows = value.shape[0]
    out = jnp.dot(jnp.concatenate(parts, axis=0), zero_one, preferred_element_type=jnp.float32)
    return (out[2 * rows :] + out[rows : 2 * rows]) + out[:rows]


def row_pairs(top, bottom, sum_ref):
    tiles = top.shape[1] // LANES
    for tile in range(tiles):
        columns = slice(tile * LANES, (tile + 1) * LANES)
        sum_ref[tile, :SUBLANES] = top[:, columns]
        sum_ref[tile, SUBLANES:] = bottom[:, columns]
    return jnp.concatenate(
        [
            sum_ref[tile, pl.ds(0, SUBLANES, stride=2), :] + sum_ref[tile, pl.ds(1, SUBLANES, stride=2), :]
            for tile in range(tiles)
        ],
        axis=1,
    )


def lane_pairs(pieces):
    lanes = pieces[0].shape[1]
    pick = (iota((lanes, lanes // 2), 0) // 2 == iota((lanes, lanes // 2), 1)).astype(jnp.bfloat16)
    pooled = exact_dot(jnp.concatenate(pieces, axis=0), pick)
    return [pooled[SUBLANES * i : SUBLANES * (i + 1)] for i in range(len(pieces))]


def join_halo(near, beyond, starts):
    row = iota(near.shape, 0)
    up, down = turned(beyond, 3, 0), turned(beyond, -3, 0)
    right = jnp.where((row == 3) | (row == 7), up, jnp.where(row == 6, turned(beyond, 5, 0), near))
    left = jnp.where((row == 0) | (row == 4), down, jnp.where(row == 5, up, near))
    return jnp.where(starts, right, left)


def beyond_halo(joined, starts):
    row = iota(joined.shape, 0)
    up, down = turned(joined, 3, 0), turned(joined, -3, 0)
    right = jnp.where(row == 1, turned(joined, -5, 0), down)
    left = jnp.where(row == 2, down, up)
    return jnp.where(starts, right, left)


def join_third(near, third):
    row = iota(near.shape, 0)
    return jnp.where(
        row == 3, turned(third, 3, 0), jnp.where(row == 4, turned(third, -3, 0), near)
    )


def third_halo(joined):
    return jnp.where(iota(joined.shape, 0) < REACH, turned(joined, -3, 0), turned(joined, 3, 0))


def pack_kernel(n_far, log_ref, source_ref, *refs):
    *halo_refs, own_ref, first_ref, second_ref, far_ref, sum_ref = refs
    layers, rows, lanes = log_ref.shape
    ix, iy = lax.axis_index("gx"), lax.axis_index("gy")
    even, starts, low = iy % 2 == 0, iy == 0, ix % 4 < 2
    half = lanes // 2
    upper = iota((SUBLANES, lanes), 0) < REACH
    wide = len(halo_refs) == 2

    def halo(a, layer):
        got = tuple(ref[a * layers + layer] for ref in halo_refs)
        return from_right(even, got), from_left(even, got)

    def rows_of(a, layer):
        right, left = halo(a, layer)
        return jnp.where(upper, right, left) if wide else right

    def join(log_tile, source_tile):
        if wide:
            return [log_tile, source_tile]
        return [jnp.where(upper == starts, log_tile, turned(source_tile, REACH, 0))]

    log_rows, source_rows = ([rows_of(a, layer) for layer in range(layers)] for a in range(2))
    own = []
    for layer in range(layers):
        own += join(log_rows[layer], source_rows[layer])
    pieces = []
    for x in range(2):
        for ref in (log_ref, source_ref):
            both = ref[2 * x] + ref[2 * x + 1]
            pieces.append(row_pairs(both[:SUBLANES], both[SUBLANES:], sum_ref))
    sums = []
    for a in range(2):
        for x in range(2):
            near, beyond = halo(a, 2 * x), halo(a, 2 * x + 1)
            sums.append((near[0] + beyond[0], near[1] + beyond[1]))
    if wide:
        pieces += [row_pairs(*both, sum_ref) for both in sums]
    else:
        pieces += [row_pairs(sums[x][0], sums[2 + x][0], sum_ref) for x in range(2)]
    log0, source0, log1, source1, *halos = lane_pairs(pieces)
    logs, sources = (log0 * 0.125, log1 * 0.125), (source0, source1)
    if wide:
        halos = [halos[0] * 0.125, halos[1] * 0.125, halos[2], halos[3]]
    else:
        scale = jnp.where(iota((SUBLANES, half), 0) < REACH, 0.125, 1.0)
        halos = [tile * scale for tile in halos]

    def pair(left, right):
        return jnp.concatenate([left, right], axis=1)

    own += [pair(logs[x], sources[x]) for x in range(2)]
    own += [pair(halos[i], halos[i + 1]) for i in range(0, len(halos), 2)]
    for i, tile in enumerate(own):
        own_ref[i] = tile

    def near_tiles(order):
        near, beyond = order[0] // 2, order[-1] // 2
        tiles = join(join_third(log_rows[order[0]], log_rows[order[2]]), source_rows[order[0]])
        tiles += join(log_rows[order[1]], source_rows[order[1]])
        if wide:
            tiles += [
                pair(halos[near], halos[beyond]),
                pair(halos[2 + near], halos[2 + beyond]),
                pair(sources[beyond], sources[beyond]),
            ]
        else:
            tiles += [pair(join_halo(halos[near], halos[beyond], starts), sources[beyond])]
        return tiles

    forward = list(range(layers))
    for i, (right, left) in enumerate(zip(near_tiles(forward[::-1]), near_tiles(forward))):
        first_ref[i] = jnp.where(ix % 2 == 0, right, left)
        second_ref[i] = jnp.where(ix % 2 == 0, left, right)
    for x, inner, outer in ((0, 1, 0), (1, 0, 1)):
        tiles = (pair(logs[inner], logs[outer]), pair(sources[inner], halos[inner]))
        if x == 0:
            right = tiles
    for i in range(2):
        far_ref[0, i] = jnp.where(low, right[i], tiles[i])
        if n_far == 2:
            far_ref[1, i] = jnp.where(low, tiles[i], right[i])


def pack(log_perm, source, got, n_far):
    layers, rows, lanes = log_perm.shape
    wide = len(got) == 2

    def tiles(*count):
        return jax.ShapeDtypeStruct((*count, SUBLANES, lanes), jnp.float32)

    near = 7 if wide else 3
    return pl.pallas_call(
        functools.partial(pack_kernel, n_far),
        out_shape=(tiles(len(got) * (layers + 1) + 2), tiles(near), tiles(near), tiles(n_far, 2)),
        in_specs=[VMEM] * (2 + len(got)),
        out_specs=(VMEM,) * 4,
        scratch_shapes=[pltpu.VMEM((lanes // LANES, 2 * SUBLANES, LANES), jnp.float32)],
        compiler_params=pltpu.CompilerParams(vmem_limit_bytes=8 << 20),
        cost_estimate=pl.CostEstimate(flops=5_000_000, bytes_accessed=700_000, transcendentals=0),
        name="pack",
    )(log_perm, source, *got)


def pool_kernel(first_ref, second_ref, out_ref, sum_ref):
    layers = REACH
    even = lax.axis_index("gx") % 2 == 0
    pieces = []
    for ref, on_right in ((first_ref, even), (second_ref, jnp.logical_not(even))):
        for x in range(2):
            both = ref[2 * x] + ref[2 * x + 1]
            pieces.append(row_pairs(both[:SUBLANES], both[SUBLANES:], sum_ref))
        both = ref[layers + 1] + jnp.where(on_right, ref[layers], ref[layers + 2])
        pieces.append(row_pairs(both[:SUBLANES], both[SUBLANES:], sum_ref))
    tiles = lane_pairs(pieces)
    for block in range(2):
        log0, log1, source = tiles[3 * block : 3 * block + 3]
        out_ref[block, 0] = jnp.concatenate([log0 * 0.125, log1 * 0.125], axis=1)
        out_ref[block, 1] = jnp.concatenate([source, source], axis=1)


def pool(first, second):
    _, rows, lanes = first.shape
    return pl.pallas_call(
        pool_kernel,
        out_shape=jax.ShapeDtypeStruct((2, 2, SUBLANES, lanes), jnp.float32),
        in_specs=[VMEM] * 2,
        out_specs=VMEM,
        scratch_shapes=[pltpu.VMEM((lanes // LANES, 2 * SUBLANES, LANES), jnp.float32)],
        compiler_params=pltpu.CompilerParams(vmem_limit_bytes=8 << 20),
        cost_estimate=pl.CostEstimate(flops=5_000_000, bytes_accessed=600_000, transcendentals=0),
        name="pool",
    )(first, second)


def lane_rows(ref, start, size):
    return ref[pl.ds(pl.multiple_of(start, SUBLANES), size), :]


def coarse_kernel(peers, places, n_far, low_ref, high_ref, own_ref, pool_ref, *refs):
    near_refs, far_refs = refs[:2], refs[2 : 2 + n_far]
    early_ref, late_ref, out_ref, wide_ref, *scratch = refs[2 + n_far :]
    ix, iy, iz = (lax.axis_index(axis) for axis in AXES)
    nx, ny, nz = peers
    both_sides = ny > 2
    lanes = own_ref.shape[2] // 2
    rows = SUBLANES
    even, low, starts = ix % 2 == 0, ix % 4 < 2, iy == 0
    strips = (2 if both_sides else 1) * REACH
    near_strips = 4 if both_sides else 2
    top = iota((rows, lanes + LANES), 0) < REACH

    def with_lanes(core, ref, start):
        return jnp.concatenate([core, lane_rows(ref, start, rows)], axis=1)

    def columns(half):
        return slice(half * lanes, (half + 1) * lanes)

    def own(slot, half):
        start = places["own_pooled"] + (2 * slot + half) * rows
        return with_lanes(own_ref[strips + slot, :, columns(half)], early_ref, start)

    def pooled(side, slot, half):
        block = jnp.where(even, 0, 1) if side > 0 else jnp.where(even, 1, 0)
        start = places["pooled"] + block * (4 * rows) + (2 * slot + half) * rows
        return with_lanes(pool_ref[block, slot, :, columns(half)], early_ref, start)

    def near(side, slot, half):
        pick = from_left if side < 0 else from_right
        core = pick(even, tuple(ref[near_strips + slot, :, columns(half)] for ref in near_refs))
        start = pick(even, tuple(places["near_pooled"])) + (2 * slot + half) * rows
        return with_lanes(core, late_ref, start)

    def far(side, slot, half):
        pick = from_left if side < 0 else from_right
        core = pick(low, tuple(ref[slot, :, columns(half)] for ref in far_refs))
        return with_lanes(core, late_ref, pick(low, tuple(places["far"])))

    def split(tile, a):
        other = turned(tile, REACH, 0)
        return jnp.where(top, tile, other) if a == 0 else jnp.where(top, other, tile)

    def window(a, k):
        block, layer = k // 2 - 2, k % 2
        nearest = layer == (1 if block < 0 else 0)
        if abs(block) == 2:
            if a == 1:
                core = far(block, 1, 0)
                return jnp.concatenate([core, jnp.zeros_like(core)], axis=0)
            halo = far(block, 1, 1)
            halo = halo if both_sides else split(halo, 0)
            return jnp.concatenate([far(block, 0, 0 if nearest else 1), halo], axis=0)
        if block == 0:
            core = own(layer, a)
            halo = own(2 + a, layer) if both_sides else split(own(2, layer), a)
            return jnp.concatenate([core, halo], axis=0)
        if a == 0:
            core = pooled(block, 0, layer)
        elif nearest:
            core = pooled(block, 1, 0)
        else:
            core = near(block, 2, 0) if both_sides else near(block, 0, 1)
        if both_sides:
            halo = near(block, a, 0 if nearest else 1)
        else:
            joined = near(block, 0, 0)
            halo = split(joined if nearest else beyond_halo(joined, starts), a)
        return jnp.concatenate([core, halo], axis=0)

    def open_face(inside):
        return jnp.where(inside, 4.0, 0.0)

    faces = [4.0] * 9
    faces[1], faces[3] = open_face(ix > 1), open_face(ix > 0)
    faces[5], faces[7] = open_face(ix < nx - 1), open_face(ix < nx - 2)
    shape = (2 * rows, lanes + LANES)
    iterate(
        2 + 2 * REACH,
        functools.partial(window, 0),
        functools.partial(window, 1),
        faces,
        numerators(shape, 0, rows, iy, ny, 2.0),
        numerators(shape, 1, lanes, iz, nz, 2.0),
        jnp.full((1, shape[1]), low_ref[0]),
        jnp.full((1, shape[1]), high_ref[0]),
        8.0 * storage_rate,
        scratch,
    )
    p_ref = scratch[-1]
    widen = (iota((lanes, 2 * lanes), 0) == iota((lanes, 2 * lanes), 1) // 2).astype(jnp.bfloat16)
    pressure = jnp.concatenate([p_ref[REACH + x, :rows, :lanes] for x in range(2)], axis=0)
    wide = exact_dot(pressure, widen)
    for x in range(2):
        for tile in range(2 * lanes // LANES):
            part = slice(tile * LANES, (tile + 1) * LANES)
            for half in range(2):
                wide_ref[tile, pl.ds(half, rows, stride=2), :] = wide[x * rows : (x + 1) * rows, part]
            for twin in range(2):
                out_ref[2 * x + twin, :, part] = wide_ref[tile]


def coarse_level(low_bound, high_bound, own, pooled, near, far, early, late, places, peers):
    lanes = own.shape[2] // 2
    window = (2 + 2 * REACH, 2 * SUBLANES, lanes + LANES)
    return pl.pallas_call(
        functools.partial(coarse_kernel, peers, places, len(far)),
        out_shape=jax.ShapeDtypeStruct((REACH, 2 * SUBLANES, 2 * lanes), jnp.float32),
        in_specs=[SMEM, SMEM] + [VMEM] * (6 + len(far)),
        out_specs=VMEM,
        scratch_shapes=[pltpu.VMEM((2 * lanes // LANES, 2 * SUBLANES, LANES), jnp.float32)]
        + window_scratch(*window),
        compiler_params=pltpu.CompilerParams(vmem_limit_bytes=24 << 20),
        cost_estimate=pl.CostEstimate(flops=20_000_000, bytes_accessed=4_000_000, transcendentals=0),
        name="coarse_level",
    )(low_bound, high_bound, own, pooled, *near, *far, early, late)


def fine_kernel(
    peers,
    places,
    low_ref,
    high_ref,
    log_ref,
    source_ref,
    own_ref,
    first_ref,
    second_ref,
    first_near_ref,
    second_near_ref,
    early_ref,
    late_ref,
    spread_ref,
    fine_ref,
    diff_ref,
    *refs,
):
    layers, rows, lanes = fine_ref.shape
    ix, iy, iz = (lax.axis_index(axis) for axis in AXES)
    nx, ny, nz = peers
    both_sides = ny > 2
    even = ix % 2 == 0
    count = 3 * layers

    def with_lanes(core, ref, start):
        return jnp.concatenate([core, lane_rows(ref, start, core.shape[0])], axis=1)

    def near(side, slot):
        pick = from_left if side < 0 else from_right
        core = pick(even, (first_near_ref[slot], second_near_ref[slot]))
        return with_lanes(core, late_ref, pick(even, tuple(places["near_strips"])) + slot * SUBLANES)

    def window(a, k):
        side, layer = k // layers - 1, k % layers
        if side == 0:
            core = (log_ref, source_ref)[a][layer]
            core = with_lanes(core, early_ref, places["own"] + (a * layers + layer) * rows)
            slot = 2 * layer + a if both_sides else layer
            halo = with_lanes(own_ref[slot], early_ref, places["own_strips"] + slot * SUBLANES)
            if a == 1 and not both_sides:
                halo = turned(halo, REACH, 0)
        else:
            pick = from_left if side < 0 else from_right
            slot = layer if a == 0 else layers + layer - (1 if side < 0 else 0)
            core = pick(even, (first_ref[slot], second_ref[slot]))
            core = with_lanes(core, early_ref, pick(even, tuple(places["raw"])) + slot * rows)
            distance = layers - layer if side < 0 else layer + 1
            if both_sides:
                halo = near(side, (2 if distance == 2 else 0) + a)
            else:
                halo = near(side, 1 if distance == 2 else 0)
                if a == 1:
                    halo = turned(halo, REACH, 0)
            if a == 0 and distance > 2:
                halo = third_halo(halo)
        return jnp.concatenate([core, halo], axis=0)

    faces = [2.0] * (count - 1)
    faces[layers - 1] = jnp.where(ix > 0, 2.0, 0.0)
    faces[2 * layers - 1] = jnp.where(ix < nx - 1, 2.0, 0.0)
    shape = (rows + 2 * REACH, lanes + LANES)
    iterate(
        count,
        functools.partial(window, 0),
        functools.partial(window, 1),
        faces,
        numerators(shape, 0, rows, iy, ny, 1.0),
        numerators(shape, 1, lanes, iz, nz, 1.0),
        jnp.full((1, shape[1]), low_ref[0]),
        jnp.full((1, shape[1]), high_ref[0]),
        storage_rate,
        refs,
    )
    p_ref = refs[-1]
    for x in range(layers):
        fine = p_ref[REACH + x, :rows, :lanes]
        fine_ref[x] = fine
        diff_ref[x] = fine - spread_ref[x]


def fine_level(low_bound, high_bound, log_perm, source, own, raw, near, early, late, spread, places, peers):
    layers, rows, lanes = log_perm.shape
    window = (layers + 2 * REACH, rows + 2 * REACH, lanes + LANES)
    out = jax.ShapeDtypeStruct(log_perm.shape, jnp.float32)
    return pl.pallas_call(
        functools.partial(fine_kernel, peers, places),
        out_shape=(out, out),
        in_specs=[SMEM, SMEM] + [VMEM] * 10,
        out_specs=(VMEM, VMEM),
        scratch_shapes=window_scratch(*window),
        compiler_params=pltpu.CompilerParams(vmem_limit_bytes=24 << 20),
        cost_estimate=pl.CostEstimate(flops=20_000_000, bytes_accessed=10_000_000, transcendentals=0),
        name="fine_level",
    )(low_bound, high_bound, log_perm, source, own, *raw, *near, early, late, spread)


class LaneTiles:
    def __init__(self):
        self.offset, self.parts = 0, []

    def add(self, array):
        start = self.offset
        self.parts.append(array.reshape(-1, array.shape[-1]))
        self.offset += self.parts[-1].shape[0]
        return start

    def add_halves(self, array):
        half = array.shape[-1] // 2
        return self.add(array.reshape(-1, SUBLANES, 2, half).swapaxes(1, 2))

    def swapped(self, peers):
        last = jnp.concatenate([part[:, -LANES:] for part in self.parts])
        first = jnp.concatenate([part[:, :LANES] for part in self.parts])
        got = swap("gz", peers, last, first)
        if len(got) == 1:
            return got[0]
        even = lax.axis_index("gz") % 2 == 0
        return jnp.where(iota(last.shape, 1) < LANES // 2, from_right(even, got), from_left(even, got))


def shards(peers, log_perm, source, low_bound, high_bound):
    nx, ny, nz = peers
    layers, rows, lanes = log_perm.shape
    assert layers == REACH and rows == 2 * SUBLANES and nx > 2
    to_right, to_left = jnp.concatenate([log_perm, source[1:]]), jnp.concatenate([log_perm, source[:-1]])
    second = second_swap("gx", nx, to_right, to_left)
    stacked = jnp.concatenate([log_perm, source])
    got_rows = swap("gy", ny, stacked[:, rows - SUBLANES :], stacked[:, :SUBLANES])
    raw = (first_swap("gx", nx, to_right, to_left), second)
    far_groups = far_pairs(nx)
    own, for_first, for_second, for_far = pack(log_perm, source, got_rows, len(far_groups))
    second = permute(for_second, "gx", nx, neighbour_pairs(nx, 1))
    near = (permute(for_first, "gx", nx, neighbour_pairs(nx, 0)), second)
    far = tuple(permute(for_far[i], "gx", nx, group) for i, group in enumerate(far_groups))
    pooled = pool(*raw)
    strips = len(got_rows) * layers
    near_strips = 2 * len(got_rows)
    places, early, late = {}, LaneTiles(), LaneTiles()
    places["own"] = early.add(stacked)
    places["own_strips"] = early.add(own[:strips])
    places["own_pooled"] = early.add_halves(own[strips:])
    places["raw"] = [early.add(block) for block in raw]
    places["pooled"] = early.add_halves(pooled)
    places["near_strips"] = [late.add(block[:near_strips]) for block in near]
    places["near_pooled"] = [late.add_halves(block[near_strips:]) for block in near]
    places["far"] = [late.add(block[0, :, : lanes // 2]) for block in far]
    early, late = early.swapped(nz), late.swapped(nz)
    spread = coarse_level(low_bound, high_bound, own, pooled, near, far, early, late, places, peers)
    return fine_level(
        low_bound, high_bound, log_perm, source, own, raw, near, early, late, spread, places, peers
    )


def solution(mesh):
    peers = tuple(mesh.shape[axis] for axis in AXES)
    split = P(("groups", "gx"), "gy", "gz")
    return jax.shard_map(
        functools.partial(shards, peers),
        mesh=mesh,
        in_specs=(split, split, P(), P()),
        out_specs=(split, split),
        check_vma=False,
    )
```

time: 23.4 us -> 22.4 us (0.957)
  waiting for transfers between devices: 6.6 us -> 4.98 us
  starting transfers between devices: 9.27 us -> 9.69 us
    ppermute x6, waiting for transfers between devices: 6.31 us -> 4.97 us  [permute(): return lax.ppermute(value, (axis, 'gz'), moves)]
    ppermute x1 -> x2, starting transfers between devices: 0.07 us -> 0.56 us  [permute(): lax.ppermute(value, axis, [pair for i, j in pairs for pair in ((i, j), (j...]
    ppermute x1 -> x2, waiting for transfers between devices: 0.29 us -> 0.01 us  [permute(): lax.ppermute(value, axis, [pair for i, j in pairs for pair in ((i, j), (j...]
    pallas_call x3 -> x4, Pallas kernels: 3.96 us -> 4.19 us  [the longest x1 2.96 us: fine_level(): pl.pallas_call(functools.partial(fine_kernel, peers, places), out_shape=(...]
  transfers between devices with their start and end apart: 7 -> 8, of which waited for: 3 -> 2; matrix products, arithmetic and copies ran while one was open for 1% -> 1% of each run, Pallas kernels for 1% -> 1%
where the time goes in v5:
time: 22.4 us; the launch traced here: 22.3 us
  starting transfers between devices  9.69 us (43%)
  waiting for transfers between devices  4.98 us (22%)
  Pallas kernels  4.19 us (19%)
  between operations  2.22 us (10%)
  local copies, waits for them, and re-layouts  1.08 us (5%)
    ppermute x6, starting transfers between devices, permute(): return lax.ppermute(value, (axis, 'gz'), moves)  9.13 us
    ppermute x6, waiting for transfers between devices, permute(): return lax.ppermute(value, (axis, 'gz'), moves)  4.97 us
    pallas_call x1, Pallas kernels, fine_level(): pl.pallas_call(functools.partial(fine_kernel, peers, places), out_shape=(...  2.96 us
    unnamed x14, local copies, waits for them, and re-layouts  1.02 us
    pallas_call x1, Pallas kernels, coarse_level(): pl.pallas_call(functools.partial(coarse_kernel, peers, places, len(far)),...  0.78 us
    ppermute x2, starting transfers between devices, permute(): lax.ppermute(value, axis, [pair for i, j in pairs for pair in ((i, j), (j...  0.56 us
  transfers between devices with their start and end apart: 8, of which 2 were waited for; matrix products, arithmetic and copies ran while one was open for 1% of the time, Pallas kernels for 1%

profile of v5, /device:TPU:0, one launch (start us, length us, event | category | flops | bytes accessed | tf_op | source)
XLA Modules:
  0.0 22.3 jit_solution(1546673122149981512)
XLA Ops:
  0.6 0.0 copy-start
  0.6 1.0 %constant_dynamic-update-slice_fusion.1 = f32[8,16,512]{2,1,0:T(8,128)S(1)} fusion(f32[4,16,512]{2,1,0:T(8,128)} %log_ref.3), kind=kLoop, calls=%fused_computation.14 | loop fusion | bytes 262144
  1.6 0.0 copy-done
  1.7 0.0 copy-start.1
  1.7 3.0 %collective-permute-start = (f32[8,8,512]{2,1,0:T(8,128)S(1)}, f32[8,8,512]{2,1,0:T(8,128)S(1)}, u32[]{:S(2)}, u32[]{:S(2)}) collective-permute-start(f32[8,8,512]{2,1,0:T(8,128)S(1)} %slice_select_fusion), channel_id=1, source_target_pairs={{0,2},{1,3},{2,0},{3,1},{4,6},{5,7},{6,4},{7,5},{8,10},{9,11},{10,... | collective-permute-start | bytes 393224 | tf_op jit(solution)/shard_map/ppermute | solution.py:41
  4.7 0.0 copy-done.1
  4.8 1.6 %collective-permute-start.1 = (f32[7,16,512]{2,1,0:T(8,128)S(1)}, f32[7,16,512]{2,1,0:T(8,128)S(1)}, u32[]{:S(2)}, u32[]{:S(2)}) collective-permute-start(f32[7,16,512]{2,1,0:T(8,128)S(1)} %get-tuple-element.11), channel_id=1, source_target_pairs={{0,4},{1,5},{4,0},{5,1},{8,12},{9,13},{12,8},{13,9},{2,6},{3,7},{6... | collective-permute-start | bytes 688136 | tf_op jit(solution)/shard_map/ppermute | solution.py:41
  6.4 0.0 collective-permute-start.2
  6.4 1.8 %collective-permute-done.refs_0_ = f32[8,8,512]{2,1,0:T(8,128)S(1)} collective-permute-done((f32[8,8,512]{2,1,0:T(8,128)S(1)}, f32[8,8,512]{2,1,0:T(8,128)S(1)}, u32[]{:S(2)}, u32[]{:S(2)}) %collective-permute-start) | collective-permute-done | bytes 131104 | tf_op jit(solution)/shard_map/ppermute | solution.py:41
  8.2 0.2 %pack.1 = (f32[7,8,512]{2,1,0:T(8,128)S(1)}, f32[3,8,512]{2,1,0:T(8,128)S(1)}, f32[3,8,512]{2,1,0:T(8,128)S(1)}, f32[1,2,8,512]{3,2,1,0:T(8,128)S(1)}) custom-call(f32[4,16,512]{2,1,0:T(8,128)S(1)} %copy-done.1, f32[4,16,512]{2,1,0:T(8,128)S(1)} %copy-done, f32[8,8,512]{2,1,0:T(8,128)S(1)} %collective-permute-done.refs_0_), custom_call_target="tpu_custom_call" | custom-call | flops 5000000 | bytes 700000 | tf_op jit(solution)/shard_map/pack/pallas_call | solution.py:293
  8.4 1.9 %collective-permute-start.3 = (f32[3,8,512]{2,1,0:T(8,128)S(1)}, f32[3,8,512]{2,1,0:T(8,128)S(1)}, u32[]{:S(2)}, u32[]{:S(2)}) collective-permute-start(f32[3,8,512]{2,1,0:T(8,128)S(1)} %get-tuple-element.7), channel_id=1, source_target_pairs={{0,4},{1,5},{4,0},{5,1},{8,12},{9,13},{12,8},{13,9},{2,6},{3,7},{6... | collective-permute-start | bytes 147464 | tf_op jit(solution)/shard_map/ppermute | solution.py:41
  10.3 0.0 collective-permute-start.4
  10.3 2.6 %collective-permute-start.6 = (f32[2,8,512]{2,1,0:T(8,128)S(1)}, f32[2,8,512]{2,1,0:T(8,128)S(1)}, u32[]{:S(2)}, u32[]{:S(2)}) collective-permute-start(f32[2,8,512]{2,1,0:T(8,128)S(1)} %bitcast.35), channel_id=1, source_target_pairs={{0,8},{1,9},{4,12},{5,13},{8,0},{9,1},{12,4},{13,5},{2,10},{3,11},... | collective-permute-start | bytes 98312 | tf_op jit(solution)/shard_map/ppermute | solution.py:41
  12.9 3.2 %collective-permute-done.6.refs_2_ = f32[2,8,512]{2,1,0:T(8,128)S(1)} collective-permute-done((f32[2,8,512]{2,1,0:T(8,128)S(1)}, f32[2,8,512]{2,1,0:T(8,128)S(1)}, u32[]{:S(2)}, u32[]{:S(2)}) %collective-permute-start.6) | collective-permute-done | bytes 32800 | tf_op jit(solution)/shard_map/ppermute | solution.py:41
  16.2 0.0 collective-permute-done.3.refs_0_.first_near_ref
  16.2 0.0 collective-permute-done.4.refs_1_.second_near_ref
  16.3 0.0 collective-permute-done.1.first_ref
  16.3 0.0 collective-permute-done.2.second_ref
  16.3 0.2 pool.1.pool_ref
  16.6 0.1 collective-permute-start.5
  16.7 0.5 %collective-permute-start.7 = (f32[72,128]{1,0:T(8,128)S(1)}, f32[72,128]{1,0:T(8,128)S(1)}, u32[]{:S(2)}, u32[]{:S(2)}) collective-permute-start(f32[72,128]{1,0:T(8,128)S(1)} %broadcast_select_fusion.1), channel_id=1, source_target_pairs={{0,1},{1,0},{2,3},{3,2},{4,5},{5,4},{6,7},{7,6},{8,9},{9,8},{10,11... | collective-permute-start | bytes 110600 | tf_op jit(solution)/shard_map/ppermute | solution.py:32
  18.5 0.0 collective-permute-done.7.refs_4_.late_ref
  18.5 0.0 collective-permute-done.5.refs_3_.early_ref
  18.5 0.8 %coarse_level.1.spread_ref = f32[4,16,512]{2,1,0:T(8,128)S(1)} custom-call(f32[1]{0:T(128)S(6)} %copy.25.low_ref, f32[1]{0:T(128)S(6)} %copy.26.high_ref, f32[7,8,512]{2,1,0:T(8,128)S(1)} %get-tuple-element.6.own_ref, f32[2,2,8,512]{3,2,1,0:T(8,128)S(1)} %pool.1.pool_ref, f32[3,8,512]{2,1,0:T(8,128)S(1)} %collective-permute-done.3.refs_0_.first_near_ref, ...), custom_call_target="tpu_custom_call" | custom-call | flops 20000000 | bytes 4000000 | tf_op jit(solution)/shard_map/coarse_level/pallas_call | solution.py:445
  19.3 3.0 %fine_level.1 = (f32[4,16,512]{2,1,0:T(8,128)}, f32[4,16,512]{2,1,0:T(8,128)}) custom-call(f32[1]{0:T(128)S(6)} %copy.25.low_ref, f32[1]{0:T(128)S(6)} %copy.26.high_ref, f32[4,16,512]{2,1,0:T(8,128)S(1)} %copy-done.1, f32[4,16,512]{2,1,0:T(8,128)S(1)} %copy-done, f32[7,8,512]{2,1,0:T(8,128)S(1)} %get-tuple-element.6.own_ref, ...), custom_call_target="tpu_custom_call" | custom-call | flops 20000000 | bytes 10000000 | tf_op jit(solution)/shard_map/fine_level/pallas_call | solution.py:544
  (24 shorter events, 0.2 us)
Async XLA Ops:
  0.6 1.0 %copy-start = (f32[4,16,512]{2,1,0:T(8,128)S(1)}, f32[4,16,512]{2,1,0:T(8,128)}, u32[]{:S(2)}) copy-start(f32[4,16,512]{2,1,0:T(8,128)} %source_ref.3) | copy-start | bytes 393220
  1.7 3.0 %copy-start.1 = (f32[4,16,512]{2,1,0:T(8,128)S(1)}, f32[4,16,512]{2,1,0:T(8,128)}, u32[]{:S(2)}) copy-start(f32[4,16,512]{2,1,0:T(8,128)} %log_ref.3) | copy-start | bytes 393220
  1.7 6.5 %collective-permute-start = (f32[8,8,512]{2,1,0:T(8,128)S(1)}, f32[8,8,512]{2,1,0:T(8,128)S(1)}, u32[]{:S(2)}, u32[]{:S(2)}) collective-permute-start(f32[8,8,512]{2,1,0:T(8,128)S(1)} %slice_select_fusion), channel_id=1, source_target_pairs={{0,2},{1,3},{2,0},{3,1},{4,6},{5,7},{6,4},{7,5},{8,10},{9,11},{10,... | collective-permute-start | bytes 393224 | tf_op jit(solution)/shard_map/ppermute | solution.py:41
  4.8 11.5 %collective-permute-start.1 = (f32[7,16,512]{2,1,0:T(8,128)S(1)}, f32[7,16,512]{2,1,0:T(8,128)S(1)}, u32[]{:S(2)}, u32[]{:S(2)}) collective-permute-start(f32[7,16,512]{2,1,0:T(8,128)S(1)} %get-tuple-element.11), channel_id=1, source_target_pairs={{0,4},{1,5},{4,0},{5,1},{8,12},{9,13},{12,8},{13,9},{2,6},{3,7},{6... | collective-permute-start | bytes 688136 | tf_op jit(solution)/shard_map/ppermute | solution.py:41
  6.4 9.9 %collective-permute-start.2 = (f32[7,16,512]{2,1,0:T(8,128)S(1)}, f32[7,16,512]{2,1,0:T(8,128)S(1)}, u32[]{:S(2)}, u32[]{:S(2)}) collective-permute-start(f32[7,16,512]{2,1,0:T(8,128)S(1)} %get-tuple-element.10), channel_id=1, source_target_pairs={{0,1},{1,0},{4,8},{5,9},{8,4},{9,5},{12,13},{13,12},{2,3},{3,2},{6... | collective-permute-start | bytes 688136 | tf_op jit(solution)/shard_map/ppermute | solution.py:41
  8.4 7.7 %collective-permute-start.3 = (f32[3,8,512]{2,1,0:T(8,128)S(1)}, f32[3,8,512]{2,1,0:T(8,128)S(1)}, u32[]{:S(2)}, u32[]{:S(2)}) collective-permute-start(f32[3,8,512]{2,1,0:T(8,128)S(1)} %get-tuple-element.7), channel_id=1, source_target_pairs={{0,4},{1,5},{4,0},{5,1},{8,12},{9,13},{12,8},{13,9},{2,6},{3,7},{6... | collective-permute-start | bytes 147464 | tf_op jit(solution)/shard_map/ppermute | solution.py:41
  10.3 5.8 %collective-permute-start.4 = (f32[3,8,512]{2,1,0:T(8,128)S(1)}, f32[3,8,512]{2,1,0:T(8,128)S(1)}, u32[]{:S(2)}, u32[]{:S(2)}) collective-permute-start(f32[3,8,512]{2,1,0:T(8,128)S(1)} %get-tuple-element.8), channel_id=1, source_target_pairs={{0,1},{1,0},{4,8},{5,9},{8,4},{9,5},{12,13},{13,12},{2,3},{3,2},{6... | collective-permute-start | bytes 147464 | tf_op jit(solution)/shard_map/ppermute | solution.py:41
  10.3 5.8 %collective-permute-start.6 = (f32[2,8,512]{2,1,0:T(8,128)S(1)}, f32[2,8,512]{2,1,0:T(8,128)S(1)}, u32[]{:S(2)}, u32[]{:S(2)}) collective-permute-start(f32[2,8,512]{2,1,0:T(8,128)S(1)} %bitcast.35), channel_id=1, source_target_pairs={{0,8},{1,9},{4,12},{5,13},{8,0},{9,1},{12,4},{13,5},{2,10},{3,11},... | collective-permute-start | bytes 98312 | tf_op jit(solution)/shard_map/ppermute | solution.py:41
  16.6 1.9 %collective-permute-start.5 = (f32[496,128]{1,0:T(8,128)S(1)}, f32[496,128]{1,0:T(8,128)S(1)}, u32[]{:S(2)}, u32[]{:S(2)}) collective-permute-start(f32[496,128]{1,0:T(8,128)S(1)} %broadcast_select_fusion), channel_id=1, source_target_pairs={{0,1},{1,0},{2,3},{3,2},{4,5},{5,4},{6,7},{7,6},{8,9},{9,8},{10,11... | collective-permute-start | bytes 761864 | tf_op jit(solution)/shard_map/ppermute | solution.py:32
  16.7 1.8 %collective-permute-start.7 = (f32[72,128]{1,0:T(8,128)S(1)}, f32[72,128]{1,0:T(8,128)S(1)}, u32[]{:S(2)}, u32[]{:S(2)}) collective-permute-start(f32[72,128]{1,0:T(8,128)S(1)} %broadcast_select_fusion.1), channel_id=1, source_target_pairs={{0,1},{1,0},{2,3},{3,2},{4,5},{5,4},{6,7},{7,6},{8,9},{9,8},{10,11... | collective-permute-start | bytes 110600 | tf_op jit(solution)/shard_map/ppermute | solution.py:32

commit v6 on v5

--- a/solution.py
+++ b/solution.py
@@ -198,92 +198,155 @@
     return jnp.where(iota(joined.shape, 0) < REACH, turned(joined, -3, 0), turned(joined, 3, 0))
 
 
-def pack_kernel(n_far, log_ref, source_ref, *refs):
-    *halo_refs, own_ref, first_ref, second_ref, far_ref, sum_ref = refs
+def prep_kernel(log_ref, source_ref, pooled_ref, left_ref, right_ref, sum_ref):
     layers, rows, lanes = log_ref.shape
-    ix, iy = lax.axis_index("gx"), lax.axis_index("gy")
-    even, starts, low = iy % 2 == 0, iy == 0, ix % 4 < 2
     half = lanes // 2
     upper = iota((SUBLANES, lanes), 0) < REACH
-    wide = len(halo_refs) == 2
-
-    def halo(a, layer):
-        got = tuple(ref[a * layers + layer] for ref in halo_refs)
-        return from_right(even, got), from_left(even, got)
-
-    def rows_of(a, layer):
-        right, left = halo(a, layer)
-        return jnp.where(upper, right, left) if wide else right
-
-    def join(log_tile, source_tile):
-        if wide:
-            return [log_tile, source_tile]
-        return [jnp.where(upper == starts, log_tile, turned(source_tile, REACH, 0))]
-
-    log_rows, source_rows = ([rows_of(a, layer) for layer in range(layers)] for a in range(2))
-    own = []
-    for layer in range(layers):
-        own += join(log_rows[layer], source_rows[layer])
     pieces = []
     for x in range(2):
         for ref in (log_ref, source_ref):
             both = ref[2 * x] + ref[2 * x + 1]
             pieces.append(row_pairs(both[:SUBLANES], both[SUBLANES:], sum_ref))
-    sums = []
-    for a in range(2):
-        for x in range(2):
-            near, beyond = halo(a, 2 * x), halo(a, 2 * x + 1)
-            sums.append((near[0] + beyond[0], near[1] + beyond[1]))
+    log0, source0, log1, source1 = lane_pairs(pieces)
+    log0, log1 = log0 * 0.125, log1 * 0.125
+    pooled_ref[0] = jnp.concatenate([log0, source0], axis=1)
+    pooled_ref[1] = jnp.concatenate([log1, source1], axis=1)
+    for layer in range(layers):
+        left_ref[layer] = jnp.where(
+            upper, log_ref[layer, :SUBLANES], turned(source_ref[layer, :SUBLANES], REACH, 0)
+        )
+        right_ref[layer] = jnp.where(
+            upper, turned(source_ref[layer, SUBLANES:], REACH, 0), log_ref[layer, SUBLANES:]
+        )
+    pair = iota((SUBLANES, half), 0) // 2
+
+    def four(*tiles):
+        merged = jnp.where(
+            pair == 0, tiles[0], jnp.where(pair == 1, tiles[1], jnp.where(pair == 2, tiles[2], tiles[3]))
+        )
+        return jnp.concatenate([merged, merged], axis=1)
+
+    left_ref[layers] = four(turned(log1, -2, 0), log0, turned(source1, 2, 0), turned(source0, 4, 0))
+    right_ref[layers] = four(turned(log0, -4, 0), turned(log1, -2, 0), source0, turned(source1, 2, 0))
+
+
+def prep(log_perm, source):
+    layers, rows, lanes = log_perm.shape
+
+    def tiles(count):
+        return jax.ShapeDtypeStruct((count, SUBLANES, lanes), jnp.float32)
+
+    return pl.pallas_call(
+        prep_kernel,
+        out_shape=(tiles(2), tiles(layers + 1), tiles(layers + 1)),
+        in_specs=[VMEM] * 2,
+        out_specs=(VMEM,) * 3,
+        scratch_shapes=[pltpu.VMEM((lanes // LANES, 2 * SUBLANES, LANES), jnp.float32)],
+        compiler_params=pltpu.CompilerParams(vmem_limit_bytes=8 << 20),
+        cost_estimate=pl.CostEstimate(flops=5_000_000, bytes_accessed=700_000, transcendentals=0),
+        name="prep",
+    )(log_perm, source)
+
+
+def pack_kernel(wide, n_far, pooled_ref, *refs):
+    *got_refs, halo_ref, first_ref, second_ref, far_ref, sum_ref = refs
+    layers, lanes = got_refs[0].shape[0] - 1, got_refs[0].shape[2]
+    ix, iy = lax.axis_index("gx"), lax.axis_index("gy")
+    even, starts, low = iy % 2 == 0, iy == 0, ix % 4 < 2
+    half = lanes // 2
+    upper = iota((SUBLANES, lanes), 0) < REACH
+    row = iota((SUBLANES, half), 0)
+
+    def got(slot):
+        tiles = tuple(ref[slot] for ref in got_refs)
+        return from_right(even, tiles), from_left(even, tiles)
+
+    strips = [got(layer) for layer in range(layers)]
+    extra = [tile[:, :half] for tile in got(layers)]
+    pieces = []
+    for side in range(2 if wide else 1):
+        both = [strips[2 * x][side] + strips[2 * x + 1][side] for x in range(2)]
+        pieces.append(row_pairs(*both, sum_ref))
+    fine_rows = lane_pairs(pieces)
+
+    def right_halos(rows, extra):
+        rows = jnp.where(row % 4 < 2, rows * 0.125, rows)
+        return [
+            jnp.where(row < 2, near, jnp.where((row == 4) | (row == 5), far, more))
+            for near, far, more in (
+                (rows, turned(rows, 2, 0), extra),
+                (turned(rows, 4, 0), turned(rows, -2, 0), turned(extra, 2, 0)),
+            )
+        ]
+
+    def left_halos(rows, extra):
+        rows = jnp.where(row % 4 >= 2, rows * 0.125, rows)
+        return [
+            jnp.where((row == 2) | (row == 3), near, jnp.where(row >= 6, far, more))
+            for near, far, more in (
+                (rows, turned(rows, -2, 0), extra),
+                (turned(rows, 4, 0), turned(rows, 2, 0), turned(extra, -2, 0)),
+            )
+        ]
+
+    right, left = right_halos(fine_rows[0], extra[0]), left_halos(fine_rows[-1], extra[1])
     if wide:
-        pieces += [row_pairs(*both, sum_ref) for both in sums]
+        top = row < REACH
+        halos = [jnp.where(top, right[x], turned(left[x], REACH, 0)) for x in range(2)]
+        halos += [jnp.where(top, turned(right[x], REACH, 0), left[x]) for x in range(2)]
     else:
-        pieces += [row_pairs(sums[x][0], sums[2 + x][0], sum_ref) for x in range(2)]
-    log0, source0, log1, source1, *halos = lane_pairs(pieces)
-    logs, sources = (log0 * 0.125, log1 * 0.125), (source0, source1)
-    if wide:
-        halos = [halos[0] * 0.125, halos[1] * 0.125, halos[2], halos[3]]
-    else:
-        scale = jnp.where(iota((SUBLANES, half), 0) < REACH, 0.125, 1.0)
-        halos = [tile * scale for tile in halos]
+        halos = [jnp.where(starts, right[x], left[x]) for x in range(2)]
 
     def pair(left, right):
         return jnp.concatenate([left, right], axis=1)
 
-    own += [pair(logs[x], sources[x]) for x in range(2)]
-    own += [pair(halos[i], halos[i + 1]) for i in range(0, len(halos), 2)]
-    for i, tile in enumerate(own):
-        own_ref[i] = tile
+    for i in range(len(halos) // 2):
+        halo_ref[i] = pair(halos[2 * i], halos[2 * i + 1])
+    logs = [pooled_ref[x, :, :half] for x in range(2)]
+    sources = [pooled_ref[x, :, half:] for x in range(2)]
 
     def near_tiles(order):
         near, beyond = order[0] // 2, order[-1] // 2
-        tiles = join(join_third(log_rows[order[0]], log_rows[order[2]]), source_rows[order[0]])
-        tiles += join(log_rows[order[1]], source_rows[order[1]])
         if wide:
-            tiles += [
+            log_rows = [jnp.where(upper, *strips[layer]) for layer in range(layers)]
+            source_rows = [turned(jnp.where(upper, *strips[layer][::-1]), REACH, 0) for layer in range(layers)]
+            return [
+                join_third(log_rows[order[0]], log_rows[order[2]]),
+                source_rows[order[0]],
+                log_rows[order[1]],
+                source_rows[order[1]],
                 pair(halos[near], halos[beyond]),
                 pair(halos[2 + near], halos[2 + beyond]),
                 pair(sources[beyond], sources[beyond]),
             ]
-        else:
-            tiles += [pair(join_halo(halos[near], halos[beyond], starts), sources[beyond])]
-        return tiles
+        nearest, third = strips[order[0]][0], strips[order[2]][0]
+        place = iota((SUBLANES, lanes), 0)
+        joined = jnp.where(
+            starts,
+            jnp.where(place == 3, turned(third, 3, 0), nearest),
+            jnp.where(place == 4, turned(third, -3, 0), nearest),
+        )
+        return [
+            joined,
+            strips[order[1]][0],
+            pair(join_halo(halos[near], halos[beyond], starts), sources[beyond]),
+        ]
 
     forward = list(range(layers))
     for i, (right, left) in enumerate(zip(near_tiles(forward[::-1]), near_tiles(forward))):
         first_ref[i] = jnp.where(ix % 2 == 0, right, left)
         second_ref[i] = jnp.where(ix % 2 == 0, left, right)
-    for x, inner, outer in ((0, 1, 0), (1, 0, 1)):
-        tiles = (pair(logs[inner], logs[outer]), pair(sources[inner], halos[inner]))
-        if x == 0:
-            right = tiles
+    far = [
+        (pair(logs[inner], logs[1 - inner]), pair(sources[inner], halos[inner])) for inner in (1, 0)
+    ]
     for i in range(2):
-        far_ref[0, i] = jnp.where(low, right[i], tiles[i])
+        far_ref[0, i] = jnp.where(low, far[0][i], far[1][i])
         if n_far == 2:
-            far_ref[1, i] = jnp.where(low, tiles[i], right[i])
-
-
-def pack(log_perm, source, got, n_far):
-    layers, rows, lanes = log_perm.shape
+            far_ref[1, i] = jnp.where(low, far[1][i], far[0][i])
+
+
+def pack(pooled, got, n_far):
+    slots, rows, lanes = got[0].shape
     wide = len(got) == 2
 
     def tiles(*count):
@@ -291,15 +354,15 @@
 
     near = 7 if wide else 3
     return pl.pallas_call(
-        functools.partial(pack_kernel, n_far),
-        out_shape=(tiles(len(got) * (layers + 1) + 2), tiles(near), tiles(near), tiles(n_far, 2)),
-        in_specs=[VMEM] * (2 + len(got)),
+        functools.partial(pack_kernel, wide, n_far),
+        out_shape=(tiles(len(got)), tiles(near), tiles(near), tiles(n_far, 2)),
+        in_specs=[VMEM] * (1 + len(got)),
         out_specs=(VMEM,) * 4,
         scratch_shapes=[pltpu.VMEM((lanes // LANES, 2 * SUBLANES, LANES), jnp.float32)],
         compiler_params=pltpu.CompilerParams(vmem_limit_bytes=8 << 20),
         cost_estimate=pl.CostEstimate(flops=5_000_000, bytes_accessed=700_000, transcendentals=0),
         name="pack",
-    )(log_perm, source, *got)
+    )(pooled, *got)
 
 
 def pool_kernel(first_ref, second_ref, out_ref, sum_ref):
@@ -337,7 +400,7 @@
     return ref[pl.ds(pl.multiple_of(start, SUBLANES), size), :]
 
 
-def coarse_kernel(peers, places, n_far, low_ref, high_ref, own_ref, pool_ref, *refs):
+def coarse_kernel(peers, places, n_far, low_ref, high_ref, own_ref, halo_ref, pool_ref, *refs):
     near_refs, far_refs = refs[:2], refs[2 : 2 + n_far]
     early_ref, late_ref, out_ref, wide_ref, *scratch = refs[2 + n_far :]
     ix, iy, iz = (lax.axis_index(axis) for axis in AXES)
@@ -346,7 +409,6 @@
     lanes = own_ref.shape[2] // 2
     rows = SUBLANES
     even, low, starts = ix % 2 == 0, ix % 4 < 2, iy == 0
-    strips = (2 if both_sides else 1) * REACH
     near_strips = 4 if both_sides else 2
     top = iota((rows, lanes + LANES), 0) < REACH
 
@@ -357,8 +419,10 @@
         return slice(half * lanes, (half + 1) * lanes)
 
     def own(slot, half):
-        start = places["own_pooled"] + (2 * slot + half) * rows
-        return with_lanes(own_ref[strips + slot, :, columns(half)], early_ref, start)
+        ref, start = (own_ref, places["own_pooled"]) if slot < 2 else (halo_ref, places["own_halos"])
+        slot = slot % 2
+        start = start + (2 * slot + half) * rows
+        return with_lanes(ref[slot, :, columns(half)], early_ref, start)
 
     def pooled(side, slot, half):
         block = jnp.where(even, 0, 1) if side > 0 else jnp.where(even, 1, 0)
@@ -439,20 +503,20 @@
                 out_ref[2 * x + twin, :, part] = wide_ref[tile]
 
 
-def coarse_level(low_bound, high_bound, own, pooled, near, far, early, late, places, peers):
+def coarse_level(low_bound, high_bound, own, halos, pooled, near, far, early, late, places, peers):
     lanes = own.shape[2] // 2
     window = (2 + 2 * REACH, 2 * SUBLANES, lanes + LANES)
     return pl.pallas_call(
         functools.partial(coarse_kernel, peers, places, len(far)),
         out_shape=jax.ShapeDtypeStruct((REACH, 2 * SUBLANES, 2 * lanes), jnp.float32),
-        in_specs=[SMEM, SMEM] + [VMEM] * (6 + len(far)),
+        in_specs=[SMEM, SMEM] + [VMEM] * (7 + len(far)),
         out_specs=VMEM,
         scratch_shapes=[pltpu.VMEM((2 * lanes // LANES, 2 * SUBLANES, LANES), jnp.float32)]
         + window_scratch(*window),
         compiler_params=pltpu.CompilerParams(vmem_limit_bytes=24 << 20),
         cost_estimate=pl.CostEstimate(flops=20_000_000, bytes_accessed=4_000_000, transcendentals=0),
         name="coarse_level",
-    )(low_bound, high_bound, own, pooled, *near, *far, early, late)
+    )(low_bound, high_bound, own, halos, pooled, *near, *far, early, late)
 
 
 def fine_kernel(
@@ -462,7 +526,6 @@
     high_ref,
     log_ref,
     source_ref,
-    own_ref,
     first_ref,
     second_ref,
     first_near_ref,
@@ -470,10 +533,10 @@
     early_ref,
     late_ref,
     spread_ref,
-    fine_ref,
-    diff_ref,
     *refs,
 ):
+    *got_refs, fine_ref, diff_ref = refs[:-7]
+    refs = refs[-7:]
     layers, rows, lanes = fine_ref.shape
     ix, iy, iz = (lax.axis_index(axis) for axis in AXES)
     nx, ny, nz = peers
@@ -494,9 +557,16 @@
         if side == 0:
             core = (log_ref, source_ref)[a][layer]
             core = with_lanes(core, early_ref, places["own"] + (a * layers + layer) * rows)
-            slot = 2 * layer + a if both_sides else layer
-            halo = with_lanes(own_ref[slot], early_ref, places["own_strips"] + slot * SUBLANES)
-            if a == 1 and not both_sides:
+            tiles = tuple(
+                with_lanes(ref[layer], early_ref, start + layer * SUBLANES)
+                for ref, start in zip(got_refs, places["own_strips"])
+            )
+            halo = tiles[0]
+            if both_sides:
+                sides = from_right(iy % 2 == 0, tiles), from_left(iy % 2 == 0, tiles)
+                upper = iota(halo.shape, 0) < REACH
+                halo = jnp.where(upper, *(sides if a == 0 else sides[::-1]))
+            if a == 1:
                 halo = turned(halo, REACH, 0)
         else:
             pick = from_left if side < 0 else from_right
@@ -537,20 +607,20 @@
         diff_ref[x] = fine - spread_ref[x]
 
 
-def fine_level(low_bound, high_bound, log_perm, source, own, raw, near, early, late, spread, places, peers):
+def fine_level(low_bound, high_bound, log_perm, source, got, raw, near, early, late, spread, places, peers):
     layers, rows, lanes = log_perm.shape
     window = (layers + 2 * REACH, rows + 2 * REACH, lanes + LANES)
     out = jax.ShapeDtypeStruct(log_perm.shape, jnp.float32)
     return pl.pallas_call(
         functools.partial(fine_kernel, peers, places),
         out_shape=(out, out),
-        in_specs=[SMEM, SMEM] + [VMEM] * 10,
+        in_specs=[SMEM, SMEM] + [VMEM] * (9 + len(got)),
         out_specs=(VMEM, VMEM),
         scratch_shapes=window_scratch(*window),
         compiler_params=pltpu.CompilerParams(vmem_limit_bytes=24 << 20),
         cost_estimate=pl.CostEstimate(flops=20_000_000, bytes_accessed=10_000_000, transcendentals=0),
         name="fine_level",
-    )(low_bound, high_bound, log_perm, source, own, *raw, *near, early, late, spread)
+    )(low_bound, high_bound, log_perm, source, *raw, *near, early, late, spread, *got)
 
 
 class LaneTiles:
@@ -581,32 +651,34 @@
     nx, ny, nz = peers
     layers, rows, lanes = log_perm.shape
     assert layers == REACH and rows == 2 * SUBLANES and nx > 2
+    own, rows_left, rows_right = prep(log_perm, source)
+    got = swap("gy", ny, rows_right, rows_left)
     to_right, to_left = jnp.concatenate([log_perm, source[1:]]), jnp.concatenate([log_perm, source[:-1]])
     second = second_swap("gx", nx, to_right, to_left)
-    stacked = jnp.concatenate([log_perm, source])
-    got_rows = swap("gy", ny, stacked[:, rows - SUBLANES :], stacked[:, :SUBLANES])
     raw = (first_swap("gx", nx, to_right, to_left), second)
     far_groups = far_pairs(nx)
-    own, for_first, for_second, for_far = pack(log_perm, source, got_rows, len(far_groups))
+    halos, for_first, for_second, for_far = pack(own, got, len(far_groups))
+    far = tuple(permute(for_far[i], "gx", nx, group) for i, group in enumerate(far_groups))
     second = permute(for_second, "gx", nx, neighbour_pairs(nx, 1))
     near = (permute(for_first, "gx", nx, neighbour_pairs(nx, 0)), second)
-    far = tuple(permute(for_far[i], "gx", nx, group) for i, group in enumerate(far_groups))
     pooled = pool(*raw)
-    strips = len(got_rows) * layers
-    near_strips = 2 * len(got_rows)
+    near_strips = 2 * len(got)
     places, early, late = {}, LaneTiles(), LaneTiles()
-    places["own"] = early.add(stacked)
-    places["own_strips"] = early.add(own[:strips])
-    places["own_pooled"] = early.add_halves(own[strips:])
+    places["own"] = early.add(jnp.concatenate([log_perm, source]))
+    places["own_strips"] = [early.add(tiles[:layers]) for tiles in got]
+    places["own_pooled"] = early.add_halves(own)
+    places["own_halos"] = early.add_halves(halos)
     places["raw"] = [early.add(block) for block in raw]
     places["pooled"] = early.add_halves(pooled)
     places["near_strips"] = [late.add(block[:near_strips]) for block in near]
     places["near_pooled"] = [late.add_halves(block[near_strips:]) for block in near]
     places["far"] = [late.add(block[0, :, : lanes // 2]) for block in far]
     early, late = early.swapped(nz), late.swapped(nz)
-    spread = coarse_level(low_bound, high_bound, own, pooled, near, far, early, late, places, peers)
+    spread = coarse_level(
+        low_bound, high_bound, own, halos, pooled, near, far, early, late, places, peers
+    )
     return fine_level(
-        low_bound, high_bound, log_perm, source, own, raw, near, early, late, spread, places, peers
+        low_bound, high_bound, log_perm, source, got, raw, near, early, late, spread, places, peers
     )
 
 

time: 22.4 us -> 24.1 us (1.076)
  waiting for transfers between devices: 4.98 us -> 6.57 us
    ppermute x6, waiting for transfers between devices: 4.97 us -> 6.57 us  [permute(): return lax.ppermute(value, (axis, 'gz'), moves)]
    slice x1, local copies, waits for them, and re-layouts: 0.01 us -> 0.99 us  [shards(): source[:-1]]
    unnamed x14, local copies, waits for them, and re-layouts: 1.02 us -> 0.07 us
  transfers between devices with their start and end apart: 8 -> 8, of which waited for: 2 -> 2; matrix products, arithmetic and copies ran while one was open for 1% -> 0% of each run, Pallas kernels for 1% -> 2%
where the time goes in v6:
time: 24.1 us; the launch traced here: 23.9 us
  starting transfers between devices  9.55 us (40%)
  waiting for transfers between devices  6.57 us (27%)
  Pallas kernels  4.33 us (18%)
  between operations  2.23 us (9%)
  local copies, waits for them, and re-layouts  1.1 us (5%)
    ppermute x6, starting transfers between devices, permute(): return lax.ppermute(value, (axis, 'gz'), moves)  8.99 us
    ppermute x6, waiting for transfers between devices, permute(): return lax.ppermute(value, (axis, 'gz'), moves)  6.57 us
    pallas_call x1, Pallas kernels, fine_level(): pl.pallas_call(functools.partial(fine_kernel, peers, places), out_shape=(...  2.96 us
    slice x1, local copies, waits for them, and re-layouts, shards(): source[:-1]  0.99 us
    pallas_call x1, Pallas kernels, coarse_level(): pl.pallas_call(functools.partial(coarse_kernel, peers, places, len(far)),...  0.78 us
    ppermute x2, starting transfers between devices, permute(): lax.ppermute(value, axis, [pair for i, j in pairs for pair in ((i, j), (j...  0.56 us
  transfers between devices with their start and end apart: 8, of which 2 were waited for; matrix products, arithmetic and copies ran while one was open for 0% of the time, Pallas kernels for 2%

profile of v6, /device:TPU:0, one launch (start us, length us, event | category | flops | bytes accessed | tf_op | source)
XLA Modules:
  0.0 23.9 jit_solution(1409865360468128557)
XLA Ops:
  0.6 0.0 copy-start.1
  0.6 1.0 %fusion.2 = (f32[3,16,512]{2,1,0:T(8,128)S(1)}, f32[3,16,512]{2,1,0:T(8,128)S(1)}) fusion(f32[4,16,512]{2,1,0:T(8,128)} %source_ref.3), kind=kLoop, calls=%fused_computation.36 | loop fusion | bytes 393216 | tf_op jit(solution)/shard_map/slice | solution.py:656
  1.7 0.0 copy-done.1
  1.7 0.0 copy-start
  1.7 3.1 %collective-permute-start = (f32[7,16,512]{2,1,0:T(8,128)S(1)}, f32[7,16,512]{2,1,0:T(8,128)S(1)}, u32[]{:S(2)}, u32[]{:S(2)}) collective-permute-start(f32[7,16,512]{2,1,0:T(8,128)S(1)} %get-tuple-element.17), channel_id=1, source_target_pairs={{0,4},{1,5},{4,0},{5,1},{8,12},{9,13},{12,8},{13,9},{2,6},{3,7},{6... | collective-permute-start | bytes 688136 | tf_op jit(solution)/shard_map/ppermute | solution.py:41
  4.8 0.0 collective-permute-start.1
  4.8 0.0 copy-done
  4.8 0.2 prep.1
  5.1 1.6 %collective-permute-start.2 = (f32[5,8,512]{2,1,0:T(8,128)S(1)}, f32[5,8,512]{2,1,0:T(8,128)S(1)}, u32[]{:S(2)}, u32[]{:S(2)}) collective-permute-start(f32[5,8,512]{2,1,0:T(8,128)S(1)} %broadcast_select_fusion.1), channel_id=1, source_target_pairs={{0,2},{1,3},{2,0},{3,1},{4,6},{5,7},{6,4},{7,5},{8,10},{9,11},{10,... | collective-permute-start | bytes 245768 | tf_op jit(solution)/shard_map/ppermute | solution.py:41
  6.7 3.3 %collective-permute-done.2.refs_0_ = f32[5,8,512]{2,1,0:T(8,128)S(1)} collective-permute-done((f32[5,8,512]{2,1,0:T(8,128)S(1)}, f32[5,8,512]{2,1,0:T(8,128)S(1)}, u32[]{:S(2)}, u32[]{:S(2)}) %collective-permute-start.2) | collective-permute-done | bytes 81952 | tf_op jit(solution)/shard_map/ppermute | solution.py:41
  10.0 0.2 pack.1
  10.2 2.8 %collective-permute-start.3 = (f32[3,8,512]{2,1,0:T(8,128)S(1)}, f32[3,8,512]{2,1,0:T(8,128)S(1)}, u32[]{:S(2)}, u32[]{:S(2)}) collective-permute-start(f32[3,8,512]{2,1,0:T(8,128)S(1)} %get-tuple-element.12), channel_id=1, source_target_pairs={{0,4},{1,5},{4,0},{5,1},{8,12},{9,13},{12,8},{13,9},{2,6},{3,7},{6... | collective-permute-start | bytes 147464 | tf_op jit(solution)/shard_map/ppermute | solution.py:41
  13.0 0.0 collective-permute-start.4
  13.0 1.5 %collective-permute-start.6 = (f32[2,8,512]{2,1,0:T(8,128)S(1)}, f32[2,8,512]{2,1,0:T(8,128)S(1)}, u32[]{:S(2)}, u32[]{:S(2)}) collective-permute-start(f32[2,8,512]{2,1,0:T(8,128)S(1)} %bitcast.42), channel_id=1, source_target_pairs={{0,8},{1,9},{4,12},{5,13},{8,0},{9,1},{12,4},{13,5},{2,10},{3,11},... | collective-permute-start | bytes 98312 | tf_op jit(solution)/shard_map/ppermute | solution.py:41
  14.5 3.2 %collective-permute-done.6.refs_2_ = f32[2,8,512]{2,1,0:T(8,128)S(1)} collective-permute-done((f32[2,8,512]{2,1,0:T(8,128)S(1)}, f32[2,8,512]{2,1,0:T(8,128)S(1)}, u32[]{:S(2)}, u32[]{:S(2)}) %collective-permute-start.6) | collective-permute-done | bytes 32800 | tf_op jit(solution)/shard_map/ppermute | solution.py:41
  17.8 0.0 collective-permute-done.3.refs_0_.first_near_ref
  17.8 0.0 collective-permute-done.4.refs_1_.second_near_ref
  17.9 0.0 collective-permute-done.first_ref
  17.9 0.0 collective-permute-done.1.second_ref
  18.0 0.2 pool.1.pool_ref
  18.2 0.1 collective-permute-start.5
  18.3 0.5 %collective-permute-start.7 = (f32[72,128]{1,0:T(8,128)S(1)}, f32[72,128]{1,0:T(8,128)S(1)}, u32[]{:S(2)}, u32[]{:S(2)}) collective-permute-start(f32[72,128]{1,0:T(8,128)S(1)} %broadcast_select_fusion.2), channel_id=1, source_target_pairs={{0,1},{1,0},{2,3},{3,2},{4,5},{5,4},{6,7},{7,6},{8,9},{9,8},{10,11... | collective-permute-start | bytes 110600 | tf_op jit(solution)/shard_map/ppermute | solution.py:32
  20.1 0.0 collective-permute-done.7.refs_4_.late_ref
  20.1 0.0 collective-permute-done.5.refs_3_.early_ref
  20.1 0.8 %coarse_level.1.spread_ref = f32[4,16,512]{2,1,0:T(8,128)S(1)} custom-call(f32[1]{0:T(128)S(6)} %copy.26.low_ref, f32[1]{0:T(128)S(6)} %copy.27.high_ref, f32[2,8,512]{2,1,0:T(8,128)S(1)} %get-tuple-element.9.pooled_ref.own_ref, f32[1,8,512]{2,1,0:T(8,128)S(1)} %get-tuple-element.14.halo_ref, f32[2,2,8,512]{3,2,1,0:T(8,128)S(1)} %pool.1.pool_ref, ...), custom_call_target="tpu_custom_call" | custom-call | flops 20000000 | bytes 4000000 | tf_op jit(solution)/shard_map/coarse_level/pallas_call | solution.py:509
  20.9 3.0 %fine_level.1 = (f32[4,16,512]{2,1,0:T(8,128)}, f32[4,16,512]{2,1,0:T(8,128)}) custom-call(f32[1]{0:T(128)S(6)} %copy.26.low_ref, f32[1]{0:T(128)S(6)} %copy.27.high_ref, f32[4,16,512]{2,1,0:T(8,128)S(1)} %copy-done.1, f32[4,16,512]{2,1,0:T(8,128)S(1)} %copy-done, f32[7,16,512]{2,1,0:T(8,128)S(1)} %collective-permute-done.first_ref, ...), custom_call_target="tpu_custom_call" | custom-call | flops 20000000 | bytes 10000000 | tf_op jit(solution)/shard_map/fine_level/pallas_call | solution.py:614
  (23 shorter events, 0.2 us)
Async XLA Ops:
  0.6 1.0 %copy-start.1 = (f32[4,16,512]{2,1,0:T(8,128)S(1)}, f32[4,16,512]{2,1,0:T(8,128)}, u32[]{:S(2)}) copy-start(f32[4,16,512]{2,1,0:T(8,128)} %log_ref.3) | copy-start | bytes 393220
  1.7 3.2 %copy-start = (f32[4,16,512]{2,1,0:T(8,128)S(1)}, f32[4,16,512]{2,1,0:T(8,128)}, u32[]{:S(2)}) copy-start(f32[4,16,512]{2,1,0:T(8,128)} %source_ref.3) | copy-start | bytes 393220
  1.7 16.2 %collective-permute-start = (f32[7,16,512]{2,1,0:T(8,128)S(1)}, f32[7,16,512]{2,1,0:T(8,128)S(1)}, u32[]{:S(2)}, u32[]{:S(2)}) collective-permute-start(f32[7,16,512]{2,1,0:T(8,128)S(1)} %get-tuple-element.17), channel_id=1, source_target_pairs={{0,4},{1,5},{4,0},{5,1},{8,12},{9,13},{12,8},{13,9},{2,6},{3,7},{6... | collective-permute-start | bytes 688136 | tf_op jit(solution)/shard_map/ppermute | solution.py:41
  4.8 13.1 %collective-permute-start.1 = (f32[7,16,512]{2,1,0:T(8,128)S(1)}, f32[7,16,512]{2,1,0:T(8,128)S(1)}, u32[]{:S(2)}, u32[]{:S(2)}) collective-permute-start(f32[7,16,512]{2,1,0:T(8,128)S(1)} %get-tuple-element.16), channel_id=1, source_target_pairs={{0,1},{1,0},{4,8},{5,9},{8,4},{9,5},{12,13},{13,12},{2,3},{3,2},{6... | collective-permute-start | bytes 688136 | tf_op jit(solution)/shard_map/ppermute | solution.py:41
  5.1 4.9 %collective-permute-start.2 = (f32[5,8,512]{2,1,0:T(8,128)S(1)}, f32[5,8,512]{2,1,0:T(8,128)S(1)}, u32[]{:S(2)}, u32[]{:S(2)}) collective-permute-start(f32[5,8,512]{2,1,0:T(8,128)S(1)} %broadcast_select_fusion.1), channel_id=1, source_target_pairs={{0,2},{1,3},{2,0},{3,1},{4,6},{5,7},{6,4},{7,5},{8,10},{9,11},{10,... | collective-permute-start | bytes 245768 | tf_op jit(solution)/shard_map/ppermute | solution.py:41
  10.2 7.6 %collective-permute-start.3 = (f32[3,8,512]{2,1,0:T(8,128)S(1)}, f32[3,8,512]{2,1,0:T(8,128)S(1)}, u32[]{:S(2)}, u32[]{:S(2)}) collective-permute-start(f32[3,8,512]{2,1,0:T(8,128)S(1)} %get-tuple-element.12), channel_id=1, source_target_pairs={{0,4},{1,5},{4,0},{5,1},{8,12},{9,13},{12,8},{13,9},{2,6},{3,7},{6... | collective-permute-start | bytes 147464 | tf_op jit(solution)/shard_map/ppermute | solution.py:41
  13.0 4.9 %collective-permute-start.4 = (f32[3,8,512]{2,1,0:T(8,128)S(1)}, f32[3,8,512]{2,1,0:T(8,128)S(1)}, u32[]{:S(2)}, u32[]{:S(2)}) collective-permute-start(f32[3,8,512]{2,1,0:T(8,128)S(1)} %get-tuple-element.13), channel_id=1, source_target_pairs={{0,1},{1,0},{4,8},{5,9},{8,4},{9,5},{12,13},{13,12},{2,3},{3,2},{6... | collective-permute-start | bytes 147464 | tf_op jit(solution)/shard_map/ppermute | solution.py:41
  13.0 4.8 %collective-permute-start.6 = (f32[2,8,512]{2,1,0:T(8,128)S(1)}, f32[2,8,512]{2,1,0:T(8,128)S(1)}, u32[]{:S(2)}, u32[]{:S(2)}) collective-permute-start(f32[2,8,512]{2,1,0:T(8,128)S(1)} %bitcast.42), channel_id=1, source_target_pairs={{0,8},{1,9},{4,12},{5,13},{8,0},{9,1},{12,4},{13,5},{2,10},{3,11},... | collective-permute-start | bytes 98312 | tf_op jit(solution)/shard_map/ppermute | solution.py:41
  18.2 1.9 %collective-permute-start.5 = (f32[496,128]{1,0:T(8,128)S(1)}, f32[496,128]{1,0:T(8,128)S(1)}, u32[]{:S(2)}, u32[]{:S(2)}) collective-permute-start(f32[496,128]{1,0:T(8,128)S(1)} %broadcast_select_fusion), channel_id=1, source_target_pairs={{0,1},{1,0},{2,3},{3,2},{4,5},{5,4},{6,7},{7,6},{8,9},{9,8},{10,11... | collective-permute-start | bytes 761864 | tf_op jit(solution)/shard_map/ppermute | solution.py:32
  18.3 1.8 %collective-permute-start.7 = (f32[72,128]{1,0:T(8,128)S(1)}, f32[72,128]{1,0:T(8,128)S(1)}, u32[]{:S(2)}, u32[]{:S(2)}) collective-permute-start(f32[72,128]{1,0:T(8,128)S(1)} %broadcast_select_fusion.2), channel_id=1, source_target_pairs={{0,1},{1,0},{2,3},{3,2},{4,5},{5,4},{6,7},{7,6},{8,9},{9,8},{10,11... | collective-permute-start | bytes 110600 | tf_op jit(solution)/shard_map/ppermute | solution.py:32

commit v7 on v6

v7 whole, which is shorter than its diff:
```python
import functools

import jax
import jax.numpy as jnp
from jax import lax
from jax.experimental import pallas as pl
from jax.experimental.pallas import tpu as pltpu
from jax.sharding import PartitionSpec as P

DEGREE = 3
REACH = DEGREE + 1
LANES = 128
SUBLANES = 8
storage_rate = 0.1
AXES = ("gx", "gy", "gz")
VMEM = pl.BlockSpec(memory_space=pltpu.VMEM)
ANY = pl.BlockSpec(memory_space=pl.ANY)


AHEAD = pl.CostEstimate(flops=50_000_000_000, bytes_accessed=1_000_000, transcendentals=0)


def iota(shape, dim):
    return lax.broadcasted_iota(jnp.int32, shape, dim)


def turned(value, shift, axis):
    size = value.shape[axis]
    return pltpu.roll(value, shift % size, axis)


def permute(value, axis, peers, pairs):
    cores = lax.axis_size("gz")
    if axis == "gz" or cores % 2:
        return lax.ppermute(value, axis, [pair for i, j in pairs for pair in ((i, j), (j, i))])
    partner = {}
    for i, j in pairs:
        partner[i], partner[j] = j, i
    moves = [
        (i * cores + core, partner[i] * cores + core if i in partner else i * cores + (core ^ 1))
        for i in range(peers)
        for core in range(cores)
    ]
    return lax.ppermute(value, (axis, "gz"), moves)


def neighbour_pairs(peers, start):
    return [(i, i + 1) for i in range(start, peers - 1, 2)]


def first_swap(axis, peers, right, left):
    even = lax.axis_index(axis) % 2 == 0
    return permute(jnp.where(even, right, left), axis, peers, neighbour_pairs(peers, 0))


def second_swap(axis, peers, right, left):
    even = lax.axis_index(axis) % 2 == 0
    return permute(jnp.where(even, left, right), axis, peers, neighbour_pairs(peers, 1))


def swap(axis, peers, right, left):
    got = (first_swap(axis, peers, right, left),)
    return got if peers == 2 else got + (second_swap(axis, peers, right, left),)


def far_pairs(peers):
    pairs = [(i, i + 2) for i in range(peers - 2)]
    groups = [[pair for pair in pairs if pair[0] % 4 < 2], [pair for pair in pairs if pair[0] % 4 >= 2]]
    return [group for group in groups if group]


def from_right(is_first, got):
    return got[0] if len(got) == 1 else jnp.where(is_first, got[0], got[1])


def from_left(is_first, got):
    return got[0] if len(got) == 1 else jnp.where(is_first, got[1], got[0])


def inverse(value):
    guess = pl.reciprocal(value, approx=True)
    return guess * (2.0 - value * guess)


def numerators(shape, dim, own, index, peers, face_scale):
    place = iota(shape, dim)
    right = jnp.where(index < peers - 1, 2.0 * face_scale, 0.0)
    left = jnp.where(index > 0, 2.0 * face_scale, 0.0)
    return jnp.where(
        place == own - 1, right, jnp.where(place == shape[dim] - 1, left, 2.0 * face_scale)
    )


def iterate(count, log_at, source_at, x_faces, y_top, z_top, coef_ref, storage, refs):
    tx_ref, ty_ref, tz_ref, w_ref, d_ref, r_ref, p_ref = refs
    rows, lanes = y_top.shape

    def coefficient(i):
        return jnp.concatenate(
            [jnp.concatenate([coef_ref[i]] * (lanes // LANES), axis=1)] * (rows // SUBLANES), axis=0
        )

    over_theta = coefficient(0)
    after = jnp.exp(-log_at(0))
    tx_before = None
    for k in range(count):
        here = after
        if k + 1 < count:
            after = jnp.exp(-log_at(k + 1))
            tx = x_faces[k] * inverse(here + after)
            tx_ref[k] = tx
        if 1 <= k <= count - 2:
            ty = y_top * inverse(here + turned(here, -1, 0))
            tz = z_top * inverse(here + turned(here, -1, 1))
            diagonal = storage + (tx_before + tx) + (ty + turned(ty, 1, 0)) + (tz + turned(tz, 1, 1))
            w = inverse(diagonal)
            source = source_at(k)
            d_ref[k] = source * (over_theta * w)
            if 2 <= k <= count - 3:
                ty_ref[k] = ty
                tz_ref[k] = tz
                w_ref[k] = w
                r_ref[k] = source
        tx_before = tx
    for step in range(DEGREE):
        first, last = 2 + step, count - 2 - step
        keep, gain = coefficient(1 + 2 * step), coefficient(2 + 2 * step)
        here = d_ref[first]
        fx_before = tx_ref[first - 1] * (d_ref[first - 1] - here)
        for k in range(first, last):
            after = d_ref[k + 1]
            fx = tx_ref[k] * (here - after)
            fy = ty_ref[k] * (here - turned(here, -1, 0))
            fz = tz_ref[k] * (here - turned(here, -1, 1))
            applied = storage * here + (fx - fx_before) + (fy - turned(fy, 1, 0)) + (fz - turned(fz, 1, 1))
            residual = r_ref[k] - applied
            fresh = keep * here + gain * (residual * w_ref[k])
            if REACH <= k < count - REACH:
                so_far = here if step == 0 else p_ref[k]
                p_ref[k] = so_far + fresh
            if step < DEGREE - 1:
                r_ref[k] = residual
                d_ref[k] = fresh
            here, fx_before = after, fx


def coefficients_kernel(low_ref, high_ref, after_ref, coef_ref, bounds_ref, sems):
    copies = [
        pltpu.make_async_copy(ref, bounds_ref.at[i], sems.at[i]) for i, ref in enumerate((low_ref, high_ref))
    ]
    for copy in copies:
        copy.start()
    for copy in copies:
        copy.wait()
    low, high = (jnp.full((SUBLANES, LANES), bounds_ref[i, 0]) for i in range(2))
    theta, delta = (high + low) * 0.5, (high - low) * 0.5
    sigma = theta / delta
    rho = 1.0 / sigma
    coef_ref[0] = 1.0 / theta
    for step in range(DEGREE):
        rho_next = 1.0 / (2.0 * sigma - rho)
        coef_ref[1 + 2 * step] = rho_next * rho
        coef_ref[2 + 2 * step] = 2.0 * rho_next / delta
        rho = rho_next


def chebyshev_coefficients(low_bound, high_bound, after):
    return pl.pallas_call(
        coefficients_kernel,
        out_shape=jax.ShapeDtypeStruct((1 + 2 * DEGREE, SUBLANES, LANES), jnp.float32),
        in_specs=[pl.BlockSpec(memory_space=pltpu.HBM)] * 2 + [ANY],
        out_specs=VMEM,
        scratch_shapes=[pltpu.SMEM((2, 1), jnp.float32), pltpu.SemaphoreType.DMA((2,))],
        compiler_params=pltpu.CompilerParams(vmem_limit_bytes=4 << 20),
        cost_estimate=pl.CostEstimate(flops=1_000_000, bytes_accessed=100_000, transcendentals=0),
        name="coefficients",
    )(low_bound, high_bound, after)


def put(ref, tile, value):
    for i in range(value.shape[1] // LANES):
        ref[(tile + i) * SUBLANES : (tile + i + 1) * SUBLANES, :] = value[:, i * LANES : (i + 1) * LANES]


def take(ref, tile, count):
    tiles = [ref[(tile + i) * SUBLANES : (tile + i + 1) * SUBLANES, :] for i in range(count)]
    return tiles[0] if count == 1 else jnp.concatenate(tiles, axis=1)


def edges(value):
    lanes = value.shape[-1]
    value = value if isinstance(value, jax.Array) else value.at
    return value[:, lanes - LANES :], value[:, :LANES]


def write_lanes(ref, pairs):
    starts = lax.axis_index("gz") == 0
    each = LANES // SUBLANES
    group = iota((SUBLANES, LANES), 1) // SUBLANES
    for base in range(0, len(pairs), each):
        merged = None
        for j, (last, first) in enumerate(pairs[base : base + each]):
            moved = turned(jnp.where(starts, last, first), SUBLANES * j, 1)
            place = jnp.where(starts, (j - 1) % each, j)
            merged = moved if merged is None else jnp.where(group == place, moved, merged)
        row = base // each * SUBLANES
        ref[row : row + SUBLANES, :] = merged


def read_lanes(ref, slot):
    each = LANES // SUBLANES
    row = slot // each * SUBLANES
    return turned(ref[row : row + SUBLANES, :], -SUBLANES * (slot % each), 1)


def early_slots(layers, row_tiles, n_got):
    keys = [("own", a, layer, i) for a in range(2) for layer in range(layers) for i in range(row_tiles)]
    keys += [("got", g, layer) for g in range(n_got) for layer in range(layers)]
    keys += [("pooled", x, a) for x in range(2) for a in range(2)]
    keys += [("halo", i, half) for i in range(n_got) for half in range(2)]
    keys += [
        ("raw", side, slot, i)
        for side in range(2)
        for slot in range(2 * layers - 1)
        for i in range(row_tiles)
    ]
    keys += [("near", side, i) for side in range(2) for i in range(3)]
    return {key: i for i, key in enumerate(keys)}


def near_layout(lanes, wide):
    whole, half = lanes // LANES, lanes // LANES // 2
    if wide:
        parts = [("log1", whole), ("source1", whole), ("log2", whole), ("source2", whole)]
        parts += [(name, half) for name in ("halo0", "halo1", "halo2", "halo3", "source")]
    else:
        parts = [("strip", whole), ("halo", half), ("source", half), ("row", 1)]
    layout, start = {}, 0
    for name, count in parts:
        layout[name] = (start, count)
        start += count
    return layout, start


def late_slots(lanes, wide):
    names = list(near_layout(lanes, wide)[0])
    keys = [(side, name) for side in range(2) for name in names] + [(side, "far") for side in range(2)]
    return {key: i for i, key in enumerate(keys)}


def rows_to_lanes(row_tile, count):
    return jnp.concatenate(
        [jnp.broadcast_to(row_tile[j : j + 1], (SUBLANES, LANES)) for j in range(count)], axis=1
    )


def packed_rows(slots):
    each = LANES // SUBLANES
    return jax.ShapeDtypeStruct((-(-len(slots) // each) * SUBLANES, LANES), jnp.float32)


def window_scratch(count, rows, lanes):
    return [pltpu.VMEM((count, rows, lanes), jnp.float32)] * 7


def exact_dot(value, zero_one):
    parts = []
    for _ in range(3):
        part = value.astype(jnp.bfloat16)
        parts.append(part)
        value = value - part.astype(jnp.float32)
    rows = value.shape[0]
    out = jnp.dot(jnp.concatenate(parts, axis=0), zero_one, preferred_element_type=jnp.float32)
    return (out[2 * rows :] + out[rows : 2 * rows]) + out[:rows]


def row_pairs(top, bottom, sum_ref):
    tiles = top.shape[1] // LANES
    for tile in range(tiles):
        columns = slice(tile * LANES, (tile + 1) * LANES)
        sum_ref[tile, :SUBLANES] = top[:, columns]
        sum_ref[tile, SUBLANES:] = bottom[:, columns]
    return jnp.concatenate(
        [
            sum_ref[tile, pl.ds(0, SUBLANES, stride=2), :] + sum_ref[tile, pl.ds(1, SUBLANES, stride=2), :]
            for tile in range(tiles)
        ],
        axis=1,
    )


def lane_pairs(pieces):
    lanes = pieces[0].shape[1]
    pick = (iota((lanes, lanes // 2), 0) // 2 == iota((lanes, lanes // 2), 1)).astype(jnp.bfloat16)
    pooled = exact_dot(jnp.concatenate(pieces, axis=0), pick)
    return [pooled[SUBLANES * i : SUBLANES * (i + 1)] for i in range(len(pieces))]


def join_halo(near, beyond, starts):
    row = iota(near.shape, 0)
    up, down = turned(beyond, 3, 0), turned(beyond, -3, 0)
    right = jnp.where((row == 3) | (row == 7), up, jnp.where(row == 6, turned(beyond, 5, 0), near))
    left = jnp.where((row == 0) | (row == 4), down, jnp.where(row == 5, up, near))
    return jnp.where(starts, right, left)


def beyond_halo(joined, starts):
    row = iota(joined.shape, 0)
    up, down = turned(joined, 3, 0), turned(joined, -3, 0)
    right = jnp.where(row == 1, turned(joined, -5, 0), down)
    left = jnp.where(row == 2, down, up)
    return jnp.where(starts, right, left)


def join_third(near, third):
    row = iota(near.shape, 0)
    return jnp.where(
        row == 3, turned(third, 3, 0), jnp.where(row == 4, turned(third, -3, 0), near)
    )


def third_halo(joined):
    return jnp.where(iota(joined.shape, 0) < REACH, turned(joined, -3, 0), turned(joined, 3, 0))


def prep_kernel(log_ref, source_ref, pooled_ref, *refs):
    *out_refs, sum_ref = refs
    layers, rows, lanes = log_ref.shape
    starts = lax.axis_index("gy") == 0

    def put(slot, left, right):
        if len(out_refs) == 1:
            out_refs[0][slot] = jnp.where(starts, right, left)
        else:
            out_refs[0][slot], out_refs[1][slot] = left, right

    half = lanes // 2
    upper = iota((SUBLANES, lanes), 0) < REACH
    pieces = []
    for x in range(2):
        for ref in (log_ref, source_ref):
            both = ref[2 * x] + ref[2 * x + 1]
            pieces.append(row_pairs(both[:SUBLANES], both[SUBLANES:], sum_ref))
    log0, source0, log1, source1 = lane_pairs(pieces)
    log0, log1 = log0 * 0.125, log1 * 0.125
    pooled_ref[0] = jnp.concatenate([log0, source0], axis=1)
    pooled_ref[1] = jnp.concatenate([log1, source1], axis=1)
    for layer in range(layers):
        put(
            layer,
            jnp.where(upper, log_ref[layer, :SUBLANES], turned(source_ref[layer, :SUBLANES], REACH, 0)),
            jnp.where(upper, turned(source_ref[layer, SUBLANES:], REACH, 0), log_ref[layer, SUBLANES:]),
        )
    pair = iota((SUBLANES, half), 0) // 2

    def four(*tiles):
        merged = jnp.where(
            pair == 0, tiles[0], jnp.where(pair == 1, tiles[1], jnp.where(pair == 2, tiles[2], tiles[3]))
        )
        return jnp.concatenate([merged, merged], axis=1)

    put(
        layers,
        four(turned(log1, -2, 0), log0, turned(source1, 2, 0), turned(source0, 4, 0)),
        four(turned(log0, -4, 0), turned(log1, -2, 0), source0, turned(source1, 2, 0)),
    )


def prep(log_perm, source, ny):
    layers, rows, lanes = log_perm.shape
    outs = 1 if ny == 2 else 2

    def tiles(count):
        return jax.ShapeDtypeStruct((count, SUBLANES, lanes), jnp.float32)

    return pl.pallas_call(
        prep_kernel,
        out_shape=(tiles(2),) + (tiles(layers + 1),) * outs,
        in_specs=[VMEM] * 2,
        out_specs=(VMEM,) * (1 + outs),
        scratch_shapes=[pltpu.VMEM((lanes // LANES, 2 * SUBLANES, LANES), jnp.float32)],
        compiler_params=pltpu.CompilerParams(vmem_limit_bytes=8 << 20),
        cost_estimate=pl.CostEstimate(flops=5_000_000, bytes_accessed=700_000, transcendentals=0),
        name="prep",
    )(log_perm, source)


def raw_kernel(to_right_if_odd, log_ref, source_ref, after_ref, out_ref):
    layers = log_ref.shape[0]
    odd = lax.axis_index("gx") % 2
    skip = odd if to_right_if_odd else 1 - odd
    for layer in range(layers):
        out_ref[layer] = log_ref[layer]
    for layer in range(layers - 1):
        out_ref[layers + layer] = source_ref[layer + skip]


def raw_block(log_perm, source, after, to_right_if_odd):
    layers, rows, lanes = log_perm.shape
    return pl.pallas_call(
        functools.partial(raw_kernel, to_right_if_odd),
        out_shape=jax.ShapeDtypeStruct((2 * layers - 1, rows, lanes), jnp.float32),
        in_specs=[VMEM, VMEM, ANY],
        out_specs=VMEM,
        compiler_params=pltpu.CompilerParams(vmem_limit_bytes=8 << 20),
        cost_estimate=pl.CostEstimate(flops=1_000_000, bytes_accessed=500_000, transcendentals=0),
        name="raw_block",
    )(log_perm, source, after)


def pack_far_kernel(wide, pooled_ref, *refs):
    n_got = 2 if wide else 1
    got_refs, halo_ref, far_refs, sum_ref = refs[:n_got], refs[n_got], refs[n_got + 1 : -1], refs[-1]
    layers, lanes = got_refs[0].shape[0] - 1, got_refs[0].shape[2]
    ix, iy = lax.axis_index("gx"), lax.axis_index("gy")
    even, starts, low = iy % 2 == 0, iy == 0, ix % 4 < 2
    half = lanes // 2
    upper = iota((SUBLANES, lanes), 0) < REACH
    row = iota((SUBLANES, half), 0)

    def got(slot):
        tiles = tuple(ref[slot] for ref in got_refs)
        return from_right(even, tiles), from_left(even, tiles)

    strips = [got(layer) for layer in range(layers)]
    extra = [tile[:, :half] for tile in got(layers)]
    pieces = []
    for side in range(2 if wide else 1):
        both = [strips[2 * x][side] + strips[2 * x + 1][side] for x in range(2)]
        pieces.append(row_pairs(*both, sum_ref))
    fine_rows = lane_pairs(pieces)

    def right_halos(rows, extra):
        rows = jnp.where(row % 4 < 2, rows * 0.125, rows)
        return [
            jnp.where(row < 2, near, jnp.where((row == 4) | (row == 5), far, more))
            for near, far, more in (
                (rows, turned(rows, 2, 0), extra),
                (turned(rows, 4, 0), turned(rows, -2, 0), turned(extra, 2, 0)),
            )
        ]

    def left_halos(rows, extra):
        rows = jnp.where(row % 4 >= 2, rows * 0.125, rows)
        return [
            jnp.where((row == 2) | (row == 3), near, jnp.where(row >= 6, far, more))
            for near, far, more in (
                (rows, turned(rows, -2, 0), extra),
                (turned(rows, 4, 0), turned(rows, 2, 0), turned(extra, -2, 0)),
            )
        ]

    right, left = right_halos(fine_rows[0], extra[0]), left_halos(fine_rows[-1], extra[1])
    if wide:
        top = row < REACH
        halos = [jnp.where(top, right[x], turned(left[x], REACH, 0)) for x in range(2)]
        halos += [jnp.where(top, turned(right[x], REACH, 0), left[x]) for x in range(2)]
    else:
        halos = [jnp.where(starts, right[x], left[x]) for x in range(2)]

    def pair(left, right):
        return jnp.concatenate([left, right], axis=1)

    for i in range(len(halos) // 2):
        halo_ref[i] = pair(halos[2 * i], halos[2 * i + 1])
    logs = [pooled_ref[x, :, :half] for x in range(2)]
    sources = [pooled_ref[x, :, half:] for x in range(2)]

    far = [(logs[inner], logs[1 - inner], sources[inner], halos[inner]) for inner in (1, 0)]
    for group, ref in enumerate(far_refs):
        for i, (right, left) in enumerate(zip(*far)):
            put(ref, i * (half // LANES), jnp.where(low, *((right, left) if group == 0 else (left, right))))
        for spare in range(4 * (half // LANES), ref.shape[0] // SUBLANES):
            put(ref, spare, jnp.zeros((SUBLANES, LANES), jnp.float32))


def pack_far(pooled, got, n_far):
    slots, rows, lanes = got[0].shape
    wide = len(got) == 2
    far_rows = max(2 * lanes // LANES, 0 if wide else near_layout(lanes, wide)[1]) * SUBLANES
    out_shape = (jax.ShapeDtypeStruct((len(got), SUBLANES, lanes), jnp.float32),) + (
        jax.ShapeDtypeStruct((far_rows, LANES), jnp.float32),
    ) * n_far
    halos, *far = pl.pallas_call(
        functools.partial(pack_far_kernel, wide),
        out_shape=out_shape,
        in_specs=[VMEM] * (1 + len(got)),
        out_specs=(VMEM,) * len(out_shape),
        scratch_shapes=[pltpu.VMEM((lanes // LANES, 2 * SUBLANES, LANES), jnp.float32)],
        compiler_params=pltpu.CompilerParams(vmem_limit_bytes=8 << 20),
        cost_estimate=AHEAD,
        name="pack_far",
    )(pooled, *got)
    return halos, far


def pack_near_kernel(wide, pooled_ref, halo_ref, after_ref, *refs):
    *got_refs, first_ref, second_ref = refs
    layers, lanes = got_refs[0].shape[0] - 1, got_refs[0].shape[2]
    ix, iy = lax.axis_index("gx"), lax.axis_index("gy")
    even, starts = iy % 2 == 0, iy == 0
    half = lanes // 2
    upper = iota((SUBLANES, lanes), 0) < REACH

    def got(slot):
        tiles = tuple(ref[slot] for ref in got_refs)
        return from_right(even, tiles), from_left(even, tiles)

    strips = [got(layer) for layer in range(layers)]
    halos = [halo_ref[i // 2, :, (i % 2) * half : (i % 2 + 1) * half] for i in range(4 if wide else 2)]
    sources = [pooled_ref[x, :, half:] for x in range(2)]

    def near_tiles(order):
        near, beyond = order[0] // 2, order[-1] // 2
        if wide:
            log_rows = [jnp.where(upper, *strips[layer]) for layer in range(layers)]
            source_rows = [turned(jnp.where(upper, *strips[layer][::-1]), REACH, 0) for layer in range(layers)]
            return {
                "log1": join_third(log_rows[order[0]], log_rows[order[2]]),
                "source1": source_rows[order[0]],
                "log2": log_rows[order[1]],
                "source2": source_rows[order[1]],
                "halo0": halos[near],
                "halo1": halos[beyond],
                "halo2": halos[2 + near],
                "halo3": halos[2 + beyond],
                "source": sources[beyond],
            }
        first, second, third = (strips[layer][0] for layer in order[:3])
        place = iota((SUBLANES, lanes), 0)
        right = jnp.where(place == 3, turned(third, 3, 0), jnp.where(place >= 6, turned(second, -2, 0), first))
        left = jnp.where(place == 4, turned(third, -3, 0), jnp.where(place < 2, turned(second, 2, 0), first))
        line = jnp.where(starts, second[4:5], second[3:4])
        lines = jnp.zeros((SUBLANES, LANES), jnp.float32)
        for j in range(lanes // LANES):
            lines = jnp.where(iota(lines.shape, 0) == j, line[:, j * LANES : (j + 1) * LANES], lines)
        return {
            "strip": jnp.where(starts, right, left),
            "halo": join_halo(halos[near], halos[beyond], starts),
            "source": sources[beyond],
            "row": lines,
        }

    forward = list(range(layers))
    layout, _ = near_layout(lanes, wide)
    right, left = near_tiles(forward[::-1]), near_tiles(forward)
    for name, (start, _) in layout.items():
        put(first_ref, start, jnp.where(ix % 2 == 0, right[name], left[name]))
        put(second_ref, start, jnp.where(ix % 2 == 0, left[name], right[name]))


def pack_near(pooled, halos, after, got):
    slots, rows, lanes = got[0].shape
    wide = len(got) == 2
    out = jax.ShapeDtypeStruct((near_layout(lanes, wide)[1] * SUBLANES, LANES), jnp.float32)
    return pl.pallas_call(
        functools.partial(pack_near_kernel, wide),
        out_shape=(out, out),
        in_specs=[VMEM, VMEM, ANY] + [VMEM] * len(got),
        out_specs=(VMEM,) * 2,
        compiler_params=pltpu.CompilerParams(vmem_limit_bytes=8 << 20),
        cost_estimate=AHEAD,
        name="pack_near",
    )(pooled, halos, after, *got)


def landed_kernel(after_ref, log_ref, source_ref, pooled_ref, halo_ref, first_ref, second_ref, *refs):
    *got_refs, out_ref, sent_ref, sum_ref = refs
    layers, rows, lanes = log_ref.shape
    half = lanes // 2
    even = lax.axis_index("gx") % 2 == 0
    slots = early_slots(layers, rows // SUBLANES, len(got_refs))
    pairs = {}
    for a, ref in enumerate((log_ref, source_ref)):
        for layer in range(layers):
            for i in range(rows // SUBLANES):
                pairs["own", a, layer, i] = edges(ref.at[layer, i * SUBLANES : (i + 1) * SUBLANES])
    for g, ref in enumerate(got_refs):
        for layer in range(layers):
            pairs["got", g, layer] = edges(ref.at[layer])
    for i in range(2):
        for x in range(2):
            columns = slice(x * half, (x + 1) * half)
            pairs["pooled", i, x] = edges(pooled_ref.at[i, :, columns])
            if i < len(got_refs):
                pairs["halo", i, x] = edges(halo_ref.at[i, :, columns])
    pieces = []
    for side, pick in enumerate((from_left, from_right)):

        def block(slot):
            return pick(even, (first_ref[slot], second_ref[slot]))

        for slot in range(2 * layers - 1):
            for i in range(rows // SUBLANES):
                part = slice(i * SUBLANES, (i + 1) * SUBLANES)
                ends = [edges(ref.at[slot, part]) for ref in (first_ref, second_ref)]
                pairs["raw", side, slot, i] = [
                    pick(even, tuple(end[...] for end in both)) for both in zip(*ends)
                ]
        nearest = layers + 1 if side == 0 else layers
        for top in (0, 2, nearest):
            both = block(top) + block(top + 1)
            pieces.append(row_pairs(both[:SUBLANES], both[SUBLANES:], sum_ref))
    tiles = lane_pairs(pieces)
    for side in range(2):
        for i in range(3):
            tile = tiles[3 * side + i] * (0.125 if i < 2 else 1.0)
            put(out_ref, (3 * side + i) * (half // LANES), tile)
            pairs["near", side, i] = edges(tile)
    write_lanes(sent_ref, [tuple(end[...] for end in pairs[key]) for key in slots])


def landed(after, log_perm, source, pooled, halos, raw, got):
    layers, rows, lanes = log_perm.shape
    slots = early_slots(layers, rows // SUBLANES, len(got))
    return pl.pallas_call(
        landed_kernel,
        out_shape=(
            jax.ShapeDtypeStruct((6 * (lanes // 2 // LANES) * SUBLANES, LANES), jnp.float32),
            packed_rows(slots),
        ),
        in_specs=[ANY] + [VMEM] * (6 + len(got)),
        out_specs=(VMEM,) * 2,
        scratch_shapes=[pltpu.VMEM((lanes // LANES, 2 * SUBLANES, LANES), jnp.float32)],
        compiler_params=pltpu.CompilerParams(vmem_limit_bytes=16 << 20),
        cost_estimate=pl.CostEstimate(flops=1_000_000, bytes_accessed=1_000_000, transcendentals=0),
        name="landed",
    )(after, log_perm, source, pooled, halos, *raw, *got)


def near_part(refs, even, lanes, wide, side, name):
    start, count = near_layout(lanes, wide)[0][name]
    pick = from_left if side == 0 else from_right
    got = pick(even, tuple(take(ref, start, count) for ref in refs))
    return rows_to_lanes(got, lanes // LANES) if name == "row" else got


def far_part(refs, low, lanes, side, i):
    count = lanes // 2 // LANES
    pick = from_left if side == 0 else from_right
    return pick(low, tuple(take(ref, i * count, count) for ref in refs))


def late_kernel(lanes, wide, after_ref, first_ref, second_ref, *refs):
    *far_refs, sent_ref = refs
    even, low = lax.axis_index("gx") % 2 == 0, lax.axis_index("gx") % 4 < 2
    pairs = []
    for side, name in late_slots(lanes, wide):
        if name == "far":
            pairs.append(edges(far_part(far_refs, low, lanes, side, 0)))
        else:
            pairs.append(edges(near_part((first_ref, second_ref), even, lanes, wide, side, name)))
    write_lanes(sent_ref, pairs)


def late_lanes(after, near, far, lanes, wide):
    return pl.pallas_call(
        functools.partial(late_kernel, lanes, wide),
        out_shape=packed_rows(late_slots(lanes, wide)),
        in_specs=[ANY] + [VMEM] * (2 + len(far)),
        out_specs=VMEM,
        compiler_params=pltpu.CompilerParams(vmem_limit_bytes=8 << 20),
        cost_estimate=pl.CostEstimate(flops=1_000_000, bytes_accessed=200_000, transcendentals=0),
        name="late_lanes",
    )(after, *near, *far)


def coarse_kernel(peers, n_far, own_ref, halo_ref, pool_ref, first_ref, second_ref, *refs):
    near_refs, far_refs = (first_ref, second_ref), refs[:n_far]
    early_ref, late_ref, coef_ref, out_ref, wide_ref, *scratch = refs[n_far:]
    ix, iy, iz = (lax.axis_index(axis) for axis in AXES)
    nx, ny, nz = peers
    wide = ny > 2
    fine_lanes = own_ref.shape[2]
    lanes, rows = fine_lanes // 2, SUBLANES
    even, low, starts = ix % 2 == 0, ix % 4 < 2, iy == 0
    top = iota((rows, lanes + LANES), 0) < REACH
    early = early_slots(REACH, 2, 2 if wide else 1)
    late = late_slots(fine_lanes, wide)

    def columns(half):
        return slice(half * lanes, (half + 1) * lanes)

    def with_early(core, *key):
        return jnp.concatenate([core, read_lanes(early_ref, early[key])], axis=1)

    def near(side, name):
        core = near_part(near_refs, even, fine_lanes, wide, side, name)
        return jnp.concatenate([core, read_lanes(late_ref, late[side, name])], axis=1)

    def far(side, i):
        core = far_part(far_refs, low, fine_lanes, side, i)
        return jnp.concatenate([core, read_lanes(late_ref, late[side, "far"])], axis=1)

    def split(tile, a):
        other = turned(tile, REACH, 0)
        return jnp.where(top, tile, other) if a == 0 else jnp.where(top, other, tile)

    def window(a, k):
        block, layer = k // 2 - 2, k % 2
        nearest = layer == (1 if block < 0 else 0)
        side = 0 if block < 0 else 1
        if abs(block) == 2:
            if a == 1:
                core = far(side, 2)
                return jnp.concatenate([core, jnp.zeros_like(core)], axis=0)
            halo = far(side, 3)
            halo = halo if wide else split(halo, 0)
            return jnp.concatenate([far(side, 0 if nearest else 1), halo], axis=0)
        if block == 0:
            core = with_early(own_ref[layer, :, columns(a)], "pooled", layer, a)
            if wide:
                halo = with_early(halo_ref[a, :, columns(layer)], "halo", a, layer)
            else:
                halo = split(with_early(halo_ref[0, :, columns(layer)], "halo", 0, layer), a)
            return jnp.concatenate([core, halo], axis=0)
        if a == 0 or nearest:
            i = layer if a == 0 else 2
            core = take(pool_ref, (3 * side + i) * (lanes // LANES), lanes // LANES)
            core = with_early(core, "near", side, i)
        else:
            core = near(side, "source")
        if wide:
            halo = near(side, f"halo{2 * a + (0 if nearest else 1)}")
        else:
            joined = near(side, "halo")
            halo = split(joined if nearest else beyond_halo(joined, starts), a)
        return jnp.concatenate([core, halo], axis=0)

    def open_face(inside):
        return jnp.where(inside, 4.0, 0.0)

    faces = [4.0] * 9
    faces[1], faces[3] = open_face(ix > 1), open_face(ix > 0)
    faces[5], faces[7] = open_face(ix < nx - 1), open_face(ix < nx - 2)
    shape = (2 * rows, lanes + LANES)
    iterate(
        2 + 2 * REACH,
        functools.partial(window, 0),
        functools.partial(window, 1),
        faces,
        numerators(shape, 0, rows, iy, ny, 2.0),
        numerators(shape, 1, lanes, iz, nz, 2.0),
        coef_ref,
        8.0 * storage_rate,
        scratch,
    )
    p_ref = scratch[-1]
    widen = (iota((lanes, 2 * lanes), 0) == iota((lanes, 2 * lanes), 1) // 2).astype(jnp.bfloat16)
    pressure = jnp.concatenate([p_ref[REACH + x, :rows, :lanes] for x in range(2)], axis=0)
    spread = exact_dot(pressure, widen)
    for x in range(2):
        for tile in range(2 * lanes // LANES):
            part = slice(tile * LANES, (tile + 1) * LANES)
            for half in range(2):
                wide_ref[tile, pl.ds(half, rows, stride=2), :] = spread[x * rows : (x + 1) * rows, part]
            for twin in range(2):
                out_ref[2 * x + twin, :, part] = wide_ref[tile]


def coarse_level(own, halos, pooled, near, far, early, late, coefficients, peers):
    lanes = own.shape[2] // 2
    window = (2 + 2 * REACH, 2 * SUBLANES, lanes + LANES)
    return pl.pallas_call(
        functools.partial(coarse_kernel, peers, len(far)),
        out_shape=jax.ShapeDtypeStruct((REACH, 2 * SUBLANES, 2 * lanes), jnp.float32),
        in_specs=[VMEM] * (8 + len(far)),
        out_specs=VMEM,
        scratch_shapes=[pltpu.VMEM((2 * lanes // LANES, 2 * SUBLANES, LANES), jnp.float32)]
        + window_scratch(*window),
        compiler_params=pltpu.CompilerParams(vmem_limit_bytes=24 << 20),
        cost_estimate=pl.CostEstimate(flops=20_000_000, bytes_accessed=4_000_000, transcendentals=0),
        name="coarse_level",
    )(own, halos, pooled, *near, *far, early, late, coefficients)


def fine_kernel(peers, n_far, log_ref, source_ref, *refs):
    layers, rows, lanes = log_ref.shape
    ix, iy, iz = (lax.axis_index(axis) for axis in AXES)
    nx, ny, nz = peers
    wide = ny > 2
    n_got = 2 if wide else 1
    got_refs, refs = refs[:n_got], refs[n_got:]
    second_ref, first_ref = refs[:2]
    second_near_ref, first_near_ref, early_ref, late_ref, spread_ref = refs[2 + n_far : 7 + n_far]
    coef_ref, fine_ref, diff_ref, *scratch = refs[7 + n_far :]
    even, starts = ix % 2 == 0, iy == 0
    count = 3 * layers
    upper = iota((SUBLANES, lanes + LANES), 0) < REACH
    early = early_slots(layers, rows // SUBLANES, n_got)
    late = late_slots(lanes, wide)

    def with_early(core, *keys):
        tile = jnp.concatenate([read_lanes(early_ref, early[key]) for key in keys], axis=0)
        return jnp.concatenate([core, tile], axis=1)

    def near(side, name):
        core = near_part((first_near_ref, second_near_ref), even, lanes, wide, side, name)
        return jnp.concatenate([core, read_lanes(late_ref, late[side, name])], axis=1)

    def near_halo(a, side, distance):
        if wide:
            tile = near(side, ("log" if a == 0 else "source") + ("2" if distance == 2 else "1"))
        elif a == 1:
            return near(side, "row") if distance == 2 else turned(near(side, "strip"), REACH, 0)
        else:
            tile = near(side, "strip")
            if distance == 2:
                return jnp.where(starts, turned(tile, 2, 0), turned(tile, -2, 0))
        return third_halo(tile) if a == 0 and distance > 2 else tile

    def window(a, k):
        block, layer = k // layers - 1, k % layers
        if block == 0:
            core = (log_ref, source_ref)[a][layer]
            core = with_early(core, *(("own", a, layer, i) for i in range(rows // SUBLANES)))
            tiles = tuple(with_early(ref[layer], ("got", g, layer)) for g, ref in enumerate(got_refs))
            halo = tiles[0]
            if wide:
                sides = from_right(iy % 2 == 0, tiles), from_left(iy % 2 == 0, tiles)
                halo = jnp.where(upper, *(sides if a == 0 else sides[::-1]))
            if a == 1:
                halo = turned(halo, REACH, 0)
            return jnp.concatenate([core, halo], axis=0)
        side, pick = (0, from_left) if block < 0 else (1, from_right)
        slot = layer if a == 0 else layers + layer - (1 if block < 0 else 0)
        core = pick(even, (first_ref[slot], second_ref[slot]))
        core = with_early(core, *(("raw", side, slot, i) for i in range(rows // SUBLANES)))
        halo = near_halo(a, side, layers - layer if block < 0 else layer + 1)
        return jnp.concatenate([core, halo], axis=0)

    faces = [2.0] * (count - 1)
    faces[layers - 1] = jnp.where(ix > 0, 2.0, 0.0)
    faces[2 * layers - 1] = jnp.where(ix < nx - 1, 2.0, 0.0)
    shape = (rows + 2 * REACH, lanes + LANES)
    iterate(
        count,
        functools.partial(window, 0),
        functools.partial(window, 1),
        faces,
        numerators(shape, 0, rows, iy, ny, 1.0),
        numerators(shape, 1, lanes, iz, nz, 1.0),
        coef_ref,
        storage_rate,
        scratch,
    )
    p_ref = scratch[-1]
    for x in range(layers):
        fine = p_ref[REACH + x, :rows, :lanes]
        fine_ref[x] = fine
        diff_ref[x] = fine - spread_ref[x]


def fine_level(log_perm, source, got, raw, far, near, early, late, spread, coefficients, peers):
    layers, rows, lanes = log_perm.shape
    window = (layers + 2 * REACH, rows + 2 * REACH, lanes + LANES)
    out = jax.ShapeDtypeStruct(log_perm.shape, jnp.float32)
    return pl.pallas_call(
        functools.partial(fine_kernel, peers, len(far)),
        out_shape=(out, out),
        in_specs=[VMEM] * (4 + len(got)) + [ANY] * len(far) + [VMEM] * 6,
        out_specs=(VMEM, VMEM),
        scratch_shapes=window_scratch(*window),
        compiler_params=pltpu.CompilerParams(vmem_limit_bytes=24 << 20),
        cost_estimate=pl.CostEstimate(flops=20_000_000, bytes_accessed=10_000_000, transcendentals=0),
        name="fine_level",
    )(log_perm, source, *got, *raw[::-1], *far, *near[::-1], early, late, spread, coefficients)


def shards(peers, log_perm, source, low_bound, high_bound):
    nx, ny, nz = peers
    layers, rows, lanes = log_perm.shape
    assert layers == REACH and rows == 2 * SUBLANES and nx > 2 and nz == 2
    own, *rows_sent = prep(log_perm, source, ny)
    if ny == 2:
        got = (permute(rows_sent[0], "gy", ny, [(0, 1)]),)
    else:
        got = swap("gy", ny, rows_sent[1], rows_sent[0])
    for_second = raw_block(log_perm, source, rows_sent[0], True)
    second = permute(for_second, "gx", nx, neighbour_pairs(nx, 1))
    for_first = raw_block(log_perm, source, for_second, False)
    raw = (permute(for_first, "gx", nx, neighbour_pairs(nx, 0)), second)
    far_groups = far_pairs(nx)
    halos, for_far = pack_far(own, got, len(far_groups))
    far = [permute(tiles, "gx", nx, group) for tiles, group in zip(for_far, far_groups)]
    for_first, for_second = pack_near(own, halos, for_far[0], got)
    second = permute(for_second, "gx", nx, neighbour_pairs(nx, 1))
    near = (permute(for_first, "gx", nx, neighbour_pairs(nx, 0)), second)
    pooled, early_sent = landed(for_first, log_perm, source, own, halos, raw, got)
    early = lax.ppermute(early_sent, "gz", [(0, 1), (1, 0)])
    late_sent = late_lanes(early_sent, near, far, lanes, ny > 2)
    late = lax.ppermute(late_sent, "gz", [(0, 1), (1, 0)])
    coefficients = chebyshev_coefficients(low_bound, high_bound, late_sent)
    spread = coarse_level(own, halos, pooled, near, far, early, late, coefficients, peers)
    return fine_level(log_perm, source, got, raw, far, near, early, late, spread, coefficients, peers)


def solution(mesh):
    peers = tuple(mesh.shape[axis] for axis in AXES)
    split = P(("groups", "gx"), "gy", "gz")
    return jax.shard_map(
        functools.partial(shards, peers),
        mesh=mesh,
        in_specs=(split, split, P(), P()),
        out_specs=(split, split),
        check_vma=False,
    )
```

time: 24.1 us -> 22.1 us (0.917)
  waiting for transfers between devices: 6.57 us -> 2.26 us
  Pallas kernels: 4.33 us -> 5.4 us
  starting transfers between devices: 9.55 us -> 10.3 us
  local copies, waits for them, and re-layouts: 1.1 us -> 1.81 us
    ppermute x6, waiting for transfers between devices: 6.57 us -> 2.26 us  [permute(): return lax.ppermute(value, (axis, 'gz'), moves)]
    unnamed x14 -> x8, local copies, waits for them, and re-layouts: 0.07 us -> 1.81 us
    ppermute x6, starting transfers between devices: 8.99 us -> 10.3 us  [permute(): return lax.ppermute(value, (axis, 'gz'), moves)]
    pallas_call x5 -> x10, Pallas kernels: 4.33 us -> 5.4 us  [the longest x1 3.12 us: fine_level(): pl.pallas_call(functools.partial(fine_kernel, peers, len(far)), out_shape...]
    slice x3 -> x0, local copies, waits for them, and re-layouts: 1 us -> none  [the longest x1 0.99 us: shards(): source[:-1]]
    ppermute x2, starting transfers between devices: 0.56 us -> 0.06 us  [the longest x1 0.03 us: shards(): early = lax.ppermute(early_sent, 'gz', [(0, 1), (1, 0)])]
  transfers between devices with their start and end apart: 8 -> 8, of which waited for: 2 -> 3; matrix products, arithmetic and copies ran while one was open for 0% -> 0% of each run, Pallas kernels for 2% -> 6%
where the time goes in v7:
time: 22.1 us; the launch traced here: 21.8 us
  starting transfers between devices  10.3 us (47%)
  Pallas kernels  5.4 us (24%)
  waiting for transfers between devices  2.26 us (10%)
  between operations  2.04 us (9%)
  local copies, waits for them, and re-layouts  1.81 us (8%)
    ppermute x6, starting transfers between devices, permute(): return lax.ppermute(value, (axis, 'gz'), moves)  10.3 us
    pallas_call x1, Pallas kernels, fine_level(): pl.pallas_call(functools.partial(fine_kernel, peers, len(far)), out_shape...  3.12 us
    ppermute x6, waiting for transfers between devices, permute(): return lax.ppermute(value, (axis, 'gz'), moves)  2.26 us
    unnamed x8, local copies, waits for them, and re-layouts  1.81 us
    pallas_call x1, Pallas kernels, coarse_level(): pl.pallas_call(functools.partial(coarse_kernel, peers, len(far)), out_sha...  0.85 us
    pallas_call x1, Pallas kernels, chebyshev_coefficients(): pl.pallas_call(coefficients_kernel, out_shape=jax.ShapeDtypeStruct((1 + 2...  0.61 us
  transfers between devices with their start and end apart: 8, of which 3 were waited for; matrix products, arithmetic and copies ran while one was open for 0% of the time, Pallas kernels for 6%

profile of v7, /device:TPU:0, one launch (start us, length us, event | category | flops | bytes accessed | tf_op | source)
XLA Modules:
  0.0 21.8 jit_solution(8930542691587393743)
XLA Ops:
  0.6 0.0 copy-start
  0.6 0.9 %copy-done = f32[4,16,512]{2,1,0:T(8,128)S(1)} copy-done((f32[4,16,512]{2,1,0:T(8,128)S(1)}, f32[4,16,512]{2,1,0:T(8,128)}, u32[]{:S(2)}) %copy-start) | copy-done | bytes 131096
  1.5 0.0 copy-start.2
  1.5 0.9 %copy-done.2 = f32[4,16,512]{2,1,0:T(8,128)S(1)} copy-done((f32[4,16,512]{2,1,0:T(8,128)S(1)}, f32[4,16,512]{2,1,0:T(8,128)}, u32[]{:S(2)}) %copy-start.2) | copy-done | bytes 131096
  2.4 0.2 prep.1
  2.6 3.0 %collective-permute-start = (f32[5,8,512]{2,1,0:T(8,128)S(1)}, f32[5,8,512]{2,1,0:T(8,128)S(1)}, u32[]{:S(2)}, u32[]{:S(2)}) collective-permute-start(f32[5,8,512]{2,1,0:T(8,128)S(1)} %get-tuple-element.10.after_ref), channel_id=1, source_target_pairs={{0,2},{1,3},{2,0},{3,1},{4,6},{5,7},{6,4},{7,5},{8,10},{9,11},{10,... | collective-permute-start | bytes 245768 | tf_op jit(solution)/shard_map/ppermute | solution.py:44
  5.7 0.1 collective-permute-start.1
  5.8 3.2 %collective-permute-start.2 = (f32[7,16,512]{2,1,0:T(8,128)S(1)}, f32[7,16,512]{2,1,0:T(8,128)S(1)}, u32[]{:S(2)}, u32[]{:S(2)}) collective-permute-start(f32[7,16,512]{2,1,0:T(8,128)S(1)} %raw_block.3), channel_id=1, source_target_pairs={{0,4},{1,5},{4,0},{5,1},{8,12},{9,13},{12,8},{13,9},{2,6},{3,7},{6... | collective-permute-start | bytes 688136 | tf_op jit(solution)/shard_map/ppermute | solution.py:44
  9.0 0.0 collective-permute-done.refs_0_
  9.0 0.2 pack_far.1
  9.2 2.3 %collective-permute-start.3 = (f32[72,128]{1,0:T(8,128)S(1)}, f32[72,128]{1,0:T(8,128)S(1)}, u32[]{:S(2)}, u32[]{:S(2)}) collective-permute-start(f32[72,128]{1,0:T(8,128)S(1)} %get-tuple-element.12.after_ref), channel_id=1, source_target_pairs={{0,8},{1,9},{4,12},{5,13},{8,0},{9,1},{12,4},{13,5},{2,10},{3,11},... | collective-permute-start | bytes 110600 | tf_op jit(solution)/shard_map/ppermute | solution.py:44
  11.4 0.0 copy-start.1
  11.4 0.0 copy-start.3
  11.5 0.1 collective-permute-start.4
  11.5 1.6 %collective-permute-start.5 = (f32[72,128]{1,0:T(8,128)S(1)}, f32[72,128]{1,0:T(8,128)S(1)}, u32[]{:S(2)}, u32[]{:S(2)}) collective-permute-start(f32[72,128]{1,0:T(8,128)S(1)} %get-tuple-element.15.after_ref), channel_id=1, source_target_pairs={{0,4},{1,5},{4,0},{5,1},{8,12},{9,13},{12,8},{13,9},{2,6},{3,7},{6... | collective-permute-start | bytes 110600 | tf_op jit(solution)/shard_map/ppermute | solution.py:44
  13.2 1.2 %collective-permute-done.2.first_ref.refs_2_ = f32[7,16,512]{2,1,0:T(8,128)S(1)} collective-permute-done((f32[7,16,512]{2,1,0:T(8,128)S(1)}, f32[7,16,512]{2,1,0:T(8,128)S(1)}, u32[]{:S(2)}, u32[]{:S(2)}) %collective-permute-start.2) | collective-permute-done | bytes 229408 | tf_op jit(solution)/shard_map/ppermute | solution.py:44
  14.4 0.0 collective-permute-done.1.second_ref.refs_1_
  14.4 0.0 copy-done.1
  14.4 0.0 copy-done.3
  14.4 0.3 %landed.1 = (f32[96,128]{1,0:T(8,128)S(1)}, f32[32,128]{1,0:T(8,128)S(1)}) custom-call(f32[72,128]{1,0:T(8,128)S(1)} %get-tuple-element.15.after_ref, f32[4,16,512]{2,1,0:T(8,128)S(1)} %copy-done.1, f32[4,16,512]{2,1,0:T(8,128)S(1)} %copy-done.3, f32[2,8,512]{2,1,0:T(8,128)S(1)} %get-tuple-element.11.pooled_ref.own_ref, ...), custom_call_target="tpu_custom_call" | custom-call | flops 1000000 | bytes 1000000 | tf_op jit(solution)/shard_map/landed/pallas_call | solution.py:616
  14.7 0.0 collective-permute-start.6
  14.8 0.6 %collective-permute-done.3.refs_0_.refs_3_ = f32[72,128]{1,0:T(8,128)S(1)} collective-permute-done((f32[72,128]{1,0:T(8,128)S(1)}, f32[72,128]{1,0:T(8,128)S(1)}, u32[]{:S(2)}, u32[]{:S(2)}) %collective-permute-start.3) | collective-permute-done | bytes 36896 | tf_op jit(solution)/shard_map/ppermute | solution.py:44
  15.4 0.0 collective-permute-done.4.second_ref.refs_4_
  15.4 0.4 %collective-permute-done.5.first_ref.refs_5_ = f32[72,128]{1,0:T(8,128)S(1)} collective-permute-done((f32[72,128]{1,0:T(8,128)S(1)}, f32[72,128]{1,0:T(8,128)S(1)}, u32[]{:S(2)}, u32[]{:S(2)}) %collective-permute-start.5) | collective-permute-done | bytes 36896 | tf_op jit(solution)/shard_map/ppermute | solution.py:44
  15.8 0.1 late_lanes.1.after_ref
  15.9 0.0 collective-permute-start.7
  17.2 0.6 %coefficients.1.refs_3_.refs_9_ = f32[7,8,128]{2,1,0:T(8,128)S(1)} custom-call(f32[1]{0:T(128)S(6)} %copy.6.low_ref, f32[1]{0:T(128)S(6)} %copy.7.high_ref, f32[8,128]{1,0:T(8,128)S(1)} %late_lanes.1.after_ref), custom_call_target="tpu_custom_call" | custom-call | flops 1000000 | bytes 100000 | tf_op jit(solution)/shard_map/coefficients/pallas_call | solution.py:168
  17.8 0.0 collective-permute-done.7.refs_2_.refs_7_
  17.8 0.0 collective-permute-done.6.refs_1_.refs_6_
  17.8 0.9 %coarse_level.1.refs_8_ = f32[4,16,512]{2,1,0:T(8,128)S(1)} custom-call(f32[2,8,512]{2,1,0:T(8,128)S(1)} %get-tuple-element.11.pooled_ref.own_ref, f32[1,8,512]{2,1,0:T(8,128)S(1)} %get-tuple-element.13.halo_ref, f32[96,128]{1,0:T(8,128)S(1)} %get-tuple-element.17.pool_ref, f32[72,128]{1,0:T(8,128)S(1)} %collective-permute-done.5.first_ref.refs_5_, ...), custom_call_target="tpu_custom_call" | custom-call | flops 20000000 | bytes 4000000 | tf_op jit(solution)/shard_map/coarse_level/pallas_call | solution.py:764
  18.7 3.1 %fine_level.1 = (f32[4,16,512]{2,1,0:T(8,128)}, f32[4,16,512]{2,1,0:T(8,128)}) custom-call(f32[4,16,512]{2,1,0:T(8,128)S(1)} %copy-done.1, f32[4,16,512]{2,1,0:T(8,128)S(1)} %copy-done.3, f32[5,8,512]{2,1,0:T(8,128)S(1)} %collective-permute-done.refs_0_, f32[7,16,512]{2,1,0:T(8,128)S(1)} %collective-permute-done.1.second_ref.refs_1_, ...), custom_call_target="tpu_custom_call" | custom-call | flops 20000000 | bytes 10000000 | tf_op jit(solution)/shard_map/fine_level/pallas_call | solution.py:858
  (3 shorter events, 0.1 us)
Async XLA Ops:
  0.6 0.9 %copy-start = (f32[4,16,512]{2,1,0:T(8,128)S(1)}, f32[4,16,512]{2,1,0:T(8,128)}, u32[]{:S(2)}) copy-start(f32[4,16,512]{2,1,0:T(8,128)} %log_ref.9) | copy-start | bytes 393220
  1.5 0.9 %copy-start.2 = (f32[4,16,512]{2,1,0:T(8,128)S(1)}, f32[4,16,512]{2,1,0:T(8,128)}, u32[]{:S(2)}) copy-start(f32[4,16,512]{2,1,0:T(8,128)} %source_ref.9) | copy-start | bytes 393220
  2.6 6.3 %collective-permute-start = (f32[5,8,512]{2,1,0:T(8,128)S(1)}, f32[5,8,512]{2,1,0:T(8,128)S(1)}, u32[]{:S(2)}, u32[]{:S(2)}) collective-permute-start(f32[5,8,512]{2,1,0:T(8,128)S(1)} %get-tuple-element.10.after_ref), channel_id=1, source_target_pairs={{0,2},{1,3},{2,0},{3,1},{4,6},{5,7},{6,4},{7,5},{8,10},{9,11},{10,... | collective-permute-start | bytes 245768 | tf_op jit(solution)/shard_map/ppermute | solution.py:44
  5.7 8.8 %collective-permute-start.1 = (f32[7,16,512]{2,1,0:T(8,128)S(1)}, f32[7,16,512]{2,1,0:T(8,128)S(1)}, u32[]{:S(2)}, u32[]{:S(2)}) collective-permute-start(f32[7,16,512]{2,1,0:T(8,128)S(1)} %raw_block.2.after_ref), channel_id=1, source_target_pairs={{0,1},{1,0},{4,8},{5,9},{8,4},{9,5},{12,13},{13,12},{2,3},{3,2},{6... | collective-permute-start | bytes 688136 | tf_op jit(solution)/shard_map/ppermute | solution.py:44
  5.8 8.6 %collective-permute-start.2 = (f32[7,16,512]{2,1,0:T(8,128)S(1)}, f32[7,16,512]{2,1,0:T(8,128)S(1)}, u32[]{:S(2)}, u32[]{:S(2)}) collective-permute-start(f32[7,16,512]{2,1,0:T(8,128)S(1)} %raw_block.3), channel_id=1, source_target_pairs={{0,4},{1,5},{4,0},{5,1},{8,12},{9,13},{12,8},{13,9},{2,6},{3,7},{6... | collective-permute-start | bytes 688136 | tf_op jit(solution)/shard_map/ppermute | solution.py:44
  9.2 6.2 %collective-permute-start.3 = (f32[72,128]{1,0:T(8,128)S(1)}, f32[72,128]{1,0:T(8,128)S(1)}, u32[]{:S(2)}, u32[]{:S(2)}) collective-permute-start(f32[72,128]{1,0:T(8,128)S(1)} %get-tuple-element.12.after_ref), channel_id=1, source_target_pairs={{0,8},{1,9},{4,12},{5,13},{8,0},{9,1},{12,4},{13,5},{2,10},{3,11},... | collective-permute-start | bytes 110600 | tf_op jit(solution)/shard_map/ppermute | solution.py:44
  11.4 3.0 %copy-start.1 = (f32[4,16,512]{2,1,0:T(8,128)S(1)}, f32[4,16,512]{2,1,0:T(8,128)}, u32[]{:S(2)}) copy-start(f32[4,16,512]{2,1,0:T(8,128)} %log_ref.9) | copy-start | bytes 393220
  11.4 3.0 %copy-start.3 = (f32[4,16,512]{2,1,0:T(8,128)S(1)}, f32[4,16,512]{2,1,0:T(8,128)}, u32[]{:S(2)}) copy-start(f32[4,16,512]{2,1,0:T(8,128)} %source_ref.9) | copy-start | bytes 393220
  11.5 3.9 %collective-permute-start.4 = (f32[72,128]{1,0:T(8,128)S(1)}, f32[72,128]{1,0:T(8,128)S(1)}, u32[]{:S(2)}, u32[]{:S(2)}) collective-permute-start(f32[72,128]{1,0:T(8,128)S(1)} %get-tuple-element.14), channel_id=1, source_target_pairs={{0,1},{1,0},{4,8},{5,9},{8,4},{9,5},{12,13},{13,12},{2,3},{3,2},{6... | collective-permute-start | bytes 110600 | tf_op jit(solution)/shard_map/ppermute | solution.py:44
  11.5 4.3 %collective-permute-start.5 = (f32[72,128]{1,0:T(8,128)S(1)}, f32[72,128]{1,0:T(8,128)S(1)}, u32[]{:S(2)}, u32[]{:S(2)}) collective-permute-start(f32[72,128]{1,0:T(8,128)S(1)} %get-tuple-element.15.after_ref), channel_id=1, source_target_pairs={{0,4},{1,5},{4,0},{5,1},{8,12},{9,13},{12,8},{13,9},{2,6},{3,7},{6... | collective-permute-start | bytes 110600 | tf_op jit(solution)/shard_map/ppermute | solution.py:44
  14.7 3.1 %collective-permute-start.6 = (f32[32,128]{1,0:T(8,128)S(1)}, f32[32,128]{1,0:T(8,128)S(1)}, u32[]{:S(2)}, u32[]{:S(2)}) collective-permute-start(f32[32,128]{1,0:T(8,128)S(1)} %get-tuple-element.16.after_ref), channel_id=1, source_target_pairs={{0,1},{1,0},{2,3},{3,2},{4,5},{5,4},{6,7},{7,6},{8,9},{9,8},{10,11... | collective-permute-start | bytes 49160 | tf_op jit(solution)/shard_map/ppermute | solution.py:890
  15.9 1.9 %collective-permute-start.7 = (f32[8,128]{1,0:T(8,128)S(1)}, f32[8,128]{1,0:T(8,128)S(1)}, u32[]{:S(2)}, u32[]{:S(2)}) collective-permute-start(f32[8,128]{1,0:T(8,128)S(1)} %late_lanes.1.after_ref), channel_id=1, source_target_pairs={{0,1},{1,0},{2,3},{3,2},{4,5},{5,4},{6,7},{7,6},{8,9},{9,8},{10,11... | collective-permute-start | bytes 12296 | tf_op jit(solution)/shard_map/ppermute | solution.py:892

commit v8 on v7

--- a/solution.py
+++ b/solution.py
@@ -15,6 +15,7 @@
 AXES = ("gx", "gy", "gz")
 VMEM = pl.BlockSpec(memory_space=pltpu.VMEM)
 ANY = pl.BlockSpec(memory_space=pl.ANY)
+HBM = pl.BlockSpec(memory_space=pltpu.HBM)
 
 
 AHEAD = pl.CostEstimate(flops=50_000_000_000, bytes_accessed=1_000_000, transcendentals=0)
@@ -168,7 +169,7 @@
     return pl.pallas_call(
         coefficients_kernel,
         out_shape=jax.ShapeDtypeStruct((1 + 2 * DEGREE, SUBLANES, LANES), jnp.float32),
-        in_specs=[pl.BlockSpec(memory_space=pltpu.HBM)] * 2 + [ANY],
+        in_specs=[HBM] * 2 + [ANY],
         out_specs=VMEM,
         scratch_shapes=[pltpu.SMEM((2, 1), jnp.float32), pltpu.SemaphoreType.DMA((2,))],
         compiler_params=pltpu.CompilerParams(vmem_limit_bytes=4 << 20),
@@ -323,8 +324,14 @@
     return jnp.where(iota(joined.shape, 0) < REACH, turned(joined, -3, 0), turned(joined, 3, 0))
 
 
-def prep_kernel(log_ref, source_ref, pooled_ref, *refs):
+def parts(both_ref):
+    layers = both_ref.shape[0] // 2
+    return both_ref.at[:layers], both_ref.at[layers:]
+
+
+def prep_kernel(both_ref, pooled_ref, *refs):
     *out_refs, sum_ref = refs
+    log_ref, source_ref = parts(both_ref)
     layers, rows, lanes = log_ref.shape
     starts = lax.axis_index("gy") == 0
 
@@ -366,8 +373,8 @@
     )
 
 
-def prep(log_perm, source, ny):
-    layers, rows, lanes = log_perm.shape
+def prep(both, ny):
+    layers, rows, lanes = both.shape[0] // 2, *both.shape[1:]
     outs = 1 if ny == 2 else 2
 
     def tiles(count):
@@ -376,16 +383,17 @@
     return pl.pallas_call(
         prep_kernel,
         out_shape=(tiles(2),) + (tiles(layers + 1),) * outs,
-        in_specs=[VMEM] * 2,
+        in_specs=[VMEM],
         out_specs=(VMEM,) * (1 + outs),
         scratch_shapes=[pltpu.VMEM((lanes // LANES, 2 * SUBLANES, LANES), jnp.float32)],
         compiler_params=pltpu.CompilerParams(vmem_limit_bytes=8 << 20),
         cost_estimate=pl.CostEstimate(flops=5_000_000, bytes_accessed=700_000, transcendentals=0),
         name="prep",
-    )(log_perm, source)
-
-
-def raw_kernel(to_right_if_odd, log_ref, source_ref, after_ref, out_ref):
+    )(both)
+
+
+def raw_kernel(to_right_if_odd, both_ref, after_ref, out_ref):
+    log_ref, source_ref = parts(both_ref)
     layers = log_ref.shape[0]
     odd = lax.axis_index("gx") % 2
     skip = odd if to_right_if_odd else 1 - odd
@@ -395,17 +403,17 @@
         out_ref[layers + layer] = source_ref[layer + skip]
 
 
-def raw_block(log_perm, source, after, to_right_if_odd):
-    layers, rows, lanes = log_perm.shape
+def raw_block(both, after, to_right_if_odd):
+    layers, rows, lanes = both.shape[0] // 2, *both.shape[1:]
     return pl.pallas_call(
         functools.partial(raw_kernel, to_right_if_odd),
         out_shape=jax.ShapeDtypeStruct((2 * layers - 1, rows, lanes), jnp.float32),
-        in_specs=[VMEM, VMEM, ANY],
+        in_specs=[VMEM, ANY],
         out_specs=VMEM,
         compiler_params=pltpu.CompilerParams(vmem_limit_bytes=8 << 20),
         cost_estimate=pl.CostEstimate(flops=1_000_000, bytes_accessed=500_000, transcendentals=0),
         name="raw_block",
-    )(log_perm, source, after)
+    )(both, after)
 
 
 def pack_far_kernel(wide, pooled_ref, *refs):
@@ -564,8 +572,9 @@
     )(pooled, halos, after, *got)
 
 
-def landed_kernel(after_ref, log_ref, source_ref, pooled_ref, halo_ref, first_ref, second_ref, *refs):
+def landed_kernel(after_ref, both_ref, pooled_ref, halo_ref, first_ref, second_ref, *refs):
     *got_refs, out_ref, sent_ref, sum_ref = refs
+    log_ref, source_ref = parts(both_ref)
     layers, rows, lanes = log_ref.shape
     half = lanes // 2
     even = lax.axis_index("gx") % 2 == 0
@@ -610,8 +619,8 @@
     write_lanes(sent_ref, [tuple(end[...] for end in pairs[key]) for key in slots])
 
 
-def landed(after, log_perm, source, pooled, halos, raw, got):
-    layers, rows, lanes = log_perm.shape
+def landed(after, both, pooled, halos, raw, got):
+    layers, rows, lanes = both.shape[0] // 2, *both.shape[1:]
     slots = early_slots(layers, rows // SUBLANES, len(got))
     return pl.pallas_call(
         landed_kernel,
@@ -619,13 +628,13 @@
             jax.ShapeDtypeStruct((6 * (lanes // 2 // LANES) * SUBLANES, LANES), jnp.float32),
             packed_rows(slots),
         ),
-        in_specs=[ANY] + [VMEM] * (6 + len(got)),
+        in_specs=[ANY] + [VMEM] * (5 + len(got)),
         out_specs=(VMEM,) * 2,
         scratch_shapes=[pltpu.VMEM((lanes // LANES, 2 * SUBLANES, LANES), jnp.float32)],
         compiler_params=pltpu.CompilerParams(vmem_limit_bytes=16 << 20),
         cost_estimate=pl.CostEstimate(flops=1_000_000, bytes_accessed=1_000_000, transcendentals=0),
         name="landed",
-    )(after, log_perm, source, pooled, halos, *raw, *got)
+    )(after, both, pooled, halos, *raw, *got)
 
 
 def near_part(refs, even, lanes, wide, side, name):
@@ -774,7 +783,8 @@
     )(own, halos, pooled, *near, *far, early, late, coefficients)
 
 
-def fine_kernel(peers, n_far, log_ref, source_ref, *refs):
+def fine_kernel(peers, n_far, both_ref, *refs):
+    log_ref, source_ref = parts(both_ref)
     layers, rows, lanes = log_ref.shape
     ix, iy, iz = (lax.axis_index(axis) for axis in AXES)
     nx, ny, nz = peers
@@ -851,34 +861,35 @@
         diff_ref[x] = fine - spread_ref[x]
 
 
-def fine_level(log_perm, source, got, raw, far, near, early, late, spread, coefficients, peers):
-    layers, rows, lanes = log_perm.shape
+def fine_level(both, got, raw, far, near, early, late, spread, coefficients, peers):
+    layers, rows, lanes = spread.shape
     window = (layers + 2 * REACH, rows + 2 * REACH, lanes + LANES)
-    out = jax.ShapeDtypeStruct(log_perm.shape, jnp.float32)
+    out = jax.ShapeDtypeStruct(spread.shape, jnp.float32)
     return pl.pallas_call(
         functools.partial(fine_kernel, peers, len(far)),
         out_shape=(out, out),
-        in_specs=[VMEM] * (4 + len(got)) + [ANY] * len(far) + [VMEM] * 6,
+        in_specs=[VMEM] * (3 + len(got)) + [ANY] * len(far) + [VMEM] * 6,
         out_specs=(VMEM, VMEM),
         scratch_shapes=window_scratch(*window),
         compiler_params=pltpu.CompilerParams(vmem_limit_bytes=24 << 20),
         cost_estimate=pl.CostEstimate(flops=20_000_000, bytes_accessed=10_000_000, transcendentals=0),
         name="fine_level",
-    )(log_perm, source, *got, *raw[::-1], *far, *near[::-1], early, late, spread, coefficients)
+    )(both, *got, *raw[::-1], *far, *near[::-1], early, late, spread, coefficients)
 
 
 def shards(peers, log_perm, source, low_bound, high_bound):
     nx, ny, nz = peers
     layers, rows, lanes = log_perm.shape
     assert layers == REACH and rows == 2 * SUBLANES and nx > 2 and nz == 2
-    own, *rows_sent = prep(log_perm, source, ny)
+    both = jnp.concatenate([log_perm, source])
+    own, *rows_sent = prep(both, ny)
     if ny == 2:
         got = (permute(rows_sent[0], "gy", ny, [(0, 1)]),)
     else:
         got = swap("gy", ny, rows_sent[1], rows_sent[0])
-    for_second = raw_block(log_perm, source, rows_sent[0], True)
+    for_second = raw_block(both, rows_sent[0], True)
     second = permute(for_second, "gx", nx, neighbour_pairs(nx, 1))
-    for_first = raw_block(log_perm, source, for_second, False)
+    for_first = raw_block(both, for_second, False)
     raw = (permute(for_first, "gx", nx, neighbour_pairs(nx, 0)), second)
     far_groups = far_pairs(nx)
     halos, for_far = pack_far(own, got, len(far_groups))
@@ -886,13 +897,13 @@
     for_first, for_second = pack_near(own, halos, for_far[0], got)
     second = permute(for_second, "gx", nx, neighbour_pairs(nx, 1))
     near = (permute(for_first, "gx", nx, neighbour_pairs(nx, 0)), second)
-    pooled, early_sent = landed(for_first, log_perm, source, own, halos, raw, got)
+    coefficients = chebyshev_coefficients(low_bound, high_bound, for_first)
+    pooled, early_sent = landed(coefficients, both, own, halos, raw, got)
     early = lax.ppermute(early_sent, "gz", [(0, 1), (1, 0)])
     late_sent = late_lanes(early_sent, near, far, lanes, ny > 2)
     late = lax.ppermute(late_sent, "gz", [(0, 1), (1, 0)])
-    coefficients = chebyshev_coefficients(low_bound, high_bound, late_sent)
     spread = coarse_level(own, halos, pooled, near, far, early, late, coefficients, peers)
-    return fine_level(log_perm, source, got, raw, far, near, early, late, spread, coefficients, peers)
+    return fine_level(both, got, raw, far, near, early, late, spread, coefficients, peers)
 
 
 def solution(mesh):

time: 22.1 us -> 20.4 us (0.923)
  waiting for transfers between devices: 2.26 us -> 1.3 us
  local copies, waits for them, and re-layouts: 1.81 us -> 0.97 us
    ppermute x6, waiting for transfers between devices: 2.26 us -> 0.32 us  [permute(): return lax.ppermute(value, (axis, 'gz'), moves)]
    ppermute x1, waiting for transfers between devices: 0.01 us -> 0.98 us  [shards(): late = lax.ppermute(late_sent, 'gz', [(0, 1), (1, 0)])]
    unnamed x8 -> x3, local copies, waits for them, and re-layouts: 1.81 us -> 0.96 us
  transfers between devices with their start and end apart: 8 -> 8, of which waited for: 3 -> 2; matrix products, arithmetic and copies ran while one was open for 0% -> 0% of each run, Pallas kernels for 6% -> 6%
where the time goes in v8:
time: 20.4 us; the launch traced here: 20.2 us
  starting transfers between devices  10.5 us (51%)
  Pallas kernels  5.41 us (27%)
  between operations  2.06 us (10%)
  waiting for transfers between devices  1.3 us (6%)
  local copies, waits for them, and re-layouts  0.97 us (5%)
    ppermute x6, starting transfers between devices, permute(): return lax.ppermute(value, (axis, 'gz'), moves)  10.3 us
    pallas_call x1, Pallas kernels, fine_level(): pl.pallas_call(functools.partial(fine_kernel, peers, len(far)), out_shape...  3.13 us
    ppermute x1, waiting for transfers between devices, shards(): late = lax.ppermute(late_sent, 'gz', [(0, 1), (1, 0)])  0.98 us
    unnamed x3, local copies, waits for them, and re-layouts  0.96 us
    pallas_call x1, Pallas kernels, coarse_level(): pl.pallas_call(functools.partial(coarse_kernel, peers, len(far)), out_sha...  0.85 us
    pallas_call x1, Pallas kernels, chebyshev_coefficients(): pl.pallas_call(coefficients_kernel, out_shape=jax.ShapeDtypeStruct((1 + 2...  0.61 us
  transfers between devices with their start and end apart: 8, of which 2 were waited for; matrix products, arithmetic and copies ran while one was open for 0% of the time, Pallas kernels for 6%

profile of v8, /device:TPU:0, one launch (start us, length us, event | category | flops | bytes accessed | tf_op | source)
XLA Modules:
  0.0 20.2 jit_solution(15964648324415893586)
XLA Ops:
  0.6 0.0 copy-start
  0.6 0.9 %constant_dynamic-update-slice_fusion.1 = f32[8,16,512]{2,1,0:T(8,128)S(1)} fusion(f32[4,16,512]{2,1,0:T(8,128)} %param.4), kind=kLoop, calls=%fused_computation.1 | loop fusion | bytes 262144
  1.6 0.0 copy-done
  1.6 0.2 prep.1
  1.8 3.0 %collective-permute-start = (f32[5,8,512]{2,1,0:T(8,128)S(1)}, f32[5,8,512]{2,1,0:T(8,128)S(1)}, u32[]{:S(2)}, u32[]{:S(2)}) collective-permute-start(f32[5,8,512]{2,1,0:T(8,128)S(1)} %get-tuple-element.10.after_ref), channel_id=1, source_target_pairs={{0,2},{1,3},{2,0},{3,1},{4,6},{5,7},{6,4},{7,5},{8,10},{9,11},{10,... | collective-permute-start | bytes 245768 | tf_op jit(solution)/shard_map/ppermute | solution.py:45
  4.9 0.1 collective-permute-start.1
  5.0 3.2 %collective-permute-start.2 = (f32[7,16,512]{2,1,0:T(8,128)S(1)}, f32[7,16,512]{2,1,0:T(8,128)S(1)}, u32[]{:S(2)}, u32[]{:S(2)}) collective-permute-start(f32[7,16,512]{2,1,0:T(8,128)S(1)} %raw_block.3), channel_id=1, source_target_pairs={{0,4},{1,5},{4,0},{5,1},{8,12},{9,13},{12,8},{13,9},{2,6},{3,7},{6... | collective-permute-start | bytes 688136 | tf_op jit(solution)/shard_map/ppermute | solution.py:45
  8.2 0.0 collective-permute-done.refs_0_
  8.2 0.2 pack_far.1
  8.3 2.3 %collective-permute-start.3 = (f32[72,128]{1,0:T(8,128)S(1)}, f32[72,128]{1,0:T(8,128)S(1)}, u32[]{:S(2)}, u32[]{:S(2)}) collective-permute-start(f32[72,128]{1,0:T(8,128)S(1)} %get-tuple-element.12.after_ref), channel_id=1, source_target_pairs={{0,8},{1,9},{4,12},{5,13},{8,0},{9,1},{12,4},{13,5},{2,10},{3,11},... | collective-permute-start | bytes 110600 | tf_op jit(solution)/shard_map/ppermute | solution.py:45
  10.6 0.1 collective-permute-start.4
  10.7 1.6 %collective-permute-start.5 = (f32[72,128]{1,0:T(8,128)S(1)}, f32[72,128]{1,0:T(8,128)S(1)}, u32[]{:S(2)}, u32[]{:S(2)}) collective-permute-start(f32[72,128]{1,0:T(8,128)S(1)} %get-tuple-element.15.after_ref), channel_id=1, source_target_pairs={{0,4},{1,5},{4,0},{5,1},{8,12},{9,13},{12,8},{13,9},{2,6},{3,7},{6... | collective-permute-start | bytes 110600 | tf_op jit(solution)/shard_map/ppermute | solution.py:45
  13.7 0.6 %coefficients.1.after_ref.refs_3_.refs_9_ = f32[7,8,128]{2,1,0:T(8,128)S(1)} custom-call(f32[1]{0:T(128)S(6)} %copy.7.low_ref, f32[1]{0:T(128)S(6)} %copy.8.high_ref, f32[72,128]{1,0:T(8,128)S(1)} %get-tuple-element.15.after_ref), custom_call_target="tpu_custom_call" | custom-call | flops 1000000 | bytes 100000 | tf_op jit(solution)/shard_map/coefficients/pallas_call | solution.py:169
  14.3 0.0 collective-permute-done.2.first_ref.refs_2_
  14.3 0.0 collective-permute-done.1.second_ref.refs_1_
  14.3 0.3 %landed.1 = (f32[96,128]{1,0:T(8,128)S(1)}, f32[32,128]{1,0:T(8,128)S(1)}) custom-call(f32[7,8,128]{2,1,0:T(8,128)S(1)} %coefficients.1.after_ref.refs_3_.refs_9_, f32[8,16,512]{2,1,0:T(8,128)S(1)} %constant_dynamic-update-slice_fusion.both_ref, f32[2,8,512]{2,1,0:T(8,128)S(1)} %get-tuple-element.11.pooled_ref.own_ref, ...), custom_call_target="tpu_custom_call" | custom-call | flops 1000000 | bytes 1000000 | tf_op jit(solution)/shard_map/landed/pallas_call | solution.py:625
  14.6 0.0 collective-permute-start.6
  14.6 0.0 collective-permute-done.3.refs_0_.refs_3_
  14.7 0.0 collective-permute-done.4.second_ref.refs_4_
  14.7 0.3 %collective-permute-done.5.first_ref.refs_5_ = f32[72,128]{1,0:T(8,128)S(1)} collective-permute-done((f32[72,128]{1,0:T(8,128)S(1)}, f32[72,128]{1,0:T(8,128)S(1)}, u32[]{:S(2)}, u32[]{:S(2)}) %collective-permute-start.5) | collective-permute-done | bytes 36896 | tf_op jit(solution)/shard_map/ppermute | solution.py:45
  15.0 0.1 late_lanes.1
  15.1 0.2 %collective-permute-start.7 = (f32[8,128]{1,0:T(8,128)S(1)}, f32[8,128]{1,0:T(8,128)S(1)}, u32[]{:S(2)}, u32[]{:S(2)}) collective-permute-start(f32[8,128]{1,0:T(8,128)S(1)} %late_lanes.1), channel_id=1, source_target_pairs={{0,1},{1,0},{2,3},{3,2},{4,5},{5,4},{6,7},{7,6},{8,9},{9,8},{10,11... | collective-permute-start | bytes 12296 | tf_op jit(solution)/shard_map/ppermute | solution.py:904
  15.3 1.0 %collective-permute-done.7.refs_2_.refs_7_ = f32[8,128]{1,0:T(8,128)S(1)} collective-permute-done((f32[8,128]{1,0:T(8,128)S(1)}, f32[8,128]{1,0:T(8,128)S(1)}, u32[]{:S(2)}, u32[]{:S(2)}) %collective-permute-start.7) | collective-permute-done | bytes 4128 | tf_op jit(solution)/shard_map/ppermute | solution.py:904
  16.2 0.0 collective-permute-done.6.refs_1_.refs_6_
  16.2 0.9 %coarse_level.1.refs_8_ = f32[4,16,512]{2,1,0:T(8,128)S(1)} custom-call(f32[2,8,512]{2,1,0:T(8,128)S(1)} %get-tuple-element.11.pooled_ref.own_ref, f32[1,8,512]{2,1,0:T(8,128)S(1)} %get-tuple-element.13.halo_ref, f32[96,128]{1,0:T(8,128)S(1)} %get-tuple-element.17.pool_ref, f32[72,128]{1,0:T(8,128)S(1)} %collective-permute-done.5.first_ref.refs_5_, ...), custom_call_target="tpu_custom_call" | custom-call | flops 20000000 | bytes 4000000 | tf_op jit(solution)/shard_map/coarse_level/pallas_call | solution.py:773
  17.1 3.1 %fine_level.1 = (f32[4,16,512]{2,1,0:T(8,128)}, f32[4,16,512]{2,1,0:T(8,128)}) custom-call(f32[8,16,512]{2,1,0:T(8,128)S(1)} %constant_dynamic-update-slice_fusion.both_ref, f32[5,8,512]{2,1,0:T(8,128)S(1)} %collective-permute-done.refs_0_, f32[7,16,512]{2,1,0:T(8,128)S(1)} %collective-permute-done.1.second_ref.refs_1_, ...), custom_call_target="tpu_custom_call" | custom-call | flops 20000000 | bytes 10000000 | tf_op jit(solution)/shard_map/fine_level/pallas_call | solution.py:868
  (4 shorter events, 0.1 us)
Async XLA Ops:
  0.6 1.0 %copy-start = (f32[4,16,512]{2,1,0:T(8,128)S(1)}, f32[4,16,512]{2,1,0:T(8,128)}, u32[]{:S(2)}) copy-start(f32[4,16,512]{2,1,0:T(8,128)} %param.5) | copy-start | bytes 393220
  1.8 6.3 %collective-permute-start = (f32[5,8,512]{2,1,0:T(8,128)S(1)}, f32[5,8,512]{2,1,0:T(8,128)S(1)}, u32[]{:S(2)}, u32[]{:S(2)}) collective-permute-start(f32[5,8,512]{2,1,0:T(8,128)S(1)} %get-tuple-element.10.after_ref), channel_id=1, source_target_pairs={{0,2},{1,3},{2,0},{3,1},{4,6},{5,7},{6,4},{7,5},{8,10},{9,11},{10,... | collective-permute-start | bytes 245768 | tf_op jit(solution)/shard_map/ppermute | solution.py:45
  4.9 9.4 %collective-permute-start.1 = (f32[7,16,512]{2,1,0:T(8,128)S(1)}, f32[7,16,512]{2,1,0:T(8,128)S(1)}, u32[]{:S(2)}, u32[]{:S(2)}) collective-permute-start(f32[7,16,512]{2,1,0:T(8,128)S(1)} %raw_block.2.after_ref), channel_id=1, source_target_pairs={{0,1},{1,0},{4,8},{5,9},{8,4},{9,5},{12,13},{13,12},{2,3},{3,2},{6... | collective-permute-start | bytes 688136 | tf_op jit(solution)/shard_map/ppermute | solution.py:45
  5.0 9.3 %collective-permute-start.2 = (f32[7,16,512]{2,1,0:T(8,128)S(1)}, f32[7,16,512]{2,1,0:T(8,128)S(1)}, u32[]{:S(2)}, u32[]{:S(2)}) collective-permute-start(f32[7,16,512]{2,1,0:T(8,128)S(1)} %raw_block.3), channel_id=1, source_target_pairs={{0,4},{1,5},{4,0},{5,1},{8,12},{9,13},{12,8},{13,9},{2,6},{3,7},{6... | collective-permute-start | bytes 688136 | tf_op jit(solution)/shard_map/ppermute | solution.py:45
  8.3 6.3 %collective-permute-start.3 = (f32[72,128]{1,0:T(8,128)S(1)}, f32[72,128]{1,0:T(8,128)S(1)}, u32[]{:S(2)}, u32[]{:S(2)}) collective-permute-start(f32[72,128]{1,0:T(8,128)S(1)} %get-tuple-element.12.after_ref), channel_id=1, source_target_pairs={{0,8},{1,9},{4,12},{5,13},{8,0},{9,1},{12,4},{13,5},{2,10},{3,11},... | collective-permute-start | bytes 110600 | tf_op jit(solution)/shard_map/ppermute | solution.py:45
  10.6 4.0 %collective-permute-start.4 = (f32[72,128]{1,0:T(8,128)S(1)}, f32[72,128]{1,0:T(8,128)S(1)}, u32[]{:S(2)}, u32[]{:S(2)}) collective-permute-start(f32[72,128]{1,0:T(8,128)S(1)} %get-tuple-element.14), channel_id=1, source_target_pairs={{0,1},{1,0},{4,8},{5,9},{8,4},{9,5},{12,13},{13,12},{2,3},{3,2},{6... | collective-permute-start | bytes 110600 | tf_op jit(solution)/shard_map/ppermute | solution.py:45
  10.7 4.3 %collective-permute-start.5 = (f32[72,128]{1,0:T(8,128)S(1)}, f32[72,128]{1,0:T(8,128)S(1)}, u32[]{:S(2)}, u32[]{:S(2)}) collective-permute-start(f32[72,128]{1,0:T(8,128)S(1)} %get-tuple-element.15.after_ref), channel_id=1, source_target_pairs={{0,4},{1,5},{4,0},{5,1},{8,12},{9,13},{12,8},{13,9},{2,6},{3,7},{6... | collective-permute-start | bytes 110600 | tf_op jit(solution)/shard_map/ppermute | solution.py:45
  14.6 1.6 %collective-permute-start.6 = (f32[32,128]{1,0:T(8,128)S(1)}, f32[32,128]{1,0:T(8,128)S(1)}, u32[]{:S(2)}, u32[]{:S(2)}) collective-permute-start(f32[32,128]{1,0:T(8,128)S(1)} %get-tuple-element.16.after_ref), channel_id=1, source_target_pairs={{0,1},{1,0},{2,3},{3,2},{4,5},{5,4},{6,7},{7,6},{8,9},{9,8},{10,11... | collective-permute-start | bytes 49160 | tf_op jit(solution)/shard_map/ppermute | solution.py:902
  15.1 1.2 %collective-permute-start.7 = (f32[8,128]{1,0:T(8,128)S(1)}, f32[8,128]{1,0:T(8,128)S(1)}, u32[]{:S(2)}, u32[]{:S(2)}) collective-permute-start(f32[8,128]{1,0:T(8,128)S(1)} %late_lanes.1), channel_id=1, source_target_pairs={{0,1},{1,0},{2,3},{3,2},{4,5},{5,4},{6,7},{7,6},{8,9},{9,8},{10,11... | collective-permute-start | bytes 12296 | tf_op jit(solution)/shard_map/ppermute | solution.py:904

commit v9 on v8

--- a/solution.py
+++ b/solution.py
@@ -83,66 +83,131 @@
     return guess * (2.0 - value * guess)
 
 
-def numerators(shape, dim, own, index, peers, face_scale):
-    place = iota(shape, dim)
+def row_numerators(rows, own, index, peers, face_scale):
+    place = iota((rows, LANES), 0)
     right = jnp.where(index < peers - 1, 2.0 * face_scale, 0.0)
     left = jnp.where(index > 0, 2.0 * face_scale, 0.0)
-    return jnp.where(
-        place == own - 1, right, jnp.where(place == shape[dim] - 1, left, 2.0 * face_scale)
-    )
-
-
-def iterate(count, log_at, source_at, x_faces, y_top, z_top, coef_ref, storage, refs):
-    tx_ref, ty_ref, tz_ref, w_ref, d_ref, r_ref, p_ref = refs
-    rows, lanes = y_top.shape
-
-    def coefficient(i):
-        return jnp.concatenate(
-            [jnp.concatenate([coef_ref[i]] * (lanes // LANES), axis=1)] * (rows // SUBLANES), axis=0
-        )
-
-    over_theta = coefficient(0)
-    after = jnp.exp(-log_at(0))
+    return jnp.where(place == own - 1, right, jnp.where(place == rows - 1, left, 2.0 * face_scale))
+
+
+def lane_numerators(rows, index, peers, face_scale):
+    place = iota((rows, LANES), 1)
+    right = jnp.where(index < peers - 1, 2.0 * face_scale, 0.0)
+    left = jnp.where(index > 0, 2.0 * face_scale, 0.0)
+    return [jnp.where(place == LANES - 1, side, 2.0 * face_scale) for side in (right, left)]
+
+
+def lane_tiles(value):
+    return [value[:, i : i + LANES] for i in range(0, value.shape[1], LANES)]
+
+
+def beside(tiles, shift):
+    moved = [turned(tile, shift, 1) for tile in tiles]
+    lane = iota(tiles[0].shape, 1)
+    seam = LANES - 1 if shift < 0 else 0
+    return [
+        jnp.where(lane == seam, moved[(j - shift) % len(tiles)], moved[j]) for j in range(len(tiles))
+    ]
+
+
+def store_rows(ref, k, j, value):
+    rows = value.shape[0]
+    ref[k, j, SUBLANES : SUBLANES + rows] = value
+    ref[k, j, SUBLANES - 1 : SUBLANES] = value[rows - 1 :]
+    ref[k, j, SUBLANES + rows : SUBLANES + rows + 1] = value[:1]
+
+
+def iterate(count, own_rows, rows, tiles, log_at, source_at, x_faces, y_top, z_top, coef_ref, storage, emit, refs):
+    k_ref, tx_ref, ty_ref, tzr_ref, tzl_ref, diag_ref, w_ref, d_ref, r_ref, p_ref = refs
+    own_tiles = tiles - 1
+
+    def away(k):
+        return max(0, REACH - k, k - (count - 1 - REACH))
+
+    def extent(k, step):
+        left = DEGREE - step - away(k)
+        return None if left < 0 else (own_rows, own_tiles) if left == 0 else (rows, tiles)
+
+    def coefficient(i, size):
+        return jnp.concatenate([coef_ref[i]] * (size // SUBLANES), axis=0)
+
+    z_tops = [z_top[0] if j == own_tiles - 1 else z_top[1] if j == own_tiles else None for j in range(tiles)]
+
+    def resistance(k):
+        return [jnp.exp(-tile) for tile in lane_tiles(log_at(k))]
+
+    after = resistance(0)
     tx_before = None
     for k in range(count):
         here = after
         if k + 1 < count:
-            after = jnp.exp(-log_at(k + 1))
-            tx = x_faces[k] * inverse(here + after)
-            tx_ref[k] = tx
-        if 1 <= k <= count - 2:
-            ty = y_top * inverse(here + turned(here, -1, 0))
-            tz = z_top * inverse(here + turned(here, -1, 1))
-            diagonal = storage + (tx_before + tx) + (ty + turned(ty, 1, 0)) + (tz + turned(tz, 1, 1))
-            w = inverse(diagonal)
-            source = source_at(k)
-            d_ref[k] = source * (over_theta * w)
-            if 2 <= k <= count - 3:
-                ty_ref[k] = ty
-                tz_ref[k] = tz
-                w_ref[k] = w
-                r_ref[k] = source
+            after = resistance(k + 1)
+            outer = max(away(k), away(k + 1))
+            size, number = (rows, tiles) if outer < REACH else (own_rows, own_tiles)
+            tx = [x_faces[k] * inverse(here[j][:size] + after[j][:size]) for j in range(number)]
+            for j in range(number):
+                tx_ref[k, j, :size] = tx[j]
+        if away(k) <= DEGREE:
+            size, number = extent(k, 0)
+            right = beside(here, -1)
+            tz = []
+            for j in range(tiles):
+                scale = z_tops[j][:size] if z_tops[j] is not None else z_top[2]
+                tz.append(scale * inverse(here[j][:size] + right[j][:size]))
+            tz_left = beside(tz, 1)
+            source = lane_tiles(source_at(k))
+            for j in range(number):
+                store_rows(k_ref, k, j, here[j])
+                ty = y_top * inverse(here[j] + k_ref[k, j, SUBLANES + 1 : SUBLANES + 1 + rows])
+                store_rows(ty_ref, k, j, ty)
+                ty_before = ty_ref[k, j, SUBLANES - 1 : SUBLANES - 1 + size]
+                diagonal = storage + (tx_before[j][:size] + tx[j][:size])
+                diagonal = diagonal + (ty[:size] + ty_before) + (tz[j] + tz_left[j])
+                w = inverse(diagonal)
+                direction = source[j][:size] * (coefficient(0, size) * w)
+                if (size, number) == (rows, tiles):
+                    store_rows(d_ref.at[0], k, j, direction)
+                else:
+                    d_ref[0, k, j, SUBLANES : SUBLANES + size] = direction
+                if extent(k, 1) is not None:
+                    tzr_ref[k, j, :size] = tz[j]
+                    tzl_ref[k, j, :size] = tz_left[j]
+                    diag_ref[k, j, :size] = diagonal
+                    w_ref[k, j, :size] = w
+                    r_ref[k, j, :size] = source[j][:size]
         tx_before = tx
-    for step in range(DEGREE):
-        first, last = 2 + step, count - 2 - step
-        keep, gain = coefficient(1 + 2 * step), coefficient(2 + 2 * step)
-        here = d_ref[first]
-        fx_before = tx_ref[first - 1] * (d_ref[first - 1] - here)
-        for k in range(first, last):
-            after = d_ref[k + 1]
-            fx = tx_ref[k] * (here - after)
-            fy = ty_ref[k] * (here - turned(here, -1, 0))
-            fz = tz_ref[k] * (here - turned(here, -1, 1))
-            applied = storage * here + (fx - fx_before) + (fy - turned(fy, 1, 0)) + (fz - turned(fz, 1, 1))
-            residual = r_ref[k] - applied
-            fresh = keep * here + gain * (residual * w_ref[k])
-            if REACH <= k < count - REACH:
-                so_far = here if step == 0 else p_ref[k]
-                p_ref[k] = so_far + fresh
-            if step < DEGREE - 1:
-                r_ref[k] = residual
-                d_ref[k] = fresh
-            here, fx_before = after, fx
+    for step in range(1, DEGREE + 1):
+        old, new = d_ref.at[(step - 1) % 2], d_ref.at[step % 2]
+        for k in range(count):
+            if extent(k, step) is None:
+                continue
+            size, number = extent(k, step)
+            middle = slice(SUBLANES, SUBLANES + size)
+            keep, gain = coefficient(2 * step - 1, size), coefficient(2 * step, size)
+            here = [old[k, j, middle] for j in range(tiles)]
+            right, left = beside(here, -1), beside(here, 1)
+            for j in range(number):
+                applied = tx_ref[k, j, :size] * old[k + 1, j, middle] + tx_ref[k - 1, j, :size] * old[k - 1, j, middle]
+                applied += (
+                    ty_ref[k, j, middle] * old[k, j, SUBLANES + 1 : SUBLANES + 1 + size]
+                    + ty_ref[k, j, SUBLANES - 1 : SUBLANES - 1 + size] * old[k, j, SUBLANES - 1 : SUBLANES - 1 + size]
+                )
+                applied += tzr_ref[k, j, :size] * right[j] + tzl_ref[k, j, :size] * left[j]
+                residual = r_ref[k, j, :size] - (diag_ref[k, j, :size] * here[j] - applied)
+                fresh = keep * here[j] + gain * (residual * w_ref[k, j, :size])
+                if away(k) == 0 and j < own_tiles:
+                    so_far = here[j][:own_rows] if step == 1 else p_ref[k, j]
+                    total = so_far + fresh[:own_rows]
+                    if step == DEGREE:
+                        emit(k - REACH, j, total)
+                    else:
+                        p_ref[k, j] = total
+                if step < DEGREE:
+                    r_ref[k, j, :size] = residual
+                    if (size, number) == (rows, tiles):
+                        store_rows(new, k, j, fresh)
+                    else:
+                        new[k, j, middle] = fresh
 
 
 def coefficients_kernel(low_ref, high_ref, after_ref, coef_ref, bounds_ref, sems):
@@ -260,8 +325,12 @@
     return jax.ShapeDtypeStruct((-(-len(slots) // each) * SUBLANES, LANES), jnp.float32)
 
 
-def window_scratch(count, rows, lanes):
-    return [pltpu.VMEM((count, rows, lanes), jnp.float32)] * 7
+def window_scratch(count, own_rows, rows, tiles):
+    plain = pltpu.VMEM((count, tiles, rows, LANES), jnp.float32)
+    margins = pltpu.VMEM((count, tiles, rows + 2 * SUBLANES, LANES), jnp.float32)
+    pair = pltpu.VMEM((2, count, tiles, rows + 2 * SUBLANES, LANES), jnp.float32)
+    total = pltpu.VMEM((count, tiles, own_rows, LANES), jnp.float32)
+    return [margins, plain, margins, plain, plain, plain, plain, pair, plain, total]
 
 
 def exact_dot(value, zero_one):
@@ -742,22 +811,28 @@
     faces = [4.0] * 9
     faces[1], faces[3] = open_face(ix > 1), open_face(ix > 0)
     faces[5], faces[7] = open_face(ix < nx - 1), open_face(ix < nx - 2)
-    shape = (2 * rows, lanes + LANES)
+    *scratch, p_ref = scratch
+
+    def emit(layer, tile, value):
+        p_ref[layer * rows : (layer + 1) * rows, tile * LANES : (tile + 1) * LANES] = value
+
     iterate(
         2 + 2 * REACH,
+        rows,
+        2 * rows,
+        lanes // LANES + 1,
         functools.partial(window, 0),
         functools.partial(window, 1),
         faces,
-        numerators(shape, 0, rows, iy, ny, 2.0),
-        numerators(shape, 1, lanes, iz, nz, 2.0),
+        row_numerators(2 * rows, rows, iy, ny, 2.0),
+        lane_numerators(2 * rows, iz, nz, 2.0) + [4.0],
         coef_ref,
         8.0 * storage_rate,
+        emit,
         scratch,
     )
-    p_ref = scratch[-1]
     widen = (iota((lanes, 2 * lanes), 0) == iota((lanes, 2 * lanes), 1) // 2).astype(jnp.bfloat16)
-    pressure = jnp.concatenate([p_ref[REACH + x, :rows, :lanes] for x in range(2)], axis=0)
-    spread = exact_dot(pressure, widen)
+    spread = exact_dot(p_ref[...], widen)
     for x in range(2):
         for tile in range(2 * lanes // LANES):
             part = slice(tile * LANES, (tile + 1) * LANES)
@@ -769,14 +844,15 @@
 
 def coarse_level(own, halos, pooled, near, far, early, late, coefficients, peers):
     lanes = own.shape[2] // 2
-    window = (2 + 2 * REACH, 2 * SUBLANES, lanes + LANES)
+    window = (2 + 2 * REACH, SUBLANES, 2 * SUBLANES, lanes // LANES + 1)
     return pl.pallas_call(
         functools.partial(coarse_kernel, peers, len(far)),
         out_shape=jax.ShapeDtypeStruct((REACH, 2 * SUBLANES, 2 * lanes), jnp.float32),
         in_specs=[VMEM] * (8 + len(far)),
         out_specs=VMEM,
         scratch_shapes=[pltpu.VMEM((2 * lanes // LANES, 2 * SUBLANES, LANES), jnp.float32)]
-        + window_scratch(*window),
+        + window_scratch(*window)
+        + [pltpu.VMEM((2 * SUBLANES, lanes), jnp.float32)],
         compiler_params=pltpu.CompilerParams(vmem_limit_bytes=24 << 20),
         cost_estimate=pl.CostEstimate(flops=20_000_000, bytes_accessed=4_000_000, transcendentals=0),
         name="coarse_level",
@@ -842,28 +918,32 @@
     faces = [2.0] * (count - 1)
     faces[layers - 1] = jnp.where(ix > 0, 2.0, 0.0)
     faces[2 * layers - 1] = jnp.where(ix < nx - 1, 2.0, 0.0)
-    shape = (rows + 2 * REACH, lanes + LANES)
+
+    def emit(layer, tile, value):
+        part = slice(tile * LANES, (tile + 1) * LANES)
+        fine_ref[layer, :, part] = value
+        diff_ref[layer, :, part] = value - spread_ref[layer, :, part]
+
     iterate(
         count,
+        rows,
+        rows + 2 * REACH,
+        lanes // LANES + 1,
         functools.partial(window, 0),
         functools.partial(window, 1),
         faces,
-        numerators(shape, 0, rows, iy, ny, 1.0),
-        numerators(shape, 1, lanes, iz, nz, 1.0),
+        row_numerators(rows + 2 * REACH, rows, iy, ny, 1.0),
+        lane_numerators(rows + 2 * REACH, iz, nz, 1.0) + [2.0],
         coef_ref,
         storage_rate,
+        emit,
         scratch,
     )
-    p_ref = scratch[-1]
-    for x in range(layers):
-        fine = p_ref[REACH + x, :rows, :lanes]
-        fine_ref[x] = fine
-        diff_ref[x] = fine - spread_ref[x]
 
 
 def fine_level(both, got, raw, far, near, early, late, spread, coefficients, peers):
     layers, rows, lanes = spread.shape
-    window = (layers + 2 * REACH, rows + 2 * REACH, lanes + LANES)
+    window = (layers + 2 * REACH, rows, rows + 2 * REACH, lanes // LANES + 1)
     out = jax.ShapeDtypeStruct(spread.shape, jnp.float32)
     return pl.pallas_call(
         functools.partial(fine_kernel, peers, len(far)),

time: 20.4 us -> 19.7 us (0.966)
  Pallas kernels: 5.41 us -> 4.66 us
    pallas_call x1, Pallas kernels: 3.13 us -> 2.53 us  [fine_level(): pl.pallas_call(functools.partial(fine_kernel, peers, len(far)), out_shape...]
where the time goes in v9:
time: 19.7 us; the launch traced here: 19.5 us
  starting transfers between devices  10.5 us (53%)
  Pallas kernels  4.66 us (24%)
  between operations  2.06 us (10%)
  waiting for transfers between devices  1.3 us (7%)
  local copies, waits for them, and re-layouts  0.97 us (5%)
    ppermute x6, starting transfers between devices, permute(): return lax.ppermute(value, (axis, 'gz'), moves)  10.3 us
    pallas_call x1, Pallas kernels, fine_level(): pl.pallas_call(functools.partial(fine_kernel, peers, len(far)), out_shape...  2.53 us
    ppermute x1, waiting for transfers between devices, shards(): late = lax.ppermute(late_sent, 'gz', [(0, 1), (1, 0)])  0.98 us
    unnamed x3, local copies, waits for them, and re-layouts  0.96 us
    pallas_call x1, Pallas kernels, coarse_level(): pl.pallas_call(functools.partial(coarse_kernel, peers, len(far)), out_sha...  0.7 us
    pallas_call x1, Pallas kernels, chebyshev_coefficients(): pl.pallas_call(coefficients_kernel, out_shape=jax.ShapeDtypeStruct((1 + 2...  0.61 us
  transfers between devices with their start and end apart: 8, of which 2 were waited for; matrix products, arithmetic and copies ran while one was open for 0% of the time, Pallas kernels for 6%

profile of v9, /device:TPU:0, one launch (start us, length us, event | category | flops | bytes accessed | tf_op | source)
XLA Modules:
  0.0 19.5 jit_solution(10205437360350154735)
XLA Ops:
  0.6 0.0 copy-start
  0.6 0.9 %constant_dynamic-update-slice_fusion.1 = f32[8,16,512]{2,1,0:T(8,128)S(1)} fusion(f32[4,16,512]{2,1,0:T(8,128)} %param.4), kind=kLoop, calls=%fused_computation.1 | loop fusion | bytes 262144
  1.6 0.0 copy-done
  1.6 0.2 %prep.1 = (f32[2,8,512]{2,1,0:T(8,128)S(1)}, f32[5,8,512]{2,1,0:T(8,128)S(1)}) custom-call(f32[8,16,512]{2,1,0:T(8,128)S(1)} %constant_dynamic-update-slice_fusion.both_ref), custom_call_target="tpu_custom_call" | custom-call | flops 5000000 | bytes 700000 | tf_op jit(solution)/shard_map/prep/pallas_call | solution.py:452
  1.8 3.0 %collective-permute-start = (f32[5,8,512]{2,1,0:T(8,128)S(1)}, f32[5,8,512]{2,1,0:T(8,128)S(1)}, u32[]{:S(2)}, u32[]{:S(2)}) collective-permute-start(f32[5,8,512]{2,1,0:T(8,128)S(1)} %get-tuple-element.10.after_ref), channel_id=1, source_target_pairs={{0,2},{1,3},{2,0},{3,1},{4,6},{5,7},{6,4},{7,5},{8,10},{9,11},{10,... | collective-permute-start | bytes 245768 | tf_op jit(solution)/shard_map/ppermute | solution.py:45
  4.9 0.1 collective-permute-start.1
  5.0 3.2 %collective-permute-start.2 = (f32[7,16,512]{2,1,0:T(8,128)S(1)}, f32[7,16,512]{2,1,0:T(8,128)S(1)}, u32[]{:S(2)}, u32[]{:S(2)}) collective-permute-start(f32[7,16,512]{2,1,0:T(8,128)S(1)} %raw_block.3), channel_id=1, source_target_pairs={{0,4},{1,5},{4,0},{5,1},{8,12},{9,13},{12,8},{13,9},{2,6},{3,7},{6... | collective-permute-start | bytes 688136 | tf_op jit(solution)/shard_map/ppermute | solution.py:45
  8.2 0.0 collective-permute-done.refs_0_
  8.2 0.2 pack_far.1
  8.3 2.3 %collective-permute-start.3 = (f32[72,128]{1,0:T(8,128)S(1)}, f32[72,128]{1,0:T(8,128)S(1)}, u32[]{:S(2)}, u32[]{:S(2)}) collective-permute-start(f32[72,128]{1,0:T(8,128)S(1)} %get-tuple-element.12.after_ref), channel_id=1, source_target_pairs={{0,8},{1,9},{4,12},{5,13},{8,0},{9,1},{12,4},{13,5},{2,10},{3,11},... | collective-permute-start | bytes 110600 | tf_op jit(solution)/shard_map/ppermute | solution.py:45
  10.6 0.1 collective-permute-start.4
  10.7 1.6 %collective-permute-start.5 = (f32[72,128]{1,0:T(8,128)S(1)}, f32[72,128]{1,0:T(8,128)S(1)}, u32[]{:S(2)}, u32[]{:S(2)}) collective-permute-start(f32[72,128]{1,0:T(8,128)S(1)} %get-tuple-element.15.after_ref), channel_id=1, source_target_pairs={{0,4},{1,5},{4,0},{5,1},{8,12},{9,13},{12,8},{13,9},{2,6},{3,7},{6... | collective-permute-start | bytes 110600 | tf_op jit(solution)/shard_map/ppermute | solution.py:45
  13.7 0.6 %coefficients.1.after_ref.refs_3_.refs_9_ = f32[7,8,128]{2,1,0:T(8,128)S(1)} custom-call(f32[1]{0:T(128)S(6)} %copy.7.low_ref, f32[1]{0:T(128)S(6)} %copy.8.high_ref, f32[72,128]{1,0:T(8,128)S(1)} %get-tuple-element.15.after_ref), custom_call_target="tpu_custom_call" | custom-call | flops 1000000 | bytes 100000 | tf_op jit(solution)/shard_map/coefficients/pallas_call | solution.py:234
  14.3 0.0 collective-permute-done.2.first_ref.refs_2_
  14.3 0.0 collective-permute-done.1.second_ref.refs_1_
  14.3 0.3 %landed.1 = (f32[96,128]{1,0:T(8,128)S(1)}, f32[32,128]{1,0:T(8,128)S(1)}) custom-call(f32[7,8,128]{2,1,0:T(8,128)S(1)} %coefficients.1.after_ref.refs_3_.refs_9_, f32[8,16,512]{2,1,0:T(8,128)S(1)} %constant_dynamic-update-slice_fusion.both_ref, f32[2,8,512]{2,1,0:T(8,128)S(1)} %get-tuple-element.11.pooled_ref.own_ref, ...), custom_call_target="tpu_custom_call" | custom-call | flops 1000000 | bytes 1000000 | tf_op jit(solution)/shard_map/landed/pallas_call | solution.py:694
  14.6 0.0 collective-permute-start.6
  14.6 0.0 collective-permute-done.3.refs_0_.refs_3_
  14.7 0.0 collective-permute-done.4.second_ref.refs_4_
  14.7 0.3 %collective-permute-done.5.first_ref.refs_5_ = f32[72,128]{1,0:T(8,128)S(1)} collective-permute-done((f32[72,128]{1,0:T(8,128)S(1)}, f32[72,128]{1,0:T(8,128)S(1)}, u32[]{:S(2)}, u32[]{:S(2)}) %collective-permute-start.5) | collective-permute-done | bytes 36896 | tf_op jit(solution)/shard_map/ppermute | solution.py:45
  15.0 0.1 late_lanes.1
  15.1 0.2 %collective-permute-start.7 = (f32[8,128]{1,0:T(8,128)S(1)}, f32[8,128]{1,0:T(8,128)S(1)}, u32[]{:S(2)}, u32[]{:S(2)}) collective-permute-start(f32[8,128]{1,0:T(8,128)S(1)} %late_lanes.1), channel_id=1, source_target_pairs={{0,1},{1,0},{2,3},{3,2},{4,5},{5,4},{6,7},{7,6},{8,9},{9,8},{10,11... | collective-permute-start | bytes 12296 | tf_op jit(solution)/shard_map/ppermute | solution.py:984
  15.3 1.0 %collective-permute-done.7.refs_2_.refs_7_ = f32[8,128]{1,0:T(8,128)S(1)} collective-permute-done((f32[8,128]{1,0:T(8,128)S(1)}, f32[8,128]{1,0:T(8,128)S(1)}, u32[]{:S(2)}, u32[]{:S(2)}) %collective-permute-start.7) | collective-permute-done | bytes 4128 | tf_op jit(solution)/shard_map/ppermute | solution.py:984
  16.2 0.0 collective-permute-done.6.refs_1_.refs_6_
  16.2 0.7 %coarse_level.1.refs_8_ = f32[4,16,512]{2,1,0:T(8,128)S(1)} custom-call(f32[2,8,512]{2,1,0:T(8,128)S(1)} %get-tuple-element.11.pooled_ref.own_ref, f32[1,8,512]{2,1,0:T(8,128)S(1)} %get-tuple-element.13.halo_ref, f32[96,128]{1,0:T(8,128)S(1)} %get-tuple-element.17.pool_ref, f32[72,128]{1,0:T(8,128)S(1)} %collective-permute-done.5.first_ref.refs_5_, ...), custom_call_target="tpu_custom_call" | custom-call | flops 20000000 | bytes 4000000 | tf_op jit(solution)/shard_map/coarse_level/pallas_call | solution.py:848
  17.0 2.5 %fine_level.1 = (f32[4,16,512]{2,1,0:T(8,128)}, f32[4,16,512]{2,1,0:T(8,128)}) custom-call(f32[8,16,512]{2,1,0:T(8,128)S(1)} %constant_dynamic-update-slice_fusion.both_ref, f32[5,8,512]{2,1,0:T(8,128)S(1)} %collective-permute-done.refs_0_, f32[7,16,512]{2,1,0:T(8,128)S(1)} %collective-permute-done.1.second_ref.refs_1_, ...), custom_call_target="tpu_custom_call" | custom-call | flops 20000000 | bytes 10000000 | tf_op jit(solution)/shard_map/fine_level/pallas_call | solution.py:948
  (4 shorter events, 0.1 us)
Async XLA Ops:
  0.6 1.0 %copy-start = (f32[4,16,512]{2,1,0:T(8,128)S(1)}, f32[4,16,512]{2,1,0:T(8,128)}, u32[]{:S(2)}) copy-start(f32[4,16,512]{2,1,0:T(8,128)} %param.5) | copy-start | bytes 393220
  1.8 6.3 %collective-permute-start = (f32[5,8,512]{2,1,0:T(8,128)S(1)}, f32[5,8,512]{2,1,0:T(8,128)S(1)}, u32[]{:S(2)}, u32[]{:S(2)}) collective-permute-start(f32[5,8,512]{2,1,0:T(8,128)S(1)} %get-tuple-element.10.after_ref), channel_id=1, source_target_pairs={{0,2},{1,3},{2,0},{3,1},{4,6},{5,7},{6,4},{7,5},{8,10},{9,11},{10,... | collective-permute-start | bytes 245768 | tf_op jit(solution)/shard_map/ppermute | solution.py:45
  4.9 9.4 %collective-permute-start.1 = (f32[7,16,512]{2,1,0:T(8,128)S(1)}, f32[7,16,512]{2,1,0:T(8,128)S(1)}, u32[]{:S(2)}, u32[]{:S(2)}) collective-permute-start(f32[7,16,512]{2,1,0:T(8,128)S(1)} %raw_block.2.after_ref), channel_id=1, source_target_pairs={{0,1},{1,0},{4,8},{5,9},{8,4},{9,5},{12,13},{13,12},{2,3},{3,2},{6... | collective-permute-start | bytes 688136 | tf_op jit(solution)/shard_map/ppermute | solution.py:45
  5.0 9.3 %collective-permute-start.2 = (f32[7,16,512]{2,1,0:T(8,128)S(1)}, f32[7,16,512]{2,1,0:T(8,128)S(1)}, u32[]{:S(2)}, u32[]{:S(2)}) collective-permute-start(f32[7,16,512]{2,1,0:T(8,128)S(1)} %raw_block.3), channel_id=1, source_target_pairs={{0,4},{1,5},{4,0},{5,1},{8,12},{9,13},{12,8},{13,9},{2,6},{3,7},{6... | collective-permute-start | bytes 688136 | tf_op jit(solution)/shard_map/ppermute | solution.py:45
  8.3 6.3 %collective-permute-start.3 = (f32[72,128]{1,0:T(8,128)S(1)}, f32[72,128]{1,0:T(8,128)S(1)}, u32[]{:S(2)}, u32[]{:S(2)}) collective-permute-start(f32[72,128]{1,0:T(8,128)S(1)} %get-tuple-element.12.after_ref), channel_id=1, source_target_pairs={{0,8},{1,9},{4,12},{5,13},{8,0},{9,1},{12,4},{13,5},{2,10},{3,11},... | collective-permute-start | bytes 110600 | tf_op jit(solution)/shard_map/ppermute | solution.py:45
  10.6 4.0 %collective-permute-start.4 = (f32[72,128]{1,0:T(8,128)S(1)}, f32[72,128]{1,0:T(8,128)S(1)}, u32[]{:S(2)}, u32[]{:S(2)}) collective-permute-start(f32[72,128]{1,0:T(8,128)S(1)} %get-tuple-element.14), channel_id=1, source_target_pairs={{0,1},{1,0},{4,8},{5,9},{8,4},{9,5},{12,13},{13,12},{2,3},{3,2},{6... | collective-permute-start | bytes 110600 | tf_op jit(solution)/shard_map/ppermute | solution.py:45
  10.7 4.3 %collective-permute-start.5 = (f32[72,128]{1,0:T(8,128)S(1)}, f32[72,128]{1,0:T(8,128)S(1)}, u32[]{:S(2)}, u32[]{:S(2)}) collective-permute-start(f32[72,128]{1,0:T(8,128)S(1)} %get-tuple-element.15.after_ref), channel_id=1, source_target_pairs={{0,4},{1,5},{4,0},{5,1},{8,12},{9,13},{12,8},{13,9},{2,6},{3,7},{6... | collective-permute-start | bytes 110600 | tf_op jit(solution)/shard_map/ppermute | solution.py:45
  14.6 1.6 %collective-permute-start.6 = (f32[32,128]{1,0:T(8,128)S(1)}, f32[32,128]{1,0:T(8,128)S(1)}, u32[]{:S(2)}, u32[]{:S(2)}) collective-permute-start(f32[32,128]{1,0:T(8,128)S(1)} %get-tuple-element.16.after_ref), channel_id=1, source_target_pairs={{0,1},{1,0},{2,3},{3,2},{4,5},{5,4},{6,7},{7,6},{8,9},{9,8},{10,11... | collective-permute-start | bytes 49160 | tf_op jit(solution)/shard_map/ppermute | solution.py:982
  15.1 1.2 %collective-permute-start.7 = (f32[8,128]{1,0:T(8,128)S(1)}, f32[8,128]{1,0:T(8,128)S(1)}, u32[]{:S(2)}, u32[]{:S(2)}) collective-permute-start(f32[8,128]{1,0:T(8,128)S(1)} %late_lanes.1), channel_id=1, source_target_pairs={{0,1},{1,0},{2,3},{3,2},{4,5},{5,4},{6,7},{7,6},{8,9},{9,8},{10,11... | collective-permute-start | bytes 12296 | tf_op jit(solution)/shard_map/ppermute | solution.py:984

commit v10 on v9

--- a/solution.py
+++ b/solution.py
@@ -238,7 +238,7 @@
         out_specs=VMEM,
         scratch_shapes=[pltpu.SMEM((2, 1), jnp.float32), pltpu.SemaphoreType.DMA((2,))],
         compiler_params=pltpu.CompilerParams(vmem_limit_bytes=4 << 20),
-        cost_estimate=pl.CostEstimate(flops=1_000_000, bytes_accessed=100_000, transcendentals=0),
+        cost_estimate=pl.CostEstimate(flops=1000000, bytes_accessed=500_000, transcendentals=0),
         name="coefficients",
     )(low_bound, high_bound, after)
 
@@ -398,7 +398,7 @@
     return both_ref.at[:layers], both_ref.at[layers:]
 
 
-def prep_kernel(both_ref, pooled_ref, *refs):
+def prep_kernel(both_ref, after_ref, pooled_ref, *refs):
     *out_refs, sum_ref = refs
     log_ref, source_ref = parts(both_ref)
     layers, rows, lanes = log_ref.shape
@@ -442,7 +442,7 @@
     )
 
 
-def prep(both, ny):
+def prep(both, after, ny):
     layers, rows, lanes = both.shape[0] // 2, *both.shape[1:]
     outs = 1 if ny == 2 else 2
 
@@ -452,16 +452,17 @@
     return pl.pallas_call(
         prep_kernel,
         out_shape=(tiles(2),) + (tiles(layers + 1),) * outs,
-        in_specs=[VMEM],
+        in_specs=[VMEM, ANY],
         out_specs=(VMEM,) * (1 + outs),
         scratch_shapes=[pltpu.VMEM((lanes // LANES, 2 * SUBLANES, LANES), jnp.float32)],
         compiler_params=pltpu.CompilerParams(vmem_limit_bytes=8 << 20),
         cost_estimate=pl.CostEstimate(flops=5_000_000, bytes_accessed=700_000, transcendentals=0),
         name="prep",
-    )(both)
-
-
-def raw_kernel(to_right_if_odd, both_ref, after_ref, out_ref):
+    )(both, after)
+
+
+def raw_kernel(to_right_if_odd, both_ref, *refs):
+    out_ref = refs[-1]
     log_ref, source_ref = parts(both_ref)
     layers = log_ref.shape[0]
     odd = lax.axis_index("gx") % 2
@@ -472,17 +473,17 @@
         out_ref[layers + layer] = source_ref[layer + skip]
 
 
-def raw_block(both, after, to_right_if_odd):
+def raw_block(both, to_right_if_odd, *after):
     layers, rows, lanes = both.shape[0] // 2, *both.shape[1:]
     return pl.pallas_call(
         functools.partial(raw_kernel, to_right_if_odd),
         out_shape=jax.ShapeDtypeStruct((2 * layers - 1, rows, lanes), jnp.float32),
-        in_specs=[VMEM, ANY],
+        in_specs=[VMEM] + [ANY] * len(after),
         out_specs=VMEM,
         compiler_params=pltpu.CompilerParams(vmem_limit_bytes=8 << 20),
         cost_estimate=pl.CostEstimate(flops=1_000_000, bytes_accessed=500_000, transcendentals=0),
         name="raw_block",
-    )(both, after)
+    )(both, *after)
 
 
 def pack_far_kernel(wide, pooled_ref, *refs):
@@ -565,7 +566,7 @@
         out_specs=(VMEM,) * len(out_shape),
         scratch_shapes=[pltpu.VMEM((lanes // LANES, 2 * SUBLANES, LANES), jnp.float32)],
         compiler_params=pltpu.CompilerParams(vmem_limit_bytes=8 << 20),
-        cost_estimate=AHEAD,
+        cost_estimate=pl.CostEstimate(flops=1000000, bytes_accessed=500_000, transcendentals=0),
         name="pack_far",
     )(pooled, *got)
     return halos, far
@@ -636,12 +637,12 @@
         in_specs=[VMEM, VMEM, ANY] + [VMEM] * len(got),
         out_specs=(VMEM,) * 2,
         compiler_params=pltpu.CompilerParams(vmem_limit_bytes=8 << 20),
-        cost_estimate=AHEAD,
+        cost_estimate=pl.CostEstimate(flops=1000000, bytes_accessed=500_000, transcendentals=0),
         name="pack_near",
     )(pooled, halos, after, *got)
 
 
-def landed_kernel(after_ref, both_ref, pooled_ref, halo_ref, first_ref, second_ref, *refs):
+def landed_kernel(after_ref, both_ref, pooled_ref, halo_ref, second_ref, first_ref, *refs):
     *got_refs, out_ref, sent_ref, sum_ref = refs
     log_ref, source_ref = parts(both_ref)
     layers, rows, lanes = log_ref.shape
@@ -703,7 +704,7 @@
         compiler_params=pltpu.CompilerParams(vmem_limit_bytes=16 << 20),
         cost_estimate=pl.CostEstimate(flops=1_000_000, bytes_accessed=1_000_000, transcendentals=0),
         name="landed",
-    )(after, both, pooled, halos, *raw, *got)
+    )(after, both, pooled, halos, *raw[::-1], *got)
 
 
 def near_part(refs, even, lanes, wide, side, name):
@@ -962,15 +963,15 @@
     layers, rows, lanes = log_perm.shape
     assert layers == REACH and rows == 2 * SUBLANES and nx > 2 and nz == 2
     both = jnp.concatenate([log_perm, source])
-    own, *rows_sent = prep(both, ny)
+    for_second = raw_block(both, True)
+    second = permute(for_second, "gx", nx, neighbour_pairs(nx, 1))
+    for_first = raw_block(both, False, for_second)
+    raw = (permute(for_first, "gx", nx, neighbour_pairs(nx, 0)), second)
+    own, *rows_sent = prep(both, for_first, ny)
     if ny == 2:
         got = (permute(rows_sent[0], "gy", ny, [(0, 1)]),)
     else:
         got = swap("gy", ny, rows_sent[1], rows_sent[0])
-    for_second = raw_block(both, rows_sent[0], True)
-    second = permute(for_second, "gx", nx, neighbour_pairs(nx, 1))
-    for_first = raw_block(both, for_second, False)
-    raw = (permute(for_first, "gx", nx, neighbour_pairs(nx, 0)), second)
     far_groups = far_pairs(nx)
     halos, for_far = pack_far(own, got, len(far_groups))
     far = [permute(tiles, "gx", nx, group) for tiles, group in zip(for_far, far_groups)]

time: 19.7 us -> 21.1 us (1.071)
  waiting for transfers between devices: 1.3 us -> 4.88 us
  starting transfers between devices: 10.5 us -> 8.39 us
    ppermute x6, waiting for transfers between devices: 0.32 us -> 3.79 us  [permute(): return lax.ppermute(value, (axis, 'gz'), moves)]
    ppermute x6, starting transfers between devices: 10.3 us -> 8.26 us  [permute(): return lax.ppermute(value, (axis, 'gz'), moves)]
  transfers between devices with their start and end apart: 8 -> 8, of which waited for: 2 -> 3; matrix products, arithmetic and copies ran while one was open for 0% -> 0% of each run, Pallas kernels for 6% -> 7%
where the time goes in v10:
time: 21.1 us; the launch traced here: 21 us
  starting transfers between devices  8.39 us (40%)
  waiting for transfers between devices  4.88 us (23%)
  Pallas kernels  4.66 us (22%)
  between operations  2.05 us (10%)
  local copies, waits for them, and re-layouts  0.97 us (5%)
    ppermute x6, starting transfers between devices, permute(): return lax.ppermute(value, (axis, 'gz'), moves)  8.26 us
    ppermute x6, waiting for transfers between devices, permute(): return lax.ppermute(value, (axis, 'gz'), moves)  3.79 us
    pallas_call x1, Pallas kernels, fine_level(): pl.pallas_call(functools.partial(fine_kernel, peers, len(far)), out_shape...  2.52 us
    ppermute x1, waiting for transfers between devices, shards(): late = lax.ppermute(late_sent, 'gz', [(0, 1), (1, 0)])  1.08 us
    unnamed x3, local copies, waits for them, and re-layouts  0.96 us
    pallas_call x1, Pallas kernels, coarse_level(): pl.pallas_call(functools.partial(coarse_kernel, peers, len(far)), out_sha...  0.7 us
    pallas_call x1, Pallas kernels, chebyshev_coefficients(): pl.pallas_call(coefficients_kernel, out_shape=jax.ShapeDtypeStruct((1 + 2...  0.61 us
  transfers between devices with their start and end apart: 8, of which 3 were waited for; matrix products, arithmetic and copies ran while one was open for 0% of the time, Pallas kernels for 7%

profile of v10, /device:TPU:0, one launch (start us, length us, event | category | flops | bytes accessed | tf_op | source)
XLA Modules:
  0.0 21.0 jit_solution(11304802507923986335)
XLA Ops:
  0.6 0.0 copy-start
  0.6 0.9 %constant_dynamic-update-slice_fusion.1 = f32[8,16,512]{2,1,0:T(8,128)S(1)} fusion(f32[4,16,512]{2,1,0:T(8,128)} %param.4), kind=kLoop, calls=%fused_computation.1 | loop fusion | bytes 262144
  1.6 0.0 copy-done
  1.7 3.1 %collective-permute-start.2 = (f32[7,16,512]{2,1,0:T(8,128)S(1)}, f32[7,16,512]{2,1,0:T(8,128)S(1)}, u32[]{:S(2)}, u32[]{:S(2)}) collective-permute-start(f32[7,16,512]{2,1,0:T(8,128)S(1)} %raw_block.3.after_ref), channel_id=1, source_target_pairs={{0,4},{1,5},{4,0},{5,1},{8,12},{9,13},{12,8},{13,9},{2,6},{3,7},{6... | collective-permute-start | bytes 688136 | tf_op jit(solution)/shard_map/ppermute | solution.py:45
  4.8 0.0 collective-permute-start.1
  4.8 0.2 prep.1
  5.0 1.6 %collective-permute-start = (f32[5,8,512]{2,1,0:T(8,128)S(1)}, f32[5,8,512]{2,1,0:T(8,128)S(1)}, u32[]{:S(2)}, u32[]{:S(2)}) collective-permute-start(f32[5,8,512]{2,1,0:T(8,128)S(1)} %get-tuple-element.10), channel_id=1, source_target_pairs={{0,2},{1,3},{2,0},{3,1},{4,6},{5,7},{6,4},{7,5},{8,10},{9,11},{10,... | collective-permute-start | bytes 245768 | tf_op jit(solution)/shard_map/ppermute | solution.py:45
  6.5 3.4 %collective-permute-done.refs_0_ = f32[5,8,512]{2,1,0:T(8,128)S(1)} collective-permute-done((f32[5,8,512]{2,1,0:T(8,128)S(1)}, f32[5,8,512]{2,1,0:T(8,128)S(1)}, u32[]{:S(2)}, u32[]{:S(2)}) %collective-permute-start) | collective-permute-done | bytes 81952 | tf_op jit(solution)/shard_map/ppermute | solution.py:45
  9.9 0.2 pack_far.1
  10.1 2.2 %collective-permute-start.3 = (f32[72,128]{1,0:T(8,128)S(1)}, f32[72,128]{1,0:T(8,128)S(1)}, u32[]{:S(2)}, u32[]{:S(2)}) collective-permute-start(f32[72,128]{1,0:T(8,128)S(1)} %get-tuple-element.12.after_ref), channel_id=1, source_target_pairs={{0,8},{1,9},{4,12},{5,13},{8,0},{9,1},{12,4},{13,5},{2,10},{3,11},... | collective-permute-start | bytes 110600 | tf_op jit(solution)/shard_map/ppermute | solution.py:45
  12.3 0.1 collective-permute-start.4
  12.4 1.3 %collective-permute-start.5 = (f32[72,128]{1,0:T(8,128)S(1)}, f32[72,128]{1,0:T(8,128)S(1)}, u32[]{:S(2)}, u32[]{:S(2)}) collective-permute-start(f32[72,128]{1,0:T(8,128)S(1)} %get-tuple-element.15.after_ref), channel_id=1, source_target_pairs={{0,4},{1,5},{4,0},{5,1},{8,12},{9,13},{12,8},{13,9},{2,6},{3,7},{6... | collective-permute-start | bytes 110600 | tf_op jit(solution)/shard_map/ppermute | solution.py:45
  15.0 0.6 %coefficients.1.after_ref.refs_3_.refs_9_ = f32[7,8,128]{2,1,0:T(8,128)S(1)} custom-call(f32[1]{0:T(128)S(6)} %copy.7.low_ref, f32[1]{0:T(128)S(6)} %copy.8.high_ref, f32[72,128]{1,0:T(8,128)S(1)} %get-tuple-element.15.after_ref), custom_call_target="tpu_custom_call" | custom-call | flops 1000000 | bytes 500000 | tf_op jit(solution)/shard_map/coefficients/pallas_call | solution.py:234
  15.6 0.0 collective-permute-done.2.first_ref.refs_2_
  15.6 0.0 collective-permute-done.1.second_ref.refs_1_
  15.7 0.3 %landed.1 = (f32[96,128]{1,0:T(8,128)S(1)}, f32[32,128]{1,0:T(8,128)S(1)}) custom-call(f32[7,8,128]{2,1,0:T(8,128)S(1)} %coefficients.1.after_ref.refs_3_.refs_9_, f32[8,16,512]{2,1,0:T(8,128)S(1)} %constant_dynamic-update-slice_fusion.both_ref, f32[2,8,512]{2,1,0:T(8,128)S(1)} %get-tuple-element.11.pooled_ref.own_ref, ...), custom_call_target="tpu_custom_call" | custom-call | flops 1000000 | bytes 1000000 | tf_op jit(solution)/shard_map/landed/pallas_call | solution.py:695
  16.0 0.0 collective-permute-start.6
  16.0 0.0 collective-permute-done.3.refs_0_.refs_3_
  16.0 0.0 collective-permute-done.4.second_ref.refs_4_
  16.0 0.4 %collective-permute-done.5.first_ref.refs_5_ = f32[72,128]{1,0:T(8,128)S(1)} collective-permute-done((f32[72,128]{1,0:T(8,128)S(1)}, f32[72,128]{1,0:T(8,128)S(1)}, u32[]{:S(2)}, u32[]{:S(2)}) %collective-permute-start.5) | collective-permute-done | bytes 36896 | tf_op jit(solution)/shard_map/ppermute | solution.py:45
  16.4 0.1 late_lanes.1
  16.5 0.1 collective-permute-start.7
  16.6 1.1 %collective-permute-done.7.refs_2_.refs_7_ = f32[8,128]{1,0:T(8,128)S(1)} collective-permute-done((f32[8,128]{1,0:T(8,128)S(1)}, f32[8,128]{1,0:T(8,128)S(1)}, u32[]{:S(2)}, u32[]{:S(2)}) %collective-permute-start.7) | collective-permute-done | bytes 4128 | tf_op jit(solution)/shard_map/ppermute | solution.py:985
  17.7 0.0 collective-permute-done.6.refs_1_.refs_6_
  17.7 0.7 %coarse_level.1.refs_8_ = f32[4,16,512]{2,1,0:T(8,128)S(1)} custom-call(f32[2,8,512]{2,1,0:T(8,128)S(1)} %get-tuple-element.11.pooled_ref.own_ref, f32[1,8,512]{2,1,0:T(8,128)S(1)} %get-tuple-element.13.halo_ref, f32[96,128]{1,0:T(8,128)S(1)} %get-tuple-element.17.pool_ref, f32[72,128]{1,0:T(8,128)S(1)} %collective-permute-done.5.first_ref.refs_5_, ...), custom_call_target="tpu_custom_call" | custom-call | flops 20000000 | bytes 4000000 | tf_op jit(solution)/shard_map/coarse_level/pallas_call | solution.py:849
  18.4 2.5 %fine_level.1 = (f32[4,16,512]{2,1,0:T(8,128)}, f32[4,16,512]{2,1,0:T(8,128)}) custom-call(f32[8,16,512]{2,1,0:T(8,128)S(1)} %constant_dynamic-update-slice_fusion.both_ref, f32[5,8,512]{2,1,0:T(8,128)S(1)} %collective-permute-done.refs_0_, f32[7,16,512]{2,1,0:T(8,128)S(1)} %collective-permute-done.1.second_ref.refs_1_, ...), custom_call_target="tpu_custom_call" | custom-call | flops 20000000 | bytes 10000000 | tf_op jit(solution)/shard_map/fine_level/pallas_call | solution.py:949
  (4 shorter events, 0.1 us)
Async XLA Ops:
  0.6 1.0 %copy-start = (f32[4,16,512]{2,1,0:T(8,128)S(1)}, f32[4,16,512]{2,1,0:T(8,128)}, u32[]{:S(2)}) copy-start(f32[4,16,512]{2,1,0:T(8,128)} %param.5) | copy-start | bytes 393220
  1.7 14.0 %collective-permute-start.2 = (f32[7,16,512]{2,1,0:T(8,128)S(1)}, f32[7,16,512]{2,1,0:T(8,128)S(1)}, u32[]{:S(2)}, u32[]{:S(2)}) collective-permute-start(f32[7,16,512]{2,1,0:T(8,128)S(1)} %raw_block.3.after_ref), channel_id=1, source_target_pairs={{0,4},{1,5},{4,0},{5,1},{8,12},{9,13},{12,8},{13,9},{2,6},{3,7},{6... | collective-permute-start | bytes 688136 | tf_op jit(solution)/shard_map/ppermute | solution.py:45
  4.8 10.9 %collective-permute-start.1 = (f32[7,16,512]{2,1,0:T(8,128)S(1)}, f32[7,16,512]{2,1,0:T(8,128)S(1)}, u32[]{:S(2)}, u32[]{:S(2)}) collective-permute-start(f32[7,16,512]{2,1,0:T(8,128)S(1)} %raw_block.2.refs_0_), channel_id=1, source_target_pairs={{0,1},{1,0},{4,8},{5,9},{8,4},{9,5},{12,13},{13,12},{2,3},{3,2},{6... | collective-permute-start | bytes 688136 | tf_op jit(solution)/shard_map/ppermute | solution.py:45
  5.0 4.9 %collective-permute-start = (f32[5,8,512]{2,1,0:T(8,128)S(1)}, f32[5,8,512]{2,1,0:T(8,128)S(1)}, u32[]{:S(2)}, u32[]{:S(2)}) collective-permute-start(f32[5,8,512]{2,1,0:T(8,128)S(1)} %get-tuple-element.10), channel_id=1, source_target_pairs={{0,2},{1,3},{2,0},{3,1},{4,6},{5,7},{6,4},{7,5},{8,10},{9,11},{10,... | collective-permute-start | bytes 245768 | tf_op jit(solution)/shard_map/ppermute | solution.py:45
  10.1 5.9 %collective-permute-start.3 = (f32[72,128]{1,0:T(8,128)S(1)}, f32[72,128]{1,0:T(8,128)S(1)}, u32[]{:S(2)}, u32[]{:S(2)}) collective-permute-start(f32[72,128]{1,0:T(8,128)S(1)} %get-tuple-element.12.after_ref), channel_id=1, source_target_pairs={{0,8},{1,9},{4,12},{5,13},{8,0},{9,1},{12,4},{13,5},{2,10},{3,11},... | collective-permute-start | bytes 110600 | tf_op jit(solution)/shard_map/ppermute | solution.py:45
  12.3 3.7 %collective-permute-start.4 = (f32[72,128]{1,0:T(8,128)S(1)}, f32[72,128]{1,0:T(8,128)S(1)}, u32[]{:S(2)}, u32[]{:S(2)}) collective-permute-start(f32[72,128]{1,0:T(8,128)S(1)} %get-tuple-element.14), channel_id=1, source_target_pairs={{0,1},{1,0},{4,8},{5,9},{8,4},{9,5},{12,13},{13,12},{2,3},{3,2},{6... | collective-permute-start | bytes 110600 | tf_op jit(solution)/shard_map/ppermute | solution.py:45
  12.4 4.0 %collective-permute-start.5 = (f32[72,128]{1,0:T(8,128)S(1)}, f32[72,128]{1,0:T(8,128)S(1)}, u32[]{:S(2)}, u32[]{:S(2)}) collective-permute-start(f32[72,128]{1,0:T(8,128)S(1)} %get-tuple-element.15.after_ref), channel_id=1, source_target_pairs={{0,4},{1,5},{4,0},{5,1},{8,12},{9,13},{12,8},{13,9},{2,6},{3,7},{6... | collective-permute-start | bytes 110600 | tf_op jit(solution)/shard_map/ppermute | solution.py:45
  16.0 1.8 %collective-permute-start.6 = (f32[32,128]{1,0:T(8,128)S(1)}, f32[32,128]{1,0:T(8,128)S(1)}, u32[]{:S(2)}, u32[]{:S(2)}) collective-permute-start(f32[32,128]{1,0:T(8,128)S(1)} %get-tuple-element.16.after_ref), channel_id=1, source_target_pairs={{0,1},{1,0},{2,3},{3,2},{4,5},{5,4},{6,7},{7,6},{8,9},{9,8},{10,11... | collective-permute-start | bytes 49160 | tf_op jit(solution)/shard_map/ppermute | solution.py:983
  16.5 1.2 %collective-permute-start.7 = (f32[8,128]{1,0:T(8,128)S(1)}, f32[8,128]{1,0:T(8,128)S(1)}, u32[]{:S(2)}, u32[]{:S(2)}) collective-permute-start(f32[8,128]{1,0:T(8,128)S(1)} %late_lanes.1), channel_id=1, source_target_pairs={{0,1},{1,0},{2,3},{3,2},{4,5},{5,4},{6,7},{7,6},{8,9},{9,8},{10,11... | collective-permute-start | bytes 12296 | tf_op jit(solution)/shard_map/ppermute | solution.py:985

commit v11 on v9

--- a/solution.py
+++ b/solution.py
@@ -259,39 +259,36 @@
     return value[:, lanes - LANES :], value[:, :LANES]
 
 
-def write_lanes(ref, pairs):
+def write_lanes(pairs):
     starts = lax.axis_index("gz") == 0
-    each = LANES // SUBLANES
-    group = iota((SUBLANES, LANES), 1) // SUBLANES
-    for base in range(0, len(pairs), each):
-        merged = None
-        for j, (last, first) in enumerate(pairs[base : base + each]):
-            moved = turned(jnp.where(starts, last, first), SUBLANES * j, 1)
-            place = jnp.where(starts, (j - 1) % each, j)
-            merged = moved if merged is None else jnp.where(group == place, moved, merged)
-        row = base // each * SUBLANES
-        ref[row : row + SUBLANES, :] = merged
-
-
-def read_lanes(ref, slot):
-    each = LANES // SUBLANES
-    row = slot // each * SUBLANES
-    return turned(ref[row : row + SUBLANES, :], -SUBLANES * (slot % each), 1)
-
-
-def early_slots(layers, row_tiles, n_got):
+    each = LANES // REACH
+    group = iota((SUBLANES, LANES), 1) // REACH
+    merged = None
+    for j, (last, first) in enumerate(pairs):
+        moved = turned(jnp.where(starts, last, first), REACH * j, 1)
+        place = jnp.where(starts, (j - 1) % each, j)
+        merged = moved if merged is None else jnp.where(group == place, moved, merged)
+    return merged
+
+
+def read_lanes(tile, slot):
+    return turned(tile, -REACH * slot, 1)
+
+
+def add_lanes(tile, slot, value):
+    starts = lax.axis_index("gz") == 0
+    group = iota((SUBLANES, LANES), 1) // REACH
+    place = jnp.where(starts, slot, (slot - 1) % (LANES // REACH))
+    return jnp.where(group == place, turned(value, REACH * slot, 1), tile)
+
+
+def lane_slots(layers, row_tiles, n_got):
     keys = [("own", a, layer, i) for a in range(2) for layer in range(layers) for i in range(row_tiles)]
+    keys += [("pooled", x, a) for x in range(2) for a in range(2)]
+    shared = len(keys)
+    keys += [("halo", i, half) for i in range(n_got) for half in range(2)]
     keys += [("got", g, layer) for g in range(n_got) for layer in range(layers)]
-    keys += [("pooled", x, a) for x in range(2) for a in range(2)]
-    keys += [("halo", i, half) for i in range(n_got) for half in range(2)]
-    keys += [
-        ("raw", side, slot, i)
-        for side in range(2)
-        for slot in range(2 * layers - 1)
-        for i in range(row_tiles)
-    ]
-    keys += [("near", side, i) for side in range(2) for i in range(3)]
-    return {key: i for i, key in enumerate(keys)}
+    return {key: i for i, key in enumerate(keys)}, shared
 
 
 def near_layout(lanes, wide):
@@ -302,27 +299,21 @@
     else:
         parts = [("strip", whole), ("halo", half), ("source", half), ("row", 1)]
     layout, start = {}, 0
-    for name, count in parts:
+    for name, count in parts + [("lanes", 1)]:
         layout[name] = (start, count)
         start += count
     return layout, start
 
 
-def late_slots(lanes, wide):
-    names = list(near_layout(lanes, wide)[0])
-    keys = [(side, name) for side in range(2) for name in names] + [(side, "far") for side in range(2)]
-    return {key: i for i, key in enumerate(keys)}
+def near_lane_slots(lanes, wide, shared):
+    names = [name for name in near_layout(lanes, wide)[0] if name not in ("source", "lanes")]
+    return {name: shared + i for i, name in enumerate(names)}
 
 
 def rows_to_lanes(row_tile, count):
     return jnp.concatenate(
         [jnp.broadcast_to(row_tile[j : j + 1], (SUBLANES, LANES)) for j in range(count)], axis=1
     )
-
-
-def packed_rows(slots):
-    each = LANES // SUBLANES
-    return jax.ShapeDtypeStruct((-(-len(slots) // each) * SUBLANES, LANES), jnp.float32)
 
 
 def window_scratch(count, own_rows, rows, tiles):
@@ -485,12 +476,11 @@
     )(both, after)
 
 
-def pack_far_kernel(wide, pooled_ref, *refs):
-    n_got = 2 if wide else 1
-    got_refs, halo_ref, far_refs, sum_ref = refs[:n_got], refs[n_got], refs[n_got + 1 : -1], refs[-1]
+def halos_kernel(wide, both_ref, pooled_ref, *refs):
+    *got_refs, halo_ref, sent_ref, sum_ref = refs
     layers, lanes = got_refs[0].shape[0] - 1, got_refs[0].shape[2]
-    ix, iy = lax.axis_index("gx"), lax.axis_index("gy")
-    even, starts, low = iy % 2 == 0, iy == 0, ix % 4 < 2
+    iy = lax.axis_index("gy")
+    even, starts = iy % 2 == 0, iy == 0
     half = lanes // 2
     upper = iota((SUBLANES, lanes), 0) < REACH
     row = iota((SUBLANES, half), 0)
@@ -540,38 +530,76 @@
 
     for i in range(len(halos) // 2):
         halo_ref[i] = pair(halos[2 * i], halos[2 * i + 1])
-    logs = [pooled_ref[x, :, :half] for x in range(2)]
-    sources = [pooled_ref[x, :, half:] for x in range(2)]
-
-    far = [(logs[inner], logs[1 - inner], sources[inner], halos[inner]) for inner in (1, 0)]
-    for group, ref in enumerate(far_refs):
-        for i, (right, left) in enumerate(zip(*far)):
-            put(ref, i * (half // LANES), jnp.where(low, *((right, left) if group == 0 else (left, right))))
-        for spare in range(4 * (half // LANES), ref.shape[0] // SUBLANES):
-            put(ref, spare, jnp.zeros((SUBLANES, LANES), jnp.float32))
-
-
-def pack_far(pooled, got, n_far):
+    pairs = {}
+    rows = both_ref.shape[1]
+    for a, ref in enumerate(parts(both_ref)):
+        for layer in range(layers):
+            for i in range(rows // SUBLANES):
+                pairs["own", a, layer, i] = edges(ref[layer, i * SUBLANES : (i + 1) * SUBLANES])
+    for x in range(2):
+        for a in range(2):
+            pairs["pooled", x, a] = edges(pooled_ref[x, :, a * half : (a + 1) * half])
+    for i, halo in enumerate(halos):
+        pairs["halo", i // 2, i % 2] = edges(halo)
+    for g, ref in enumerate(got_refs):
+        for layer in range(layers):
+            pairs["got", g, layer] = edges(ref[layer])
+    slots, _ = lane_slots(layers, rows // SUBLANES, len(got_refs))
+    sent_ref[...] = write_lanes([pairs[key] for key in slots])
+
+
+def pooled_halos(both, pooled, got):
     slots, rows, lanes = got[0].shape
-    wide = len(got) == 2
-    far_rows = max(2 * lanes // LANES, 0 if wide else near_layout(lanes, wide)[1]) * SUBLANES
-    out_shape = (jax.ShapeDtypeStruct((len(got), SUBLANES, lanes), jnp.float32),) + (
-        jax.ShapeDtypeStruct((far_rows, LANES), jnp.float32),
-    ) * n_far
-    halos, *far = pl.pallas_call(
-        functools.partial(pack_far_kernel, wide),
-        out_shape=out_shape,
-        in_specs=[VMEM] * (1 + len(got)),
-        out_specs=(VMEM,) * len(out_shape),
+    return pl.pallas_call(
+        functools.partial(halos_kernel, len(got) == 2),
+        out_shape=(
+            jax.ShapeDtypeStruct((len(got), SUBLANES, lanes), jnp.float32),
+            jax.ShapeDtypeStruct((SUBLANES, LANES), jnp.float32),
+        ),
+        in_specs=[VMEM] * (2 + len(got)),
+        out_specs=(VMEM,) * 2,
         scratch_shapes=[pltpu.VMEM((lanes // LANES, 2 * SUBLANES, LANES), jnp.float32)],
         compiler_params=pltpu.CompilerParams(vmem_limit_bytes=8 << 20),
         cost_estimate=AHEAD,
+        name="halos",
+    )(both, pooled, *got)
+
+
+def pack_far_kernel(wide, pooled_ref, halo_ref, lanes_ref, *far_refs):
+    half = pooled_ref.shape[2] // 2
+    low = lax.axis_index("gx") % 4 < 2
+
+    def tiles(inner):
+        return (
+            pooled_ref[inner, :, :half],
+            pooled_ref[1 - inner, :, :half],
+            pooled_ref[inner, :, half:],
+            halo_ref[0, :, inner * half : (inner + 1) * half],
+        )
+
+    for group, ref in enumerate(far_refs):
+        for i, (right, left) in enumerate(zip(tiles(1), tiles(0))):
+            put(ref, i * (half // LANES), jnp.where(low, *((right, left) if group == 0 else (left, right))))
+        put(ref, 4 * (half // LANES), lanes_ref[...])
+        for spare in range(4 * (half // LANES) + 1, ref.shape[0] // SUBLANES):
+            put(ref, spare, jnp.zeros((SUBLANES, LANES), jnp.float32))
+
+
+def pack_far(pooled, halos, early, n_far, wide):
+    _, rows, lanes = pooled.shape
+    far_rows = max(2 * lanes // LANES + 1, 0 if wide else near_layout(lanes, wide)[1]) * SUBLANES
+    return pl.pallas_call(
+        functools.partial(pack_far_kernel, wide),
+        out_shape=(jax.ShapeDtypeStruct((far_rows, LANES), jnp.float32),) * n_far,
+        in_specs=[VMEM] * 3,
+        out_specs=(VMEM,) * n_far,
+        compiler_params=pltpu.CompilerParams(vmem_limit_bytes=8 << 20),
+        cost_estimate=pl.CostEstimate(flops=1_000_000, bytes_accessed=500_000, transcendentals=0),
         name="pack_far",
-    )(pooled, *got)
-    return halos, far
-
-
-def pack_near_kernel(wide, pooled_ref, halo_ref, after_ref, *refs):
+    )(pooled, halos, early)
+
+
+def pack_near_kernel(wide, pooled_ref, halo_ref, early_ref, after_ref, *refs):
     *got_refs, first_ref, second_ref = refs
     layers, lanes = got_refs[0].shape[0] - 1, got_refs[0].shape[2]
     ix, iy = lax.axis_index("gx"), lax.axis_index("gy")
@@ -587,8 +615,19 @@
     halos = [halo_ref[i // 2, :, (i % 2) * half : (i % 2 + 1) * half] for i in range(4 if wide else 2)]
     sources = [pooled_ref[x, :, half:] for x in range(2)]
 
-    def near_tiles(order):
+    slots, shared = lane_slots(layers, 2, len(got_refs))
+
+    def strip_lanes(layer):
+        tiles = tuple(read_lanes(early_ref[...], slots["got", g, layer]) for g in range(len(got_refs)))
+        return from_right(even, tiles), from_left(even, tiles)
+
+    def halo_lanes(i):
+        return read_lanes(early_ref[...], slots["halo", i // 2, i % 2])
+
+    def near_tiles(order, strips, halos):
         near, beyond = order[0] // 2, order[-1] // 2
+        width = strips[0][0].shape[1]
+        upper = iota((SUBLANES, width), 0) < REACH
         if wide:
             log_rows = [jnp.where(upper, *strips[layer]) for layer in range(layers)]
             source_rows = [turned(jnp.where(upper, *strips[layer][::-1]), REACH, 0) for layer in range(layers)]
@@ -601,109 +640,88 @@
                 "halo1": halos[beyond],
                 "halo2": halos[2 + near],
                 "halo3": halos[2 + beyond],
-                "source": sources[beyond],
             }
         first, second, third = (strips[layer][0] for layer in order[:3])
-        place = iota((SUBLANES, lanes), 0)
+        place = iota((SUBLANES, width), 0)
         right = jnp.where(place == 3, turned(third, 3, 0), jnp.where(place >= 6, turned(second, -2, 0), first))
         left = jnp.where(place == 4, turned(third, -3, 0), jnp.where(place < 2, turned(second, 2, 0), first))
         line = jnp.where(starts, second[4:5], second[3:4])
-        lines = jnp.zeros((SUBLANES, LANES), jnp.float32)
-        for j in range(lanes // LANES):
-            lines = jnp.where(iota(lines.shape, 0) == j, line[:, j * LANES : (j + 1) * LANES], lines)
+        if width == LANES:
+            lines = jnp.broadcast_to(line, (SUBLANES, LANES))
+        else:
+            lines = jnp.zeros((SUBLANES, LANES), jnp.float32)
+            for j in range(width // LANES):
+                lines = jnp.where(iota(lines.shape, 0) == j, line[:, j * LANES : (j + 1) * LANES], lines)
         return {
             "strip": jnp.where(starts, right, left),
             "halo": join_halo(halos[near], halos[beyond], starts),
-            "source": sources[beyond],
             "row": lines,
         }
 
+    def side(order):
+        tiles = near_tiles(order, strips, halos)
+        tiles["source"] = sources[order[-1] // 2]
+        lanes_tile = early_ref[...]
+        n_halos = 4 if wide else 2
+        beside = near_tiles(
+            order, [strip_lanes(layer) for layer in range(layers)], [halo_lanes(i) for i in range(n_halos)]
+        )
+        for name, slot in near_lane_slots(lanes, wide, shared).items():
+            lanes_tile = add_lanes(lanes_tile, slot, beside[name])
+        tiles["lanes"] = lanes_tile
+        return tiles
+
     forward = list(range(layers))
     layout, _ = near_layout(lanes, wide)
-    right, left = near_tiles(forward[::-1]), near_tiles(forward)
+    right, left = side(forward[::-1]), side(forward)
     for name, (start, _) in layout.items():
         put(first_ref, start, jnp.where(ix % 2 == 0, right[name], left[name]))
         put(second_ref, start, jnp.where(ix % 2 == 0, left[name], right[name]))
 
 
-def pack_near(pooled, halos, after, got):
+def pack_near(pooled, halos, early, after, got):
     slots, rows, lanes = got[0].shape
     wide = len(got) == 2
     out = jax.ShapeDtypeStruct((near_layout(lanes, wide)[1] * SUBLANES, LANES), jnp.float32)
     return pl.pallas_call(
         functools.partial(pack_near_kernel, wide),
         out_shape=(out, out),
-        in_specs=[VMEM, VMEM, ANY] + [VMEM] * len(got),
+        in_specs=[VMEM] * 3 + [ANY] + [VMEM] * len(got),
         out_specs=(VMEM,) * 2,
         compiler_params=pltpu.CompilerParams(vmem_limit_bytes=8 << 20),
-        cost_estimate=AHEAD,
+        cost_estimate=pl.CostEstimate(flops=1_000_000, bytes_accessed=500_000, transcendentals=0),
         name="pack_near",
-    )(pooled, halos, after, *got)
-
-
-def landed_kernel(after_ref, both_ref, pooled_ref, halo_ref, first_ref, second_ref, *refs):
-    *got_refs, out_ref, sent_ref, sum_ref = refs
-    log_ref, source_ref = parts(both_ref)
-    layers, rows, lanes = log_ref.shape
-    half = lanes // 2
+    )(pooled, halos, early, after, *got)
+
+
+def pool_kernel(after_ref, first_ref, second_ref, out_ref, sum_ref):
+    layers = REACH
     even = lax.axis_index("gx") % 2 == 0
-    slots = early_slots(layers, rows // SUBLANES, len(got_refs))
-    pairs = {}
-    for a, ref in enumerate((log_ref, source_ref)):
-        for layer in range(layers):
-            for i in range(rows // SUBLANES):
-                pairs["own", a, layer, i] = edges(ref.at[layer, i * SUBLANES : (i + 1) * SUBLANES])
-    for g, ref in enumerate(got_refs):
-        for layer in range(layers):
-            pairs["got", g, layer] = edges(ref.at[layer])
-    for i in range(2):
-        for x in range(2):
-            columns = slice(x * half, (x + 1) * half)
-            pairs["pooled", i, x] = edges(pooled_ref.at[i, :, columns])
-            if i < len(got_refs):
-                pairs["halo", i, x] = edges(halo_ref.at[i, :, columns])
     pieces = []
     for side, pick in enumerate((from_left, from_right)):
 
         def block(slot):
             return pick(even, (first_ref[slot], second_ref[slot]))
 
-        for slot in range(2 * layers - 1):
-            for i in range(rows // SUBLANES):
-                part = slice(i * SUBLANES, (i + 1) * SUBLANES)
-                ends = [edges(ref.at[slot, part]) for ref in (first_ref, second_ref)]
-                pairs["raw", side, slot, i] = [
-                    pick(even, tuple(end[...] for end in both)) for both in zip(*ends)
-                ]
-        nearest = layers + 1 if side == 0 else layers
-        for top in (0, 2, nearest):
+        for top in (0, 2, layers + 1 if side == 0 else layers):
             both = block(top) + block(top + 1)
             pieces.append(row_pairs(both[:SUBLANES], both[SUBLANES:], sum_ref))
-    tiles = lane_pairs(pieces)
-    for side in range(2):
-        for i in range(3):
-            tile = tiles[3 * side + i] * (0.125 if i < 2 else 1.0)
-            put(out_ref, (3 * side + i) * (half // LANES), tile)
-            pairs["near", side, i] = edges(tile)
-    write_lanes(sent_ref, [tuple(end[...] for end in pairs[key]) for key in slots])
-
-
-def landed(after, both, pooled, halos, raw, got):
-    layers, rows, lanes = both.shape[0] // 2, *both.shape[1:]
-    slots = early_slots(layers, rows // SUBLANES, len(got))
+    for i, tile in enumerate(lane_pairs(pieces)):
+        put(out_ref, i * (tile.shape[1] // LANES), tile * (0.125 if i % 3 < 2 else 1.0))
+
+
+def pool(after, raw):
+    _, rows, lanes = raw[0].shape
     return pl.pallas_call(
-        landed_kernel,
-        out_shape=(
-            jax.ShapeDtypeStruct((6 * (lanes // 2 // LANES) * SUBLANES, LANES), jnp.float32),
-            packed_rows(slots),
-        ),
-        in_specs=[ANY] + [VMEM] * (5 + len(got)),
-        out_specs=(VMEM,) * 2,
+        pool_kernel,
+        out_shape=jax.ShapeDtypeStruct((6 * (lanes // 2 // LANES) * SUBLANES, LANES), jnp.float32),
+        in_specs=[ANY] + [VMEM] * 2,
+        out_specs=VMEM,
         scratch_shapes=[pltpu.VMEM((lanes // LANES, 2 * SUBLANES, LANES), jnp.float32)],
         compiler_params=pltpu.CompilerParams(vmem_limit_bytes=16 << 20),
         cost_estimate=pl.CostEstimate(flops=1_000_000, bytes_accessed=1_000_000, transcendentals=0),
-        name="landed",
-    )(after, both, pooled, halos, *raw, *got)
+        name="pool",
+    )(after, *raw)
 
 
 def near_part(refs, even, lanes, wide, side, name):
@@ -719,33 +737,9 @@
     return pick(low, tuple(take(ref, i * count, count) for ref in refs))
 
 
-def late_kernel(lanes, wide, after_ref, first_ref, second_ref, *refs):
-    *far_refs, sent_ref = refs
-    even, low = lax.axis_index("gx") % 2 == 0, lax.axis_index("gx") % 4 < 2
-    pairs = []
-    for side, name in late_slots(lanes, wide):
-        if name == "far":
-            pairs.append(edges(far_part(far_refs, low, lanes, side, 0)))
-        else:
-            pairs.append(edges(near_part((first_ref, second_ref), even, lanes, wide, side, name)))
-    write_lanes(sent_ref, pairs)
-
-
-def late_lanes(after, near, far, lanes, wide):
-    return pl.pallas_call(
-        functools.partial(late_kernel, lanes, wide),
-        out_shape=packed_rows(late_slots(lanes, wide)),
-        in_specs=[ANY] + [VMEM] * (2 + len(far)),
-        out_specs=VMEM,
-        compiler_params=pltpu.CompilerParams(vmem_limit_bytes=8 << 20),
-        cost_estimate=pl.CostEstimate(flops=1_000_000, bytes_accessed=200_000, transcendentals=0),
-        name="late_lanes",
-    )(after, *near, *far)
-
-
 def coarse_kernel(peers, n_far, own_ref, halo_ref, pool_ref, first_ref, second_ref, *refs):
     near_refs, far_refs = (first_ref, second_ref), refs[:n_far]
-    early_ref, late_ref, coef_ref, out_ref, wide_ref, *scratch = refs[n_far:]
+    early_ref, coef_ref, out_ref, wide_ref, *scratch = refs[n_far:]
     ix, iy, iz = (lax.axis_index(axis) for axis in AXES)
     nx, ny, nz = peers
     wide = ny > 2
@@ -753,22 +747,28 @@
     lanes, rows = fine_lanes // 2, SUBLANES
     even, low, starts = ix % 2 == 0, ix % 4 < 2, iy == 0
     top = iota((rows, lanes + LANES), 0) < REACH
-    early = early_slots(REACH, 2, 2 if wide else 1)
-    late = late_slots(fine_lanes, wide)
+    slots, shared = lane_slots(REACH, 2, 2 if wide else 1)
+    near_slots = near_lane_slots(fine_lanes, wide, shared)
+    own_lanes = early_ref[...]
+    near_lanes = [near_part(near_refs, even, fine_lanes, wide, side, "lanes") for side in range(2)]
+    far_lanes = [
+        pick(low, tuple(take(ref, 4 * (lanes // LANES), 1) for ref in far_refs))
+        for pick in (from_left, from_right)
+    ]
 
     def columns(half):
         return slice(half * lanes, (half + 1) * lanes)
 
-    def with_early(core, *key):
-        return jnp.concatenate([core, read_lanes(early_ref, early[key])], axis=1)
+    def join(core, tile, slot):
+        return jnp.concatenate([core, read_lanes(tile, slot)], axis=1)
 
     def near(side, name):
         core = near_part(near_refs, even, fine_lanes, wide, side, name)
-        return jnp.concatenate([core, read_lanes(late_ref, late[side, name])], axis=1)
+        return join(core, near_lanes[side], near_slots[name])
 
     def far(side, i):
         core = far_part(far_refs, low, fine_lanes, side, i)
-        return jnp.concatenate([core, read_lanes(late_ref, late[side, "far"])], axis=1)
+        return join(core, far_lanes[side], slots["pooled", 1 - side, 0])
 
     def split(tile, a):
         other = turned(tile, REACH, 0)
@@ -786,18 +786,18 @@
             halo = halo if wide else split(halo, 0)
             return jnp.concatenate([far(side, 0 if nearest else 1), halo], axis=0)
         if block == 0:
-            core = with_early(own_ref[layer, :, columns(a)], "pooled", layer, a)
+            core = join(own_ref[layer, :, columns(a)], own_lanes, slots["pooled", layer, a])
             if wide:
-                halo = with_early(halo_ref[a, :, columns(layer)], "halo", a, layer)
+                halo = join(halo_ref[a, :, columns(layer)], own_lanes, slots["halo", a, layer])
             else:
-                halo = split(with_early(halo_ref[0, :, columns(layer)], "halo", 0, layer), a)
+                halo = split(join(halo_ref[0, :, columns(layer)], own_lanes, slots["halo", 0, layer]), a)
             return jnp.concatenate([core, halo], axis=0)
         if a == 0 or nearest:
             i = layer if a == 0 else 2
             core = take(pool_ref, (3 * side + i) * (lanes // LANES), lanes // LANES)
-            core = with_early(core, "near", side, i)
         else:
-            core = near(side, "source")
+            core = near_part(near_refs, even, fine_lanes, wide, side, "source")
+        core = join(core, near_lanes[side], slots["pooled", layer, a])
         if wide:
             halo = near(side, f"halo{2 * a + (0 if nearest else 1)}")
         else:
@@ -842,13 +842,13 @@
                 out_ref[2 * x + twin, :, part] = wide_ref[tile]
 
 
-def coarse_level(own, halos, pooled, near, far, early, late, coefficients, peers):
+def coarse_level(own, halos, pooled, near, far, early, coefficients, peers):
     lanes = own.shape[2] // 2
     window = (2 + 2 * REACH, SUBLANES, 2 * SUBLANES, lanes // LANES + 1)
     return pl.pallas_call(
         functools.partial(coarse_kernel, peers, len(far)),
         out_shape=jax.ShapeDtypeStruct((REACH, 2 * SUBLANES, 2 * lanes), jnp.float32),
-        in_specs=[VMEM] * (8 + len(far)),
+        in_specs=[VMEM] * (7 + len(far)),
         out_specs=VMEM,
         scratch_shapes=[pltpu.VMEM((2 * lanes // LANES, 2 * SUBLANES, LANES), jnp.float32)]
         + window_scratch(*window)
@@ -856,7 +856,7 @@
         compiler_params=pltpu.CompilerParams(vmem_limit_bytes=24 << 20),
         cost_estimate=pl.CostEstimate(flops=20_000_000, bytes_accessed=4_000_000, transcendentals=0),
         name="coarse_level",
-    )(own, halos, pooled, *near, *far, early, late, coefficients)
+    )(own, halos, pooled, *near, *far, early, coefficients)
 
 
 def fine_kernel(peers, n_far, both_ref, *refs):
@@ -868,21 +868,23 @@
     n_got = 2 if wide else 1
     got_refs, refs = refs[:n_got], refs[n_got:]
     second_ref, first_ref = refs[:2]
-    second_near_ref, first_near_ref, early_ref, late_ref, spread_ref = refs[2 + n_far : 7 + n_far]
-    coef_ref, fine_ref, diff_ref, *scratch = refs[7 + n_far :]
+    second_near_ref, first_near_ref, early_ref, spread_ref = refs[2 + n_far : 6 + n_far]
+    near_refs = first_near_ref, second_near_ref
+    coef_ref, fine_ref, diff_ref, *scratch = refs[6 + n_far :]
     even, starts = ix % 2 == 0, iy == 0
     count = 3 * layers
     upper = iota((SUBLANES, lanes + LANES), 0) < REACH
-    early = early_slots(layers, rows // SUBLANES, n_got)
-    late = late_slots(lanes, wide)
-
-    def with_early(core, *keys):
-        tile = jnp.concatenate([read_lanes(early_ref, early[key]) for key in keys], axis=0)
-        return jnp.concatenate([core, tile], axis=1)
+    slots, shared = lane_slots(layers, rows // SUBLANES, n_got)
+    near_slots = near_lane_slots(lanes, wide, shared)
+    own_lanes = early_ref[...]
+    near_lanes = [near_part(near_refs, even, lanes, wide, side, "lanes") for side in range(2)]
+
+    def join(core, tile, *keys):
+        beside = jnp.concatenate([read_lanes(tile, key) for key in keys], axis=0)
+        return jnp.concatenate([core, beside], axis=1)
 
     def near(side, name):
-        core = near_part((first_near_ref, second_near_ref), even, lanes, wide, side, name)
-        return jnp.concatenate([core, read_lanes(late_ref, late[side, name])], axis=1)
+        return join(near_part(near_refs, even, lanes, wide, side, name), near_lanes[side], near_slots[name])
 
     def near_halo(a, side, distance):
         if wide:
@@ -899,8 +901,10 @@
         block, layer = k // layers - 1, k % layers
         if block == 0:
             core = (log_ref, source_ref)[a][layer]
-            core = with_early(core, *(("own", a, layer, i) for i in range(rows // SUBLANES)))
-            tiles = tuple(with_early(ref[layer], ("got", g, layer)) for g, ref in enumerate(got_refs))
+            core = join(core, own_lanes, *(slots["own", a, layer, i] for i in range(rows // SUBLANES)))
+            tiles = tuple(
+                join(ref[layer], own_lanes, slots["got", g, layer]) for g, ref in enumerate(got_refs)
+            )
             halo = tiles[0]
             if wide:
                 sides = from_right(iy % 2 == 0, tiles), from_left(iy % 2 == 0, tiles)
@@ -911,7 +915,7 @@
         side, pick = (0, from_left) if block < 0 else (1, from_right)
         slot = layer if a == 0 else layers + layer - (1 if block < 0 else 0)
         core = pick(even, (first_ref[slot], second_ref[slot]))
-        core = with_early(core, *(("raw", side, slot, i) for i in range(rows // SUBLANES)))
+        core = join(core, near_lanes[side], *(slots["own", a, layer, i] for i in range(rows // SUBLANES)))
         halo = near_halo(a, side, layers - layer if block < 0 else layer + 1)
         return jnp.concatenate([core, halo], axis=0)
 
@@ -941,20 +945,20 @@
     )
 
 
-def fine_level(both, got, raw, far, near, early, late, spread, coefficients, peers):
+def fine_level(both, got, raw, far, near, early, spread, coefficients, peers):
     layers, rows, lanes = spread.shape
     window = (layers + 2 * REACH, rows, rows + 2 * REACH, lanes // LANES + 1)
     out = jax.ShapeDtypeStruct(spread.shape, jnp.float32)
     return pl.pallas_call(
         functools.partial(fine_kernel, peers, len(far)),
         out_shape=(out, out),
-        in_specs=[VMEM] * (3 + len(got)) + [ANY] * len(far) + [VMEM] * 6,
+        in_specs=[VMEM] * (3 + len(got)) + [ANY] * len(far) + [VMEM] * 5,
         out_specs=(VMEM, VMEM),
         scratch_shapes=window_scratch(*window),
         compiler_params=pltpu.CompilerParams(vmem_limit_bytes=24 << 20),
         cost_estimate=pl.CostEstimate(flops=20_000_000, bytes_accessed=10_000_000, transcendentals=0),
         name="fine_level",
-    )(both, *got, *raw[::-1], *far, *near[::-1], early, late, spread, coefficients)
+    )(both, *got, *raw[::-1], *far, *near[::-1], early, spread, coefficients)
 
 
 def shards(peers, log_perm, source, low_bound, high_bound):
@@ -972,18 +976,17 @@
     for_first = raw_block(both, for_second, False)
     raw = (permute(for_first, "gx", nx, neighbour_pairs(nx, 0)), second)
     far_groups = far_pairs(nx)
-    halos, for_far = pack_far(own, got, len(far_groups))
+    halos, lanes_sent = pooled_halos(both, own, got)
+    early = lax.ppermute(lanes_sent, "gz", [(0, 1), (1, 0)])
+    for_far = pack_far(own, halos, early, len(far_groups), ny > 2)
     far = [permute(tiles, "gx", nx, group) for tiles, group in zip(for_far, far_groups)]
-    for_first, for_second = pack_near(own, halos, for_far[0], got)
+    for_first, for_second = pack_near(own, halos, early, for_far[0], got)
     second = permute(for_second, "gx", nx, neighbour_pairs(nx, 1))
     near = (permute(for_first, "gx", nx, neighbour_pairs(nx, 0)), second)
     coefficients = chebyshev_coefficients(low_bound, high_bound, for_first)
-    pooled, early_sent = landed(coefficients, both, own, halos, raw, got)
-    early = lax.ppermute(early_sent, "gz", [(0, 1), (1, 0)])
-    late_sent = late_lanes(early_sent, near, far, lanes, ny > 2)
-    late = lax.ppermute(late_sent, "gz", [(0, 1), (1, 0)])
-    spread = coarse_level(own, halos, pooled, near, far, early, late, coefficients, peers)
-    return fine_level(both, got, raw, far, near, early, late, spread, coefficients, peers)
+    pooled = pool(coefficients, raw)
+    spread = coarse_level(own, halos, pooled, near, far, early, coefficients, peers)
+    return fine_level(both, got, raw, far, near, early, spread, coefficients, peers)
 
 
 def solution(mesh):

time: 19.7 us -> 19.5 us (0.990)
  starting transfers between devices: 10.5 us -> 10.2 us
    ppermute x2 -> x1, starting transfers between devices: 0.24 us -> 0.03 us  [shards(): early = lax.ppermute(lanes_sent, 'gz', [(0, 1), (1, 0)])]
    ppermute x2 -> x1, waiting for transfers between devices: 0.98 us -> 1.15 us  [shards(): early = lax.ppermute(lanes_sent, 'gz', [(0, 1), (1, 0)])]
  transfers between devices with their start and end apart: 8 -> 7, of which waited for: 2 -> 2; matrix products, arithmetic and copies ran while one was open for 0% -> 0% of each run, Pallas kernels for 6% -> 7%
where the time goes in v11:
time: 19.5 us; the launch traced here: 19.4 us
  starting transfers between devices  10.2 us (52%)
  Pallas kernels  4.72 us (24%)
  between operations  2.06 us (11%)
  waiting for transfers between devices  1.39 us (7%)
  local copies, waits for them, and re-layouts  0.97 us (5%)
    ppermute x6, starting transfers between devices, permute(): return lax.ppermute(value, (axis, 'gz'), moves)  10.2 us
    pallas_call x1, Pallas kernels, fine_level(): pl.pallas_call(functools.partial(fine_kernel, peers, len(far)), out_shape...  2.52 us
    ppermute x1, waiting for transfers between devices, shards(): early = lax.ppermute(lanes_sent, 'gz', [(0, 1), (1, 0)])  1.15 us
    unnamed x3, local copies, waits for them, and re-layouts  0.96 us
    pallas_call x1, Pallas kernels, coarse_level(): pl.pallas_call(functools.partial(coarse_kernel, peers, len(far)), out_sha...  0.73 us
    pallas_call x1, Pallas kernels, chebyshev_coefficients(): pl.pallas_call(coefficients_kernel, out_shape=jax.ShapeDtypeStruct((1 + 2...  0.61 us
  transfers between devices with their start and end apart: 7, of which 2 were waited for; matrix products, arithmetic and copies ran while one was open for 0% of the time, Pallas kernels for 7%

profile of v11, /device:TPU:0, one launch (start us, length us, event | category | flops | bytes accessed | tf_op | source)
XLA Modules:
  0.0 19.4 jit_solution(13224243731490418440)
XLA Ops:
  0.6 0.0 copy-start
  0.6 0.9 %constant_dynamic-update-slice_fusion.1 = f32[8,16,512]{2,1,0:T(8,128)S(1)} fusion(f32[4,16,512]{2,1,0:T(8,128)} %param.4), kind=kLoop, calls=%fused_computation.1 | loop fusion | bytes 262144
  1.6 0.0 copy-done
  1.6 0.2 %prep.1 = (f32[2,8,512]{2,1,0:T(8,128)S(1)}, f32[5,8,512]{2,1,0:T(8,128)S(1)}) custom-call(f32[8,16,512]{2,1,0:T(8,128)S(1)} %constant_dynamic-update-slice_fusion.both_ref), custom_call_target="tpu_custom_call" | custom-call | flops 5000000 | bytes 700000 | tf_op jit(solution)/shard_map/prep/pallas_call | solution.py:443
  1.8 3.0 %collective-permute-start = (f32[5,8,512]{2,1,0:T(8,128)S(1)}, f32[5,8,512]{2,1,0:T(8,128)S(1)}, u32[]{:S(2)}, u32[]{:S(2)}) collective-permute-start(f32[5,8,512]{2,1,0:T(8,128)S(1)} %get-tuple-element.8.after_ref), channel_id=1, source_target_pairs={{0,2},{1,3},{2,0},{3,1},{4,6},{5,7},{6,4},{7,5},{8,10},{9,11},{10,... | collective-permute-start | bytes 245768 | tf_op jit(solution)/shard_map/ppermute | solution.py:45
  4.9 0.1 collective-permute-start.1
  5.0 3.2 %collective-permute-start.2 = (f32[7,16,512]{2,1,0:T(8,128)S(1)}, f32[7,16,512]{2,1,0:T(8,128)S(1)}, u32[]{:S(2)}, u32[]{:S(2)}) collective-permute-start(f32[7,16,512]{2,1,0:T(8,128)S(1)} %raw_block.3), channel_id=1, source_target_pairs={{0,4},{1,5},{4,0},{5,1},{8,12},{9,13},{12,8},{13,9},{2,6},{3,7},{6... | collective-permute-start | bytes 688136 | tf_op jit(solution)/shard_map/ppermute | solution.py:45
  8.2 0.0 collective-permute-done.refs_0_
  8.2 0.2 %halos.1 = (f32[1,8,512]{2,1,0:T(8,128)S(1)}, f32[8,128]{1,0:T(8,128)S(1)}) custom-call(f32[8,16,512]{2,1,0:T(8,128)S(1)} %constant_dynamic-update-slice_fusion.both_ref, f32[2,8,512]{2,1,0:T(8,128)S(1)} %get-tuple-element.9.pooled_ref.own_ref, f32[5,8,512]{2,1,0:T(8,128)S(1)} %collective-permute-done.refs_0_), custom_call_target="tpu_custom_call" | custom-call | flops 49999998976 | bytes 1000000 | tf_op jit(solution)/shard_map/halos/pallas_call | solution.py:553
  8.4 0.0 collective-permute-start.3
  8.4 1.2 %collective-permute-done.3.lanes_ref.early_ref.refs_1_.refs_6_ = f32[8,128]{1,0:T(8,128)S(1)} collective-permute-done((f32[8,128]{1,0:T(8,128)S(1)}, f32[8,128]{1,0:T(8,128)S(1)}, u32[]{:S(2)}, u32[]{:S(2)}) %collective-permute-start.3) | collective-permute-done | bytes 4128 | tf_op jit(solution)/shard_map/ppermute | solution.py:980
  9.6 2.3 %collective-permute-start.4 = (f32[80,128]{1,0:T(8,128)S(1)}, f32[80,128]{1,0:T(8,128)S(1)}, u32[]{:S(2)}, u32[]{:S(2)}) collective-permute-start(f32[80,128]{1,0:T(8,128)S(1)} %pack_far.1.after_ref), channel_id=1, source_target_pairs={{0,8},{1,9},{4,12},{5,13},{8,0},{9,1},{12,4},{13,5},{2,10},{3,11},... | collective-permute-start | bytes 122888 | tf_op jit(solution)/shard_map/ppermute | solution.py:45
  11.9 0.1 pack_near.1
  12.0 0.0 collective-permute-start.5
  12.0 1.6 %collective-permute-start.6 = (f32[80,128]{1,0:T(8,128)S(1)}, f32[80,128]{1,0:T(8,128)S(1)}, u32[]{:S(2)}, u32[]{:S(2)}) collective-permute-start(f32[80,128]{1,0:T(8,128)S(1)} %get-tuple-element.13.after_ref), channel_id=1, source_target_pairs={{0,4},{1,5},{4,0},{5,1},{8,12},{9,13},{12,8},{13,9},{2,6},{3,7},{6... | collective-permute-start | bytes 122888 | tf_op jit(solution)/shard_map/ppermute | solution.py:45
  15.0 0.6 %coefficients.1.after_ref.refs_2_.refs_8_ = f32[7,8,128]{2,1,0:T(8,128)S(1)} custom-call(f32[1]{0:T(128)S(6)} %copy.7.low_ref, f32[1]{0:T(128)S(6)} %copy.8.high_ref, f32[80,128]{1,0:T(8,128)S(1)} %get-tuple-element.13.after_ref), custom_call_target="tpu_custom_call" | custom-call | flops 1000000 | bytes 100000 | tf_op jit(solution)/shard_map/coefficients/pallas_call | solution.py:234
  15.6 0.0 collective-permute-done.2.first_ref.refs_2_
  15.6 0.0 collective-permute-done.1.second_ref.refs_1_
  15.6 0.2 %pool.1.pool_ref = f32[96,128]{1,0:T(8,128)S(1)} custom-call(f32[7,8,128]{2,1,0:T(8,128)S(1)} %coefficients.1.after_ref.refs_2_.refs_8_, f32[7,16,512]{2,1,0:T(8,128)S(1)} %collective-permute-done.2.first_ref.refs_2_, f32[7,16,512]{2,1,0:T(8,128)S(1)} %collective-permute-done.1.second_ref.refs_1_), custom_call_target="tpu_custom_call" | custom-call | flops 1000000 | bytes 1000000 | tf_op jit(solution)/shard_map/pool/pallas_call | solution.py:715
  15.9 0.0 collective-permute-done.4.refs_0_.refs_3_
  15.9 0.0 collective-permute-done.5.second_ref.refs_4_
  15.9 0.2 %collective-permute-done.6.first_ref.refs_5_ = f32[80,128]{1,0:T(8,128)S(1)} collective-permute-done((f32[80,128]{1,0:T(8,128)S(1)}, f32[80,128]{1,0:T(8,128)S(1)}, u32[]{:S(2)}, u32[]{:S(2)}) %collective-permute-start.6) | collective-permute-done | bytes 40992 | tf_op jit(solution)/shard_map/ppermute | solution.py:45
  16.1 0.7 %coarse_level.1.refs_7_ = f32[4,16,512]{2,1,0:T(8,128)S(1)} custom-call(f32[2,8,512]{2,1,0:T(8,128)S(1)} %get-tuple-element.9.pooled_ref.own_ref, f32[1,8,512]{2,1,0:T(8,128)S(1)} %get-tuple-element.10.halo_ref, f32[96,128]{1,0:T(8,128)S(1)} %pool.1.pool_ref, f32[80,128]{1,0:T(8,128)S(1)} %collective-permute-done.6.first_ref.refs_5_, ...), custom_call_target="tpu_custom_call" | custom-call | flops 20000000 | bytes 4000000 | tf_op jit(solution)/shard_map/coarse_level/pallas_call | solution.py:848
  16.8 2.5 %fine_level.1 = (f32[4,16,512]{2,1,0:T(8,128)}, f32[4,16,512]{2,1,0:T(8,128)}) custom-call(f32[8,16,512]{2,1,0:T(8,128)S(1)} %constant_dynamic-update-slice_fusion.both_ref, f32[5,8,512]{2,1,0:T(8,128)S(1)} %collective-permute-done.refs_0_, f32[7,16,512]{2,1,0:T(8,128)S(1)} %collective-permute-done.1.second_ref.refs_1_, ...), custom_call_target="tpu_custom_call" | custom-call | flops 20000000 | bytes 10000000 | tf_op jit(solution)/shard_map/fine_level/pallas_call | solution.py:952
  (4 shorter events, 0.1 us)
Async XLA Ops:
  0.6 1.0 %copy-start = (f32[4,16,512]{2,1,0:T(8,128)S(1)}, f32[4,16,512]{2,1,0:T(8,128)}, u32[]{:S(2)}) copy-start(f32[4,16,512]{2,1,0:T(8,128)} %param.5) | copy-start | bytes 393220
  1.8 6.3 %collective-permute-start = (f32[5,8,512]{2,1,0:T(8,128)S(1)}, f32[5,8,512]{2,1,0:T(8,128)S(1)}, u32[]{:S(2)}, u32[]{:S(2)}) collective-permute-start(f32[5,8,512]{2,1,0:T(8,128)S(1)} %get-tuple-element.8.after_ref), channel_id=1, source_target_pairs={{0,2},{1,3},{2,0},{3,1},{4,6},{5,7},{6,4},{7,5},{8,10},{9,11},{10,... | collective-permute-start | bytes 245768 | tf_op jit(solution)/shard_map/ppermute | solution.py:45
  4.9 10.7 %collective-permute-start.1 = (f32[7,16,512]{2,1,0:T(8,128)S(1)}, f32[7,16,512]{2,1,0:T(8,128)S(1)}, u32[]{:S(2)}, u32[]{:S(2)}) collective-permute-start(f32[7,16,512]{2,1,0:T(8,128)S(1)} %raw_block.2.after_ref), channel_id=1, source_target_pairs={{0,1},{1,0},{4,8},{5,9},{8,4},{9,5},{12,13},{13,12},{2,3},{3,2},{6... | collective-permute-start | bytes 688136 | tf_op jit(solution)/shard_map/ppermute | solution.py:45
  5.0 10.6 %collective-permute-start.2 = (f32[7,16,512]{2,1,0:T(8,128)S(1)}, f32[7,16,512]{2,1,0:T(8,128)S(1)}, u32[]{:S(2)}, u32[]{:S(2)}) collective-permute-start(f32[7,16,512]{2,1,0:T(8,128)S(1)} %raw_block.3), channel_id=1, source_target_pairs={{0,4},{1,5},{4,0},{5,1},{8,12},{9,13},{12,8},{13,9},{2,6},{3,7},{6... | collective-permute-start | bytes 688136 | tf_op jit(solution)/shard_map/ppermute | solution.py:45
  8.4 1.2 %collective-permute-start.3 = (f32[8,128]{1,0:T(8,128)S(1)}, f32[8,128]{1,0:T(8,128)S(1)}, u32[]{:S(2)}, u32[]{:S(2)}) collective-permute-start(f32[8,128]{1,0:T(8,128)S(1)} %get-tuple-element.11), channel_id=1, source_target_pairs={{0,1},{1,0},{2,3},{3,2},{4,5},{5,4},{6,7},{7,6},{8,9},{9,8},{10,11... | collective-permute-start | bytes 12296 | tf_op jit(solution)/shard_map/ppermute | solution.py:980
  9.6 6.3 %collective-permute-start.4 = (f32[80,128]{1,0:T(8,128)S(1)}, f32[80,128]{1,0:T(8,128)S(1)}, u32[]{:S(2)}, u32[]{:S(2)}) collective-permute-start(f32[80,128]{1,0:T(8,128)S(1)} %pack_far.1.after_ref), channel_id=1, source_target_pairs={{0,8},{1,9},{4,12},{5,13},{8,0},{9,1},{12,4},{13,5},{2,10},{3,11},... | collective-permute-start | bytes 122888 | tf_op jit(solution)/shard_map/ppermute | solution.py:45
  12.0 3.9 %collective-permute-start.5 = (f32[80,128]{1,0:T(8,128)S(1)}, f32[80,128]{1,0:T(8,128)S(1)}, u32[]{:S(2)}, u32[]{:S(2)}) collective-permute-start(f32[80,128]{1,0:T(8,128)S(1)} %get-tuple-element.12), channel_id=1, source_target_pairs={{0,1},{1,0},{4,8},{5,9},{8,4},{9,5},{12,13},{13,12},{2,3},{3,2},{6... | collective-permute-start | bytes 122888 | tf_op jit(solution)/shard_map/ppermute | solution.py:45
  12.0 4.1 %collective-permute-start.6 = (f32[80,128]{1,0:T(8,128)S(1)}, f32[80,128]{1,0:T(8,128)S(1)}, u32[]{:S(2)}, u32[]{:S(2)}) collective-permute-start(f32[80,128]{1,0:T(8,128)S(1)} %get-tuple-element.13.after_ref), channel_id=1, source_target_pairs={{0,4},{1,5},{4,0},{5,1},{8,12},{9,13},{12,8},{13,9},{2,6},{3,7},{6... | collective-permute-start | bytes 122888 | tf_op jit(solution)/shard_map/ppermute | solution.py:45

commit v12 on v11

--- a/solution.py
+++ b/solution.py
@@ -15,7 +15,6 @@
 AXES = ("gx", "gy", "gz")
 VMEM = pl.BlockSpec(memory_space=pltpu.VMEM)
 ANY = pl.BlockSpec(memory_space=pl.ANY)
-HBM = pl.BlockSpec(memory_space=pltpu.HBM)
 
 
 AHEAD = pl.CostEstimate(flops=50_000_000_000, bytes_accessed=1_000_000, transcendentals=0)
@@ -210,15 +209,8 @@
                         new[k, j, middle] = fresh
 
 
-def coefficients_kernel(low_ref, high_ref, after_ref, coef_ref, bounds_ref, sems):
-    copies = [
-        pltpu.make_async_copy(ref, bounds_ref.at[i], sems.at[i]) for i, ref in enumerate((low_ref, high_ref))
-    ]
-    for copy in copies:
-        copy.start()
-    for copy in copies:
-        copy.wait()
-    low, high = (jnp.full((SUBLANES, LANES), bounds_ref[i, 0]) for i in range(2))
+def coefficients_kernel(low_ref, high_ref, after_ref, coef_ref):
+    low, high = (jnp.full((SUBLANES, LANES), ref[0]) for ref in (low_ref, high_ref))
     theta, delta = (high + low) * 0.5, (high - low) * 0.5
     sigma = theta / delta
     rho = 1.0 / sigma
@@ -234,9 +226,8 @@
     return pl.pallas_call(
         coefficients_kernel,
         out_shape=jax.ShapeDtypeStruct((1 + 2 * DEGREE, SUBLANES, LANES), jnp.float32),
-        in_specs=[HBM] * 2 + [ANY],
+        in_specs=[pl.BlockSpec(memory_space=pltpu.SMEM)] * 2 + [ANY],
         out_specs=VMEM,
-        scratch_shapes=[pltpu.SMEM((2, 1), jnp.float32), pltpu.SemaphoreType.DMA((2,))],
         compiler_params=pltpu.CompilerParams(vmem_limit_bytes=4 << 20),
         cost_estimate=pl.CostEstimate(flops=1_000_000, bytes_accessed=100_000, transcendentals=0),
         name="coefficients",
@@ -581,13 +572,11 @@
         for i, (right, left) in enumerate(zip(tiles(1), tiles(0))):
             put(ref, i * (half // LANES), jnp.where(low, *((right, left) if group == 0 else (left, right))))
         put(ref, 4 * (half // LANES), lanes_ref[...])
-        for spare in range(4 * (half // LANES) + 1, ref.shape[0] // SUBLANES):
-            put(ref, spare, jnp.zeros((SUBLANES, LANES), jnp.float32))
 
 
 def pack_far(pooled, halos, early, n_far, wide):
     _, rows, lanes = pooled.shape
-    far_rows = max(2 * lanes // LANES + 1, 0 if wide else near_layout(lanes, wide)[1]) * SUBLANES
+    far_rows = (2 * lanes // LANES + 1) * SUBLANES
     return pl.pallas_call(
         functools.partial(pack_far_kernel, wide),
         out_shape=(jax.ShapeDtypeStruct((far_rows, LANES), jnp.float32),) * n_far,

time: 19.5 us -> 20.8 us (1.067)
  waiting for transfers between devices: 1.39 us -> 3.26 us
  Pallas kernels: 4.72 us -> 4.13 us
    ppermute x6, waiting for transfers between devices: 0.24 us -> 2.1 us  [permute(): return lax.ppermute(value, (axis, 'gz'), moves)]
    pallas_call x1, Pallas kernels: 0.61 us -> 0.02 us  [chebyshev_coefficients(): pl.pallas_call(coefficients_kernel, out_shape=jax.ShapeDtypeStruct((1 + 2...]
  transfers between devices with their start and end apart: 7 -> 7, of which waited for: 2 -> 2; matrix products, arithmetic and copies ran while one was open for 0% -> 0% of each run, Pallas kernels for 7% -> 3%
where the time goes in v12:
time: 20.8 us; the launch traced here: 20.6 us
  starting transfers between devices  10.2 us (49%)
  Pallas kernels  4.13 us (20%)
  waiting for transfers between devices  3.26 us (16%)
  between operations  2.03 us (10%)
  local copies, waits for them, and re-layouts  0.97 us (5%)
    ppermute x6, starting transfers between devices, permute(): return lax.ppermute(value, (axis, 'gz'), moves)  10.2 us
    pallas_call x1, Pallas kernels, fine_level(): pl.pallas_call(functools.partial(fine_kernel, peers, len(far)), out_shape...  2.52 us
    ppermute x6, waiting for transfers between devices, permute(): return lax.ppermute(value, (axis, 'gz'), moves)  2.1 us
    ppermute x1, waiting for transfers between devices, shards(): early = lax.ppermute(lanes_sent, 'gz', [(0, 1), (1, 0)])  1.15 us
    unnamed x3, local copies, waits for them, and re-layouts  0.96 us
    pallas_call x1, Pallas kernels, coarse_level(): pl.pallas_call(functools.partial(coarse_kernel, peers, len(far)), out_sha...  0.73 us
  transfers between devices with their start and end apart: 7, of which 2 were waited for; matrix products, arithmetic and copies ran while one was open for 0% of the time, Pallas kernels for 3%

profile of v12, /device:TPU:0, one launch (start us, length us, event | category | flops | bytes accessed | tf_op | source)
XLA Modules:
  0.0 20.6 jit_solution(13917280057367259874)
XLA Ops:
  0.6 0.0 copy-start
  0.6 0.9 %constant_dynamic-update-slice_fusion.1 = f32[8,16,512]{2,1,0:T(8,128)S(1)} fusion(f32[4,16,512]{2,1,0:T(8,128)} %param.4), kind=kLoop, calls=%fused_computation.1 | loop fusion | bytes 262144
  1.6 0.0 copy-done
  1.6 0.2 prep.1
  1.8 3.0 %collective-permute-start = (f32[5,8,512]{2,1,0:T(8,128)S(1)}, f32[5,8,512]{2,1,0:T(8,128)S(1)}, u32[]{:S(2)}, u32[]{:S(2)}) collective-permute-start(f32[5,8,512]{2,1,0:T(8,128)S(1)} %get-tuple-element.8.after_ref), channel_id=1, source_target_pairs={{0,2},{1,3},{2,0},{3,1},{4,6},{5,7},{6,4},{7,5},{8,10},{9,11},{10,... | collective-permute-start | bytes 245768 | tf_op jit(solution)/shard_map/ppermute | solution.py:44
  4.9 0.1 collective-permute-start.1
  5.0 3.2 %collective-permute-start.2 = (f32[7,16,512]{2,1,0:T(8,128)S(1)}, f32[7,16,512]{2,1,0:T(8,128)S(1)}, u32[]{:S(2)}, u32[]{:S(2)}) collective-permute-start(f32[7,16,512]{2,1,0:T(8,128)S(1)} %raw_block.3), channel_id=1, source_target_pairs={{0,4},{1,5},{4,0},{5,1},{8,12},{9,13},{12,8},{13,9},{2,6},{3,7},{6... | collective-permute-start | bytes 688136 | tf_op jit(solution)/shard_map/ppermute | solution.py:44
  8.2 0.0 collective-permute-done.refs_0_
  8.2 0.2 %halos.1 = (f32[1,8,512]{2,1,0:T(8,128)S(1)}, f32[8,128]{1,0:T(8,128)S(1)}) custom-call(f32[8,16,512]{2,1,0:T(8,128)S(1)} %constant_dynamic-update-slice_fusion.both_ref, f32[2,8,512]{2,1,0:T(8,128)S(1)} %get-tuple-element.9.pooled_ref.own_ref, f32[5,8,512]{2,1,0:T(8,128)S(1)} %collective-permute-done.refs_0_), custom_call_target="tpu_custom_call" | custom-call | flops 49999998976 | bytes 1000000 | tf_op jit(solution)/shard_map/halos/pallas_call | solution.py:544
  8.4 0.0 collective-permute-start.3
  8.4 1.2 %collective-permute-done.3.lanes_ref.early_ref.refs_1_.refs_6_ = f32[8,128]{1,0:T(8,128)S(1)} collective-permute-done((f32[8,128]{1,0:T(8,128)S(1)}, f32[8,128]{1,0:T(8,128)S(1)}, u32[]{:S(2)}, u32[]{:S(2)}) %collective-permute-start.3) | collective-permute-done | bytes 4128 | tf_op jit(solution)/shard_map/ppermute | solution.py:969
  9.6 0.1 pack_near.1
  9.7 0.2 collective-permute-start.5
  9.9 2.6 %collective-permute-start.6 = (f32[80,128]{1,0:T(8,128)S(1)}, f32[80,128]{1,0:T(8,128)S(1)}, u32[]{:S(2)}, u32[]{:S(2)}) collective-permute-start(f32[80,128]{1,0:T(8,128)S(1)} %get-tuple-element.13.after_ref), channel_id=1, source_target_pairs={{0,4},{1,5},{4,0},{5,1},{8,12},{9,13},{12,8},{13,9},{2,6},{3,7},{6... | collective-permute-start | bytes 122888 | tf_op jit(solution)/shard_map/ppermute | solution.py:44
  12.5 1.2 %collective-permute-start.4 = (f32[72,128]{1,0:T(8,128)S(1)}, f32[72,128]{1,0:T(8,128)S(1)}, u32[]{:S(2)}, u32[]{:S(2)}) collective-permute-start(f32[72,128]{1,0:T(8,128)S(1)} %pack_far.1.after_ref), channel_id=1, source_target_pairs={{0,8},{1,9},{4,12},{5,13},{8,0},{9,1},{12,4},{13,5},{2,10},{3,11},... | collective-permute-start | bytes 110600 | tf_op jit(solution)/shard_map/ppermute | solution.py:44
  15.0 0.0 collective-permute-done.2.first_ref.refs_2_
  15.0 0.0 collective-permute-done.1.second_ref.refs_1_
  15.0 0.2 %pool.1.pool_ref = f32[96,128]{1,0:T(8,128)S(1)} custom-call(f32[7,8,128]{2,1,0:T(8,128)S(1)} %coefficients.1.after_ref.refs_2_.refs_8_, f32[7,16,512]{2,1,0:T(8,128)S(1)} %collective-permute-done.2.first_ref.refs_2_, f32[7,16,512]{2,1,0:T(8,128)S(1)} %collective-permute-done.1.second_ref.refs_1_), custom_call_target="tpu_custom_call" | custom-call | flops 1000000 | bytes 1000000 | tf_op jit(solution)/shard_map/pool/pallas_call | solution.py:704
  15.3 2.1 %collective-permute-done.4.refs_0_.refs_3_ = f32[72,128]{1,0:T(8,128)S(1)} collective-permute-done((f32[72,128]{1,0:T(8,128)S(1)}, f32[72,128]{1,0:T(8,128)S(1)}, u32[]{:S(2)}, u32[]{:S(2)}) %collective-permute-start.4) | collective-permute-done | bytes 36896 | tf_op jit(solution)/shard_map/ppermute | solution.py:44
  17.4 0.0 collective-permute-done.5.second_ref.refs_4_
  17.4 0.0 collective-permute-done.6.first_ref.refs_5_
  17.4 0.7 %coarse_level.1.refs_7_ = f32[4,16,512]{2,1,0:T(8,128)S(1)} custom-call(f32[2,8,512]{2,1,0:T(8,128)S(1)} %get-tuple-element.9.pooled_ref.own_ref, f32[1,8,512]{2,1,0:T(8,128)S(1)} %get-tuple-element.10.halo_ref, f32[96,128]{1,0:T(8,128)S(1)} %pool.1.pool_ref, f32[80,128]{1,0:T(8,128)S(1)} %collective-permute-done.6.first_ref.refs_5_, ...), custom_call_target="tpu_custom_call" | custom-call | flops 20000000 | bytes 4000000 | tf_op jit(solution)/shard_map/coarse_level/pallas_call | solution.py:837
  18.1 2.5 %fine_level.1 = (f32[4,16,512]{2,1,0:T(8,128)}, f32[4,16,512]{2,1,0:T(8,128)}) custom-call(f32[8,16,512]{2,1,0:T(8,128)S(1)} %constant_dynamic-update-slice_fusion.both_ref, f32[5,8,512]{2,1,0:T(8,128)S(1)} %collective-permute-done.refs_0_, f32[7,16,512]{2,1,0:T(8,128)S(1)} %collective-permute-done.1.second_ref.refs_1_, ...), custom_call_target="tpu_custom_call" | custom-call | flops 20000000 | bytes 10000000 | tf_op jit(solution)/shard_map/fine_level/pallas_call | solution.py:941
  (5 shorter events, 0.1 us)
Async XLA Ops:
  0.6 1.0 %copy-start = (f32[4,16,512]{2,1,0:T(8,128)S(1)}, f32[4,16,512]{2,1,0:T(8,128)}, u32[]{:S(2)}) copy-start(f32[4,16,512]{2,1,0:T(8,128)} %param.5) | copy-start | bytes 393220
  1.8 6.3 %collective-permute-start = (f32[5,8,512]{2,1,0:T(8,128)S(1)}, f32[5,8,512]{2,1,0:T(8,128)S(1)}, u32[]{:S(2)}, u32[]{:S(2)}) collective-permute-start(f32[5,8,512]{2,1,0:T(8,128)S(1)} %get-tuple-element.8.after_ref), channel_id=1, source_target_pairs={{0,2},{1,3},{2,0},{3,1},{4,6},{5,7},{6,4},{7,5},{8,10},{9,11},{10,... | collective-permute-start | bytes 245768 | tf_op jit(solution)/shard_map/ppermute | solution.py:44
  4.9 10.2 %collective-permute-start.1 = (f32[7,16,512]{2,1,0:T(8,128)S(1)}, f32[7,16,512]{2,1,0:T(8,128)S(1)}, u32[]{:S(2)}, u32[]{:S(2)}) collective-permute-start(f32[7,16,512]{2,1,0:T(8,128)S(1)} %raw_block.2.after_ref), channel_id=1, source_target_pairs={{0,1},{1,0},{4,8},{5,9},{8,4},{9,5},{12,13},{13,12},{2,3},{3,2},{6... | collective-permute-start | bytes 688136 | tf_op jit(solution)/shard_map/ppermute | solution.py:44
  5.0 10.1 %collective-permute-start.2 = (f32[7,16,512]{2,1,0:T(8,128)S(1)}, f32[7,16,512]{2,1,0:T(8,128)S(1)}, u32[]{:S(2)}, u32[]{:S(2)}) collective-permute-start(f32[7,16,512]{2,1,0:T(8,128)S(1)} %raw_block.3), channel_id=1, source_target_pairs={{0,4},{1,5},{4,0},{5,1},{8,12},{9,13},{12,8},{13,9},{2,6},{3,7},{6... | collective-permute-start | bytes 688136 | tf_op jit(solution)/shard_map/ppermute | solution.py:44
  8.4 1.2 %collective-permute-start.3 = (f32[8,128]{1,0:T(8,128)S(1)}, f32[8,128]{1,0:T(8,128)S(1)}, u32[]{:S(2)}, u32[]{:S(2)}) collective-permute-start(f32[8,128]{1,0:T(8,128)S(1)} %get-tuple-element.11), channel_id=1, source_target_pairs={{0,1},{1,0},{2,3},{3,2},{4,5},{5,4},{6,7},{7,6},{8,9},{9,8},{10,11... | collective-permute-start | bytes 12296 | tf_op jit(solution)/shard_map/ppermute | solution.py:969
  9.7 7.6 %collective-permute-start.5 = (f32[80,128]{1,0:T(8,128)S(1)}, f32[80,128]{1,0:T(8,128)S(1)}, u32[]{:S(2)}, u32[]{:S(2)}) collective-permute-start(f32[80,128]{1,0:T(8,128)S(1)} %get-tuple-element.12), channel_id=1, source_target_pairs={{0,1},{1,0},{4,8},{5,9},{8,4},{9,5},{12,13},{13,12},{2,3},{3,2},{6... | collective-permute-start | bytes 122888 | tf_op jit(solution)/shard_map/ppermute | solution.py:44
  9.9 7.5 %collective-permute-start.6 = (f32[80,128]{1,0:T(8,128)S(1)}, f32[80,128]{1,0:T(8,128)S(1)}, u32[]{:S(2)}, u32[]{:S(2)}) collective-permute-start(f32[80,128]{1,0:T(8,128)S(1)} %get-tuple-element.13.after_ref), channel_id=1, source_target_pairs={{0,4},{1,5},{4,0},{5,1},{8,12},{9,13},{12,8},{13,9},{2,6},{3,7},{6... | collective-permute-start | bytes 122888 | tf_op jit(solution)/shard_map/ppermute | solution.py:44
  12.5 4.9 %collective-permute-start.4 = (f32[72,128]{1,0:T(8,128)S(1)}, f32[72,128]{1,0:T(8,128)S(1)}, u32[]{:S(2)}, u32[]{:S(2)}) collective-permute-start(f32[72,128]{1,0:T(8,128)S(1)} %pack_far.1.after_ref), channel_id=1, source_target_pairs={{0,8},{1,9},{4,12},{5,13},{8,0},{9,1},{12,4},{13,5},{2,10},{3,11},... | collective-permute-start | bytes 110600 | tf_op jit(solution)/shard_map/ppermute | solution.py:44

commit v13 on v12

--- a/solution.py
+++ b/solution.py
@@ -572,11 +572,13 @@
         for i, (right, left) in enumerate(zip(tiles(1), tiles(0))):
             put(ref, i * (half // LANES), jnp.where(low, *((right, left) if group == 0 else (left, right))))
         put(ref, 4 * (half // LANES), lanes_ref[...])
+        for spare in range(4 * (half // LANES) + 1, ref.shape[0] // SUBLANES):
+            put(ref, spare, jnp.zeros((SUBLANES, LANES), jnp.float32))
 
 
 def pack_far(pooled, halos, early, n_far, wide):
     _, rows, lanes = pooled.shape
-    far_rows = (2 * lanes // LANES + 1) * SUBLANES
+    far_rows = max(2 * lanes // LANES + 1, 0 if wide else near_layout(lanes, wide)[1]) * SUBLANES
     return pl.pallas_call(
         functools.partial(pack_far_kernel, wide),
         out_shape=(jax.ShapeDtypeStruct((far_rows, LANES), jnp.float32),) * n_far,
@@ -726,7 +728,7 @@
     return pick(low, tuple(take(ref, i * count, count) for ref in refs))
 
 
-def coarse_kernel(peers, n_far, own_ref, halo_ref, pool_ref, first_ref, second_ref, *refs):
+def coarse_part(peers, n_far, own_ref, halo_ref, pool_ref, first_ref, second_ref, *refs):
     near_refs, far_refs = (first_ref, second_ref), refs[:n_far]
     early_ref, coef_ref, out_ref, wide_ref, *scratch = refs[n_far:]
     ix, iy, iz = (lax.axis_index(axis) for axis in AXES)
@@ -831,24 +833,7 @@
                 out_ref[2 * x + twin, :, part] = wide_ref[tile]
 
 
-def coarse_level(own, halos, pooled, near, far, early, coefficients, peers):
-    lanes = own.shape[2] // 2
-    window = (2 + 2 * REACH, SUBLANES, 2 * SUBLANES, lanes // LANES + 1)
-    return pl.pallas_call(
-        functools.partial(coarse_kernel, peers, len(far)),
-        out_shape=jax.ShapeDtypeStruct((REACH, 2 * SUBLANES, 2 * lanes), jnp.float32),
-        in_specs=[VMEM] * (7 + len(far)),
-        out_specs=VMEM,
-        scratch_shapes=[pltpu.VMEM((2 * lanes // LANES, 2 * SUBLANES, LANES), jnp.float32)]
-        + window_scratch(*window)
-        + [pltpu.VMEM((2 * SUBLANES, lanes), jnp.float32)],
-        compiler_params=pltpu.CompilerParams(vmem_limit_bytes=24 << 20),
-        cost_estimate=pl.CostEstimate(flops=20_000_000, bytes_accessed=4_000_000, transcendentals=0),
-        name="coarse_level",
-    )(own, halos, pooled, *near, *far, early, coefficients)
-
-
-def fine_kernel(peers, n_far, both_ref, *refs):
+def levels_kernel(peers, n_far, both_ref, *refs):
     log_ref, source_ref = parts(both_ref)
     layers, rows, lanes = log_ref.shape
     ix, iy, iz = (lax.axis_index(axis) for axis in AXES)
@@ -857,9 +842,24 @@
     n_got = 2 if wide else 1
     got_refs, refs = refs[:n_got], refs[n_got:]
     second_ref, first_ref = refs[:2]
-    second_near_ref, first_near_ref, early_ref, spread_ref = refs[2 + n_far : 6 + n_far]
+    far_refs = refs[2 : 2 + n_far]
+    second_near_ref, first_near_ref, early_ref, coef_ref = refs[2 + n_far : 6 + n_far]
     near_refs = first_near_ref, second_near_ref
-    coef_ref, fine_ref, diff_ref, *scratch = refs[6 + n_far :]
+    own_ref, halo_ref, pool_ref, fine_ref, diff_ref, *scratch = refs[6 + n_far :]
+    scratch, (spread_ref, *coarse_scratch) = scratch[:10], scratch[10:]
+    coarse_part(
+        peers,
+        n_far,
+        own_ref,
+        halo_ref,
+        pool_ref,
+        *near_refs,
+        *far_refs,
+        early_ref,
+        coef_ref,
+        spread_ref,
+        *coarse_scratch,
+    )
     even, starts = ix % 2 == 0, iy == 0
     count = 3 * layers
     upper = iota((SUBLANES, lanes + LANES), 0) < REACH
@@ -934,20 +934,26 @@
     )
 
 
-def fine_level(both, got, raw, far, near, early, spread, coefficients, peers):
-    layers, rows, lanes = spread.shape
-    window = (layers + 2 * REACH, rows, rows + 2 * REACH, lanes // LANES + 1)
-    out = jax.ShapeDtypeStruct(spread.shape, jnp.float32)
+def levels(both, got, raw, far, near, early, coefficients, own, halos, pooled, peers):
+    layers, rows, lanes = both.shape[0] // 2, *both.shape[1:]
+    half = lanes // 2
+    out = jax.ShapeDtypeStruct((layers, rows, lanes), jnp.float32)
     return pl.pallas_call(
-        functools.partial(fine_kernel, peers, len(far)),
+        functools.partial(levels_kernel, peers, len(far)),
         out_shape=(out, out),
-        in_specs=[VMEM] * (3 + len(got)) + [ANY] * len(far) + [VMEM] * 5,
+        in_specs=[VMEM] * (10 + len(got) + len(far)),
         out_specs=(VMEM, VMEM),
-        scratch_shapes=window_scratch(*window),
-        compiler_params=pltpu.CompilerParams(vmem_limit_bytes=24 << 20),
+        scratch_shapes=window_scratch(3 * layers, rows, rows + 2 * REACH, lanes // LANES + 1)
+        + [
+            pltpu.VMEM((layers, rows, lanes), jnp.float32),
+            pltpu.VMEM((lanes // LANES, rows, LANES), jnp.float32),
+        ]
+        + window_scratch(2 + 2 * REACH, SUBLANES, 2 * SUBLANES, half // LANES + 1)
+        + [pltpu.VMEM((2 * SUBLANES, half), jnp.float32)],
+        compiler_params=pltpu.CompilerParams(vmem_limit_bytes=32 << 20),
         cost_estimate=pl.CostEstimate(flops=20_000_000, bytes_accessed=10_000_000, transcendentals=0),
-        name="fine_level",
-    )(both, *got, *raw[::-1], *far, *near[::-1], early, spread, coefficients)
+        name="levels",
+    )(both, *got, *raw[::-1], *far, *near[::-1], early, coefficients, own, halos, pooled)
 
 
 def shards(peers, log_perm, source, low_bound, high_bound):
@@ -974,8 +980,7 @@
     near = (permute(for_first, "gx", nx, neighbour_pairs(nx, 0)), second)
     coefficients = chebyshev_coefficients(low_bound, high_bound, for_first)
     pooled = pool(coefficients, raw)
-    spread = coarse_level(own, halos, pooled, near, far, early, coefficients, peers)
-    return fine_level(both, got, raw, far, near, early, spread, coefficients, peers)
+    return levels(both, got, raw, far, near, early, coefficients, own, halos, pooled, peers)
 
 
 def solution(mesh):

time: 20.8 us -> 19.3 us (0.928)
  waiting for transfers between devices: 3.26 us -> 1.99 us
  Pallas kernels: 4.13 us -> 3.87 us
    ppermute x6, waiting for transfers between devices: 2.1 us -> 0.84 us  [permute(): return lax.ppermute(value, (axis, 'gz'), moves)]
    pallas_call x2 -> x1, Pallas kernels: 3.25 us -> 2.99 us  [levels(): pl.pallas_call(functools.partial(levels_kernel, peers, len(far)), out_sha...]
  transfers between devices with their start and end apart: 7 -> 7, of which waited for: 2 -> 2; matrix products, arithmetic and copies ran while one was open for 0% -> 0% of each run, Pallas kernels for 3% -> 4%
where the time goes in v13:
time: 19.3 us; the launch traced here: 19.1 us
  starting transfers between devices  10.2 us (53%)
  Pallas kernels  3.87 us (20%)
  between operations  2.05 us (11%)
  waiting for transfers between devices  1.99 us (10%)
  local copies, waits for them, and re-layouts  0.97 us (5%)
    ppermute x6, starting transfers between devices, permute(): return lax.ppermute(value, (axis, 'gz'), moves)  10.2 us
    pallas_call x1, Pallas kernels, levels(): pl.pallas_call(functools.partial(levels_kernel, peers, len(far)), out_sha...  2.99 us
    ppermute x1, waiting for transfers between devices, shards(): early = lax.ppermute(lanes_sent, 'gz', [(0, 1), (1, 0)])  1.15 us
    unnamed x3, local copies, waits for them, and re-layouts  0.96 us
    ppermute x6, waiting for transfers between devices, permute(): return lax.ppermute(value, (axis, 'gz'), moves)  0.84 us
  transfers between devices with their start and end apart: 7, of which 2 were waited for; matrix products, arithmetic and copies ran while one was open for 0% of the time, Pallas kernels for 4%

profile of v13, /device:TPU:0, one launch (start us, length us, event | category | flops | bytes accessed | tf_op | source)
XLA Modules:
  0.0 19.1 jit_solution(12953251021282390442)
XLA Ops:
  0.6 0.0 copy-start
  0.6 0.9 %constant_dynamic-update-slice_fusion.1 = f32[8,16,512]{2,1,0:T(8,128)S(1)} fusion(f32[4,16,512]{2,1,0:T(8,128)} %param.4), kind=kLoop, calls=%fused_computation.1 | loop fusion | bytes 262144
  1.6 0.0 copy-done
  1.6 0.2 %prep.1 = (f32[2,8,512]{2,1,0:T(8,128)S(1)}, f32[5,8,512]{2,1,0:T(8,128)S(1)}) custom-call(f32[8,16,512]{2,1,0:T(8,128)S(1)} %constant_dynamic-update-slice_fusion.both_ref), custom_call_target="tpu_custom_call" | custom-call | flops 5000000 | bytes 700000 | tf_op jit(solution)/shard_map/prep/pallas_call | solution.py:434
  1.8 3.0 %collective-permute-start = (f32[5,8,512]{2,1,0:T(8,128)S(1)}, f32[5,8,512]{2,1,0:T(8,128)S(1)}, u32[]{:S(2)}, u32[]{:S(2)}) collective-permute-start(f32[5,8,512]{2,1,0:T(8,128)S(1)} %get-tuple-element.8.after_ref), channel_id=1, source_target_pairs={{0,2},{1,3},{2,0},{3,1},{4,6},{5,7},{6,4},{7,5},{8,10},{9,11},{10,... | collective-permute-start | bytes 245768 | tf_op jit(solution)/shard_map/ppermute | solution.py:44
  4.9 0.1 collective-permute-start.1
  5.0 3.2 %collective-permute-start.2 = (f32[7,16,512]{2,1,0:T(8,128)S(1)}, f32[7,16,512]{2,1,0:T(8,128)S(1)}, u32[]{:S(2)}, u32[]{:S(2)}) collective-permute-start(f32[7,16,512]{2,1,0:T(8,128)S(1)} %raw_block.3), channel_id=1, source_target_pairs={{0,4},{1,5},{4,0},{5,1},{8,12},{9,13},{12,8},{13,9},{2,6},{3,7},{6... | collective-permute-start | bytes 688136 | tf_op jit(solution)/shard_map/ppermute | solution.py:44
  8.2 0.0 collective-permute-done.refs_0_
  8.2 0.2 %halos.1 = (f32[1,8,512]{2,1,0:T(8,128)S(1)}, f32[8,128]{1,0:T(8,128)S(1)}) custom-call(f32[8,16,512]{2,1,0:T(8,128)S(1)} %constant_dynamic-update-slice_fusion.both_ref, f32[2,8,512]{2,1,0:T(8,128)S(1)} %get-tuple-element.9.pooled_ref.refs_8_, f32[5,8,512]{2,1,0:T(8,128)S(1)} %collective-permute-done.refs_0_), custom_call_target="tpu_custom_call" | custom-call | flops 49999998976 | bytes 1000000 | tf_op jit(solution)/shard_map/halos/pallas_call | solution.py:544
  8.4 0.0 collective-permute-start.3
  8.4 1.2 %collective-permute-done.3.lanes_ref.early_ref.refs_6_ = f32[8,128]{1,0:T(8,128)S(1)} collective-permute-done((f32[8,128]{1,0:T(8,128)S(1)}, f32[8,128]{1,0:T(8,128)S(1)}, u32[]{:S(2)}, u32[]{:S(2)}) %collective-permute-start.3) | collective-permute-done | bytes 4128 | tf_op jit(solution)/shard_map/ppermute | solution.py:975
  9.6 2.3 %collective-permute-start.4 = (f32[80,128]{1,0:T(8,128)S(1)}, f32[80,128]{1,0:T(8,128)S(1)}, u32[]{:S(2)}, u32[]{:S(2)}) collective-permute-start(f32[80,128]{1,0:T(8,128)S(1)} %pack_far.1.after_ref), channel_id=1, source_target_pairs={{0,8},{1,9},{4,12},{5,13},{8,0},{9,1},{12,4},{13,5},{2,10},{3,11},... | collective-permute-start | bytes 122888 | tf_op jit(solution)/shard_map/ppermute | solution.py:44
  11.9 0.1 pack_near.1
  12.0 0.0 collective-permute-start.5
  12.0 1.6 %collective-permute-start.6 = (f32[80,128]{1,0:T(8,128)S(1)}, f32[80,128]{1,0:T(8,128)S(1)}, u32[]{:S(2)}, u32[]{:S(2)}) collective-permute-start(f32[80,128]{1,0:T(8,128)S(1)} %get-tuple-element.13.after_ref), channel_id=1, source_target_pairs={{0,4},{1,5},{4,0},{5,1},{8,12},{9,13},{12,8},{13,9},{2,6},{3,7},{6... | collective-permute-start | bytes 122888 | tf_op jit(solution)/shard_map/ppermute | solution.py:44
  15.0 0.0 collective-permute-done.2.first_ref.refs_2_
  15.0 0.0 collective-permute-done.1.second_ref.refs_1_
  15.0 0.2 %pool.1.refs_10_ = f32[96,128]{1,0:T(8,128)S(1)} custom-call(f32[7,8,128]{2,1,0:T(8,128)S(1)} %coefficients.1.after_ref.refs_7_, f32[7,16,512]{2,1,0:T(8,128)S(1)} %collective-permute-done.2.first_ref.refs_2_, f32[7,16,512]{2,1,0:T(8,128)S(1)} %collective-permute-done.1.second_ref.refs_1_), custom_call_target="tpu_custom_call" | custom-call | flops 1000000 | bytes 1000000 | tf_op jit(solution)/shard_map/pool/pallas_call | solution.py:706
  15.3 0.0 collective-permute-done.4.refs_3_
  15.3 0.0 collective-permute-done.5.refs_4_
  15.3 0.8 %collective-permute-done.6.refs_5_ = f32[80,128]{1,0:T(8,128)S(1)} collective-permute-done((f32[80,128]{1,0:T(8,128)S(1)}, f32[80,128]{1,0:T(8,128)S(1)}, u32[]{:S(2)}, u32[]{:S(2)}) %collective-permute-start.6) | collective-permute-done | bytes 40992 | tf_op jit(solution)/shard_map/ppermute | solution.py:44
  16.1 3.0 %levels.1 = (f32[4,16,512]{2,1,0:T(8,128)}, f32[4,16,512]{2,1,0:T(8,128)}) custom-call(f32[8,16,512]{2,1,0:T(8,128)S(1)} %constant_dynamic-update-slice_fusion.both_ref, f32[5,8,512]{2,1,0:T(8,128)S(1)} %collective-permute-done.refs_0_, f32[7,16,512]{2,1,0:T(8,128)S(1)} %collective-permute-done.1.second_ref.refs_1_, ...), custom_call_target="tpu_custom_call" | custom-call | flops 20000000 | bytes 10000000 | tf_op jit(solution)/shard_map/levels/pallas_call | solution.py:941
  (5 shorter events, 0.1 us)
Async XLA Ops:
  0.6 1.0 %copy-start = (f32[4,16,512]{2,1,0:T(8,128)S(1)}, f32[4,16,512]{2,1,0:T(8,128)}, u32[]{:S(2)}) copy-start(f32[4,16,512]{2,1,0:T(8,128)} %param.5) | copy-start | bytes 393220
  1.8 6.3 %collective-permute-start = (f32[5,8,512]{2,1,0:T(8,128)S(1)}, f32[5,8,512]{2,1,0:T(8,128)S(1)}, u32[]{:S(2)}, u32[]{:S(2)}) collective-permute-start(f32[5,8,512]{2,1,0:T(8,128)S(1)} %get-tuple-element.8.after_ref), channel_id=1, source_target_pairs={{0,2},{1,3},{2,0},{3,1},{4,6},{5,7},{6,4},{7,5},{8,10},{9,11},{10,... | collective-permute-start | bytes 245768 | tf_op jit(solution)/shard_map/ppermute | solution.py:44
  4.9 10.2 %collective-permute-start.1 = (f32[7,16,512]{2,1,0:T(8,128)S(1)}, f32[7,16,512]{2,1,0:T(8,128)S(1)}, u32[]{:S(2)}, u32[]{:S(2)}) collective-permute-start(f32[7,16,512]{2,1,0:T(8,128)S(1)} %raw_block.2.after_ref), channel_id=1, source_target_pairs={{0,1},{1,0},{4,8},{5,9},{8,4},{9,5},{12,13},{13,12},{2,3},{3,2},{6... | collective-permute-start | bytes 688136 | tf_op jit(solution)/shard_map/ppermute | solution.py:44
  5.0 10.0 %collective-permute-start.2 = (f32[7,16,512]{2,1,0:T(8,128)S(1)}, f32[7,16,512]{2,1,0:T(8,128)S(1)}, u32[]{:S(2)}, u32[]{:S(2)}) collective-permute-start(f32[7,16,512]{2,1,0:T(8,128)S(1)} %raw_block.3), channel_id=1, source_target_pairs={{0,4},{1,5},{4,0},{5,1},{8,12},{9,13},{12,8},{13,9},{2,6},{3,7},{6... | collective-permute-start | bytes 688136 | tf_op jit(solution)/shard_map/ppermute | solution.py:44
  8.4 1.2 %collective-permute-start.3 = (f32[8,128]{1,0:T(8,128)S(1)}, f32[8,128]{1,0:T(8,128)S(1)}, u32[]{:S(2)}, u32[]{:S(2)}) collective-permute-start(f32[8,128]{1,0:T(8,128)S(1)} %get-tuple-element.11), channel_id=1, source_target_pairs={{0,1},{1,0},{2,3},{3,2},{4,5},{5,4},{6,7},{7,6},{8,9},{9,8},{10,11... | collective-permute-start | bytes 12296 | tf_op jit(solution)/shard_map/ppermute | solution.py:975
  9.6 5.7 %collective-permute-start.4 = (f32[80,128]{1,0:T(8,128)S(1)}, f32[80,128]{1,0:T(8,128)S(1)}, u32[]{:S(2)}, u32[]{:S(2)}) collective-permute-start(f32[80,128]{1,0:T(8,128)S(1)} %pack_far.1.after_ref), channel_id=1, source_target_pairs={{0,8},{1,9},{4,12},{5,13},{8,0},{9,1},{12,4},{13,5},{2,10},{3,11},... | collective-permute-start | bytes 122888 | tf_op jit(solution)/shard_map/ppermute | solution.py:44
  12.0 3.3 %collective-permute-start.5 = (f32[80,128]{1,0:T(8,128)S(1)}, f32[80,128]{1,0:T(8,128)S(1)}, u32[]{:S(2)}, u32[]{:S(2)}) collective-permute-start(f32[80,128]{1,0:T(8,128)S(1)} %get-tuple-element.12), channel_id=1, source_target_pairs={{0,1},{1,0},{4,8},{5,9},{8,4},{9,5},{12,13},{13,12},{2,3},{3,2},{6... | collective-permute-start | bytes 122888 | tf_op jit(solution)/shard_map/ppermute | solution.py:44
  12.0 4.1 %collective-permute-start.6 = (f32[80,128]{1,0:T(8,128)S(1)}, f32[80,128]{1,0:T(8,128)S(1)}, u32[]{:S(2)}, u32[]{:S(2)}) collective-permute-start(f32[80,128]{1,0:T(8,128)S(1)} %get-tuple-element.13.after_ref), channel_id=1, source_target_pairs={{0,4},{1,5},{4,0},{5,1},{8,12},{9,13},{12,8},{13,9},{2,6},{3,7},{6... | collective-permute-start | bytes 122888 | tf_op jit(solution)/shard_map/ppermute | solution.py:44

commit v14 on v13

--- a/solution.py
+++ b/solution.py
@@ -116,7 +116,7 @@
     ref[k, j, SUBLANES + rows : SUBLANES + rows + 1] = value[:1]
 
 
-def iterate(count, own_rows, rows, tiles, log_at, source_at, x_faces, y_top, z_top, coef_ref, storage, emit, refs):
+def iterate(count, own_rows, rows, tiles, log_at, source_at, x_faces, y_top, z_top, coef_ref, storage, emit, refs, ready=None):
     k_ref, tx_ref, ty_ref, tzr_ref, tzl_ref, diag_ref, w_ref, d_ref, r_ref, p_ref = refs
     own_tiles = tiles - 1
 
@@ -133,7 +133,19 @@
     z_tops = [z_top[0] if j == own_tiles - 1 else z_top[1] if j == own_tiles else None for j in range(tiles)]
 
     def resistance(k):
-        return [jnp.exp(-tile) for tile in lane_tiles(log_at(k))]
+        logs = lane_tiles(log_at(k))
+        if ready is None:
+            return [jnp.exp(-tile) for tile in logs]
+        return [
+            jnp.concatenate([ready[0][k, j], jnp.exp(-logs[j][own_rows:])], axis=0) for j in range(own_tiles)
+        ] + [jnp.exp(-logs[own_tiles])]
+
+    def along_x(k, j, size):
+        if ready is None or j == own_tiles:
+            return tx_ref[k, j, :size]
+        if size == own_rows:
+            return ready[1][k, j]
+        return jnp.concatenate([ready[1][k, j], tx_ref[k, j, own_rows:size]], axis=0)
 
     after = resistance(0)
     tx_before = None
@@ -143,9 +155,12 @@
             after = resistance(k + 1)
             outer = max(away(k), away(k + 1))
             size, number = (rows, tiles) if outer < REACH else (own_rows, own_tiles)
-            tx = [x_faces[k] * inverse(here[j][:size] + after[j][:size]) for j in range(number)]
+            tx = []
             for j in range(number):
-                tx_ref[k, j, :size] = tx[j]
+                begin = 0 if ready is None or j == own_tiles else own_rows
+                if begin < size:
+                    tx_ref[k, j, begin:size] = x_faces[k] * inverse(here[j][begin:size] + after[j][begin:size])
+                tx.append(along_x(k, j, size))
         if away(k) <= DEGREE:
             size, number = extent(k, 0)
             right = beside(here, -1)
@@ -186,7 +201,7 @@
             here = [old[k, j, middle] for j in range(tiles)]
             right, left = beside(here, -1), beside(here, 1)
             for j in range(number):
-                applied = tx_ref[k, j, :size] * old[k + 1, j, middle] + tx_ref[k - 1, j, :size] * old[k - 1, j, middle]
+                applied = along_x(k, j, size) * old[k + 1, j, middle] + along_x(k - 1, j, size) * old[k - 1, j, middle]
                 applied += (
                     ty_ref[k, j, middle] * old[k, j, SUBLANES + 1 : SUBLANES + 1 + size]
                     + ty_ref[k, j, SUBLANES - 1 : SUBLANES - 1 + size] * old[k, j, SUBLANES - 1 : SUBLANES - 1 + size]
@@ -715,6 +730,50 @@
     )(after, *raw)
 
 
+def x_faces_of(layers, ix, nx):
+    faces = [2.0] * (3 * layers - 1)
+    faces[layers - 1] = jnp.where(ix > 0, 2.0, 0.0)
+    faces[2 * layers - 1] = jnp.where(ix < nx - 1, 2.0, 0.0)
+    return faces
+
+
+def ahead_kernel(nx, after_ref, both_ref, first_ref, second_ref, inverse_ref, tx_ref):
+    log_ref, _ = parts(both_ref)
+    layers, rows, lanes = log_ref.shape
+    ix = lax.axis_index("gx")
+    faces = x_faces_of(layers, ix, nx)
+    before = None
+    for k in range(3 * layers):
+        side, layer = k // layers - 1, k % layers
+        if side == 0:
+            log = log_ref[layer]
+        else:
+            log = (from_left if side < 0 else from_right)(ix % 2 == 0, (first_ref[layer], second_ref[layer]))
+        here = [jnp.exp(-tile) for tile in lane_tiles(log)]
+        for j, tile in enumerate(here):
+            inverse_ref[k, j] = tile
+            if k > 0:
+                tx_ref[k - 1, j] = faces[k - 1] * inverse(before[j] + tile)
+        before = here
+
+
+def ahead(after, both, raw, nx):
+    layers, rows, lanes = both.shape[0] // 2, *both.shape[1:]
+
+    def tiles(count):
+        return jax.ShapeDtypeStruct((count, lanes // LANES, rows, LANES), jnp.float32)
+
+    return pl.pallas_call(
+        functools.partial(ahead_kernel, nx),
+        out_shape=(tiles(3 * layers), tiles(3 * layers - 1)),
+        in_specs=[ANY] + [VMEM] * 3,
+        out_specs=(VMEM,) * 2,
+        compiler_params=pltpu.CompilerParams(vmem_limit_bytes=16 << 20),
+        cost_estimate=pl.CostEstimate(flops=1_000_000, bytes_accessed=1_000_000, transcendentals=0),
+        name="ahead",
+    )(after, both, *raw)
+
+
 def near_part(refs, even, lanes, wide, side, name):
     start, count = near_layout(lanes, wide)[0][name]
     pick = from_left if side == 0 else from_right
@@ -845,7 +904,7 @@
     far_refs = refs[2 : 2 + n_far]
     second_near_ref, first_near_ref, early_ref, coef_ref = refs[2 + n_far : 6 + n_far]
     near_refs = first_near_ref, second_near_ref
-    own_ref, halo_ref, pool_ref, fine_ref, diff_ref, *scratch = refs[6 + n_far :]
+    own_ref, halo_ref, pool_ref, inverse_ref, tx_ref, fine_ref, diff_ref, *scratch = refs[6 + n_far :]
     scratch, (spread_ref, *coarse_scratch) = scratch[:10], scratch[10:]
     coarse_part(
         peers,
@@ -908,9 +967,7 @@
         halo = near_halo(a, side, layers - layer if block < 0 else layer + 1)
         return jnp.concatenate([core, halo], axis=0)
 
-    faces = [2.0] * (count - 1)
-    faces[layers - 1] = jnp.where(ix > 0, 2.0, 0.0)
-    faces[2 * layers - 1] = jnp.where(ix < nx - 1, 2.0, 0.0)
+    faces = x_faces_of(layers, ix, nx)
 
     def emit(layer, tile, value):
         part = slice(tile * LANES, (tile + 1) * LANES)
@@ -931,17 +988,18 @@
         storage_rate,
         emit,
         scratch,
+        (inverse_ref, tx_ref),
     )
 
 
-def levels(both, got, raw, far, near, early, coefficients, own, halos, pooled, peers):
+def levels(both, got, raw, far, near, early, coefficients, own, halos, pooled, ready, peers):
     layers, rows, lanes = both.shape[0] // 2, *both.shape[1:]
     half = lanes // 2
     out = jax.ShapeDtypeStruct((layers, rows, lanes), jnp.float32)
     return pl.pallas_call(
         functools.partial(levels_kernel, peers, len(far)),
         out_shape=(out, out),
-        in_specs=[VMEM] * (10 + len(got) + len(far)),
+        in_specs=[VMEM] * (12 + len(got) + len(far)),
         out_specs=(VMEM, VMEM),
         scratch_shapes=window_scratch(3 * layers, rows, rows + 2 * REACH, lanes // LANES + 1)
         + [
@@ -953,7 +1011,7 @@
         compiler_params=pltpu.CompilerParams(vmem_limit_bytes=32 << 20),
         cost_estimate=pl.CostEstimate(flops=20_000_000, bytes_accessed=10_000_000, transcendentals=0),
         name="levels",
-    )(both, *got, *raw[::-1], *far, *near[::-1], early, coefficients, own, halos, pooled)
+    )(both, *got, *raw[::-1], *far, *near[::-1], early, coefficients, own, halos, pooled, *ready)
 
 
 def shards(peers, log_perm, source, low_bound, high_bound):
@@ -980,7 +1038,8 @@
     near = (permute(for_first, "gx", nx, neighbour_pairs(nx, 0)), second)
     coefficients = chebyshev_coefficients(low_bound, high_bound, for_first)
     pooled = pool(coefficients, raw)
-    return levels(both, got, raw, far, near, early, coefficients, own, halos, pooled, peers)
+    ready = ahead(pooled, both, raw, nx)
+    return levels(both, got, raw, far, near, early, coefficients, own, halos, pooled, ready, peers)
 
 
 def solution(mesh):

time: 19.3 us -> 19.3 us (level)
  no operation moved by 1% of the time
where the time goes in v14:
time: 19.3 us; the launch traced here: 19.1 us
  starting transfers between devices  10.2 us (53%)
  Pallas kernels  4.01 us (21%)
  between operations  2.05 us (11%)
  waiting for transfers between devices  1.84 us (10%)
  local copies, waits for them, and re-layouts  0.97 us (5%)
    ppermute x6, starting transfers between devices, permute(): return lax.ppermute(value, (axis, 'gz'), moves)  10.2 us
    pallas_call x1, Pallas kernels, levels(): pl.pallas_call(functools.partial(levels_kernel, peers, len(far)), out_sha...  2.98 us
    ppermute x1, waiting for transfers between devices, shards(): early = lax.ppermute(lanes_sent, 'gz', [(0, 1), (1, 0)])  1.15 us
    unnamed x3, local copies, waits for them, and re-layouts  0.96 us
    ppermute x6, waiting for transfers between devices, permute(): return lax.ppermute(value, (axis, 'gz'), moves)  0.68 us
  transfers between devices with their start and end apart: 7, of which 2 were waited for; matrix products, arithmetic and copies ran while one was open for 0% of the time, Pallas kernels for 4%

profile of v14, /device:TPU:0, one launch (start us, length us, event | category | flops | bytes accessed | tf_op | source)
XLA Modules:
  0.0 19.1 jit_solution(14767230057341125571)
XLA Ops:
  0.6 0.0 copy-start
  0.6 0.9 %constant_dynamic-update-slice_fusion.1 = f32[8,16,512]{2,1,0:T(8,128)S(1)} fusion(f32[4,16,512]{2,1,0:T(8,128)} %param.4), kind=kLoop, calls=%fused_computation.1 | loop fusion | bytes 262144
  1.6 0.0 copy-done
  1.6 0.2 %prep.1 = (f32[2,8,512]{2,1,0:T(8,128)S(1)}, f32[5,8,512]{2,1,0:T(8,128)S(1)}) custom-call(f32[8,16,512]{2,1,0:T(8,128)S(1)} %constant_dynamic-update-slice_fusion.both_ref), custom_call_target="tpu_custom_call" | custom-call | flops 5000000 | bytes 700000 | tf_op jit(solution)/shard_map/prep/pallas_call | solution.py:449
  1.8 3.0 %collective-permute-start = (f32[5,8,512]{2,1,0:T(8,128)S(1)}, f32[5,8,512]{2,1,0:T(8,128)S(1)}, u32[]{:S(2)}, u32[]{:S(2)}) collective-permute-start(f32[5,8,512]{2,1,0:T(8,128)S(1)} %get-tuple-element.10.after_ref), channel_id=1, source_target_pairs={{0,2},{1,3},{2,0},{3,1},{4,6},{5,7},{6,4},{7,5},{8,10},{9,11},{10,... | collective-permute-start | bytes 245768 | tf_op jit(solution)/shard_map/ppermute | solution.py:44
  4.9 0.1 collective-permute-start.1
  5.0 3.2 %collective-permute-start.2 = (f32[7,16,512]{2,1,0:T(8,128)S(1)}, f32[7,16,512]{2,1,0:T(8,128)S(1)}, u32[]{:S(2)}, u32[]{:S(2)}) collective-permute-start(f32[7,16,512]{2,1,0:T(8,128)S(1)} %raw_block.3), channel_id=1, source_target_pairs={{0,4},{1,5},{4,0},{5,1},{8,12},{9,13},{12,8},{13,9},{2,6},{3,7},{6... | collective-permute-start | bytes 688136 | tf_op jit(solution)/shard_map/ppermute | solution.py:44
  8.2 0.0 collective-permute-done.refs_0_
  8.2 0.2 %halos.1 = (f32[1,8,512]{2,1,0:T(8,128)S(1)}, f32[8,128]{1,0:T(8,128)S(1)}) custom-call(f32[8,16,512]{2,1,0:T(8,128)S(1)} %constant_dynamic-update-slice_fusion.both_ref, f32[2,8,512]{2,1,0:T(8,128)S(1)} %get-tuple-element.11.pooled_ref.refs_8_, f32[5,8,512]{2,1,0:T(8,128)S(1)} %collective-permute-done.refs_0_), custom_call_target="tpu_custom_call" | custom-call | flops 49999998976 | bytes 1000000 | tf_op jit(solution)/shard_map/halos/pallas_call | solution.py:559
  8.4 0.0 collective-permute-start.3
  8.4 1.2 %collective-permute-done.3.lanes_ref.early_ref.refs_6_ = f32[8,128]{1,0:T(8,128)S(1)} collective-permute-done((f32[8,128]{1,0:T(8,128)S(1)}, f32[8,128]{1,0:T(8,128)S(1)}, u32[]{:S(2)}, u32[]{:S(2)}) %collective-permute-start.3) | collective-permute-done | bytes 4128 | tf_op jit(solution)/shard_map/ppermute | solution.py:1033
  9.6 2.3 %collective-permute-start.4 = (f32[80,128]{1,0:T(8,128)S(1)}, f32[80,128]{1,0:T(8,128)S(1)}, u32[]{:S(2)}, u32[]{:S(2)}) collective-permute-start(f32[80,128]{1,0:T(8,128)S(1)} %pack_far.1.after_ref), channel_id=1, source_target_pairs={{0,8},{1,9},{4,12},{5,13},{8,0},{9,1},{12,4},{13,5},{2,10},{3,11},... | collective-permute-start | bytes 122888 | tf_op jit(solution)/shard_map/ppermute | solution.py:44
  11.9 0.1 pack_near.1
  12.0 0.0 collective-permute-start.5
  12.0 1.6 %collective-permute-start.6 = (f32[80,128]{1,0:T(8,128)S(1)}, f32[80,128]{1,0:T(8,128)S(1)}, u32[]{:S(2)}, u32[]{:S(2)}) collective-permute-start(f32[80,128]{1,0:T(8,128)S(1)} %get-tuple-element.15.after_ref), channel_id=1, source_target_pairs={{0,4},{1,5},{4,0},{5,1},{8,12},{9,13},{12,8},{13,9},{2,6},{3,7},{6... | collective-permute-start | bytes 122888 | tf_op jit(solution)/shard_map/ppermute | solution.py:44
  15.0 0.0 collective-permute-done.2.first_ref.refs_2_
  15.0 0.0 collective-permute-done.1.second_ref.refs_1_
  15.0 0.2 %pool.1.after_ref.refs_10_ = f32[96,128]{1,0:T(8,128)S(1)} custom-call(f32[7,8,128]{2,1,0:T(8,128)S(1)} %coefficients.1.after_ref.refs_7_, f32[7,16,512]{2,1,0:T(8,128)S(1)} %collective-permute-done.2.first_ref.refs_2_, f32[7,16,512]{2,1,0:T(8,128)S(1)} %collective-permute-done.1.second_ref.refs_1_), custom_call_target="tpu_custom_call" | custom-call | flops 1000000 | bytes 1000000 | tf_op jit(solution)/shard_map/pool/pallas_call | solution.py:721
  15.3 0.2 ahead.1
  15.4 0.0 collective-permute-done.4.refs_3_
  15.4 0.0 collective-permute-done.5.refs_4_
  15.4 0.7 %collective-permute-done.6.refs_5_ = f32[80,128]{1,0:T(8,128)S(1)} collective-permute-done((f32[80,128]{1,0:T(8,128)S(1)}, f32[80,128]{1,0:T(8,128)S(1)}, u32[]{:S(2)}, u32[]{:S(2)}) %collective-permute-start.6) | collective-permute-done | bytes 40992 | tf_op jit(solution)/shard_map/ppermute | solution.py:44
  16.1 3.0 %levels.1 = (f32[4,16,512]{2,1,0:T(8,128)}, f32[4,16,512]{2,1,0:T(8,128)}) custom-call(f32[8,16,512]{2,1,0:T(8,128)S(1)} %constant_dynamic-update-slice_fusion.both_ref, f32[5,8,512]{2,1,0:T(8,128)S(1)} %collective-permute-done.refs_0_, f32[7,16,512]{2,1,0:T(8,128)S(1)} %collective-permute-done.1.second_ref.refs_1_, ...), custom_call_target="tpu_custom_call" | custom-call | flops 20000000 | bytes 10000000 | tf_op jit(solution)/shard_map/levels/pallas_call | solution.py:999
  (5 shorter events, 0.1 us)
Async XLA Ops:
  0.6 1.0 %copy-start = (f32[4,16,512]{2,1,0:T(8,128)S(1)}, f32[4,16,512]{2,1,0:T(8,128)}, u32[]{:S(2)}) copy-start(f32[4,16,512]{2,1,0:T(8,128)} %param.5) | copy-start | bytes 393220
  1.8 6.3 %collective-permute-start = (f32[5,8,512]{2,1,0:T(8,128)S(1)}, f32[5,8,512]{2,1,0:T(8,128)S(1)}, u32[]{:S(2)}, u32[]{:S(2)}) collective-permute-start(f32[5,8,512]{2,1,0:T(8,128)S(1)} %get-tuple-element.10.after_ref), channel_id=1, source_target_pairs={{0,2},{1,3},{2,0},{3,1},{4,6},{5,7},{6,4},{7,5},{8,10},{9,11},{10,... | collective-permute-start | bytes 245768 | tf_op jit(solution)/shard_map/ppermute | solution.py:44
  4.9 10.2 %collective-permute-start.1 = (f32[7,16,512]{2,1,0:T(8,128)S(1)}, f32[7,16,512]{2,1,0:T(8,128)S(1)}, u32[]{:S(2)}, u32[]{:S(2)}) collective-permute-start(f32[7,16,512]{2,1,0:T(8,128)S(1)} %raw_block.2.after_ref), channel_id=1, source_target_pairs={{0,1},{1,0},{4,8},{5,9},{8,4},{9,5},{12,13},{13,12},{2,3},{3,2},{6... | collective-permute-start | bytes 688136 | tf_op jit(solution)/shard_map/ppermute | solution.py:44
  5.0 10.0 %collective-permute-start.2 = (f32[7,16,512]{2,1,0:T(8,128)S(1)}, f32[7,16,512]{2,1,0:T(8,128)S(1)}, u32[]{:S(2)}, u32[]{:S(2)}) collective-permute-start(f32[7,16,512]{2,1,0:T(8,128)S(1)} %raw_block.3), channel_id=1, source_target_pairs={{0,4},{1,5},{4,0},{5,1},{8,12},{9,13},{12,8},{13,9},{2,6},{3,7},{6... | collective-permute-start | bytes 688136 | tf_op jit(solution)/shard_map/ppermute | solution.py:44
  8.4 1.2 %collective-permute-start.3 = (f32[8,128]{1,0:T(8,128)S(1)}, f32[8,128]{1,0:T(8,128)S(1)}, u32[]{:S(2)}, u32[]{:S(2)}) collective-permute-start(f32[8,128]{1,0:T(8,128)S(1)} %get-tuple-element.13), channel_id=1, source_target_pairs={{0,1},{1,0},{2,3},{3,2},{4,5},{5,4},{6,7},{7,6},{8,9},{9,8},{10,11... | collective-permute-start | bytes 12296 | tf_op jit(solution)/shard_map/ppermute | solution.py:1033
  9.6 5.8 %collective-permute-start.4 = (f32[80,128]{1,0:T(8,128)S(1)}, f32[80,128]{1,0:T(8,128)S(1)}, u32[]{:S(2)}, u32[]{:S(2)}) collective-permute-start(f32[80,128]{1,0:T(8,128)S(1)} %pack_far.1.after_ref), channel_id=1, source_target_pairs={{0,8},{1,9},{4,12},{5,13},{8,0},{9,1},{12,4},{13,5},{2,10},{3,11},... | collective-permute-start | bytes 122888 | tf_op jit(solution)/shard_map/ppermute | solution.py:44
  12.0 3.4 %collective-permute-start.5 = (f32[80,128]{1,0:T(8,128)S(1)}, f32[80,128]{1,0:T(8,128)S(1)}, u32[]{:S(2)}, u32[]{:S(2)}) collective-permute-start(f32[80,128]{1,0:T(8,128)S(1)} %get-tuple-element.14), channel_id=1, source_target_pairs={{0,1},{1,0},{4,8},{5,9},{8,4},{9,5},{12,13},{13,12},{2,3},{3,2},{6... | collective-permute-start | bytes 122888 | tf_op jit(solution)/shard_map/ppermute | solution.py:44
  12.0 4.1 %collective-permute-start.6 = (f32[80,128]{1,0:T(8,128)S(1)}, f32[80,128]{1,0:T(8,128)S(1)}, u32[]{:S(2)}, u32[]{:S(2)}) collective-permute-start(f32[80,128]{1,0:T(8,128)S(1)} %get-tuple-element.15.after_ref), channel_id=1, source_target_pairs={{0,4},{1,5},{4,0},{5,1},{8,12},{9,13},{12,8},{13,9},{2,6},{3,7},{6... | collective-permute-start | bytes 122888 | tf_op jit(solution)/shard_map/ppermute | solution.py:44

commit v15 on v14

--- a/solution.py
+++ b/solution.py
@@ -551,7 +551,8 @@
         for layer in range(layers):
             pairs["got", g, layer] = edges(ref[layer])
     slots, _ = lane_slots(layers, rows // SUBLANES, len(got_refs))
-    sent_ref[...] = write_lanes([pairs[key] for key in slots])
+    sent_ref[...] = jnp.zeros(sent_ref.shape, jnp.float32)
+    sent_ref[:SUBLANES] = write_lanes([pairs[key] for key in slots])
 
 
 def pooled_halos(both, pooled, got):
@@ -560,7 +561,7 @@
         functools.partial(halos_kernel, len(got) == 2),
         out_shape=(
             jax.ShapeDtypeStruct((len(got), SUBLANES, lanes), jnp.float32),
-            jax.ShapeDtypeStruct((SUBLANES, LANES), jnp.float32),
+            jax.ShapeDtypeStruct((LANES, LANES), jnp.float32),
         ),
         in_specs=[VMEM] * (2 + len(got)),
         out_specs=(VMEM,) * 2,
@@ -571,7 +572,7 @@
     )(both, pooled, *got)
 
 
-def pack_far_kernel(wide, pooled_ref, halo_ref, lanes_ref, *far_refs):
+def pack_far_kernel(wide, pooled_ref, halo_ref, *far_refs):
     half = pooled_ref.shape[2] // 2
     low = lax.axis_index("gx") % 4 < 2
 
@@ -586,23 +587,22 @@
     for group, ref in enumerate(far_refs):
         for i, (right, left) in enumerate(zip(tiles(1), tiles(0))):
             put(ref, i * (half // LANES), jnp.where(low, *((right, left) if group == 0 else (left, right))))
-        put(ref, 4 * (half // LANES), lanes_ref[...])
-        for spare in range(4 * (half // LANES) + 1, ref.shape[0] // SUBLANES):
+        for spare in range(4 * (half // LANES), ref.shape[0] // SUBLANES):
             put(ref, spare, jnp.zeros((SUBLANES, LANES), jnp.float32))
 
 
-def pack_far(pooled, halos, early, n_far, wide):
+def pack_far(pooled, halos, n_far, wide):
     _, rows, lanes = pooled.shape
     far_rows = max(2 * lanes // LANES + 1, 0 if wide else near_layout(lanes, wide)[1]) * SUBLANES
     return pl.pallas_call(
         functools.partial(pack_far_kernel, wide),
         out_shape=(jax.ShapeDtypeStruct((far_rows, LANES), jnp.float32),) * n_far,
-        in_specs=[VMEM] * 3,
+        in_specs=[VMEM] * 2,
         out_specs=(VMEM,) * n_far,
         compiler_params=pltpu.CompilerParams(vmem_limit_bytes=8 << 20),
         cost_estimate=pl.CostEstimate(flops=1_000_000, bytes_accessed=500_000, transcendentals=0),
         name="pack_far",
-    )(pooled, halos, early)
+    )(pooled, halos)
 
 
 def pack_near_kernel(wide, pooled_ref, halo_ref, early_ref, after_ref, *refs):
@@ -624,11 +624,11 @@
     slots, shared = lane_slots(layers, 2, len(got_refs))
 
     def strip_lanes(layer):
-        tiles = tuple(read_lanes(early_ref[...], slots["got", g, layer]) for g in range(len(got_refs)))
+        tiles = tuple(read_lanes(early_ref[:SUBLANES], slots["got", g, layer]) for g in range(len(got_refs)))
         return from_right(even, tiles), from_left(even, tiles)
 
     def halo_lanes(i):
-        return read_lanes(early_ref[...], slots["halo", i // 2, i % 2])
+        return read_lanes(early_ref[:SUBLANES], slots["halo", i // 2, i % 2])
 
     def near_tiles(order, strips, halos):
         near, beyond = order[0] // 2, order[-1] // 2
@@ -667,7 +667,7 @@
     def side(order):
         tiles = near_tiles(order, strips, halos)
         tiles["source"] = sources[order[-1] // 2]
-        lanes_tile = early_ref[...]
+        lanes_tile = early_ref[:SUBLANES]
         n_halos = 4 if wide else 2
         beside = near_tiles(
             order, [strip_lanes(layer) for layer in range(layers)], [halo_lanes(i) for i in range(n_halos)]
@@ -787,9 +787,27 @@
     return pick(low, tuple(take(ref, i * count, count) for ref in refs))
 
 
+def far_lanes_kernel(lanes, after_ref, *refs):
+    *far_refs, sent_ref = refs
+    low = lax.axis_index("gx") % 4 < 2
+    sent_ref[...] = write_lanes([edges(far_part(far_refs, low, lanes, side, 0)) for side in range(2)])
+
+
+def far_lanes(after, far, lanes):
+    return pl.pallas_call(
+        functools.partial(far_lanes_kernel, lanes),
+        out_shape=jax.ShapeDtypeStruct((SUBLANES, LANES), jnp.float32),
+        in_specs=[ANY] + [VMEM] * len(far),
+        out_specs=VMEM,
+        compiler_params=pltpu.CompilerParams(vmem_limit_bytes=4 << 20),
+        cost_estimate=pl.CostEstimate(flops=1_000_000, bytes_accessed=100_000, transcendentals=0),
+        name="far_lanes",
+    )(after, *far)
+
+
 def coarse_part(peers, n_far, own_ref, halo_ref, pool_ref, first_ref, second_ref, *refs):
     near_refs, far_refs = (first_ref, second_ref), refs[:n_far]
-    early_ref, coef_ref, out_ref, wide_ref, *scratch = refs[n_far:]
+    early_ref, beyond_ref, coef_ref, out_ref, wide_ref, *scratch = refs[n_far:]
     ix, iy, iz = (lax.axis_index(axis) for axis in AXES)
     nx, ny, nz = peers
     wide = ny > 2
@@ -799,12 +817,8 @@
     top = iota((rows, lanes + LANES), 0) < REACH
     slots, shared = lane_slots(REACH, 2, 2 if wide else 1)
     near_slots = near_lane_slots(fine_lanes, wide, shared)
-    own_lanes = early_ref[...]
+    own_lanes = early_ref[:SUBLANES]
     near_lanes = [near_part(near_refs, even, fine_lanes, wide, side, "lanes") for side in range(2)]
-    far_lanes = [
-        pick(low, tuple(take(ref, 4 * (lanes // LANES), 1) for ref in far_refs))
-        for pick in (from_left, from_right)
-    ]
 
     def columns(half):
         return slice(half * lanes, (half + 1) * lanes)
@@ -818,7 +832,7 @@
 
     def far(side, i):
         core = far_part(far_refs, low, fine_lanes, side, i)
-        return join(core, far_lanes[side], slots["pooled", 1 - side, 0])
+        return join(core, beyond_ref[...], side)
 
     def split(tile, a):
         other = turned(tile, REACH, 0)
@@ -904,7 +918,7 @@
     far_refs = refs[2 : 2 + n_far]
     second_near_ref, first_near_ref, early_ref, coef_ref = refs[2 + n_far : 6 + n_far]
     near_refs = first_near_ref, second_near_ref
-    own_ref, halo_ref, pool_ref, inverse_ref, tx_ref, fine_ref, diff_ref, *scratch = refs[6 + n_far :]
+    own_ref, halo_ref, pool_ref, beyond_ref, inverse_ref, tx_ref, fine_ref, diff_ref, *scratch = refs[6 + n_far :]
     scratch, (spread_ref, *coarse_scratch) = scratch[:10], scratch[10:]
     coarse_part(
         peers,
@@ -915,6 +929,7 @@
         *near_refs,
         *far_refs,
         early_ref,
+        beyond_ref,
         coef_ref,
         spread_ref,
         *coarse_scratch,
@@ -924,7 +939,7 @@
     upper = iota((SUBLANES, lanes + LANES), 0) < REACH
     slots, shared = lane_slots(layers, rows // SUBLANES, n_got)
     near_slots = near_lane_slots(lanes, wide, shared)
-    own_lanes = early_ref[...]
+    own_lanes = early_ref[:SUBLANES]
     near_lanes = [near_part(near_refs, even, lanes, wide, side, "lanes") for side in range(2)]
 
     def join(core, tile, *keys):
@@ -992,14 +1007,14 @@
     )
 
 
-def levels(both, got, raw, far, near, early, coefficients, own, halos, pooled, ready, peers):
+def levels(both, got, raw, far, near, early, coefficients, own, halos, pooled, beyond, ready, peers):
     layers, rows, lanes = both.shape[0] // 2, *both.shape[1:]
     half = lanes // 2
     out = jax.ShapeDtypeStruct((layers, rows, lanes), jnp.float32)
     return pl.pallas_call(
         functools.partial(levels_kernel, peers, len(far)),
         out_shape=(out, out),
-        in_specs=[VMEM] * (12 + len(got) + len(far)),
+        in_specs=[VMEM] * (13 + len(got) + len(far)),
         out_specs=(VMEM, VMEM),
         scratch_shapes=window_scratch(3 * layers, rows, rows + 2 * REACH, lanes // LANES + 1)
         + [
@@ -1011,7 +1026,7 @@
         compiler_params=pltpu.CompilerParams(vmem_limit_bytes=32 << 20),
         cost_estimate=pl.CostEstimate(flops=20_000_000, bytes_accessed=10_000_000, transcendentals=0),
         name="levels",
-    )(both, *got, *raw[::-1], *far, *near[::-1], early, coefficients, own, halos, pooled, *ready)
+    )(both, *got, *raw[::-1], *far, *near[::-1], early, coefficients, own, halos, pooled, beyond, *ready)
 
 
 def shards(peers, log_perm, source, low_bound, high_bound):
@@ -1031,7 +1046,7 @@
     far_groups = far_pairs(nx)
     halos, lanes_sent = pooled_halos(both, own, got)
     early = lax.ppermute(lanes_sent, "gz", [(0, 1), (1, 0)])
-    for_far = pack_far(own, halos, early, len(far_groups), ny > 2)
+    for_far = pack_far(own, halos, len(far_groups), ny > 2)
     far = [permute(tiles, "gx", nx, group) for tiles, group in zip(for_far, far_groups)]
     for_first, for_second = pack_near(own, halos, early, for_far[0], got)
     second = permute(for_second, "gx", nx, neighbour_pairs(nx, 1))
@@ -1039,7 +1054,8 @@
     coefficients = chebyshev_coefficients(low_bound, high_bound, for_first)
     pooled = pool(coefficients, raw)
     ready = ahead(pooled, both, raw, nx)
-    return levels(both, got, raw, far, near, early, coefficients, own, halos, pooled, ready, peers)
+    beyond = lax.ppermute(far_lanes(coefficients, far, lanes), "gz", [(0, 1), (1, 0)])
+    return levels(both, got, raw, far, near, early, coefficients, own, halos, pooled, beyond, ready, peers)
 
 
 def solution(mesh):

time: 19.3 us -> 18.5 us (0.959)
  waiting for transfers between devices: 1.84 us -> 0.83 us
    ppermute x1, waiting for transfers between devices: 1.15 us -> 0.01 us  [shards(): early = lax.ppermute(lanes_sent, 'gz', [(0, 1), (1, 0)])]
    ppermute x0 -> x1, waiting for transfers between devices: none -> 0.72 us  [shards(): lax.ppermute(far_lanes(coefficients, far, lanes), 'gz', [(0, 1), (1, 0)])]
    ppermute x6, waiting for transfers between devices: 0.68 us -> 0.11 us  [permute(): return lax.ppermute(value, (axis, 'gz'), moves)]
  transfers between devices with their start and end apart: 7 -> 8, of which waited for: 2 -> 2; matrix products, arithmetic and copies ran while one was open for 0% -> 0% of each run, Pallas kernels for 4% -> 5%
where the time goes in v15:
time: 18.5 us; the launch traced here: 18.3 us
  starting transfers between devices  10.3 us (56%)
  Pallas kernels  4.19 us (23%)
  between operations  2.03 us (11%)
  local copies, waits for them, and re-layouts  0.97 us (5%)
  waiting for transfers between devices  0.83 us (4%)
    ppermute x6, starting transfers between devices, permute(): return lax.ppermute(value, (axis, 'gz'), moves)  10.3 us
    pallas_call x1, Pallas kernels, levels(): pl.pallas_call(functools.partial(levels_kernel, peers, len(far)), out_sha...  3.06 us
    unnamed x3, local copies, waits for them, and re-layouts  0.96 us
    ppermute x1, waiting for transfers between devices, shards(): lax.ppermute(far_lanes(coefficients, far, lanes), 'gz', [(0, 1), (1, 0)])  0.72 us
  transfers between devices with their start and end apart: 8, of which 2 were waited for; matrix products, arithmetic and copies ran while one was open for 0% of the time, Pallas kernels for 5%

profile of v15, /device:TPU:0, one launch (start us, length us, event | category | flops | bytes accessed | tf_op | source)
XLA Modules:
  0.0 18.3 jit_solution(8742087209896002257)
XLA Ops:
  0.6 0.0 copy-start
  0.6 0.9 %constant_dynamic-update-slice_fusion.1 = f32[8,16,512]{2,1,0:T(8,128)S(1)} fusion(f32[4,16,512]{2,1,0:T(8,128)} %param.4), kind=kLoop, calls=%fused_computation.1 | loop fusion | bytes 262144
  1.6 0.0 copy-done
  1.6 0.2 %prep.1 = (f32[2,8,512]{2,1,0:T(8,128)S(1)}, f32[5,8,512]{2,1,0:T(8,128)S(1)}) custom-call(f32[8,16,512]{2,1,0:T(8,128)S(1)} %constant_dynamic-update-slice_fusion.both_ref), custom_call_target="tpu_custom_call" | custom-call | flops 5000000 | bytes 700000 | tf_op jit(solution)/shard_map/prep/pallas_call | solution.py:449
  1.8 3.0 %collective-permute-start = (f32[5,8,512]{2,1,0:T(8,128)S(1)}, f32[5,8,512]{2,1,0:T(8,128)S(1)}, u32[]{:S(2)}, u32[]{:S(2)}) collective-permute-start(f32[5,8,512]{2,1,0:T(8,128)S(1)} %get-tuple-element.10.after_ref), channel_id=1, source_target_pairs={{0,2},{1,3},{2,0},{3,1},{4,6},{5,7},{6,4},{7,5},{8,10},{9,11},{10,... | collective-permute-start | bytes 245768 | tf_op jit(solution)/shard_map/ppermute | solution.py:44
  4.9 0.1 collective-permute-start.1
  5.0 3.2 %collective-permute-start.2 = (f32[7,16,512]{2,1,0:T(8,128)S(1)}, f32[7,16,512]{2,1,0:T(8,128)S(1)}, u32[]{:S(2)}, u32[]{:S(2)}) collective-permute-start(f32[7,16,512]{2,1,0:T(8,128)S(1)} %raw_block.3), channel_id=1, source_target_pairs={{0,4},{1,5},{4,0},{5,1},{8,12},{9,13},{12,8},{13,9},{2,6},{3,7},{6... | collective-permute-start | bytes 688136 | tf_op jit(solution)/shard_map/ppermute | solution.py:44
  8.2 0.0 collective-permute-done.refs_0_
  8.2 0.2 %halos.1 = (f32[1,8,512]{2,1,0:T(8,128)S(1)}, f32[128,128]{1,0:T(8,128)S(1)}) custom-call(f32[8,16,512]{2,1,0:T(8,128)S(1)} %constant_dynamic-update-slice_fusion.both_ref, f32[2,8,512]{2,1,0:T(8,128)S(1)} %get-tuple-element.11.pooled_ref.refs_8_, f32[5,8,512]{2,1,0:T(8,128)S(1)} %collective-permute-done.refs_0_), custom_call_target="tpu_custom_call" | custom-call | flops 49999998976 | bytes 1000000 | tf_op jit(solution)/shard_map/halos/pallas_call | solution.py:560
  8.4 0.0 collective-permute-start.4
  8.5 2.3 %collective-permute-start.3 = (f32[80,128]{1,0:T(8,128)S(1)}, f32[80,128]{1,0:T(8,128)S(1)}, u32[]{:S(2)}, u32[]{:S(2)}) collective-permute-start(f32[80,128]{1,0:T(8,128)S(1)} %pack_far.1.after_ref), channel_id=1, source_target_pairs={{0,8},{1,9},{4,12},{5,13},{8,0},{9,1},{12,4},{13,5},{2,10},{3,11},... | collective-permute-start | bytes 122888 | tf_op jit(solution)/shard_map/ppermute | solution.py:44
  10.7 0.0 collective-permute-done.4.early_ref.refs_6_
  10.7 0.1 pack_near.1
  10.9 0.2 %collective-permute-start.5 = (f32[80,128]{1,0:T(8,128)S(1)}, f32[80,128]{1,0:T(8,128)S(1)}, u32[]{:S(2)}, u32[]{:S(2)}) collective-permute-start(f32[80,128]{1,0:T(8,128)S(1)} %get-tuple-element.14), channel_id=1, source_target_pairs={{0,1},{1,0},{4,8},{5,9},{8,4},{9,5},{12,13},{13,12},{2,3},{3,2},{6... | collective-permute-start | bytes 122888 | tf_op jit(solution)/shard_map/ppermute | solution.py:44
  11.1 1.5 %collective-permute-start.6 = (f32[80,128]{1,0:T(8,128)S(1)}, f32[80,128]{1,0:T(8,128)S(1)}, u32[]{:S(2)}, u32[]{:S(2)}) collective-permute-start(f32[80,128]{1,0:T(8,128)S(1)} %get-tuple-element.15.after_ref), channel_id=1, source_target_pairs={{0,4},{1,5},{4,0},{5,1},{8,12},{9,13},{12,8},{13,9},{2,6},{3,7},{6... | collective-permute-start | bytes 122888 | tf_op jit(solution)/shard_map/ppermute | solution.py:44
  13.9 0.1 collective-permute-done.3.refs_0_.refs_3_
  14.0 0.1 far_lanes.1
  14.1 0.0 collective-permute-start.7
  14.1 0.0 collective-permute-done.2.first_ref.refs_2_
  14.1 0.0 collective-permute-done.1.second_ref.refs_1_
  14.1 0.2 %pool.1.after_ref.refs_10_ = f32[96,128]{1,0:T(8,128)S(1)} custom-call(f32[7,8,128]{2,1,0:T(8,128)S(1)} %coefficients.1.after_ref.refs_7_, f32[7,16,512]{2,1,0:T(8,128)S(1)} %collective-permute-done.2.first_ref.refs_2_, f32[7,16,512]{2,1,0:T(8,128)S(1)} %collective-permute-done.1.second_ref.refs_1_), custom_call_target="tpu_custom_call" | custom-call | flops 1000000 | bytes 1000000 | tf_op jit(solution)/shard_map/pool/pallas_call | solution.py:721
  14.3 0.2 ahead.1
  14.5 0.7 %collective-permute-done.7.refs_11_ = f32[8,128]{1,0:T(8,128)S(1)} collective-permute-done((f32[8,128]{1,0:T(8,128)S(1)}, f32[8,128]{1,0:T(8,128)S(1)}, u32[]{:S(2)}, u32[]{:S(2)}) %collective-permute-start.7) | collective-permute-done | bytes 4128 | tf_op jit(solution)/shard_map/ppermute | solution.py:1057
  15.2 0.0 collective-permute-done.5.refs_4_
  15.2 0.0 collective-permute-done.6.refs_5_
  15.2 3.1 %levels.1 = (f32[4,16,512]{2,1,0:T(8,128)}, f32[4,16,512]{2,1,0:T(8,128)}) custom-call(f32[8,16,512]{2,1,0:T(8,128)S(1)} %constant_dynamic-update-slice_fusion.both_ref, f32[5,8,512]{2,1,0:T(8,128)S(1)} %collective-permute-done.refs_0_, f32[7,16,512]{2,1,0:T(8,128)S(1)} %collective-permute-done.1.second_ref.refs_1_, ...), custom_call_target="tpu_custom_call" | custom-call | flops 20000000 | bytes 10000000 | tf_op jit(solution)/shard_map/levels/pallas_call | solution.py:1014
  (5 shorter events, 0.1 us)
Async XLA Ops:
  0.6 1.0 %copy-start = (f32[4,16,512]{2,1,0:T(8,128)S(1)}, f32[4,16,512]{2,1,0:T(8,128)}, u32[]{:S(2)}) copy-start(f32[4,16,512]{2,1,0:T(8,128)} %param.5) | copy-start | bytes 393220
  1.8 6.3 %collective-permute-start = (f32[5,8,512]{2,1,0:T(8,128)S(1)}, f32[5,8,512]{2,1,0:T(8,128)S(1)}, u32[]{:S(2)}, u32[]{:S(2)}) collective-permute-start(f32[5,8,512]{2,1,0:T(8,128)S(1)} %get-tuple-element.10.after_ref), channel_id=1, source_target_pairs={{0,2},{1,3},{2,0},{3,1},{4,6},{5,7},{6,4},{7,5},{8,10},{9,11},{10,... | collective-permute-start | bytes 245768 | tf_op jit(solution)/shard_map/ppermute | solution.py:44
  4.9 9.3 %collective-permute-start.1 = (f32[7,16,512]{2,1,0:T(8,128)S(1)}, f32[7,16,512]{2,1,0:T(8,128)S(1)}, u32[]{:S(2)}, u32[]{:S(2)}) collective-permute-start(f32[7,16,512]{2,1,0:T(8,128)S(1)} %raw_block.2.after_ref), channel_id=1, source_target_pairs={{0,1},{1,0},{4,8},{5,9},{8,4},{9,5},{12,13},{13,12},{2,3},{3,2},{6... | collective-permute-start | bytes 688136 | tf_op jit(solution)/shard_map/ppermute | solution.py:44
  5.0 9.1 %collective-permute-start.2 = (f32[7,16,512]{2,1,0:T(8,128)S(1)}, f32[7,16,512]{2,1,0:T(8,128)S(1)}, u32[]{:S(2)}, u32[]{:S(2)}) collective-permute-start(f32[7,16,512]{2,1,0:T(8,128)S(1)} %raw_block.3), channel_id=1, source_target_pairs={{0,4},{1,5},{4,0},{5,1},{8,12},{9,13},{12,8},{13,9},{2,6},{3,7},{6... | collective-permute-start | bytes 688136 | tf_op jit(solution)/shard_map/ppermute | solution.py:44
  8.4 2.3 %collective-permute-start.4 = (f32[128,128]{1,0:T(8,128)S(1)}, f32[128,128]{1,0:T(8,128)S(1)}, u32[]{:S(2)}, u32[]{:S(2)}) collective-permute-start(f32[128,128]{1,0:T(8,128)S(1)} %get-tuple-element.13), channel_id=1, source_target_pairs={{0,1},{1,0},{2,3},{3,2},{4,5},{5,4},{6,7},{7,6},{8,9},{9,8},{10,11... | collective-permute-start | bytes 196616 | tf_op jit(solution)/shard_map/ppermute | solution.py:1048
  8.5 5.5 %collective-permute-start.3 = (f32[80,128]{1,0:T(8,128)S(1)}, f32[80,128]{1,0:T(8,128)S(1)}, u32[]{:S(2)}, u32[]{:S(2)}) collective-permute-start(f32[80,128]{1,0:T(8,128)S(1)} %pack_far.1.after_ref), channel_id=1, source_target_pairs={{0,8},{1,9},{4,12},{5,13},{8,0},{9,1},{12,4},{13,5},{2,10},{3,11},... | collective-permute-start | bytes 122888 | tf_op jit(solution)/shard_map/ppermute | solution.py:44
  10.9 4.3 %collective-permute-start.5 = (f32[80,128]{1,0:T(8,128)S(1)}, f32[80,128]{1,0:T(8,128)S(1)}, u32[]{:S(2)}, u32[]{:S(2)}) collective-permute-start(f32[80,128]{1,0:T(8,128)S(1)} %get-tuple-element.14), channel_id=1, source_target_pairs={{0,1},{1,0},{4,8},{5,9},{8,4},{9,5},{12,13},{13,12},{2,3},{3,2},{6... | collective-permute-start | bytes 122888 | tf_op jit(solution)/shard_map/ppermute | solution.py:44
  11.1 4.1 %collective-permute-start.6 = (f32[80,128]{1,0:T(8,128)S(1)}, f32[80,128]{1,0:T(8,128)S(1)}, u32[]{:S(2)}, u32[]{:S(2)}) collective-permute-start(f32[80,128]{1,0:T(8,128)S(1)} %get-tuple-element.15.after_ref), channel_id=1, source_target_pairs={{0,4},{1,5},{4,0},{5,1},{8,12},{9,13},{12,8},{13,9},{2,6},{3,7},{6... | collective-permute-start | bytes 122888 | tf_op jit(solution)/shard_map/ppermute | solution.py:44
  14.1 1.2 %collective-permute-start.7 = (f32[8,128]{1,0:T(8,128)S(1)}, f32[8,128]{1,0:T(8,128)S(1)}, u32[]{:S(2)}, u32[]{:S(2)}) collective-permute-start(f32[8,128]{1,0:T(8,128)S(1)} %far_lanes.1), channel_id=1, source_target_pairs={{0,1},{1,0},{2,3},{3,2},{4,5},{5,4},{6,7},{7,6},{8,9},{9,8},{10,11... | collective-permute-start | bytes 12296 | tf_op jit(solution)/shard_map/ppermute | solution.py:1057
